TPU v7x, 32 devices: a whole 2x2x4 slice. The times are simulated.
32 devices in a mesh: batch: 2 (over y), gy: 4 (over z), gx: 4 (over x, core).
Axes of the slice: x: 2, y: 2, z: 4, core: 2. Of those that a mesh axis runs over, the one named last changes fastest.
Arguments:
- x_fine: bfloat16 [2, 32, 128, 256], P('batch', 'gy', 'gx'), may hold values from -6 to 6
- dy_fine: bfloat16 [2, 32, 128, 256], P('batch', 'gy', 'gx'), may hold values from -6 to 6
- x_coarse: bfloat16 [2, 16, 16, 1024], P('batch', 'gy', 'gx'), may hold values from -6 to 6
- dy_coarse: bfloat16 [2, 16, 16, 1024], P('batch', 'gy', 'gx'), may hold values from -6 to 6
- timestep: int32 [2], P('batch'), may hold values from 0 to 999
- fine_gain: float32 [256], replicated, may hold values from 0.5 to 2.5, as said below
- coarse_gain: float32 [1024], replicated, may hold values from 0.5 to 2.5, as said below
- fine_qkv: bfloat16 [256, 768], replicated, may hold values from -0.375 to 0.375
- fine_out: bfloat16 [256, 256], replicated, may hold values from -0.375 to 0.375
- coarse_qkv: bfloat16 [3, 1024, 1024], P(None, ('gy', 'gx')), may hold values from -0.1875 to 0.1875
- coarse_out: bfloat16 [1024, 1024], P(('gy', 'gx')), may hold values from -0.1875 to 0.1875
Outputs:
- dx_fine: bfloat16 [2, 32, 128, 256], P('batch', 'gy', 'gx')
- dx_coarse: bfloat16 [2, 16, 16, 1024], P('batch', 'gy', 'gx')
- grad_fine_qkv: bfloat16 [256, 768], replicated
- grad_fine_out: bfloat16 [256, 256], replicated
- grad_coarse_qkv: bfloat16 [3, 1024, 1024], P(None, ('gy', 'gx'))
- grad_coarse_out: bfloat16 [1024, 1024], P(('gy', 'gx'))
Inputs may be any that keep to these rules, and one draw needn't show every extreme that they name: `fine_gain`: the norm gains are positive. `coarse_gain`: the norm gains are positive.
All inputs are finite; a program needn't handle non-finite values.
Results may differ from a plain program's by a relative error of at most 0.017.
The roundings to bfloat16 on the way count: a program that leaves them out, or rounds other values in their place, can miss the bound.
Values may be sent and summed in bfloat16 or wider, within the bound.
No kernel may reach another device: no remote copies, remote signals or barrier semaphores. Data moves between devices by JAX's collectives and lax.ppermute only.
A program may use at most 64 MiB of HBM per device.

v0:
```python
import math

import jax
import jax.numpy as jnp
from jax import lax
from jax.experimental import pallas as pl
from jax.experimental.pallas import tpu as pltpu
from jax.sharding import PartitionSpec as P

D_F = 256
H_F = 4
D_C = 1024
HD = 64
RAD = 3
HALO = 2 * RAD

eps = 1e-06
log_span = math.log(1000.0)
side = 8
extent = side + 2 * RAD
lanes_wide = 16
scale = 1.0 / math.sqrt(HD)
vmem_bytes = 48 * 1024 * 1024


def dot(first, second, dims=((1,), (0,))):
    return lax.dot_general(first, second, (dims, ((), ())), preferred_element_type=jnp.float32)


def time_gain(gains, step_value):
    channels = gains.shape[0]
    frequency = jnp.exp(-log_span * jnp.arange(channels, dtype=jnp.float32) / channels)
    return gains * (1.0 + 0.5 * jnp.cos(step_value.astype(jnp.float32) * frequency))


def inverse_rms(floats):
    return lax.rsqrt(jnp.mean(floats * floats, axis=-1, keepdims=True) + eps)


def norm_backward(floats, inverse, factor, upstream):
    scaled = upstream * factor
    middle = jnp.mean(floats * scaled, axis=-1, keepdims=True)
    return (inverse * scaled - floats * inverse * inverse * inverse * middle).astype(jnp.bfloat16)


def round_up(value, multiple):
    return -(-value // multiple) * multiple


def fine_body(
    limits,
    x_ref,
    dy_ref,
    above_ref,
    below_ref,
    left_ref,
    right_ref,
    factor_ref,
    qkv_ref,
    out_ref,
    dx_ref,
    keep_ref,
    send_ref,
    x_grid,
    dy_grid,
    k_grid,
    v_grid,
    q_grid,
    u_grid,
    dk_grid,
    dv_grid,
    dq_grid,
    a_grid,
    bias_ref,
    total_ref,
):
    height, breadth = x_ref.shape[0], x_ref.shape[1]
    grid_rows, grid_cols = x_grid.shape[0], x_grid.shape[1]
    query_rows = dy_grid.shape[0]
    floats = jnp.float32
    factor = factor_ref[...]

    x_grid[...] = jnp.zeros_like(x_grid)
    dy_grid[...] = jnp.zeros_like(dy_grid)
    dk_grid[...] = jnp.zeros_like(dk_grid)
    dv_grid[...] = jnp.zeros_like(dv_grid)
    inner = slice(HALO, HALO + breadth)
    x_grid[0:HALO, inner] = above_ref[0:HALO].astype(floats)
    x_grid[HALO : HALO + height, inner] = x_ref[...].astype(floats)
    x_grid[HALO + height : HALO + height + HALO, inner] = below_ref[0:HALO].astype(floats)
    dy_grid[0:RAD, inner] = above_ref[HALO : HALO + RAD].astype(floats)
    dy_grid[RAD : RAD + height, inner] = dy_ref[...].astype(floats)
    dy_grid[RAD + height : RAD + height + RAD, inner] = below_ref[HALO : HALO + RAD].astype(floats)
    for strip, first in ((left_ref, 0), (right_ref, HALO + breadth)):
        span = slice(first, first + HALO)
        at = 0
        for grid, begin, count in (
            (x_grid, 0, HALO),
            (dy_grid, 0, RAD),
            (x_grid, HALO, height),
            (dy_grid, RAD, height),
            (x_grid, HALO + height, HALO),
            (dy_grid, RAD + height, RAD),
        ):
            grid[begin : begin + count, span] = strip[at : at + count].astype(floats)
            at += count

    tokens = x_grid[...].reshape(grid_rows * grid_cols, D_F)
    normed = (tokens * inverse_rms(tokens) * factor).astype(jnp.bfloat16)
    key_values = dot(normed, qkv_ref[:, D_F:]).astype(jnp.bfloat16).astype(floats)
    k_grid[...] = key_values[:, :D_F].reshape(grid_rows, grid_cols, D_F)
    v_grid[...] = key_values[:, D_F:].reshape(grid_rows, grid_cols, D_F)
    query_tokens = normed[RAD * grid_cols : (RAD + query_rows) * grid_cols]
    queries = dot(query_tokens, qkv_ref[:, :D_F]).astype(jnp.bfloat16).astype(floats) * scale
    q_grid[...] = queries.reshape(query_rows, grid_cols, D_F)
    cotangents = dy_grid[...].reshape(query_rows * grid_cols, D_F).astype(jnp.bfloat16)
    ups = dot(cotangents, out_ref[...], ((1,), (1,))).astype(jnp.bfloat16).astype(floats)
    u_grid[...] = ups.reshape(query_rows, grid_cols, D_F)

    keys_count, heads_count = extent * lanes_wide, H_F * side * side
    key_at = lax.broadcasted_iota(jnp.int32, (keys_count, heads_count), 0)
    query_at = lax.broadcasted_iota(jnp.int32, (keys_count, heads_count), 1)
    row_gap = (key_at // lanes_wide) - ((query_at // side) % side)
    col_gap = (key_at % lanes_wide) - (query_at % side)
    near = (row_gap >= 0) & (row_gap <= 2 * RAD) & (col_gap >= 0) & (col_gap <= 2 * RAD)
    bias_ref[...] = jnp.where(near, 0.0, -1e30)
    row_low, row_high, col_low, col_high = limits[0], limits[1], limits[2], limits[3]
    lone = lax.broadcasted_iota(jnp.int32, (keys_count, 1), 0)
    head_of = lax.broadcasted_iota(jnp.int32, (side * side, D_F), 1) // HD

    def spread(block):
        return jnp.concatenate(
            [jnp.where(head_of == h, block, 0.0).astype(jnp.bfloat16) for h in range(H_F)], axis=0
        )

    def collect(full):
        total = jnp.where(head_of == 0, full[: side * side], 0.0)
        for h in range(1, H_F):
            piece = full[h * side * side : (h + 1) * side * side]
            total = jnp.where(head_of == h, piece, total)
        return total.reshape(side, side, D_F)

    for block_row in range(query_rows // side):
        top = block_row * side
        for block_col in range((grid_cols - side) // side):
            start = block_col * side
            window = (slice(top, top + extent), slice(start, start + lanes_wide))
            keys = k_grid[window].reshape(keys_count, D_F).astype(jnp.bfloat16)
            values = v_grid[window].reshape(keys_count, D_F).astype(jnp.bfloat16)
            place = (slice(top, top + side), slice(start + RAD, start + RAD + side))
            wide_queries = spread(q_grid[place].reshape(side * side, D_F))
            wide_ups = spread(u_grid[place].reshape(side * side, D_F))
            key_row = lone // lanes_wide + top
            key_col = lone % lanes_wide + start
            inside = (
                (key_row >= row_low)
                & (key_row < row_high)
                & (key_col >= col_low)
                & (key_col < col_high)
            )
            scores = dot(keys, wide_queries, ((1,), (1,)))
            scores = scores + (bias_ref[...] + jnp.where(inside, 0.0, -1e30))
            raised = jnp.exp(scores - jnp.max(scores, axis=0, keepdims=True))
            shares = raised * (1.0 / jnp.sum(raised, axis=0, keepdims=True))
            products = dot(values, wide_ups, ((1,), (1,)))
            centre = jnp.sum(shares * products, axis=0, keepdims=True)
            slopes = (shares * (products - centre)).astype(jnp.bfloat16)
            weights = shares.astype(jnp.bfloat16)
            dv_grid[window] += dot(weights, wide_ups).reshape(extent, lanes_wide, D_F)
            dk_grid[window] += dot(slopes, wide_queries).reshape(extent, lanes_wide, D_F)
            block = (slice(top, top + side), slice(start, start + side))
            a_grid[block] = collect(dot(weights, values, ((0,), (0,))))
            dq_grid[block] = collect(dot(slopes, keys, ((0,), (0,))))

    count = height * breadth
    own_queries = (slice(RAD, RAD + height), slice(RAD, RAD + breadth))
    own_keys = (slice(HALO, HALO + height), inner)
    attended = a_grid[own_queries].reshape(count, D_F).astype(jnp.bfloat16)
    grad_q = (dq_grid[own_queries].reshape(count, D_F) * scale).astype(jnp.bfloat16)
    grad_k = dk_grid[own_keys].reshape(count, D_F).astype(jnp.bfloat16)
    grad_v = dv_grid[own_keys].reshape(count, D_F).astype(jnp.bfloat16)
    grad_proj = jnp.concatenate([grad_q, grad_k, grad_v], axis=1)
    picture = x_ref[...].reshape(count, D_F).astype(floats)
    inverse = inverse_rms(picture)
    own_normed = (picture * inverse * factor).astype(jnp.bfloat16)
    flat_cot = dy_ref[...].reshape(count, D_F)
    grads = jnp.concatenate(
        [
            dot(own_normed, grad_proj, ((0,), (0,))),
            dot(attended, flat_cot, ((0,), (0,))),
        ],
        axis=1,
    )
    half, columns = keep_ref.shape[0], keep_ref.shape[1]
    total_ref[...] = grads.reshape(total_ref.shape)
    for low in range(2):
        target = (keep_ref, send_ref)[low]
        for high in range(half):
            for row in range(columns):
                block = (limits[4] ^ (2 * high + low)) * columns + (limits[5] ^ row)
                target[high, row] = total_ref[block].astype(target.dtype)
    down = dot(grad_proj, qkv_ref[...], ((1,), (1,)))
    dx_ref[...] = norm_backward(picture, inverse, factor, down).reshape(height, breadth, D_F)


def fine_block(peers, limits, picture, cotangent, above, below, left, right, factor, fine_qkv, fine_out):
    height, breadth = picture.shape[0], picture.shape[1]
    query_rows = round_up(height + 2 * RAD, side)
    query_cols = round_up(breadth + 2 * RAD, side)
    grid_rows, grid_cols = query_rows + 2 * RAD, query_cols + side
    across, down = peers
    rows = D_F // (across * down)
    halves = (across // 2, down, rows, 4 * D_F)
    vmem = pl.BlockSpec(memory_space=pltpu.VMEM)
    wide = pltpu.VMEM((grid_rows, grid_cols, D_F), jnp.float32)
    middle = pltpu.VMEM((query_rows, grid_cols, D_F), jnp.float32)
    small = pltpu.VMEM((query_rows, query_cols, D_F), jnp.float32)
    return pl.pallas_call(
        fine_body,
        out_shape=(
            jax.ShapeDtypeStruct((height, breadth, D_F), jnp.bfloat16),
            jax.ShapeDtypeStruct(halves, jnp.float32),
            jax.ShapeDtypeStruct(halves, jnp.bfloat16),
        ),
        in_specs=[pl.BlockSpec(memory_space=pltpu.SMEM)] + [vmem] * 9,
        out_specs=(vmem, vmem, vmem),
        scratch_shapes=[
            wide,
            middle,
            wide,
            wide,
            middle,
            middle,
            wide,
            wide,
            small,
            small,
            pltpu.VMEM((extent * lanes_wide, H_F * side * side), jnp.float32),
            pltpu.VMEM((across * down, rows, 4 * D_F), jnp.float32),
        ],
        compiler_params=pltpu.CompilerParams(vmem_limit_bytes=vmem_bytes),
        name="fine_block",
    )(limits, picture, cotangent, above, below, left, right, factor, fine_qkv, fine_out)


def coarse_body(x_ref, dy_ref, factor_ref, qkv_ref, out_ref, parts_ref, grads_ref):
    tokens = x_ref[...].astype(jnp.float32)
    normed = (tokens * inverse_rms(tokens) * factor_ref[...]).astype(jnp.bfloat16)
    cot = dy_ref[...]
    flat_qkv = qkv_ref[...].reshape(3 * HD, D_C)
    out_rows = out_ref[...]
    projected = dot(normed, flat_qkv, ((1,), (1,))).astype(jnp.bfloat16)
    queries, keys, values = projected[:, :HD], projected[:, HD : 2 * HD], projected[:, 2 * HD :]
    ups = dot(cot, out_rows, ((1,), (1,))).astype(jnp.bfloat16)
    scores = dot(queries, keys, ((1,), (1,))) * scale
    raised = jnp.exp(scores - jnp.max(scores, axis=-1, keepdims=True))
    shares = raised * (1.0 / jnp.sum(raised, axis=-1, keepdims=True))
    weights = shares.astype(jnp.bfloat16)
    mixed = dot(weights, values).astype(jnp.bfloat16)
    products = dot(ups, values, ((1,), (1,)))
    centre = jnp.sum(shares * products, axis=-1, keepdims=True)
    slopes = (shares * (products - centre)).astype(jnp.bfloat16)
    grad_q = (dot(slopes, keys) * scale).astype(jnp.bfloat16)
    grad_k = (dot(slopes, queries, ((0,), (0,))) * scale).astype(jnp.bfloat16)
    grad_v = dot(weights, ups, ((0,), (0,))).astype(jnp.bfloat16)
    stacked = jnp.concatenate([grad_q, grad_k, grad_v], axis=1)
    parts_ref[...] = dot(stacked, flat_qkv).astype(jnp.bfloat16)
    grads_ref[: 3 * HD] = dot(stacked, normed, ((0,), (0,))).astype(grads_ref.dtype)
    grads_ref[3 * HD :] = dot(mixed, cot, ((0,), (0,))).astype(grads_ref.dtype)


def coarse_block(tokens, cotangents, factor, head_qkv, head_out):
    count = tokens.shape[0]
    vmem = pl.BlockSpec(memory_space=pltpu.VMEM)
    return pl.pallas_call(
        coarse_body,
        out_shape=(
            jax.ShapeDtypeStruct((count, D_C), jnp.bfloat16),
            jax.ShapeDtypeStruct((4 * HD, D_C), jnp.bfloat16),
        ),
        in_specs=[vmem] * 5,
        out_specs=(vmem, vmem),
        compiler_params=pltpu.CompilerParams(vmem_limit_bytes=vmem_bytes),
        name="coarse_block",
    )(tokens, cotangents, factor, head_qkv, head_out)


def place_body(place, near_ref, far_ref, qkv_ref, out_ref):
    highs, downs, rows = near_ref.shape[0], near_ref.shape[1], near_ref.shape[2]
    for low in range(2):
        for high in range(highs):
            for row in range(downs):
                block = (place[0] ^ (2 * high + low)) * downs + (place[1] ^ row)
                at = pl.ds(pl.multiple_of(block * rows, rows), rows)
                piece = (near_ref, far_ref)[low][high, row]
                qkv_ref[at] = piece[:, : 3 * D_F]
                out_ref[at] = piece[:, 3 * D_F :]


def place_blocks(place, near, far):
    vmem = pl.BlockSpec(memory_space=pltpu.VMEM)
    return pl.pallas_call(
        place_body,
        out_shape=(
            jax.ShapeDtypeStruct((D_F, 3 * D_F), jnp.bfloat16),
            jax.ShapeDtypeStruct((D_F, D_F), jnp.bfloat16),
        ),
        in_specs=[pl.BlockSpec(memory_space=pltpu.SMEM), vmem, vmem],
        out_specs=(vmem, vmem),
        compiler_params=pltpu.CompilerParams(vmem_limit_bytes=vmem_bytes),
        name="place_blocks",
    )(place, near, far)


def neighbours(low_edge, high_edge, axis):
    peers = lax.axis_size(axis)
    up = [(i, i + 1) for i in range(peers - 1)]
    down = [(i + 1, i) for i in range(peers - 1)]
    return lax.ppermute(high_edge, axis, up), lax.ppermute(low_edge, axis, down)


def swapped(value, axis, mask):
    return lax.ppermute(value, axis, [(i, i ^ mask) for i in range(lax.axis_size(axis))])


def tied(*arrays):
    return lax.optimization_barrier(arrays)


def batch_sum(partial):
    images = lax.axis_size("batch")
    if images != 2:
        return lax.psum(partial, "batch").astype(jnp.float32)
    other = lax.ppermute(partial, "batch", [(0, 1), (1, 0)])
    return partial.astype(jnp.float32) + other.astype(jnp.float32)


def wide(value):
    return value.astype(jnp.float32)


def narrow(value):
    return value.astype(jnp.bfloat16)


def all_rows(piece):
    downs = lax.axis_size("gy")
    return jnp.stack([piece] + [swapped(piece, "gy", row) for row in range(1, downs)])


def row_sum(pieces):
    total = wide(pieces[0])
    for row in range(1, pieces.shape[0]):
        total = total + wide(swapped(narrow(pieces[row]), "gy", row))
    return total


def local(
    x_fine,
    dy_fine,
    x_coarse,
    dy_coarse,
    timestep,
    fine_gain,
    coarse_gain,
    fine_qkv,
    fine_out,
    coarse_qkv,
    coarse_out,
):
    step_value = timestep[0]
    picture, cotangent = x_fine[0], dy_fine[0]
    height, breadth = picture.shape[0], picture.shape[1]
    across, downs = lax.axis_size("gx"), lax.axis_size("gy")
    assert across == 4 and downs & (downs - 1) == 0
    gx, gy = lax.axis_index("gx"), lax.axis_index("gy")

    low = jnp.concatenate([picture[:HALO], cotangent[:RAD]], axis=0)
    high = jnp.concatenate([picture[height - HALO :], cotangent[height - RAD :]], axis=0)
    above, below = neighbours(low, high, "gy")
    coarse_tokens = x_coarse[0].reshape(-1, D_C)
    own = jnp.concatenate([coarse_tokens, dy_coarse[0].reshape(-1, D_C)], axis=1)
    count = own.shape[0]
    row_group = all_rows(own)
    column = jnp.concatenate([above, picture, cotangent, below], axis=0)
    column, row_group = tied(column, row_group)
    left, right = neighbours(column[:, :HALO], column[:, breadth - HALO :], "gx")
    left, right, row_group = tied(left, right, row_group)
    pair = jnp.stack([row_group, swapped(row_group, "gx", 2)])

    row_first = gy * height - HALO
    col_first = gx * breadth - HALO
    limits = jnp.stack(
        [
            -row_first,
            downs * height - row_first,
            -col_first,
            across * breadth - col_first,
            gx,
            gy,
        ]
    ).astype(jnp.int32)
    factor = time_gain(fine_gain, step_value)[None]
    coarse_factor = time_gain(coarse_gain, step_value)[None]
    dx_picture, fine_keep, fine_send = fine_block(
        (across, downs),
        limits,
        picture,
        cotangent,
        above,
        below,
        left,
        right,
        factor,
        fine_qkv,
        fine_out,
    )
    fine_send, pair = tied(fine_send, pair)

    fine_half = fine_keep + wide(swapped(fine_send, "gx", 1))
    other_pair = swapped(pair, "gx", 1)
    fine_half, other_pair = tied(fine_half, other_pair)

    everyone = jnp.stack([pair, other_pair]).reshape(-1, 2 * D_C)
    fine_quarter = fine_half[0] + wide(swapped(narrow(fine_half[1]), "gx", 2))
    parts, coarse_partial = coarse_block(
        everyone[:, :D_C], everyone[:, D_C:], coarse_factor, coarse_qkv, coarse_out
    )
    fine_quarter, parts, coarse_partial = tied(fine_quarter, parts, coarse_partial)

    coarse_sum = narrow(batch_sum(coarse_partial))
    parts = parts.reshape(2, 2, downs, count, D_C)
    fine_piece = row_sum(fine_quarter)
    coarse_half = wide(parts[0]) + wide(swapped(parts[1], "gx", 1))
    fine_piece, coarse_half = tied(fine_piece, coarse_half)

    fine_piece = narrow(batch_sum(fine_piece))
    coarse_quarter = wide(coarse_half[0]) + wide(swapped(narrow(coarse_half[1]), "gx", 2))
    fine_piece, coarse_quarter = tied(fine_piece, coarse_quarter)

    fine_rows = all_rows(fine_piece)
    coarse_down = row_sum(coarse_quarter)
    fine_rows, coarse_down = tied(fine_rows, coarse_down)

    fine_pair = jnp.stack([fine_rows, swapped(fine_rows, "gx", 2)])
    coarse_floats = wide(coarse_tokens)
    dx_coarse = norm_backward(
        coarse_floats, inverse_rms(coarse_floats), coarse_factor, coarse_down
    )
    fine_pair, dx_coarse, coarse_sum = tied(fine_pair, dx_coarse, coarse_sum)
    grad_qkv, grad_out = place_blocks(
        jnp.stack([gx, gy]).astype(jnp.int32), fine_pair, swapped(fine_pair, "gx", 1)
    )
    return (
        dx_picture[None],
        dx_coarse.reshape(x_coarse.shape),
        grad_qkv,
        grad_out,
        coarse_sum[: 3 * HD].reshape(coarse_qkv.shape),
        coarse_sum[3 * HD :],
    )


def solution(mesh):
    placed = (
        P("batch", "gy", "gx", None),
        P("batch", "gy", "gx", None),
        P("batch", "gy", "gx", None),
        P("batch", "gy", "gx", None),
        P("batch"),
        P(),
        P(),
        P(),
        P(),
        P(None, plane_spec, None),
        P(plane_spec, None),
    )
    return jax.shard_map(
        local,
        mesh=mesh,
        in_specs=placed,
        out_specs=(
            P("batch", "gy", "gx", None),
            P("batch", "gy", "gx", None),
            P(),
            P(),
            P(None, plane_spec, None),
            P(plane_spec, None),
        ),
        check_vma=False,
    )


plane_spec = ("gy", "gx")
```

profile of v0, /device:TPU:0, one launch (start us, length us, event | category | flops | bytes accessed | tf_op | source)
XLA Modules:
  0.0 85.4 jit_solution(8848202295032497923)
XLA Ops:
  0.6 0.8 reshape_squeeze.6
  1.5 0.8 reshape_squeeze.7
  2.3 5.1 %collective-permute-start.4 = (bf16[16,2048]{1,0:T(8,128)(2,1)S(1)}, bf16[16,2048]{1,0:T(8,128)(2,1)S(1)}, u32[]{:S(2)}, u32[]{:S(2)}) collective-permute-start(bf16[16,2048]{1,0:T(8,128)(2,1)S(1)} %constant_dynamic-update-slice_fusion), channel_id=1, source_target_pairs={{0,12},{4,8},{8,4},{12,0},{1,13},{5,9},{9,5},{13,1},{2,14},{6,10},... | collective-permute-start | bytes 196616 | tf_op jit(solution)/shard_map/ppermute | solution.py:323
  7.4 0.6 collective-permute-start.2
  8.1 3.3 %collective-permute-start = (bf16[9,32,256]{2,1,0:T(8,128)(2,1)S(1)}, bf16[9,32,256]{2,1,0:T(8,128)(2,1)S(1)}, u32[]{:S(2)}, u32[]{:S(2)}) collective-permute-start(bf16[9,32,256]{2,1,0:T(8,128)(2,1)S(1)} %pad_maximum_fusion.5), channel_id=1, source_target_pairs={{0,4},{4,8},{8,12},{1,5},{5,9},{9,13},{2,6},{6,10},{10,14},{3,7},{... | collective-permute-start | bytes 442376 | tf_op jit(solution)/shard_map/ppermute | solution.py:319
  11.4 1.3 %collective-permute-start.1 = (bf16[9,32,256]{2,1,0:T(8,128)(2,1)S(1)}, bf16[9,32,256]{2,1,0:T(8,128)(2,1)S(1)}, u32[]{:S(2)}, u32[]{:S(2)}) collective-permute-start(bf16[9,32,256]{2,1,0:T(8,128)(2,1)S(1)} %pad_maximum_fusion.6), channel_id=1, source_target_pairs={{4,0},{8,4},{12,8},{5,1},{9,5},{13,9},{6,2},{10,6},{14,10},{7,3},{... | collective-permute-start | bytes 442376 | tf_op jit(solution)/shard_map/ppermute | solution.py:319
  12.7 0.2 collective-permute-done.3
  13.0 1.7 %collective-permute-done.above_ref = bf16[9,32,256]{2,1,0:T(8,128)(2,1)S(1)} collective-permute-done((bf16[9,32,256]{2,1,0:T(8,128)(2,1)S(1)}, bf16[9,32,256]{2,1,0:T(8,128)(2,1)S(1)}, u32[]{:S(2)}, u32[]{:S(2)}) %collective-permute-start) | collective-permute-done | bytes 147488 | tf_op jit(solution)/shard_map/ppermute | solution.py:319
  14.7 3.7 %collective-permute-done.1.below_ref = bf16[9,32,256]{2,1,0:T(8,128)(2,1)S(1)} collective-permute-done((bf16[9,32,256]{2,1,0:T(8,128)(2,1)S(1)}, bf16[9,32,256]{2,1,0:T(8,128)(2,1)S(1)}, u32[]{:S(2)}, u32[]{:S(2)}) %collective-permute-start.1) | collective-permute-done | bytes 147488 | tf_op jit(solution)/shard_map/ppermute | solution.py:319
  18.5 0.1 pad_maximum_fusion.1
  18.6 1.4 %collective-permute-start.5 = (bf16[34,6,256]{2,1,0:T(8,128)(2,1)S(1)}, bf16[34,6,256]{2,1,0:T(8,128)(2,1)S(1)}, u32[]{:S(2)}, u32[]{:S(2)}) collective-permute-start(bf16[34,6,256]{2,1,0:T(8,128)(2,1)S(1)} %get-tuple-element.65), channel_id=1, source_target_pairs={{0,1},{1,2},{2,3},{4,5},{5,6},{6,7},{8,9},{9,10},{10,11},{12,13},{... | collective-permute-start | bytes 313352 | tf_op jit(solution)/shard_map/ppermute | solution.py:319
  20.0 1.3 %collective-permute-start.6 = (bf16[34,6,256]{2,1,0:T(8,128)(2,1)S(1)}, bf16[34,6,256]{2,1,0:T(8,128)(2,1)S(1)}, u32[]{:S(2)}, u32[]{:S(2)}) collective-permute-start(bf16[34,6,256]{2,1,0:T(8,128)(2,1)S(1)} %get-tuple-element.64), channel_id=1, source_target_pairs={{1,0},{2,1},{3,2},{5,4},{6,5},{7,6},{9,8},{10,9},{11,10},{13,12},{... | collective-permute-start | bytes 313352 | tf_op jit(solution)/shard_map/ppermute | solution.py:319
  21.4 3.7 %collective-permute-done.6.right_ref = bf16[34,6,256]{2,1,0:T(8,128)(2,1)S(1)} collective-permute-done((bf16[34,6,256]{2,1,0:T(8,128)(2,1)S(1)}, bf16[34,6,256]{2,1,0:T(8,128)(2,1)S(1)}, u32[]{:S(2)}, u32[]{:S(2)}) %collective-permute-start.6) | collective-permute-done | bytes 104480 | tf_op jit(solution)/shard_map/ppermute | solution.py:319
  25.0 3.4 %collective-permute-start.7 = (bf16[4,16,2048]{2,1,0:T(8,128)(2,1)S(1)}, bf16[4,16,2048]{2,1,0:T(8,128)(2,1)S(1)}, u32[]{:S(2)}, u32[]{:S(2)}) collective-permute-start(bf16[4,16,2048]{2,1,0:T(8,128)(2,1)S(1)} %pad_maximum_fusion.3), channel_id=1, source_target_pairs={{0,2},{1,3},{2,0},{3,1},{4,6},{5,7},{6,4},{7,5},{8,10},{9,11},{10,... | collective-permute-start | bytes 786440 | tf_op jit(solution)/shard_map/ppermute | solution.py:323
  29.0 0.1 stack.89.limits
  29.1 0.7 copy-done.8
  29.8 0.1 add_multiply_fusion.1
  29.9 6.6 %fine_block.1 = (bf16[8,32,256]{2,1,0:T(8,128)(2,1)}, f32[2,4,16,1024]{3,2,1,0:T(8,128)S(1)}, bf16[2,4,16,1024]{3,2,1,0:T(8,128)(2,1)S(1)}) custom-call(s32[6]{0:T(128)S(1)} %stack.89.limits, bf16[8,32,256]{2,1,0:T(8,128)(2,1)S(1)} %bitcast.72, bf16[8,32,256]{2,1,0:T(8,128)(2,1)S(1)} %bitcast.74, bf16[9,32,256]{2,1,0:T(8,128)(2,1)S(1)} %collective-permute-done.above_ref, ...), custom_call_target="tpu_custom_call" | custom-call | tf_op jit(solution)/shard_map/fine_block/pallas_call | solution.py:218
  36.5 0.3 collective-permute-start.8
  36.8 0.3 collective-permute-start.9
  37.1 0.1 copy-done.6
  37.2 0.1 multiply_reduce_fusion
  37.3 0.1 add_multiply_fusion
  37.4 0.7 collective-permute-done.8
  38.1 0.1 convert_add_fusion.1
  38.2 0.7 collective-permute-done.9
  38.9 1.7 %collective-permute-start.10 = (bf16[4,16,1024]{2,1,0:T(8,128)(2,1)S(1)}, bf16[4,16,1024]{2,1,0:T(8,128)(2,1)S(1)}, u32[]{:S(2)}, u32[]{:S(2)}) collective-permute-start(bf16[4,16,1024]{2,1,0:T(8,128)(2,1)S(1)} %fusion), channel_id=1, source_target_pairs={{0,2},{1,3},{2,0},{3,1},{4,6},{5,7},{6,4},{7,5},{8,10},{9,11},{10,... | collective-permute-start | bytes 393224 | tf_op jit(solution)/shard_map/ppermute | solution.py:323
  40.6 0.1 pad_maximum_fusion
  40.7 0.1 fusion.12
  40.8 0.9 %copy-done.3 = bf16[3,64,1024]{2,1,0:T(8,128)(2,1)S(1)} copy-done((bf16[3,64,1024]{2,1,0:T(8,128)(2,1)S(1)}, bf16[3,64,1024]{2,1,0:T(8,128)(2,1)}, u32[]{:S(2)}) %copy-start.3) | copy-done | bytes 393240
  41.7 1.7 %coarse_block.1 = (bf16[256,1024]{1,0:T(8,128)(2,1)S(1)}, bf16[256,1024]{1,0:T(8,128)(2,1)S(1)}) custom-call(bf16[256,1024]{1,0:T(8,128)(2,1)S(1)} %get-tuple-element.63.x_ref, bf16[256,1024]{1,0:T(8,128)(2,1)S(1)} %get-tuple-element.62.dy_ref, f32[1,1024]{1,0:T(1,128)S(1)} %bitcast.75, bf16[3,64,1024]{2,1,0:T(8,128)(2,1)S(1)} %copy-done.3, ...), custom_call_target="tpu_custom_call" | custom-call | tf_op jit(solution)/shard_map/coarse_block/pallas_call | solution.py:275
  43.5 1.2 %collective-permute-done.10 = bf16[4,16,1024]{2,1,0:T(8,128)(2,1)S(1)} collective-permute-done((bf16[4,16,1024]{2,1,0:T(8,128)(2,1)S(1)}, bf16[4,16,1024]{2,1,0:T(8,128)(2,1)S(1)}, u32[]{:S(2)}, u32[]{:S(2)}) %collective-permute-start.10) | collective-permute-done | bytes 131104 | tf_op jit(solution)/shard_map/ppermute | solution.py:323
  44.7 2.0 %collective-permute-start.13 = (bf16[16,1024]{1,0:T(8,128)(2,1)S(1)}, bf16[16,1024]{1,0:T(8,128)(2,1)S(1)}, u32[]{:S(2)}, u32[]{:S(2)}) collective-permute-start(bf16[16,1024]{1,0:T(8,128)(2,1)S(1)} %get-tuple-element.72), channel_id=1, source_target_pairs={{0,12},{4,8},{8,4},{12,0},{1,13},{5,9},{9,5},{13,1},{2,14},{6,10},... | collective-permute-start | bytes 98312 | tf_op jit(solution)/shard_map/ppermute | solution.py:323
  46.7 1.1 %collective-permute-start.12 = (bf16[16,1024]{1,0:T(8,128)(2,1)S(1)}, bf16[16,1024]{1,0:T(8,128)(2,1)S(1)}, u32[]{:S(2)}, u32[]{:S(2)}) collective-permute-start(bf16[16,1024]{1,0:T(8,128)(2,1)S(1)} %get-tuple-element.73), channel_id=1, source_target_pairs={{0,8},{4,12},{8,0},{12,4},{1,9},{5,13},{9,1},{13,5},{2,10},{6,14},... | collective-permute-start | bytes 98312 | tf_op jit(solution)/shard_map/ppermute | solution.py:323
  47.8 1.4 %collective-permute-start.11 = (bf16[16,1024]{1,0:T(8,128)(2,1)S(1)}, bf16[16,1024]{1,0:T(8,128)(2,1)S(1)}, u32[]{:S(2)}, u32[]{:S(2)}) collective-permute-start(bf16[16,1024]{1,0:T(8,128)(2,1)S(1)} %get-tuple-element.71), channel_id=1, source_target_pairs={{0,4},{4,0},{8,12},{12,8},{1,5},{5,1},{9,13},{13,9},{2,6},{6,2},{1... | collective-permute-start | bytes 98312 | tf_op jit(solution)/shard_map/ppermute | solution.py:323
  49.2 0.1 collective-permute-start.14
  49.3 0.1 rsqrt.12
  49.4 1.5 %collective-permute-start.24 = (bf16[256,1024]{1,0:T(8,128)(2,1)S(1)}, bf16[256,1024]{1,0:T(8,128)(2,1)S(1)}, u32[]{:S(2)}, u32[]{:S(2)}) collective-permute-start(bf16[256,1024]{1,0:T(8,128)(2,1)S(1)} %get-tuple-element.56), channel_id=1, source_target_pairs={{0,16},{16,0},{1,17},{17,1},{2,18},{18,2},{3,19},{19,3},{4,20},{20... | collective-permute-start | bytes 1572872 | tf_op jit(solution)/shard_map/ppermute | solution.py:334
  50.9 0.6 collective-permute-done.12
  51.5 0.3 collective-permute-done.11
  51.9 0.1 convert_add_fusion
  51.9 1.6 %collective-permute-start.15 = (f32[16,1024]{1,0:T(8,128)S(1)}, f32[16,1024]{1,0:T(8,128)S(1)}, u32[]{:S(2)}, u32[]{:S(2)}) collective-permute-start(f32[16,1024]{1,0:T(8,128)S(1)} %fusion.11), channel_id=1, source_target_pairs={{0,16},{16,0},{1,17},{17,1},{2,18},{18,2},{3,19},{19,3},{4,20},{20... | collective-permute-start | bytes 196616 | tf_op jit(solution)/shard_map/ppermute | solution.py:334
  53.5 1.8 %collective-permute-start.16 = (bf16[4,16,1024]{2,1,0:T(8,128)(2,1)S(1)}, bf16[4,16,1024]{2,1,0:T(8,128)(2,1)S(1)}, u32[]{:S(2)}, u32[]{:S(2)}) collective-permute-start(bf16[4,16,1024]{2,1,0:T(8,128)(2,1)S(1)} %fusion.1), channel_id=1, source_target_pairs={{0,2},{1,3},{2,0},{3,1},{4,6},{5,7},{6,4},{7,5},{8,10},{9,11},{10,... | collective-permute-start | bytes 393224 | tf_op jit(solution)/shard_map/ppermute | solution.py:323
  55.3 9.7 %collective-permute-done.15 = f32[16,1024]{1,0:T(8,128)S(1)} collective-permute-done((f32[16,1024]{1,0:T(8,128)S(1)}, f32[16,1024]{1,0:T(8,128)S(1)}, u32[]{:S(2)}, u32[]{:S(2)}) %collective-permute-start.15) | collective-permute-done | bytes 65568 | tf_op jit(solution)/shard_map/ppermute | solution.py:334
  65.1 2.0 %collective-permute-start.19 = (bf16[16,1024]{1,0:T(8,128)(2,1)S(1)}, bf16[16,1024]{1,0:T(8,128)(2,1)S(1)}, u32[]{:S(2)}, u32[]{:S(2)}) collective-permute-start(bf16[16,1024]{1,0:T(8,128)(2,1)S(1)} %add_convert_fusion.1), channel_id=1, source_target_pairs={{0,12},{4,8},{8,4},{12,0},{1,13},{5,9},{9,5},{13,1},{2,14},{6,10},... | collective-permute-start | bytes 98312 | tf_op jit(solution)/shard_map/ppermute | solution.py:323
  67.1 0.2 collective-permute-start.18
  67.3 2.3 %collective-permute-start.17 = (bf16[16,1024]{1,0:T(8,128)(2,1)S(1)}, bf16[16,1024]{1,0:T(8,128)(2,1)S(1)}, u32[]{:S(2)}, u32[]{:S(2)}) collective-permute-start(bf16[16,1024]{1,0:T(8,128)(2,1)S(1)} %add_convert_fusion.1), channel_id=1, source_target_pairs={{0,4},{4,0},{8,12},{12,8},{1,5},{5,1},{9,13},{13,9},{2,6},{6,2},{1... | collective-permute-start | bytes 98312 | tf_op jit(solution)/shard_map/ppermute | solution.py:323
  69.6 2.0 %collective-permute-start.22 = (bf16[16,1024]{1,0:T(8,128)(2,1)S(1)}, bf16[16,1024]{1,0:T(8,128)(2,1)S(1)}, u32[]{:S(2)}, u32[]{:S(2)}) collective-permute-start(bf16[16,1024]{1,0:T(8,128)(2,1)S(1)} %get-tuple-element.69), channel_id=1, source_target_pairs={{0,12},{4,8},{8,4},{12,0},{1,13},{5,9},{9,5},{13,1},{2,14},{6,10},... | collective-permute-start | bytes 98312 | tf_op jit(solution)/shard_map/ppermute | solution.py:323
  71.6 0.8 collective-permute-start.21
  72.4 1.7 %collective-permute-start.20 = (bf16[16,1024]{1,0:T(8,128)(2,1)S(1)}, bf16[16,1024]{1,0:T(8,128)(2,1)S(1)}, u32[]{:S(2)}, u32[]{:S(2)}) collective-permute-start(bf16[16,1024]{1,0:T(8,128)(2,1)S(1)} %get-tuple-element.68), channel_id=1, source_target_pairs={{0,4},{4,0},{8,12},{12,8},{1,5},{5,1},{9,13},{13,9},{2,6},{6,2},{1... | collective-permute-start | bytes 98312 | tf_op jit(solution)/shard_map/ppermute | solution.py:323
  74.1 1.5 %collective-permute-done.22 = bf16[16,1024]{1,0:T(8,128)(2,1)S(1)} collective-permute-done((bf16[16,1024]{1,0:T(8,128)(2,1)S(1)}, bf16[16,1024]{1,0:T(8,128)(2,1)S(1)}, u32[]{:S(2)}, u32[]{:S(2)}) %collective-permute-start.22) | collective-permute-done | bytes 32800 | tf_op jit(solution)/shard_map/ppermute | solution.py:323
  75.6 0.9 %collective-permute-done.21 = bf16[16,1024]{1,0:T(8,128)(2,1)S(1)} collective-permute-done((bf16[16,1024]{1,0:T(8,128)(2,1)S(1)}, bf16[16,1024]{1,0:T(8,128)(2,1)S(1)}, u32[]{:S(2)}, u32[]{:S(2)}) %collective-permute-start.21) | collective-permute-done | bytes 32800 | tf_op jit(solution)/shard_map/ppermute | solution.py:323
  76.5 0.1 collective-permute-done.20
  76.7 1.8 %collective-permute-start.23 = (bf16[4,16,1024]{2,1,0:T(8,128)(2,1)S(1)}, bf16[4,16,1024]{2,1,0:T(8,128)(2,1)S(1)}, u32[]{:S(2)}, u32[]{:S(2)}) collective-permute-start(bf16[4,16,1024]{2,1,0:T(8,128)(2,1)S(1)} %pad_maximum_fusion.7), channel_id=1, source_target_pairs={{0,2},{1,3},{2,0},{3,1},{4,6},{5,7},{6,4},{7,5},{8,10},{9,11},{10,... | collective-permute-start | bytes 393224 | tf_op jit(solution)/shard_map/ppermute | solution.py:323
  78.5 0.1 fusion.7
  78.6 0.1 fusion.6
  78.7 0.2 add_convert_fusion
  78.9 2.8 %collective-permute-done.23 = bf16[4,16,1024]{2,1,0:T(8,128)(2,1)S(1)} collective-permute-done((bf16[4,16,1024]{2,1,0:T(8,128)(2,1)S(1)}, bf16[4,16,1024]{2,1,0:T(8,128)(2,1)S(1)}, u32[]{:S(2)}, u32[]{:S(2)}) %collective-permute-start.23) | collective-permute-done | bytes 131104 | tf_op jit(solution)/shard_map/ppermute | solution.py:323
  81.8 0.1 collective-permute-start.25
  81.8 0.1 pad_add_fusion.place
  81.9 0.8 slice.120
  82.7 0.7 slice.121
  83.4 0.6 reshape.64
  84.0 1.4 %place_blocks.1 = (bf16[256,768]{1,0:T(8,128)(2,1)}, bf16[256,256]{1,0:T(8,128)(2,1)}) custom-call(s32[2]{0:T(128)S(1)} %pad_add_fusion.place, bf16[2,4,16,1024]{3,2,1,0:T(8,128)(2,1)S(1)} %pad_maximum_fusion.4.near_ref, bf16[2,4,16,1024]{3,2,1,0:T(8,128)(2,1)S(1)} %collective-permute-done.25.far_ref), custom_call_target="tpu_custom_call" | custom-call | tf_op jit(solution)/shard_map/place_blocks/pallas_call | solution.py:302
  (53 shorter events, 0.6 us)
Async XLA Ops:
  0.6 7.4 %copy-start.1 = (bf16[1,8,32,256]{3,2,1,0:T(8,128)(2,1)S(1)}, bf16[1,8,32,256]{3,2,1,0:T(8,128)(2,1)}, u32[]{:S(2)}) copy-start(bf16[1,8,32,256]{3,2,1,0:T(8,128)(2,1)} %param.12) | copy-start | bytes 393220
  2.2 5.8 %copy-start = (bf16[1,8,32,256]{3,2,1,0:T(8,128)(2,1)S(1)}, bf16[1,8,32,256]{3,2,1,0:T(8,128)(2,1)}, u32[]{:S(2)}) copy-start(bf16[1,8,32,256]{3,2,1,0:T(8,128)(2,1)} %param.11) | copy-start | bytes 393220
  2.3 10.5 %collective-permute-start.4 = (bf16[16,2048]{1,0:T(8,128)(2,1)S(1)}, bf16[16,2048]{1,0:T(8,128)(2,1)S(1)}, u32[]{:S(2)}, u32[]{:S(2)}) collective-permute-start(bf16[16,2048]{1,0:T(8,128)(2,1)S(1)} %constant_dynamic-update-slice_fusion), channel_id=1, source_target_pairs={{0,12},{4,8},{8,4},{12,0},{1,13},{5,9},{9,5},{13,1},{2,14},{6,10},... | collective-permute-start | bytes 196616 | tf_op jit(solution)/shard_map/ppermute | solution.py:323
  7.4 5.6 %collective-permute-start.3 = (bf16[16,2048]{1,0:T(8,128)(2,1)S(1)}, bf16[16,2048]{1,0:T(8,128)(2,1)S(1)}, u32[]{:S(2)}, u32[]{:S(2)}) collective-permute-start(bf16[16,2048]{1,0:T(8,128)(2,1)S(1)} %constant_dynamic-update-slice_fusion), channel_id=1, source_target_pairs={{0,8},{4,12},{8,0},{12,4},{1,9},{5,13},{9,1},{13,5},{2,10},{6,14},... | collective-permute-start | bytes 196616 | tf_op jit(solution)/shard_map/ppermute | solution.py:323
  7.4 5.6 %collective-permute-start.2 = (bf16[16,2048]{1,0:T(8,128)(2,1)S(1)}, bf16[16,2048]{1,0:T(8,128)(2,1)S(1)}, u32[]{:S(2)}, u32[]{:S(2)}) collective-permute-start(bf16[16,2048]{1,0:T(8,128)(2,1)S(1)} %constant_dynamic-update-slice_fusion), channel_id=1, source_target_pairs={{0,4},{4,0},{8,12},{12,8},{1,5},{5,1},{9,13},{13,9},{2,6},{6,2},{1... | collective-permute-start | bytes 196616 | tf_op jit(solution)/shard_map/ppermute | solution.py:323
  8.1 6.7 %collective-permute-start = (bf16[9,32,256]{2,1,0:T(8,128)(2,1)S(1)}, bf16[9,32,256]{2,1,0:T(8,128)(2,1)S(1)}, u32[]{:S(2)}, u32[]{:S(2)}) collective-permute-start(bf16[9,32,256]{2,1,0:T(8,128)(2,1)S(1)} %pad_maximum_fusion.5), channel_id=1, source_target_pairs={{0,4},{4,8},{8,12},{1,5},{5,9},{9,13},{2,6},{6,10},{10,14},{3,7},{... | collective-permute-start | bytes 442376 | tf_op jit(solution)/shard_map/ppermute | solution.py:319
  11.4 7.0 %collective-permute-start.1 = (bf16[9,32,256]{2,1,0:T(8,128)(2,1)S(1)}, bf16[9,32,256]{2,1,0:T(8,128)(2,1)S(1)}, u32[]{:S(2)}, u32[]{:S(2)}) collective-permute-start(bf16[9,32,256]{2,1,0:T(8,128)(2,1)S(1)} %pad_maximum_fusion.6), channel_id=1, source_target_pairs={{4,0},{8,4},{12,8},{5,1},{9,5},{13,9},{6,2},{10,6},{14,10},{7,3},{... | collective-permute-start | bytes 442376 | tf_op jit(solution)/shard_map/ppermute | solution.py:319
  18.5 11.3 %copy-start.2 = (bf16[256,768]{1,0:T(8,128)(2,1)S(1)}, bf16[256,768]{1,0:T(8,128)(2,1)}, u32[]{:S(2)}) copy-start(bf16[256,768]{1,0:T(8,128)(2,1)} %qkv_ref.2) | copy-start | bytes 1179652
  18.5 11.3 %copy-start.4 = (bf16[256,256]{1,0:T(8,128)(2,1)S(1)}, bf16[256,256]{1,0:T(8,128)(2,1)}, u32[]{:S(2)}) copy-start(bf16[256,256]{1,0:T(8,128)(2,1)} %out_ref.2) | copy-start | bytes 393220
  18.6 2.7 %collective-permute-start.5 = (bf16[34,6,256]{2,1,0:T(8,128)(2,1)S(1)}, bf16[34,6,256]{2,1,0:T(8,128)(2,1)S(1)}, u32[]{:S(2)}, u32[]{:S(2)}) collective-permute-start(bf16[34,6,256]{2,1,0:T(8,128)(2,1)S(1)} %get-tuple-element.65), channel_id=1, source_target_pairs={{0,1},{1,2},{2,3},{4,5},{5,6},{6,7},{8,9},{9,10},{10,11},{12,13},{... | collective-permute-start | bytes 313352 | tf_op jit(solution)/shard_map/ppermute | solution.py:319
  20.0 5.0 %collective-permute-start.6 = (bf16[34,6,256]{2,1,0:T(8,128)(2,1)S(1)}, bf16[34,6,256]{2,1,0:T(8,128)(2,1)S(1)}, u32[]{:S(2)}, u32[]{:S(2)}) collective-permute-start(bf16[34,6,256]{2,1,0:T(8,128)(2,1)S(1)} %get-tuple-element.64), channel_id=1, source_target_pairs={{1,0},{2,1},{3,2},{5,4},{6,5},{7,6},{9,8},{10,9},{11,10},{13,12},{... | collective-permute-start | bytes 313352 | tf_op jit(solution)/shard_map/ppermute | solution.py:319
  25.0 11.4 %collective-permute-start.7 = (bf16[4,16,2048]{2,1,0:T(8,128)(2,1)S(1)}, bf16[4,16,2048]{2,1,0:T(8,128)(2,1)S(1)}, u32[]{:S(2)}, u32[]{:S(2)}) collective-permute-start(bf16[4,16,2048]{2,1,0:T(8,128)(2,1)S(1)} %pad_maximum_fusion.3), channel_id=1, source_target_pairs={{0,2},{1,3},{2,0},{3,1},{4,6},{5,7},{6,4},{7,5},{8,10},{9,11},{10,... | collective-permute-start | bytes 786440 | tf_op jit(solution)/shard_map/ppermute | solution.py:323
  29.1 0.7 copy-start.8
  36.5 0.8 copy-start.6
  36.5 0.8 copy-start.7
  36.5 1.6 %collective-permute-start.8 = (bf16[2,4,16,1024]{3,2,1,0:T(8,128)(2,1)S(1)}, bf16[2,4,16,1024]{3,2,1,0:T(8,128)(2,1)S(1)}, u32[]{:S(2)}, u32[]{:S(2)}) collective-permute-start(bf16[2,4,16,1024]{3,2,1,0:T(8,128)(2,1)S(1)} %get-tuple-element.42), channel_id=1, source_target_pairs={{0,1},{1,0},{2,3},{3,2},{4,5},{5,4},{6,7},{7,6},{8,9},{9,8},{10,11... | collective-permute-start | bytes 786440 | tf_op jit(solution)/shard_map/ppermute | solution.py:323
  36.8 2.0 %collective-permute-start.9 = (bf16[2,4,16,2048]{3,2,1,0:T(8,128)(2,1)S(1)}, bf16[2,4,16,2048]{3,2,1,0:T(8,128)(2,1)S(1)}, u32[]{:S(2)}, u32[]{:S(2)}) collective-permute-start(bf16[2,4,16,2048]{3,2,1,0:T(8,128)(2,1)S(1)} %pad_maximum_fusion.2), channel_id=1, source_target_pairs={{0,1},{1,0},{2,3},{3,2},{4,5},{5,4},{6,7},{7,6},{8,9},{9,8},{10,11... | collective-permute-start | bytes 1572872 | tf_op jit(solution)/shard_map/ppermute | solution.py:323
  38.9 5.7 %collective-permute-start.10 = (bf16[4,16,1024]{2,1,0:T(8,128)(2,1)S(1)}, bf16[4,16,1024]{2,1,0:T(8,128)(2,1)S(1)}, u32[]{:S(2)}, u32[]{:S(2)}) collective-permute-start(bf16[4,16,1024]{2,1,0:T(8,128)(2,1)S(1)} %fusion), channel_id=1, source_target_pairs={{0,2},{1,3},{2,0},{3,1},{4,6},{5,7},{6,4},{7,5},{8,10},{9,11},{10,... | collective-permute-start | bytes 393224 | tf_op jit(solution)/shard_map/ppermute | solution.py:323
  40.7 1.0 %copy-start.3 = (bf16[3,64,1024]{2,1,0:T(8,128)(2,1)S(1)}, bf16[3,64,1024]{2,1,0:T(8,128)(2,1)}, u32[]{:S(2)}) copy-start(bf16[3,64,1024]{2,1,0:T(8,128)(2,1)} %qkv_ref.3) | copy-start | bytes 1179652
  40.7 1.0 %copy-start.5 = (bf16[64,1024]{1,0:T(8,128)(2,1)S(1)}, bf16[64,1024]{1,0:T(8,128)(2,1)}, u32[]{:S(2)}) copy-start(bf16[64,1024]{1,0:T(8,128)(2,1)} %out_ref.3) | copy-start | bytes 393220
  44.7 6.2 %collective-permute-start.13 = (bf16[16,1024]{1,0:T(8,128)(2,1)S(1)}, bf16[16,1024]{1,0:T(8,128)(2,1)S(1)}, u32[]{:S(2)}, u32[]{:S(2)}) collective-permute-start(bf16[16,1024]{1,0:T(8,128)(2,1)S(1)} %get-tuple-element.72), channel_id=1, source_target_pairs={{0,12},{4,8},{8,4},{12,0},{1,13},{5,9},{9,5},{13,1},{2,14},{6,10},... | collective-permute-start | bytes 98312 | tf_op jit(solution)/shard_map/ppermute | solution.py:323
  46.7 4.8 %collective-permute-start.12 = (bf16[16,1024]{1,0:T(8,128)(2,1)S(1)}, bf16[16,1024]{1,0:T(8,128)(2,1)S(1)}, u32[]{:S(2)}, u32[]{:S(2)}) collective-permute-start(bf16[16,1024]{1,0:T(8,128)(2,1)S(1)} %get-tuple-element.73), channel_id=1, source_target_pairs={{0,8},{4,12},{8,0},{12,4},{1,9},{5,13},{9,1},{13,5},{2,10},{6,14},... | collective-permute-start | bytes 98312 | tf_op jit(solution)/shard_map/ppermute | solution.py:323
  47.8 4.1 %collective-permute-start.11 = (bf16[16,1024]{1,0:T(8,128)(2,1)S(1)}, bf16[16,1024]{1,0:T(8,128)(2,1)S(1)}, u32[]{:S(2)}, u32[]{:S(2)}) collective-permute-start(bf16[16,1024]{1,0:T(8,128)(2,1)S(1)} %get-tuple-element.71), channel_id=1, source_target_pairs={{0,4},{4,0},{8,12},{12,8},{1,5},{5,1},{9,13},{13,9},{2,6},{6,2},{1... | collective-permute-start | bytes 98312 | tf_op jit(solution)/shard_map/ppermute | solution.py:323
  49.2 2.7 %collective-permute-start.14 = (bf16[2,4,16,1024]{3,2,1,0:T(8,128)(2,1)S(1)}, bf16[2,4,16,1024]{3,2,1,0:T(8,128)(2,1)S(1)}, u32[]{:S(2)}, u32[]{:S(2)}) collective-permute-start(bf16[2,4,16,1024]{3,2,1,0:T(8,128)(2,1)S(1)} %bitcast.85), channel_id=1, source_target_pairs={{0,1},{1,0},{2,3},{3,2},{4,5},{5,4},{6,7},{7,6},{8,9},{9,8},{10,11... | collective-permute-start | bytes 786440 | tf_op jit(solution)/shard_map/ppermute | solution.py:323
  49.4 29.4 %collective-permute-start.24 = (bf16[256,1024]{1,0:T(8,128)(2,1)S(1)}, bf16[256,1024]{1,0:T(8,128)(2,1)S(1)}, u32[]{:S(2)}, u32[]{:S(2)}) collective-permute-start(bf16[256,1024]{1,0:T(8,128)(2,1)S(1)} %get-tuple-element.56), channel_id=1, source_target_pairs={{0,16},{16,0},{1,17},{17,1},{2,18},{18,2},{3,19},{19,3},{4,20},{20... | collective-permute-start | bytes 1572872 | tf_op jit(solution)/shard_map/ppermute | solution.py:334
  51.9 13.2 %collective-permute-start.15 = (f32[16,1024]{1,0:T(8,128)S(1)}, f32[16,1024]{1,0:T(8,128)S(1)}, u32[]{:S(2)}, u32[]{:S(2)}) collective-permute-start(f32[16,1024]{1,0:T(8,128)S(1)} %fusion.11), channel_id=1, source_target_pairs={{0,16},{16,0},{1,17},{17,1},{2,18},{18,2},{3,19},{19,3},{4,20},{20... | collective-permute-start | bytes 196616 | tf_op jit(solution)/shard_map/ppermute | solution.py:334
  53.5 11.6 %collective-permute-start.16 = (bf16[4,16,1024]{2,1,0:T(8,128)(2,1)S(1)}, bf16[4,16,1024]{2,1,0:T(8,128)(2,1)S(1)}, u32[]{:S(2)}, u32[]{:S(2)}) collective-permute-start(bf16[4,16,1024]{2,1,0:T(8,128)(2,1)S(1)} %fusion.1), channel_id=1, source_target_pairs={{0,2},{1,3},{2,0},{3,1},{4,6},{5,7},{6,4},{7,5},{8,10},{9,11},{10,... | collective-permute-start | bytes 393224 | tf_op jit(solution)/shard_map/ppermute | solution.py:323
  65.1 6.5 %collective-permute-start.19 = (bf16[16,1024]{1,0:T(8,128)(2,1)S(1)}, bf16[16,1024]{1,0:T(8,128)(2,1)S(1)}, u32[]{:S(2)}, u32[]{:S(2)}) collective-permute-start(bf16[16,1024]{1,0:T(8,128)(2,1)S(1)} %add_convert_fusion.1), channel_id=1, source_target_pairs={{0,12},{4,8},{8,4},{12,0},{1,13},{5,9},{9,5},{13,1},{2,14},{6,10},... | collective-permute-start | bytes 98312 | tf_op jit(solution)/shard_map/ppermute | solution.py:323
  67.1 5.3 %collective-permute-start.18 = (bf16[16,1024]{1,0:T(8,128)(2,1)S(1)}, bf16[16,1024]{1,0:T(8,128)(2,1)S(1)}, u32[]{:S(2)}, u32[]{:S(2)}) collective-permute-start(bf16[16,1024]{1,0:T(8,128)(2,1)S(1)} %add_convert_fusion.1), channel_id=1, source_target_pairs={{0,8},{4,12},{8,0},{12,4},{1,9},{5,13},{9,1},{13,5},{2,10},{6,14},... | collective-permute-start | bytes 98312 | tf_op jit(solution)/shard_map/ppermute | solution.py:323
  67.3 6.8 %collective-permute-start.17 = (bf16[16,1024]{1,0:T(8,128)(2,1)S(1)}, bf16[16,1024]{1,0:T(8,128)(2,1)S(1)}, u32[]{:S(2)}, u32[]{:S(2)}) collective-permute-start(bf16[16,1024]{1,0:T(8,128)(2,1)S(1)} %add_convert_fusion.1), channel_id=1, source_target_pairs={{0,4},{4,0},{8,12},{12,8},{1,5},{5,1},{9,13},{13,9},{2,6},{6,2},{1... | collective-permute-start | bytes 98312 | tf_op jit(solution)/shard_map/ppermute | solution.py:323
  69.6 6.0 %collective-permute-start.22 = (bf16[16,1024]{1,0:T(8,128)(2,1)S(1)}, bf16[16,1024]{1,0:T(8,128)(2,1)S(1)}, u32[]{:S(2)}, u32[]{:S(2)}) collective-permute-start(bf16[16,1024]{1,0:T(8,128)(2,1)S(1)} %get-tuple-element.69), channel_id=1, source_target_pairs={{0,12},{4,8},{8,4},{12,0},{1,13},{5,9},{9,5},{13,1},{2,14},{6,10},... | collective-permute-start | bytes 98312 | tf_op jit(solution)/shard_map/ppermute | solution.py:323
  71.6 4.9 %collective-permute-start.21 = (bf16[16,1024]{1,0:T(8,128)(2,1)S(1)}, bf16[16,1024]{1,0:T(8,128)(2,1)S(1)}, u32[]{:S(2)}, u32[]{:S(2)}) collective-permute-start(bf16[16,1024]{1,0:T(8,128)(2,1)S(1)} %get-tuple-element.70), channel_id=1, source_target_pairs={{0,8},{4,12},{8,0},{12,4},{1,9},{5,13},{9,1},{13,5},{2,10},{6,14},... | collective-permute-start | bytes 98312 | tf_op jit(solution)/shard_map/ppermute | solution.py:323
  72.4 4.3 %collective-permute-start.20 = (bf16[16,1024]{1,0:T(8,128)(2,1)S(1)}, bf16[16,1024]{1,0:T(8,128)(2,1)S(1)}, u32[]{:S(2)}, u32[]{:S(2)}) collective-permute-start(bf16[16,1024]{1,0:T(8,128)(2,1)S(1)} %get-tuple-element.68), channel_id=1, source_target_pairs={{0,4},{4,0},{8,12},{12,8},{1,5},{5,1},{9,13},{13,9},{2,6},{6,2},{1... | collective-permute-start | bytes 98312 | tf_op jit(solution)/shard_map/ppermute | solution.py:323
  76.7 5.0 %collective-permute-start.23 = (bf16[4,16,1024]{2,1,0:T(8,128)(2,1)S(1)}, bf16[4,16,1024]{2,1,0:T(8,128)(2,1)S(1)}, u32[]{:S(2)}, u32[]{:S(2)}) collective-permute-start(bf16[4,16,1024]{2,1,0:T(8,128)(2,1)S(1)} %pad_maximum_fusion.7), channel_id=1, source_target_pairs={{0,2},{1,3},{2,0},{3,1},{4,6},{5,7},{6,4},{7,5},{8,10},{9,11},{10,... | collective-permute-start | bytes 393224 | tf_op jit(solution)/shard_map/ppermute | solution.py:323
  81.8 2.2 %collective-permute-start.25 = (bf16[2,4,16,1024]{3,2,1,0:T(8,128)(2,1)S(1)}, bf16[2,4,16,1024]{3,2,1,0:T(8,128)(2,1)S(1)}, u32[]{:S(2)}, u32[]{:S(2)}) collective-permute-start(bf16[2,4,16,1024]{3,2,1,0:T(8,128)(2,1)S(1)} %pad_maximum_fusion.4.near_ref), channel_id=1, source_target_pairs={{0,1},{1,0},{2,3},{3,2},{4,5},{5,4},{6,7},{7,6},{8,9},{9,8},{10,11... | collective-permute-start | bytes 786440 | tf_op jit(solution)/shard_map/ppermute | solution.py:323
where the time goes:
time: 85.8 us; the launch traced here: 85.4 us
  starting transfers between devices  38.9 us (45%)
  waiting for transfers between devices  28 us (33%)
  Pallas kernels  9.67 us (11%)
  local copies, waits for them, and re-layouts  5.8 us (7%)
  between operations  1.67 us (2%)
  other arithmetic  1.27 us (1%)
    ppermute x20, starting transfers between devices, swapped(): lax.ppermute(value, axis, [(i, i ^ mask) for i in range(lax.axis_size(axi...  28.5 us
    ppermute x2, waiting for transfers between devices, batch_sum(): other = lax.ppermute(partial, 'batch', [(0, 1), (1, 0)])  9.75 us
    ppermute x20, waiting for transfers between devices, swapped(): lax.ppermute(value, axis, [(i, i ^ mask) for i in range(lax.axis_size(axi...  9.17 us
    ppermute x2, waiting for transfers between devices, neighbours(): lax.ppermute(low_edge, axis, down)  7.38 us
    pallas_call x1, Pallas kernels, fine_block(): pl.pallas_call(fine_body, out_shape=(jax.ShapeDtypeStruct((height, breadt...  6.58 us
    ppermute x2, starting transfers between devices, neighbours(): lax.ppermute(high_edge, axis, up)  4.73 us
    ppermute x2, starting transfers between devices, batch_sum(): other = lax.ppermute(partial, 'batch', [(0, 1), (1, 0)])  3.11 us
    ppermute x2, starting transfers between devices, neighbours(): lax.ppermute(low_edge, axis, down)  2.58 us
  transfers between devices with their start and end apart: 26, of which 14 were waited for; matrix products, arithmetic and copies ran while one was open for 4% of the time, Pallas kernels for 10%

commit v1 on v0

--- a/solution.py
+++ b/solution.py
@@ -197,7 +197,7 @@
         target = (keep_ref, send_ref)[low]
         for high in range(half):
             for row in range(columns):
-                block = (limits[4] ^ (2 * high + low)) * columns + (limits[5] ^ row)
+                block = (limits[4] ^ (2 * high + low)) * columns + row
                 target[high, row] = total_ref[block].astype(target.dtype)
     down = dot(grad_proj, qkv_ref[...], ((1,), (1,)))
     dx_ref[...] = norm_backward(picture, inverse, factor, down).reshape(height, breadth, D_F)
@@ -243,10 +243,29 @@
     )(limits, picture, cotangent, above, below, left, right, factor, fine_qkv, fine_out)
 
 
-def coarse_body(x_ref, dy_ref, factor_ref, qkv_ref, out_ref, parts_ref, grads_ref):
+def coarse_body(
+    x_ref,
+    dy_ref,
+    factor_ref,
+    qkv_hbm,
+    out_hbm,
+    parts_ref,
+    grads_ref,
+    qkv_ref,
+    out_ref,
+    arrived,
+):
+    fetches = [
+        pltpu.make_async_copy(qkv_hbm, qkv_ref, arrived.at[0]),
+        pltpu.make_async_copy(out_hbm, out_ref, arrived.at[1]),
+    ]
+    for fetch in fetches:
+        fetch.start()
     tokens = x_ref[...].astype(jnp.float32)
     normed = (tokens * inverse_rms(tokens) * factor_ref[...]).astype(jnp.bfloat16)
     cot = dy_ref[...]
+    for fetch in fetches:
+        fetch.wait()
     flat_qkv = qkv_ref[...].reshape(3 * HD, D_C)
     out_rows = out_ref[...]
     projected = dot(normed, flat_qkv, ((1,), (1,))).astype(jnp.bfloat16)
@@ -278,11 +297,53 @@
             jax.ShapeDtypeStruct((count, D_C), jnp.bfloat16),
             jax.ShapeDtypeStruct((4 * HD, D_C), jnp.bfloat16),
         ),
-        in_specs=[vmem] * 5,
+        in_specs=[vmem] * 3 + [pl.BlockSpec(memory_space=pl.ANY)] * 2,
         out_specs=(vmem, vmem),
+        scratch_shapes=[
+            pltpu.VMEM(head_qkv.shape, jnp.bfloat16),
+            pltpu.VMEM(head_out.shape, jnp.bfloat16),
+            pltpu.SemaphoreType.DMA((2,)),
+        ],
         compiler_params=pltpu.CompilerParams(vmem_limit_bytes=vmem_bytes),
         name="coarse_block",
     )(tokens, cotangents, factor, head_qkv, head_out)
+
+
+def pack_body(first, second, x_ref, dy_ref, own_ref):
+    own_ref[:, :D_C] = x_ref[...].astype(jnp.float32).reshape(-1, D_C).astype(jnp.bfloat16)
+    own_ref[:, D_C:] = dy_ref[...].astype(jnp.float32).reshape(-1, D_C).astype(jnp.bfloat16)
+
+
+def packed(after, tokens, cotangents):
+    vmem = pl.BlockSpec(memory_space=pltpu.VMEM)
+    count = tokens.shape[0] * tokens.shape[1]
+    return pl.pallas_call(
+        pack_body,
+        out_shape=jax.ShapeDtypeStruct((count, 2 * D_C), jnp.bfloat16),
+        in_specs=[pl.BlockSpec(memory_space=pl.ANY)] * 2 + [vmem] * 2,
+        out_specs=vmem,
+        name="pack_coarse",
+    )(*after, tokens, cotangents)
+
+
+def pair_sum_body(first, second, qkv_ref, out_ref):
+    total = (first[...].astype(jnp.float32) + second[...].astype(jnp.float32)).astype(jnp.bfloat16)
+    qkv_ref[...] = total[: 3 * HD].reshape(qkv_ref.shape)
+    out_ref[...] = total[3 * HD :]
+
+
+def pair_sum(first, second):
+    vmem = pl.BlockSpec(memory_space=pltpu.VMEM)
+    return pl.pallas_call(
+        pair_sum_body,
+        out_shape=(
+            jax.ShapeDtypeStruct((3, HD, D_C), jnp.bfloat16),
+            jax.ShapeDtypeStruct((HD, D_C), jnp.bfloat16),
+        ),
+        in_specs=[vmem, vmem],
+        out_specs=(vmem, vmem),
+        name="pair_sum",
+    )(first, second)
 
 
 def place_body(place, near_ref, far_ref, qkv_ref, out_ref):
@@ -290,7 +351,7 @@
     for low in range(2):
         for high in range(highs):
             for row in range(downs):
-                block = (place[0] ^ (2 * high + low)) * downs + (place[1] ^ row)
+                block = (place[0] ^ (2 * high + low)) * downs + row
                 at = pl.ds(pl.multiple_of(block * rows, rows), rows)
                 piece = (near_ref, far_ref)[low][high, row]
                 qkv_ref[at] = piece[:, : 3 * D_F]
@@ -328,11 +389,9 @@
 
 
 def batch_sum(partial):
-    images = lax.axis_size("batch")
-    if images != 2:
-        return lax.psum(partial, "batch").astype(jnp.float32)
-    other = lax.ppermute(partial, "batch", [(0, 1), (1, 0)])
-    return partial.astype(jnp.float32) + other.astype(jnp.float32)
+    if lax.axis_size("batch") != 2:
+        return lax.psum(partial, "batch")
+    return wide(partial) + wide(swapped(partial, "batch", 1))
 
 
 def wide(value):
@@ -378,15 +437,9 @@
     low = jnp.concatenate([picture[:HALO], cotangent[:RAD]], axis=0)
     high = jnp.concatenate([picture[height - HALO :], cotangent[height - RAD :]], axis=0)
     above, below = neighbours(low, high, "gy")
-    coarse_tokens = x_coarse[0].reshape(-1, D_C)
-    own = jnp.concatenate([coarse_tokens, dy_coarse[0].reshape(-1, D_C)], axis=1)
+    own = packed((low, high), x_coarse[0], dy_coarse[0])
     count = own.shape[0]
     row_group = all_rows(own)
-    column = jnp.concatenate([above, picture, cotangent, below], axis=0)
-    column, row_group = tied(column, row_group)
-    left, right = neighbours(column[:, :HALO], column[:, breadth - HALO :], "gx")
-    left, right, row_group = tied(left, right, row_group)
-    pair = jnp.stack([row_group, swapped(row_group, "gx", 2)])
 
     row_first = gy * height - HALO
     col_first = gx * breadth - HALO
@@ -402,6 +455,11 @@
     ).astype(jnp.int32)
     factor = time_gain(fine_gain, step_value)[None]
     coarse_factor = time_gain(coarse_gain, step_value)[None]
+    above, below, limits, factor, coarse_factor = tied(above, below, limits, factor, coarse_factor)
+    column = jnp.concatenate([above, picture, cotangent, below], axis=0)
+    left, right = neighbours(column[:, :HALO], column[:, breadth - HALO :], "gx")
+    left, right, row_group = tied(left, right, row_group)
+    pair = jnp.stack([row_group, swapped(row_group, "gx", 2)])
     dx_picture, fine_keep, fine_send = fine_block(
         (across, downs),
         limits,
@@ -421,44 +479,48 @@
     other_pair = swapped(pair, "gx", 1)
     fine_half, other_pair = tied(fine_half, other_pair)
 
+    fine_quarter = narrow(fine_half[0] + wide(swapped(narrow(fine_half[1]), "gx", 2)))
     everyone = jnp.stack([pair, other_pair]).reshape(-1, 2 * D_C)
-    fine_quarter = fine_half[0] + wide(swapped(narrow(fine_half[1]), "gx", 2))
     parts, coarse_partial = coarse_block(
         everyone[:, :D_C], everyone[:, D_C:], coarse_factor, coarse_qkv, coarse_out
     )
     fine_quarter, parts, coarse_partial = tied(fine_quarter, parts, coarse_partial)
 
-    coarse_sum = narrow(batch_sum(coarse_partial))
+    fine_quarter = narrow(batch_sum(fine_quarter))
     parts = parts.reshape(2, 2, downs, count, D_C)
-    fine_piece = row_sum(fine_quarter)
     coarse_half = wide(parts[0]) + wide(swapped(parts[1], "gx", 1))
-    fine_piece, coarse_half = tied(fine_piece, coarse_half)
-
-    fine_piece = narrow(batch_sum(fine_piece))
     coarse_quarter = wide(coarse_half[0]) + wide(swapped(narrow(coarse_half[1]), "gx", 2))
-    fine_piece, coarse_quarter = tied(fine_piece, coarse_quarter)
-
-    fine_rows = all_rows(fine_piece)
-    coarse_down = row_sum(coarse_quarter)
-    fine_rows, coarse_down = tied(fine_rows, coarse_down)
-
-    fine_pair = jnp.stack([fine_rows, swapped(fine_rows, "gx", 2)])
-    coarse_floats = wide(coarse_tokens)
+    fine_quarter, coarse_quarter, coarse_partial = tied(
+        fine_quarter, coarse_quarter, coarse_partial
+    )
+
+    pair_batch = lax.axis_size("batch") == 2
+    coarse_other = swapped(coarse_partial, "batch", 1) if pair_batch else coarse_partial
+    mask = 1
+    while mask < downs:
+        fine_quarter = narrow(wide(fine_quarter) + wide(swapped(fine_quarter, "gy", mask)))
+        if mask == 1:
+            coarse_down = row_sum(coarse_quarter)
+            fine_quarter, coarse_down = tied(fine_quarter, coarse_down)
+        mask *= 2
+    coarse_floats = wide(x_coarse[0].reshape(-1, D_C))
     dx_coarse = norm_backward(
         coarse_floats, inverse_rms(coarse_floats), coarse_factor, coarse_down
-    )
-    fine_pair, dx_coarse, coarse_sum = tied(fine_pair, dx_coarse, coarse_sum)
+    ).reshape(x_coarse.shape)
+    fine_quarter, dx_coarse = tied(fine_quarter, dx_coarse)
+
+    fine_pair = jnp.stack([fine_quarter, swapped(fine_quarter, "gx", 2)])
+    if pair_batch:
+        grad_coarse_qkv, grad_coarse_out = pair_sum(coarse_partial, coarse_other)
+    else:
+        coarse_sum = narrow(batch_sum(wide(coarse_partial)))
+        grad_coarse_qkv = coarse_sum[: 3 * HD].reshape(coarse_qkv.shape)
+        grad_coarse_out = coarse_sum[3 * HD :]
+    fine_pair, grad_coarse_qkv, grad_coarse_out = tied(fine_pair, grad_coarse_qkv, grad_coarse_out)
     grad_qkv, grad_out = place_blocks(
         jnp.stack([gx, gy]).astype(jnp.int32), fine_pair, swapped(fine_pair, "gx", 1)
     )
-    return (
-        dx_picture[None],
-        dx_coarse.reshape(x_coarse.shape),
-        grad_qkv,
-        grad_out,
-        coarse_sum[: 3 * HD].reshape(coarse_qkv.shape),
-        coarse_sum[3 * HD :],
-    )
+    return (dx_picture[None], dx_coarse, grad_qkv, grad_out, grad_coarse_qkv, grad_coarse_out)
 
 
 def solution(mesh):

time: 85.8 us -> 77.4 us (0.902)
  waiting for transfers between devices: 28 us -> 20.5 us
  Pallas kernels: 9.67 us -> 13.7 us
  starting transfers between devices: 38.9 us -> 35 us
  local copies, waits for them, and re-layouts: 5.8 us -> 4.93 us
    ppermute x2 -> x0, waiting for transfers between devices: 9.75 us -> none  [batch_sum(): other = lax.ppermute(partial, 'batch', [(0, 1), (1, 0)])]
    ppermute x20 -> x18, waiting for transfers between devices: 9.17 us -> 18.4 us  [swapped(): lax.ppermute(value, axis, [(i, i ^ mask) for i in range(lax.axis_size(axi...]
    ppermute x2, waiting for transfers between devices: 7.38 us -> 2.11 us  [neighbours(): lax.ppermute(low_edge, axis, down)]
    pallas_call x0 -> x2, Pallas kernels: none -> 3.53 us  [the longest x1 2.08 us: pair_sum(): pl.pallas_call(pair_sum_body, out_shape=(jax.ShapeDtypeStruct((3, HD, D_C...]
    ppermute x2 -> x0, starting transfers between devices: 3.11 us -> none  [batch_sum(): other = lax.ppermute(partial, 'batch', [(0, 1), (1, 0)])]
    ppermute x20 -> x18, starting transfers between devices: 28.5 us -> 26.1 us  [swapped(): lax.ppermute(value, axis, [(i, i ^ mask) for i in range(lax.axis_size(axi...]
    ppermute x2, waiting for transfers between devices: 1.72 us -> 0.01 us  [neighbours(): lax.ppermute(high_edge, axis, up)]
    ppermute x2, starting transfers between devices: 4.73 us -> 6.37 us  [neighbours(): lax.ppermute(high_edge, axis, up)]
  transfers between devices with their start and end apart: 26 -> 22, of which waited for: 14 -> 11; matrix products, arithmetic and copies ran while one was open for 4% -> 2% of each run, Pallas kernels for 10% -> 13%
where the time goes in v1:
time: 77.4 us; the launch traced here: 77 us
  starting transfers between devices  35 us (45%)
  waiting for transfers between devices  20.5 us (26%)
  Pallas kernels  13.7 us (18%)
  local copies, waits for them, and re-layouts  4.93 us (6%)
  between operations  1.69 us (2%)
  other arithmetic  1.09 us (1%)
    ppermute x18, starting transfers between devices, swapped(): lax.ppermute(value, axis, [(i, i ^ mask) for i in range(lax.axis_size(axi...  26.1 us
    ppermute x18, waiting for transfers between devices, swapped(): lax.ppermute(value, axis, [(i, i ^ mask) for i in range(lax.axis_size(axi...  18.4 us
    pallas_call x1, Pallas kernels, fine_block(): pl.pallas_call(fine_body, out_shape=(jax.ShapeDtypeStruct((height, breadt...  6.59 us
    ppermute x2, starting transfers between devices, neighbours(): lax.ppermute(high_edge, axis, up)  6.37 us
    unnamed x28, local copies, waits for them, and re-layouts  3.08 us
    ppermute x2, starting transfers between devices, neighbours(): lax.ppermute(low_edge, axis, down)  2.58 us
    pallas_call x1, Pallas kernels, coarse_block(): pl.pallas_call(coarse_body, out_shape=(jax.ShapeDtypeStruct((count, D_C),...  2.22 us
    ppermute x2, waiting for transfers between devices, neighbours(): lax.ppermute(low_edge, axis, down)  2.11 us
  transfers between devices with their start and end apart: 22, of which 11 were waited for; matrix products, arithmetic and copies ran while one was open for 2% of the time, Pallas kernels for 13%

profile of v1, /device:TPU:0, one launch (start us, length us, event | category | flops | bytes accessed | tf_op | source)
XLA Modules:
  0.0 77.0 jit_solution(18335370975285844115)
XLA Ops:
  0.6 0.9 %slice_bitcast_fusion.3 = (bf16[3,32,256]{2,1,0:T(8,128)(2,1)S(1)}, bf16[3,32,256]{2,1,0:T(8,128)(2,1)S(1)}) fusion(bf16[1,8,32,256]{3,2,1,0:T(8,128)(2,1)} %param.12), kind=kLoop, calls=%fused_computation.31 | loop fusion | bytes 196608 | tf_op jit(solution)/shard_map/slice | solution.py:437
  1.5 0.1 copy-done
  1.6 0.0 copy-start.7
  1.6 4.9 %collective-permute-start = (bf16[9,32,256]{2,1,0:T(8,128)(2,1)S(1)}, bf16[9,32,256]{2,1,0:T(8,128)(2,1)S(1)}, u32[]{:S(2)}, u32[]{:S(2)}) collective-permute-start(bf16[9,32,256]{2,1,0:T(8,128)(2,1)S(1)} %pad_maximum_fusion.4.second), channel_id=1, source_target_pairs={{0,4},{4,8},{8,12},{1,5},{5,9},{9,13},{2,6},{6,10},{10,14},{3,7},{... | collective-permute-start | bytes 442376 | tf_op jit(solution)/shard_map/ppermute | solution.py:380
  6.6 0.0 copy-start.8
  6.6 1.3 %collective-permute-start.1 = (bf16[9,32,256]{2,1,0:T(8,128)(2,1)S(1)}, bf16[9,32,256]{2,1,0:T(8,128)(2,1)S(1)}, u32[]{:S(2)}, u32[]{:S(2)}) collective-permute-start(bf16[9,32,256]{2,1,0:T(8,128)(2,1)S(1)} %pad_maximum_fusion.5.first), channel_id=1, source_target_pairs={{4,0},{8,4},{12,8},{5,1},{9,5},{13,9},{6,2},{10,6},{14,10},{7,3},{... | collective-permute-start | bytes 442376 | tf_op jit(solution)/shard_map/ppermute | solution.py:380
  7.9 0.0 copy-start.1
  7.9 1.5 %pack_coarse.1 = bf16[16,2048]{1,0:T(8,128)(2,1)} custom-call(bf16[9,32,256]{2,1,0:T(8,128)(2,1)} %copy-done.8, bf16[9,32,256]{2,1,0:T(8,128)(2,1)} %copy-done.7, bf16[4,4,1024]{2,1,0:T(4,128)(2,1)} %bitcast.73, bf16[4,4,1024]{2,1,0:T(4,128)(2,1)} %bitcast.81), custom_call_target="tpu_custom_call" | custom-call | tf_op jit(solution)/shard_map/pack_coarse/pallas_call | solution.py:320
  9.4 4.7 %collective-permute-start.6 = (bf16[16,2048]{1,0:T(8,128)(2,1)}, bf16[16,2048]{1,0:T(8,128)(2,1)S(1)}, u32[]{:S(2)}, u32[]{:S(2)}) collective-permute-start(bf16[16,2048]{1,0:T(8,128)(2,1)} %pack_coarse.1), channel_id=1, source_target_pairs={{0,12},{4,8},{8,4},{12,0},{1,13},{5,9},{9,5},{13,1},{2,14},{6,10},... | collective-permute-start | bytes 196616 | tf_op jit(solution)/shard_map/ppermute | solution.py:384
  14.1 0.6 collective-permute-start.4
  15.3 0.0 copy-done.12
  15.3 0.1 add_multiply_fusion
  15.4 0.0 copy-start.13
  15.4 0.1 stack.74.limits
  15.5 0.6 copy-done.13
  16.1 0.1 add_multiply_fusion.1
  16.2 0.0 copy-start.11
  16.2 0.0 copy-start.3
  16.2 1.4 %collective-permute-start.2 = (bf16[34,6,256]{2,1,0:T(8,128)(2,1)S(1)}, bf16[34,6,256]{2,1,0:T(8,128)(2,1)S(1)}, u32[]{:S(2)}, u32[]{:S(2)}) collective-permute-start(bf16[34,6,256]{2,1,0:T(8,128)(2,1)S(1)} %get-tuple-element.77), channel_id=1, source_target_pairs={{0,1},{1,2},{2,3},{4,5},{5,6},{6,7},{8,9},{9,10},{10,11},{12,13},{... | collective-permute-start | bytes 313352 | tf_op jit(solution)/shard_map/ppermute | solution.py:380
  17.7 1.3 %collective-permute-start.3 = (bf16[34,6,256]{2,1,0:T(8,128)(2,1)S(1)}, bf16[34,6,256]{2,1,0:T(8,128)(2,1)S(1)}, u32[]{:S(2)}, u32[]{:S(2)}) collective-permute-start(bf16[34,6,256]{2,1,0:T(8,128)(2,1)S(1)} %get-tuple-element.76), channel_id=1, source_target_pairs={{1,0},{2,1},{3,2},{5,4},{6,5},{7,6},{9,8},{10,9},{11,10},{13,12},{... | collective-permute-start | bytes 313352 | tf_op jit(solution)/shard_map/ppermute | solution.py:380
  19.0 1.5 %collective-permute-done.5 = bf16[16,2048]{1,0:T(8,128)(2,1)S(1)} collective-permute-done((bf16[16,2048]{1,0:T(8,128)(2,1)}, bf16[16,2048]{1,0:T(8,128)(2,1)S(1)}, u32[]{:S(2)}, u32[]{:S(2)}) %collective-permute-start.5) | collective-permute-done | bytes 65568 | tf_op jit(solution)/shard_map/ppermute | solution.py:384
  20.5 2.1 %collective-permute-done.3.right_ref = bf16[34,6,256]{2,1,0:T(8,128)(2,1)S(1)} collective-permute-done((bf16[34,6,256]{2,1,0:T(8,128)(2,1)S(1)}, bf16[34,6,256]{2,1,0:T(8,128)(2,1)S(1)}, u32[]{:S(2)}, u32[]{:S(2)}) %collective-permute-start.3) | collective-permute-done | bytes 104480 | tf_op jit(solution)/shard_map/ppermute | solution.py:380
  22.6 3.4 %collective-permute-start.7 = (bf16[4,16,2048]{2,1,0:T(8,128)(2,1)S(1)}, bf16[4,16,2048]{2,1,0:T(8,128)(2,1)S(1)}, u32[]{:S(2)}, u32[]{:S(2)}) collective-permute-start(bf16[4,16,2048]{2,1,0:T(8,128)(2,1)S(1)} %pad_maximum_fusion.2), channel_id=1, source_target_pairs={{0,2},{1,3},{2,0},{3,1},{4,6},{5,7},{6,4},{7,5},{8,10},{9,11},{10,... | collective-permute-start | bytes 786440 | tf_op jit(solution)/shard_map/ppermute | solution.py:384
  26.0 6.6 %fine_block.1 = (bf16[8,32,256]{2,1,0:T(8,128)(2,1)}, f32[2,4,16,1024]{3,2,1,0:T(8,128)S(1)}, bf16[2,4,16,1024]{3,2,1,0:T(8,128)(2,1)S(1)}) custom-call(s32[6]{0:T(128)S(1)} %stack.74.limits, bf16[8,32,256]{2,1,0:T(8,128)(2,1)S(1)} %bitcast.62, bf16[8,32,256]{2,1,0:T(8,128)(2,1)S(1)} %bitcast.64, bf16[9,32,256]{2,1,0:T(8,128)(2,1)S(1)} %collective-permute-done.above_ref, ...), custom_call_target="tpu_custom_call" | custom-call | tf_op jit(solution)/shard_map/fine_block/pallas_call | solution.py:218
  32.6 0.1 pad_maximum_fusion.1
  32.7 0.4 collective-permute-start.9
  33.1 0.1 collective-permute-start.8
  33.2 1.8 %collective-permute-done.8 = bf16[2,4,16,1024]{3,2,1,0:T(8,128)(2,1)S(1)} collective-permute-done((bf16[2,4,16,1024]{3,2,1,0:T(8,128)(2,1)S(1)}, bf16[2,4,16,1024]{3,2,1,0:T(8,128)(2,1)S(1)}, u32[]{:S(2)}, u32[]{:S(2)}) %collective-permute-start.8) | collective-permute-done | bytes 262176 | tf_op jit(solution)/shard_map/ppermute | solution.py:384
  35.0 0.1 convert_add_fusion.1
  35.1 2.2 %collective-permute-start.10 = (bf16[4,16,1024]{2,1,0:T(8,128)(2,1)S(1)}, bf16[4,16,1024]{2,1,0:T(8,128)(2,1)S(1)}, u32[]{:S(2)}, u32[]{:S(2)}) collective-permute-start(bf16[4,16,1024]{2,1,0:T(8,128)(2,1)S(1)} %fusion.2), channel_id=1, source_target_pairs={{0,2},{1,3},{2,0},{3,1},{4,6},{5,7},{6,4},{7,5},{8,10},{9,11},{10,... | collective-permute-start | bytes 393224 | tf_op jit(solution)/shard_map/ppermute | solution.py:384
  37.3 0.1 pad_maximum_fusion
  37.4 0.0 copy-start.4
  37.4 0.1 fusion.6
  37.5 0.9 %copy-done.4 = bf16[3,64,1024]{2,1,0:T(8,128)(2,1)S(1)} copy-done((bf16[3,64,1024]{2,1,0:T(8,128)(2,1)S(1)}, bf16[3,64,1024]{2,1,0:T(8,128)(2,1)}, u32[]{:S(2)}) %copy-start.4) | copy-done | bytes 393240
  38.4 0.0 copy-done.6
  38.4 2.2 %coarse_block.1 = (bf16[256,1024]{1,0:T(8,128)(2,1)S(1)}, bf16[256,1024]{1,0:T(8,128)(2,1)S(1)}) custom-call(bf16[256,1024]{1,0:T(8,128)(2,1)S(1)} %get-tuple-element.75.x_ref, bf16[256,1024]{1,0:T(8,128)(2,1)S(1)} %get-tuple-element.74.dy_ref, f32[1,1024]{1,0:T(1,128)S(1)} %bitcast.65, bf16[3,64,1024]{2,1,0:T(8,128)(2,1)S(1)} %copy-done.4, ...), custom_call_target="tpu_custom_call" | custom-call | tf_op jit(solution)/shard_map/coarse_block/pallas_call | solution.py:294
  40.7 0.4 collective-permute-done.10
  41.2 0.1 collective-permute-start.12
  41.3 0.6 copy-done.10
  41.9 0.1 multiply_reduce_fusion.1
  42.0 1.5 %collective-permute-start.11 = (bf16[4,16,1024]{2,1,0:T(8,128)(2,1)S(1)}, bf16[4,16,1024]{2,1,0:T(8,128)(2,1)S(1)}, u32[]{:S(2)}, u32[]{:S(2)}) collective-permute-start(bf16[4,16,1024]{2,1,0:T(8,128)(2,1)S(1)} %fusion.1), channel_id=1, source_target_pairs={{0,16},{16,0},{1,17},{17,1},{2,18},{18,2},{3,19},{19,3},{4,20},{20... | collective-permute-start | bytes 393224 | tf_op jit(solution)/shard_map/ppermute | solution.py:384
  43.5 0.1 convert_add_fusion
  43.6 1.8 %collective-permute-start.13 = (bf16[4,16,1024]{2,1,0:T(8,128)(2,1)S(1)}, bf16[4,16,1024]{2,1,0:T(8,128)(2,1)S(1)}, u32[]{:S(2)}, u32[]{:S(2)}) collective-permute-start(bf16[4,16,1024]{2,1,0:T(8,128)(2,1)S(1)} %fusion.3), channel_id=1, source_target_pairs={{0,2},{1,3},{2,0},{3,1},{4,6},{5,7},{6,4},{7,5},{8,10},{9,11},{10,... | collective-permute-start | bytes 393224 | tf_op jit(solution)/shard_map/ppermute | solution.py:384
  45.4 1.9 %collective-permute-done.11 = bf16[4,16,1024]{2,1,0:T(8,128)(2,1)S(1)} collective-permute-done((bf16[4,16,1024]{2,1,0:T(8,128)(2,1)S(1)}, bf16[4,16,1024]{2,1,0:T(8,128)(2,1)S(1)}, u32[]{:S(2)}, u32[]{:S(2)}) %collective-permute-start.11) | collective-permute-done | bytes 131104 | tf_op jit(solution)/shard_map/ppermute | solution.py:384
  47.3 1.4 %collective-permute-done.13 = bf16[4,16,1024]{2,1,0:T(8,128)(2,1)S(1)} collective-permute-done((bf16[4,16,1024]{2,1,0:T(8,128)(2,1)S(1)}, bf16[4,16,1024]{2,1,0:T(8,128)(2,1)S(1)}, u32[]{:S(2)}, u32[]{:S(2)}) %collective-permute-start.13) | collective-permute-done | bytes 131104 | tf_op jit(solution)/shard_map/ppermute | solution.py:384
  48.8 3.9 %collective-permute-start.17 = (bf16[16,1024]{1,0:T(8,128)(2,1)S(1)}, bf16[16,1024]{1,0:T(8,128)(2,1)S(1)}, u32[]{:S(2)}, u32[]{:S(2)}) collective-permute-start(bf16[16,1024]{1,0:T(8,128)(2,1)S(1)} %get-tuple-element.81), channel_id=1, source_target_pairs={{0,12},{4,8},{8,4},{12,0},{1,13},{5,9},{9,5},{13,1},{2,14},{6,10},... | collective-permute-start | bytes 98312 | tf_op jit(solution)/shard_map/ppermute | solution.py:384
  52.7 0.6 collective-permute-start.15
  53.3 0.1 rsqrt.12
  53.4 1.4 %collective-permute-start.14 = (bf16[4,16,1024]{2,1,0:T(8,128)(2,1)S(1)}, bf16[4,16,1024]{2,1,0:T(8,128)(2,1)S(1)}, u32[]{:S(2)}, u32[]{:S(2)}) collective-permute-start(bf16[4,16,1024]{2,1,0:T(8,128)(2,1)S(1)} %add_convert_fusion.2), channel_id=1, source_target_pairs={{0,4},{4,0},{8,12},{12,8},{1,5},{5,1},{9,13},{13,9},{2,6},{6,2},{1... | collective-permute-start | bytes 393224 | tf_op jit(solution)/shard_map/ppermute | solution.py:384
  54.8 1.3 %collective-permute-start.20 = (bf16[256,1024]{1,0:T(8,128)(2,1)S(1)}, bf16[256,1024]{1,0:T(8,128)(2,1)S(1)}, u32[]{:S(2)}, u32[]{:S(2)}) collective-permute-start(bf16[256,1024]{1,0:T(8,128)(2,1)S(1)} %get-tuple-element.66.first), channel_id=1, source_target_pairs={{0,16},{16,0},{1,17},{17,1},{2,18},{18,2},{3,19},{19,3},{4,20},{20... | collective-permute-start | bytes 1572872 | tf_op jit(solution)/shard_map/ppermute | solution.py:384
  56.1 1.5 %collective-permute-done.16 = bf16[16,1024]{1,0:T(8,128)(2,1)S(1)} collective-permute-done((bf16[16,1024]{1,0:T(8,128)(2,1)S(1)}, bf16[16,1024]{1,0:T(8,128)(2,1)S(1)}, u32[]{:S(2)}, u32[]{:S(2)}) %collective-permute-start.16) | collective-permute-done | bytes 32800 | tf_op jit(solution)/shard_map/ppermute | solution.py:384
  57.6 1.1 %collective-permute-done.14 = bf16[4,16,1024]{2,1,0:T(8,128)(2,1)S(1)} collective-permute-done((bf16[4,16,1024]{2,1,0:T(8,128)(2,1)S(1)}, bf16[4,16,1024]{2,1,0:T(8,128)(2,1)S(1)}, u32[]{:S(2)}, u32[]{:S(2)}) %collective-permute-start.14) | collective-permute-done | bytes 131104 | tf_op jit(solution)/shard_map/ppermute | solution.py:384
  58.7 2.2 %collective-permute-start.18 = (bf16[4,16,1024]{2,1,0:T(8,128)(2,1)S(1)}, bf16[4,16,1024]{2,1,0:T(8,128)(2,1)S(1)}, u32[]{:S(2)}, u32[]{:S(2)}) collective-permute-start(bf16[4,16,1024]{2,1,0:T(8,128)(2,1)S(1)} %add_convert_fusion.1), channel_id=1, source_target_pairs={{0,8},{4,12},{8,0},{12,4},{1,9},{5,13},{9,1},{13,5},{2,10},{6,14},... | collective-permute-start | bytes 393224 | tf_op jit(solution)/shard_map/ppermute | solution.py:384
  61.0 0.1 multiply_reduce_fusion
  61.1 0.1 subtract_convert_fusion
  61.2 0.6 reshape.59
  61.9 4.2 %collective-permute-done.18 = bf16[4,16,1024]{2,1,0:T(8,128)(2,1)S(1)} collective-permute-done((bf16[4,16,1024]{2,1,0:T(8,128)(2,1)S(1)}, bf16[4,16,1024]{2,1,0:T(8,128)(2,1)S(1)}, u32[]{:S(2)}, u32[]{:S(2)}) %collective-permute-start.18) | collective-permute-done | bytes 131104 | tf_op jit(solution)/shard_map/ppermute | solution.py:384
  66.1 1.8 %collective-permute-start.19 = (bf16[4,16,1024]{2,1,0:T(8,128)(2,1)S(1)}, bf16[4,16,1024]{2,1,0:T(8,128)(2,1)S(1)}, u32[]{:S(2)}, u32[]{:S(2)}) collective-permute-start(bf16[4,16,1024]{2,1,0:T(8,128)(2,1)S(1)} %add_convert_fusion), channel_id=1, source_target_pairs={{0,2},{1,3},{2,0},{3,1},{4,6},{5,7},{6,4},{7,5},{8,10},{9,11},{10,... | collective-permute-start | bytes 393224 | tf_op jit(solution)/shard_map/ppermute | solution.py:384
  67.9 3.2 %collective-permute-done.19 = bf16[4,16,1024]{2,1,0:T(8,128)(2,1)S(1)} collective-permute-done((bf16[4,16,1024]{2,1,0:T(8,128)(2,1)S(1)}, bf16[4,16,1024]{2,1,0:T(8,128)(2,1)S(1)}, u32[]{:S(2)}, u32[]{:S(2)}) %collective-permute-start.19) | collective-permute-done | bytes 131104 | tf_op jit(solution)/shard_map/ppermute | solution.py:384
  71.2 0.8 %copy-done.9 = bf16[256,1024]{1,0:T(8,128)(2,1)} copy-done((bf16[256,1024]{1,0:T(8,128)(2,1)}, bf16[256,1024]{1,0:T(8,128)(2,1)S(1)}, u32[]{:S(2)}) %copy-start.9) | copy-done | bytes 524312
  72.0 2.1 %pair_sum.1 = (bf16[3,64,1024]{2,1,0:T(8,128)(2,1)}, bf16[64,1024]{1,0:T(8,128)(2,1)}) custom-call(bf16[256,1024]{1,0:T(8,128)(2,1)} %copy-done.2, bf16[256,1024]{1,0:T(8,128)(2,1)} %copy-done.9), custom_call_target="tpu_custom_call" | custom-call | tf_op jit(solution)/shard_map/pair_sum/pallas_call | solution.py:337
  74.1 0.1 pad_add_fusion.place
  74.2 1.5 %collective-permute-done.21.far_ref = bf16[2,4,16,1024]{3,2,1,0:T(8,128)(2,1)S(1)} collective-permute-done((bf16[2,4,16,1024]{3,2,1,0:T(8,128)(2,1)S(1)}, bf16[2,4,16,1024]{3,2,1,0:T(8,128)(2,1)S(1)}, u32[]{:S(2)}, u32[]{:S(2)}) %collective-permute-start.21) | collective-permute-done | bytes 262176 | tf_op jit(solution)/shard_map/ppermute | solution.py:384
  75.6 1.4 %place_blocks.1 = (bf16[256,768]{1,0:T(8,128)(2,1)}, bf16[256,256]{1,0:T(8,128)(2,1)}) custom-call(s32[2]{0:T(128)S(1)} %pad_add_fusion.place, bf16[2,4,16,1024]{3,2,1,0:T(8,128)(2,1)S(1)} %pad_maximum_fusion.3.near_ref, bf16[2,4,16,1024]{3,2,1,0:T(8,128)(2,1)S(1)} %collective-permute-done.21.far_ref), custom_call_target="tpu_custom_call" | custom-call | tf_op jit(solution)/shard_map/place_blocks/pallas_call | solution.py:363
  (48 shorter events, 0.5 us)
Async XLA Ops:
  0.6 1.0 %copy-start = (bf16[1,8,32,256]{3,2,1,0:T(8,128)(2,1)S(1)}, bf16[1,8,32,256]{3,2,1,0:T(8,128)(2,1)}, u32[]{:S(2)}) copy-start(bf16[1,8,32,256]{3,2,1,0:T(8,128)(2,1)} %param.11) | copy-start | bytes 393220
  1.6 5.0 %copy-start.7 = (bf16[9,32,256]{2,1,0:T(8,128)(2,1)}, bf16[9,32,256]{2,1,0:T(8,128)(2,1)S(1)}, u32[]{:S(2)}) copy-start(bf16[9,32,256]{2,1,0:T(8,128)(2,1)S(1)} %pad_maximum_fusion.4.second) | copy-start | bytes 442372
  1.6 14.5 %collective-permute-start = (bf16[9,32,256]{2,1,0:T(8,128)(2,1)S(1)}, bf16[9,32,256]{2,1,0:T(8,128)(2,1)S(1)}, u32[]{:S(2)}, u32[]{:S(2)}) collective-permute-start(bf16[9,32,256]{2,1,0:T(8,128)(2,1)S(1)} %pad_maximum_fusion.4.second), channel_id=1, source_target_pairs={{0,4},{4,8},{8,12},{1,5},{5,9},{9,13},{2,6},{6,10},{10,14},{3,7},{... | collective-permute-start | bytes 442376 | tf_op jit(solution)/shard_map/ppermute | solution.py:380
  6.6 1.3 %copy-start.8 = (bf16[9,32,256]{2,1,0:T(8,128)(2,1)}, bf16[9,32,256]{2,1,0:T(8,128)(2,1)S(1)}, u32[]{:S(2)}) copy-start(bf16[9,32,256]{2,1,0:T(8,128)(2,1)S(1)} %pad_maximum_fusion.5.first) | copy-start | bytes 442372
  6.6 9.5 %collective-permute-start.1 = (bf16[9,32,256]{2,1,0:T(8,128)(2,1)S(1)}, bf16[9,32,256]{2,1,0:T(8,128)(2,1)S(1)}, u32[]{:S(2)}, u32[]{:S(2)}) collective-permute-start(bf16[9,32,256]{2,1,0:T(8,128)(2,1)S(1)} %pad_maximum_fusion.5.first), channel_id=1, source_target_pairs={{4,0},{8,4},{12,8},{5,1},{9,5},{13,9},{6,2},{10,6},{14,10},{7,3},{... | collective-permute-start | bytes 442376 | tf_op jit(solution)/shard_map/ppermute | solution.py:380
  7.9 8.2 %copy-start.1 = (bf16[1,8,32,256]{3,2,1,0:T(8,128)(2,1)S(1)}, bf16[1,8,32,256]{3,2,1,0:T(8,128)(2,1)}, u32[]{:S(2)}) copy-start(bf16[1,8,32,256]{3,2,1,0:T(8,128)(2,1)} %param.12) | copy-start | bytes 393220
  9.4 9.6 %collective-permute-start.6 = (bf16[16,2048]{1,0:T(8,128)(2,1)}, bf16[16,2048]{1,0:T(8,128)(2,1)S(1)}, u32[]{:S(2)}, u32[]{:S(2)}) collective-permute-start(bf16[16,2048]{1,0:T(8,128)(2,1)} %pack_coarse.1), channel_id=1, source_target_pairs={{0,12},{4,8},{8,4},{12,0},{1,13},{5,9},{9,5},{13,1},{2,14},{6,10},... | collective-permute-start | bytes 196616 | tf_op jit(solution)/shard_map/ppermute | solution.py:384
  14.1 6.4 %collective-permute-start.5 = (bf16[16,2048]{1,0:T(8,128)(2,1)}, bf16[16,2048]{1,0:T(8,128)(2,1)S(1)}, u32[]{:S(2)}, u32[]{:S(2)}) collective-permute-start(bf16[16,2048]{1,0:T(8,128)(2,1)} %pack_coarse.1), channel_id=1, source_target_pairs={{0,8},{4,12},{8,0},{12,4},{1,9},{5,13},{9,1},{13,5},{2,10},{6,14},... | collective-permute-start | bytes 196616 | tf_op jit(solution)/shard_map/ppermute | solution.py:384
  14.1 6.4 %collective-permute-start.4 = (bf16[16,2048]{1,0:T(8,128)(2,1)}, bf16[16,2048]{1,0:T(8,128)(2,1)S(1)}, u32[]{:S(2)}, u32[]{:S(2)}) collective-permute-start(bf16[16,2048]{1,0:T(8,128)(2,1)} %pack_coarse.1), channel_id=1, source_target_pairs={{0,4},{4,0},{8,12},{12,8},{1,5},{5,1},{9,13},{13,9},{2,6},{6,2},{1... | collective-permute-start | bytes 196616 | tf_op jit(solution)/shard_map/ppermute | solution.py:384
  14.6 0.7 copy-start.12
  15.4 0.7 copy-start.13
  16.2 4.3 %copy-start.11 = (bf16[16,2048]{1,0:T(8,128)(2,1)S(1)}, bf16[16,2048]{1,0:T(8,128)(2,1)}, u32[]{:S(2)}) copy-start(bf16[16,2048]{1,0:T(8,128)(2,1)} %pack_coarse.1) | copy-start | bytes 196612
  16.2 9.8 %copy-start.3 = (bf16[256,768]{1,0:T(8,128)(2,1)S(1)}, bf16[256,768]{1,0:T(8,128)(2,1)}, u32[]{:S(2)}) copy-start(bf16[256,768]{1,0:T(8,128)(2,1)} %qkv_ref.1) | copy-start | bytes 1179652
  16.2 4.3 %collective-permute-start.2 = (bf16[34,6,256]{2,1,0:T(8,128)(2,1)S(1)}, bf16[34,6,256]{2,1,0:T(8,128)(2,1)S(1)}, u32[]{:S(2)}, u32[]{:S(2)}) collective-permute-start(bf16[34,6,256]{2,1,0:T(8,128)(2,1)S(1)} %get-tuple-element.77), channel_id=1, source_target_pairs={{0,1},{1,2},{2,3},{4,5},{5,6},{6,7},{8,9},{9,10},{10,11},{12,13},{... | collective-permute-start | bytes 313352 | tf_op jit(solution)/shard_map/ppermute | solution.py:380
  17.7 5.0 %collective-permute-start.3 = (bf16[34,6,256]{2,1,0:T(8,128)(2,1)S(1)}, bf16[34,6,256]{2,1,0:T(8,128)(2,1)S(1)}, u32[]{:S(2)}, u32[]{:S(2)}) collective-permute-start(bf16[34,6,256]{2,1,0:T(8,128)(2,1)S(1)} %get-tuple-element.76), channel_id=1, source_target_pairs={{1,0},{2,1},{3,2},{5,4},{6,5},{7,6},{9,8},{10,9},{11,10},{13,12},{... | collective-permute-start | bytes 313352 | tf_op jit(solution)/shard_map/ppermute | solution.py:380
  20.5 5.5 %copy-start.5 = (bf16[256,256]{1,0:T(8,128)(2,1)S(1)}, bf16[256,256]{1,0:T(8,128)(2,1)}, u32[]{:S(2)}) copy-start(bf16[256,256]{1,0:T(8,128)(2,1)} %out_ref.1) | copy-start | bytes 393220
  22.6 10.0 %collective-permute-start.7 = (bf16[4,16,2048]{2,1,0:T(8,128)(2,1)S(1)}, bf16[4,16,2048]{2,1,0:T(8,128)(2,1)S(1)}, u32[]{:S(2)}, u32[]{:S(2)}) collective-permute-start(bf16[4,16,2048]{2,1,0:T(8,128)(2,1)S(1)} %pad_maximum_fusion.2), channel_id=1, source_target_pairs={{0,2},{1,3},{2,0},{3,1},{4,6},{5,7},{6,4},{7,5},{8,10},{9,11},{10,... | collective-permute-start | bytes 786440 | tf_op jit(solution)/shard_map/ppermute | solution.py:384
  32.7 2.4 %collective-permute-start.9 = (bf16[2,4,16,2048]{3,2,1,0:T(8,128)(2,1)S(1)}, bf16[2,4,16,2048]{3,2,1,0:T(8,128)(2,1)S(1)}, u32[]{:S(2)}, u32[]{:S(2)}) collective-permute-start(bf16[2,4,16,2048]{3,2,1,0:T(8,128)(2,1)S(1)} %pad_maximum_fusion.1), channel_id=1, source_target_pairs={{0,1},{1,0},{2,3},{3,2},{4,5},{5,4},{6,7},{7,6},{8,9},{9,8},{10,11... | collective-permute-start | bytes 1572872 | tf_op jit(solution)/shard_map/ppermute | solution.py:384
  33.1 1.9 %collective-permute-start.8 = (bf16[2,4,16,1024]{3,2,1,0:T(8,128)(2,1)S(1)}, bf16[2,4,16,1024]{3,2,1,0:T(8,128)(2,1)S(1)}, u32[]{:S(2)}, u32[]{:S(2)}) collective-permute-start(bf16[2,4,16,1024]{3,2,1,0:T(8,128)(2,1)S(1)} %get-tuple-element.50), channel_id=1, source_target_pairs={{0,1},{1,0},{2,3},{3,2},{4,5},{5,4},{6,7},{7,6},{8,9},{9,8},{10,11... | collective-permute-start | bytes 786440 | tf_op jit(solution)/shard_map/ppermute | solution.py:384
  35.1 6.0 %collective-permute-start.10 = (bf16[4,16,1024]{2,1,0:T(8,128)(2,1)S(1)}, bf16[4,16,1024]{2,1,0:T(8,128)(2,1)S(1)}, u32[]{:S(2)}, u32[]{:S(2)}) collective-permute-start(bf16[4,16,1024]{2,1,0:T(8,128)(2,1)S(1)} %fusion.2), channel_id=1, source_target_pairs={{0,2},{1,3},{2,0},{3,1},{4,6},{5,7},{6,4},{7,5},{8,10},{9,11},{10,... | collective-permute-start | bytes 393224 | tf_op jit(solution)/shard_map/ppermute | solution.py:384
  37.4 1.0 %copy-start.4 = (bf16[3,64,1024]{2,1,0:T(8,128)(2,1)S(1)}, bf16[3,64,1024]{2,1,0:T(8,128)(2,1)}, u32[]{:S(2)}) copy-start(bf16[3,64,1024]{2,1,0:T(8,128)(2,1)} %qkv_hbm.1) | copy-start | bytes 1179652
  37.4 1.0 %copy-start.6 = (bf16[64,1024]{1,0:T(8,128)(2,1)S(1)}, bf16[64,1024]{1,0:T(8,128)(2,1)}, u32[]{:S(2)}) copy-start(bf16[64,1024]{1,0:T(8,128)(2,1)} %out_hbm.1) | copy-start | bytes 393220
  40.7 14.1 %copy-start.2 = (bf16[256,1024]{1,0:T(8,128)(2,1)}, bf16[256,1024]{1,0:T(8,128)(2,1)S(1)}, u32[]{:S(2)}) copy-start(bf16[256,1024]{1,0:T(8,128)(2,1)S(1)} %get-tuple-element.66.first) | copy-start | bytes 1572868
  41.1 0.8 copy-start.10
  41.2 2.3 %collective-permute-start.12 = (bf16[2,4,16,1024]{3,2,1,0:T(8,128)(2,1)S(1)}, bf16[2,4,16,1024]{3,2,1,0:T(8,128)(2,1)S(1)}, u32[]{:S(2)}, u32[]{:S(2)}) collective-permute-start(bf16[2,4,16,1024]{3,2,1,0:T(8,128)(2,1)S(1)} %bitcast.75), channel_id=1, source_target_pairs={{0,1},{1,0},{2,3},{3,2},{4,5},{5,4},{6,7},{7,6},{8,9},{9,8},{10,11... | collective-permute-start | bytes 786440 | tf_op jit(solution)/shard_map/ppermute | solution.py:384
  42.0 5.3 %collective-permute-start.11 = (bf16[4,16,1024]{2,1,0:T(8,128)(2,1)S(1)}, bf16[4,16,1024]{2,1,0:T(8,128)(2,1)S(1)}, u32[]{:S(2)}, u32[]{:S(2)}) collective-permute-start(bf16[4,16,1024]{2,1,0:T(8,128)(2,1)S(1)} %fusion.1), channel_id=1, source_target_pairs={{0,16},{16,0},{1,17},{17,1},{2,18},{18,2},{3,19},{19,3},{4,20},{20... | collective-permute-start | bytes 393224 | tf_op jit(solution)/shard_map/ppermute | solution.py:384
  43.6 5.1 %collective-permute-start.13 = (bf16[4,16,1024]{2,1,0:T(8,128)(2,1)S(1)}, bf16[4,16,1024]{2,1,0:T(8,128)(2,1)S(1)}, u32[]{:S(2)}, u32[]{:S(2)}) collective-permute-start(bf16[4,16,1024]{2,1,0:T(8,128)(2,1)S(1)} %fusion.3), channel_id=1, source_target_pairs={{0,2},{1,3},{2,0},{3,1},{4,6},{5,7},{6,4},{7,5},{8,10},{9,11},{10,... | collective-permute-start | bytes 393224 | tf_op jit(solution)/shard_map/ppermute | solution.py:384
  48.8 7.4 %collective-permute-start.17 = (bf16[16,1024]{1,0:T(8,128)(2,1)S(1)}, bf16[16,1024]{1,0:T(8,128)(2,1)S(1)}, u32[]{:S(2)}, u32[]{:S(2)}) collective-permute-start(bf16[16,1024]{1,0:T(8,128)(2,1)S(1)} %get-tuple-element.81), channel_id=1, source_target_pairs={{0,12},{4,8},{8,4},{12,0},{1,13},{5,9},{9,5},{13,1},{2,14},{6,10},... | collective-permute-start | bytes 98312 | tf_op jit(solution)/shard_map/ppermute | solution.py:384
  52.6 4.9 %collective-permute-start.16 = (bf16[16,1024]{1,0:T(8,128)(2,1)S(1)}, bf16[16,1024]{1,0:T(8,128)(2,1)S(1)}, u32[]{:S(2)}, u32[]{:S(2)}) collective-permute-start(bf16[16,1024]{1,0:T(8,128)(2,1)S(1)} %get-tuple-element.82), channel_id=1, source_target_pairs={{0,8},{4,12},{8,0},{12,4},{1,9},{5,13},{9,1},{13,5},{2,10},{6,14},... | collective-permute-start | bytes 98312 | tf_op jit(solution)/shard_map/ppermute | solution.py:384
  52.7 4.9 %collective-permute-start.15 = (bf16[16,1024]{1,0:T(8,128)(2,1)S(1)}, bf16[16,1024]{1,0:T(8,128)(2,1)S(1)}, u32[]{:S(2)}, u32[]{:S(2)}) collective-permute-start(bf16[16,1024]{1,0:T(8,128)(2,1)S(1)} %get-tuple-element.80), channel_id=1, source_target_pairs={{0,4},{4,0},{8,12},{12,8},{1,5},{5,1},{9,13},{13,9},{2,6},{6,2},{1... | collective-permute-start | bytes 98312 | tf_op jit(solution)/shard_map/ppermute | solution.py:384
  53.4 5.3 %collective-permute-start.14 = (bf16[4,16,1024]{2,1,0:T(8,128)(2,1)S(1)}, bf16[4,16,1024]{2,1,0:T(8,128)(2,1)S(1)}, u32[]{:S(2)}, u32[]{:S(2)}) collective-permute-start(bf16[4,16,1024]{2,1,0:T(8,128)(2,1)S(1)} %add_convert_fusion.2), channel_id=1, source_target_pairs={{0,4},{4,0},{8,12},{12,8},{1,5},{5,1},{9,13},{13,9},{2,6},{6,2},{1... | collective-permute-start | bytes 393224 | tf_op jit(solution)/shard_map/ppermute | solution.py:384
  54.8 16.4 %collective-permute-start.20 = (bf16[256,1024]{1,0:T(8,128)(2,1)S(1)}, bf16[256,1024]{1,0:T(8,128)(2,1)S(1)}, u32[]{:S(2)}, u32[]{:S(2)}) collective-permute-start(bf16[256,1024]{1,0:T(8,128)(2,1)S(1)} %get-tuple-element.66.first), channel_id=1, source_target_pairs={{0,16},{16,0},{1,17},{17,1},{2,18},{18,2},{3,19},{19,3},{4,20},{20... | collective-permute-start | bytes 1572872 | tf_op jit(solution)/shard_map/ppermute | solution.py:384
  58.7 7.3 %collective-permute-start.18 = (bf16[4,16,1024]{2,1,0:T(8,128)(2,1)S(1)}, bf16[4,16,1024]{2,1,0:T(8,128)(2,1)S(1)}, u32[]{:S(2)}, u32[]{:S(2)}) collective-permute-start(bf16[4,16,1024]{2,1,0:T(8,128)(2,1)S(1)} %add_convert_fusion.1), channel_id=1, source_target_pairs={{0,8},{4,12},{8,0},{12,4},{1,9},{5,13},{9,1},{13,5},{2,10},{6,14},... | collective-permute-start | bytes 393224 | tf_op jit(solution)/shard_map/ppermute | solution.py:384
  66.1 5.0 %collective-permute-start.19 = (bf16[4,16,1024]{2,1,0:T(8,128)(2,1)S(1)}, bf16[4,16,1024]{2,1,0:T(8,128)(2,1)S(1)}, u32[]{:S(2)}, u32[]{:S(2)}) collective-permute-start(bf16[4,16,1024]{2,1,0:T(8,128)(2,1)S(1)} %add_convert_fusion), channel_id=1, source_target_pairs={{0,2},{1,3},{2,0},{3,1},{4,6},{5,7},{6,4},{7,5},{8,10},{9,11},{10,... | collective-permute-start | bytes 393224 | tf_op jit(solution)/shard_map/ppermute | solution.py:384
  71.2 0.8 %copy-start.9 = (bf16[256,1024]{1,0:T(8,128)(2,1)}, bf16[256,1024]{1,0:T(8,128)(2,1)S(1)}, u32[]{:S(2)}) copy-start(bf16[256,1024]{1,0:T(8,128)(2,1)S(1)} %collective-permute-done.20.second) | copy-start | bytes 1572868
  74.1 1.5 %collective-permute-start.21 = (bf16[2,4,16,1024]{3,2,1,0:T(8,128)(2,1)S(1)}, bf16[2,4,16,1024]{3,2,1,0:T(8,128)(2,1)S(1)}, u32[]{:S(2)}, u32[]{:S(2)}) collective-permute-start(bf16[2,4,16,1024]{3,2,1,0:T(8,128)(2,1)S(1)} %pad_maximum_fusion.3.near_ref), channel_id=1, source_target_pairs={{0,1},{1,0},{2,3},{3,2},{4,5},{5,4},{6,7},{7,6},{8,9},{9,8},{10,11... | collective-permute-start | bytes 786440 | tf_op jit(solution)/shard_map/ppermute | solution.py:384

commit v2 on v1

--- a/solution.py
+++ b/solution.py
@@ -297,7 +297,7 @@
             jax.ShapeDtypeStruct((count, D_C), jnp.bfloat16),
             jax.ShapeDtypeStruct((4 * HD, D_C), jnp.bfloat16),
         ),
-        in_specs=[vmem] * 3 + [pl.BlockSpec(memory_space=pl.ANY)] * 2,
+        in_specs=[vmem] * 3 + [pl.BlockSpec(memory_space=pltpu.HBM)] * 2,
         out_specs=(vmem, vmem),
         scratch_shapes=[
             pltpu.VMEM(head_qkv.shape, jnp.bfloat16),
@@ -309,30 +309,35 @@
     )(tokens, cotangents, factor, head_qkv, head_out)
 
 
-def pack_body(first, second, x_ref, dy_ref, own_ref):
+def pack_body(x_ref, dy_ref, own_ref):
     own_ref[:, :D_C] = x_ref[...].astype(jnp.float32).reshape(-1, D_C).astype(jnp.bfloat16)
     own_ref[:, D_C:] = dy_ref[...].astype(jnp.float32).reshape(-1, D_C).astype(jnp.bfloat16)
 
 
-def packed(after, tokens, cotangents):
+def packed(tokens, cotangents):
     vmem = pl.BlockSpec(memory_space=pltpu.VMEM)
     count = tokens.shape[0] * tokens.shape[1]
     return pl.pallas_call(
         pack_body,
         out_shape=jax.ShapeDtypeStruct((count, 2 * D_C), jnp.bfloat16),
-        in_specs=[pl.BlockSpec(memory_space=pl.ANY)] * 2 + [vmem] * 2,
+        in_specs=[vmem] * 2,
         out_specs=vmem,
+        compiler_params=pltpu.CompilerParams(vmem_limit_bytes=vmem_bytes),
         name="pack_coarse",
-    )(*after, tokens, cotangents)
-
-
-def pair_sum_body(first, second, qkv_ref, out_ref):
-    total = (first[...].astype(jnp.float32) + second[...].astype(jnp.float32)).astype(jnp.bfloat16)
-    qkv_ref[...] = total[: 3 * HD].reshape(qkv_ref.shape)
-    out_ref[...] = total[3 * HD :]
-
-
-def pair_sum(first, second):
+    )(tokens, cotangents)
+
+
+def pair_sum_body(own, first, second, qkv_ref, out_ref):
+    for part in range(4):
+        come = (first, second)[part // 2][(part % 2) * HD : (part % 2 + 1) * HD]
+        total = own[part * HD : (part + 1) * HD].astype(jnp.float32) + come.astype(jnp.float32)
+        if part < 3:
+            qkv_ref[part] = total.astype(jnp.bfloat16)
+        else:
+            out_ref[...] = total.astype(jnp.bfloat16)
+
+
+def pair_sum(own, first, second):
     vmem = pl.BlockSpec(memory_space=pltpu.VMEM)
     return pl.pallas_call(
         pair_sum_body,
@@ -340,37 +345,66 @@
             jax.ShapeDtypeStruct((3, HD, D_C), jnp.bfloat16),
             jax.ShapeDtypeStruct((HD, D_C), jnp.bfloat16),
         ),
-        in_specs=[vmem, vmem],
+        in_specs=[vmem] * 3,
         out_specs=(vmem, vmem),
+        compiler_params=pltpu.CompilerParams(vmem_limit_bytes=vmem_bytes),
         name="pair_sum",
-    )(first, second)
-
-
-def place_body(place, near_ref, far_ref, qkv_ref, out_ref):
-    highs, downs, rows = near_ref.shape[0], near_ref.shape[1], near_ref.shape[2]
+    )(own, first, second)
+
+
+def last_body(
+    place,
+    near_ref,
+    far_ref,
+    x_ref,
+    factor_ref,
+    kept_ref,
+    come_ref,
+    qkv_hbm,
+    out_hbm,
+    dx_ref,
+    sems,
+):
+    highs, rows = near_ref.shape[0], near_ref.shape[1]
+    copies = []
     for low in range(2):
         for high in range(highs):
-            for row in range(downs):
-                block = (place[0] ^ (2 * high + low)) * downs + row
-                at = pl.ds(pl.multiple_of(block * rows, rows), rows)
-                piece = (near_ref, far_ref)[low][high, row]
-                qkv_ref[at] = piece[:, : 3 * D_F]
-                out_ref[at] = piece[:, 3 * D_F :]
-
-
-def place_blocks(place, near, far):
+            source = (near_ref, far_ref)[low].at[high]
+            block = place[0] ^ (2 * high + low)
+            at = pl.ds(pl.multiple_of(block * rows, rows), rows)
+            for part, target in enumerate((qkv_hbm, out_hbm)):
+                lanes = (slice(0, 3 * D_F), slice(3 * D_F, 4 * D_F))[part]
+                copies.append(
+                    pltpu.make_async_copy(
+                        source.at[:, lanes], target.at[at, :], sems.at[low, high, part]
+                    )
+                )
+    for copy in copies:
+        copy.start()
+    tokens = x_ref[...].astype(jnp.float32).reshape(-1, D_C)
+    upstream = kept_ref[...] + come_ref[...].astype(jnp.float32)
+    grads = norm_backward(tokens, inverse_rms(tokens), factor_ref[...], upstream)
+    dx_ref[...] = grads.astype(jnp.float32).reshape(dx_ref.shape).astype(jnp.bfloat16)
+    for copy in copies:
+        copy.wait()
+
+
+def last_step(place, near, far, tokens, factor, kept, come):
     vmem = pl.BlockSpec(memory_space=pltpu.VMEM)
+    hbm = pl.BlockSpec(memory_space=pltpu.HBM)
     return pl.pallas_call(
-        place_body,
+        last_body,
         out_shape=(
             jax.ShapeDtypeStruct((D_F, 3 * D_F), jnp.bfloat16),
             jax.ShapeDtypeStruct((D_F, D_F), jnp.bfloat16),
+            jax.ShapeDtypeStruct(tokens.shape, jnp.bfloat16),
         ),
-        in_specs=[pl.BlockSpec(memory_space=pltpu.SMEM), vmem, vmem],
-        out_specs=(vmem, vmem),
+        in_specs=[pl.BlockSpec(memory_space=pltpu.SMEM)] + [vmem] * 6,
+        out_specs=(hbm, hbm, vmem),
+        scratch_shapes=[pltpu.SemaphoreType.DMA((2, near.shape[0], 2))],
         compiler_params=pltpu.CompilerParams(vmem_limit_bytes=vmem_bytes),
-        name="place_blocks",
-    )(place, near, far)
+        name="last_step",
+    )(place, near, far, tokens, factor, kept, come)
 
 
 def neighbours(low_edge, high_edge, axis):
@@ -405,13 +439,6 @@
 def all_rows(piece):
     downs = lax.axis_size("gy")
     return jnp.stack([piece] + [swapped(piece, "gy", row) for row in range(1, downs)])
-
-
-def row_sum(pieces):
-    total = wide(pieces[0])
-    for row in range(1, pieces.shape[0]):
-        total = total + wide(swapped(narrow(pieces[row]), "gy", row))
-    return total
 
 
 def local(
@@ -437,10 +464,6 @@
     low = jnp.concatenate([picture[:HALO], cotangent[:RAD]], axis=0)
     high = jnp.concatenate([picture[height - HALO :], cotangent[height - RAD :]], axis=0)
     above, below = neighbours(low, high, "gy")
-    own = packed((low, high), x_coarse[0], dy_coarse[0])
-    count = own.shape[0]
-    row_group = all_rows(own)
-
     row_first = gy * height - HALO
     col_first = gx * breadth - HALO
     limits = jnp.stack(
@@ -455,9 +478,18 @@
     ).astype(jnp.int32)
     factor = time_gain(fine_gain, step_value)[None]
     coarse_factor = time_gain(coarse_gain, step_value)[None]
-    above, below, limits, factor, coarse_factor = tied(above, below, limits, factor, coarse_factor)
+    place = gx.astype(jnp.int32)[None]
+    coarse_picture, coarse_cot = x_coarse[0], dy_coarse[0]
+    above, below, limits, place, factor, coarse_factor = tied(
+        above, below, limits, place, factor, coarse_factor
+    )
     column = jnp.concatenate([above, picture, cotangent, below], axis=0)
-    left, right = neighbours(column[:, :HALO], column[:, breadth - HALO :], "gx")
+    first, final = column[:, :HALO], column[:, breadth - HALO :]
+    first, final, coarse_picture, coarse_cot = tied(first, final, coarse_picture, coarse_cot)
+    left, right = neighbours(first, final, "gx")
+    own = packed(coarse_picture, coarse_cot)
+    count = own.shape[0]
+    row_group = all_rows(own)
     left, right, row_group = tied(left, right, row_group)
     pair = jnp.stack([row_group, swapped(row_group, "gx", 2)])
     dx_picture, fine_keep, fine_send = fine_block(
@@ -486,41 +518,55 @@
     )
     fine_quarter, parts, coarse_partial = tied(fine_quarter, parts, coarse_partial)
 
-    fine_quarter = narrow(batch_sum(fine_quarter))
+    rows = D_F // across
+    fine_quarter = narrow(batch_sum(fine_quarter)).reshape(rows, 4 * D_F)
     parts = parts.reshape(2, 2, downs, count, D_C)
-    coarse_half = wide(parts[0]) + wide(swapped(parts[1], "gx", 1))
-    coarse_quarter = wide(coarse_half[0]) + wide(swapped(narrow(coarse_half[1]), "gx", 2))
-    fine_quarter, coarse_quarter, coarse_partial = tied(
-        fine_quarter, coarse_quarter, coarse_partial
-    )
+    coarse_kept = wide(parts[0]) + wide(swapped(parts[1], "gx", 1))
+    fine_quarter, coarse_kept, coarse_partial = tied(fine_quarter, coarse_kept, coarse_partial)
 
     pair_batch = lax.axis_size("batch") == 2
-    coarse_other = swapped(coarse_partial, "batch", 1) if pair_batch else coarse_partial
+    halves = (coarse_partial[: 2 * HD], coarse_partial[2 * HD :])
+    others = [swapped(half, "batch", 1) if pair_batch else half for half in halves]
     mask = 1
     while mask < downs:
-        fine_quarter = narrow(wide(fine_quarter) + wide(swapped(fine_quarter, "gy", mask)))
-        if mask == 1:
-            coarse_down = row_sum(coarse_quarter)
-            fine_quarter, coarse_down = tied(fine_quarter, coarse_down)
+        last = 2 * mask == downs
+        coarse_kept = coarse_kept.reshape(2, -1, 2, count, D_C)
+        sent = narrow(coarse_kept[:, :, 1]).reshape(-1, D_C)
+        come = swapped(jnp.concatenate([fine_quarter, sent], axis=0), "gy", mask)
+        coarse_kept = coarse_kept[:, :, 0]
+        coarse_kept = coarse_kept + wide(come[rows:]).reshape(coarse_kept.shape)
+        fine_quarter = narrow(wide(fine_quarter) + wide(come[:rows]))
+        at = int(last)
+        fine_quarter, coarse_kept, others[at] = tied(fine_quarter, coarse_kept, others[at])
         mask *= 2
-    coarse_floats = wide(x_coarse[0].reshape(-1, D_C))
-    dx_coarse = norm_backward(
-        coarse_floats, inverse_rms(coarse_floats), coarse_factor, coarse_down
-    ).reshape(x_coarse.shape)
-    fine_quarter, dx_coarse = tied(fine_quarter, dx_coarse)
-
-    fine_pair = jnp.stack([fine_quarter, swapped(fine_quarter, "gx", 2)])
+
+    coarse_kept = coarse_kept.reshape(2, count, D_C)
+    come = swapped(jnp.concatenate([fine_quarter, narrow(coarse_kept[1])], axis=0), "gx", 2)
     if pair_batch:
-        grad_coarse_qkv, grad_coarse_out = pair_sum(coarse_partial, coarse_other)
+        grad_coarse_qkv, grad_coarse_out = pair_sum(coarse_partial, *others)
     else:
         coarse_sum = narrow(batch_sum(wide(coarse_partial)))
         grad_coarse_qkv = coarse_sum[: 3 * HD].reshape(coarse_qkv.shape)
         grad_coarse_out = coarse_sum[3 * HD :]
-    fine_pair, grad_coarse_qkv, grad_coarse_out = tied(fine_pair, grad_coarse_qkv, grad_coarse_out)
-    grad_qkv, grad_out = place_blocks(
-        jnp.stack([gx, gy]).astype(jnp.int32), fine_pair, swapped(fine_pair, "gx", 1)
-    )
-    return (dx_picture[None], dx_coarse, grad_qkv, grad_out, grad_coarse_qkv, grad_coarse_out)
+    come, grad_coarse_qkv, grad_coarse_out = tied(come, grad_coarse_qkv, grad_coarse_out)
+    fine_pair = jnp.stack([fine_quarter, come[:rows]])
+    grad_qkv, grad_out, dx_coarse = last_step(
+        place,
+        fine_pair,
+        swapped(fine_pair, "gx", 1),
+        coarse_picture,
+        coarse_factor,
+        coarse_kept[0],
+        come[rows:],
+    )
+    return (
+        dx_picture[None],
+        dx_coarse[None],
+        grad_qkv,
+        grad_out,
+        grad_coarse_qkv,
+        grad_coarse_out,
+    )
 
 
 def solution(mesh):

time: 77.4 us -> 75.2 us (0.972)
  waiting for transfers between devices: 20.5 us -> 30.1 us
  starting transfers between devices: 35 us -> 27.7 us
  Pallas kernels: 13.7 us -> 11.2 us
  local copies, waits for them, and re-layouts: 4.93 us -> 3.55 us
    ppermute x18 -> x15, starting transfers between devices: 26.1 us -> 18.8 us  [swapped(): lax.ppermute(value, axis, [(i, i ^ mask) for i in range(lax.axis_size(axi...]
    ppermute x2, waiting for transfers between devices: 2.11 us -> 6.93 us  [neighbours(): lax.ppermute(low_edge, axis, down)]
    ppermute x18 -> x15, waiting for transfers between devices: 18.4 us -> 23 us  [swapped(): lax.ppermute(value, axis, [(i, i ^ mask) for i in range(lax.axis_size(axi...]
    pallas_call x1, Pallas kernels: 1.45 us -> 0.01 us  [packed(): pl.pallas_call(pack_body, out_shape=jax.ShapeDtypeStruct((count, 2 * D_C)...]
    pallas_call x1, Pallas kernels: 2.08 us -> 0.88 us  [pair_sum(): pl.pallas_call(pair_sum_body, out_shape=(jax.ShapeDtypeStruct((3, HD, D_C...]
    unnamed x28 -> x20, local copies, waits for them, and re-layouts: 3.08 us -> 2.35 us
  transfers between devices with their start and end apart: 22 -> 19, of which waited for: 11 -> 12; matrix products, arithmetic and copies ran while one was open for 2% -> 1% of each run, Pallas kernels for 13% -> 13%
where the time goes in v2:
time: 75.2 us; the launch traced here: 74.9 us
  waiting for transfers between devices  30.1 us (40%)
  starting transfers between devices  27.7 us (37%)
  Pallas kernels  11.2 us (15%)
  local copies, waits for them, and re-layouts  3.55 us (5%)
  between operations  1.67 us (2%)
    ppermute x15, waiting for transfers between devices, swapped(): lax.ppermute(value, axis, [(i, i ^ mask) for i in range(lax.axis_size(axi...  23 us
    ppermute x15, starting transfers between devices, swapped(): lax.ppermute(value, axis, [(i, i ^ mask) for i in range(lax.axis_size(axi...  18.8 us
    ppermute x2, waiting for transfers between devices, neighbours(): lax.ppermute(low_edge, axis, down)  6.93 us
    pallas_call x1, Pallas kernels, fine_block(): pl.pallas_call(fine_body, out_shape=(jax.ShapeDtypeStruct((height, breadt...  6.59 us
    ppermute x2, starting transfers between devices, neighbours(): lax.ppermute(high_edge, axis, up)  6.22 us
    ppermute x2, starting transfers between devices, neighbours(): lax.ppermute(low_edge, axis, down)  2.72 us
    unnamed x20, local copies, waits for them, and re-layouts  2.35 us
    pallas_call x1, Pallas kernels, coarse_block(): pl.pallas_call(coarse_body, out_shape=(jax.ShapeDtypeStruct((count, D_C),...  2.22 us
  transfers between devices with their start and end apart: 19, of which 12 were waited for; matrix products, arithmetic and copies ran while one was open for 1% of the time, Pallas kernels for 13%

profile of v2, /device:TPU:0, one launch (start us, length us, event | category | flops | bytes accessed | tf_op | source)
XLA Modules:
  0.0 74.9 jit_solution(11282619317683700929)
XLA Ops:
  0.6 0.9 %slice_bitcast_fusion.5 = (bf16[3,32,256]{2,1,0:T(8,128)(2,1)S(1)}, bf16[3,32,256]{2,1,0:T(8,128)(2,1)S(1)}) fusion(bf16[1,8,32,256]{3,2,1,0:T(8,128)(2,1)} %param.12), kind=kLoop, calls=%fused_computation.33 | loop fusion | bytes 196608 | tf_op jit(solution)/shard_map/slice | solution.py:464
  1.5 0.1 copy-done
  1.6 4.9 %collective-permute-start = (bf16[9,32,256]{2,1,0:T(8,128)(2,1)S(1)}, bf16[9,32,256]{2,1,0:T(8,128)(2,1)S(1)}, u32[]{:S(2)}, u32[]{:S(2)}) collective-permute-start(bf16[9,32,256]{2,1,0:T(8,128)(2,1)S(1)} %pad_maximum_fusion.7), channel_id=1, source_target_pairs={{0,4},{4,8},{8,12},{1,5},{5,9},{9,13},{2,6},{6,10},{10,14},{3,7},{... | collective-permute-start | bytes 442376 | tf_op jit(solution)/shard_map/ppermute | solution.py:414
  6.6 0.0 copy-start.1
  6.6 1.4 %collective-permute-start.1 = (bf16[9,32,256]{2,1,0:T(8,128)(2,1)S(1)}, bf16[9,32,256]{2,1,0:T(8,128)(2,1)S(1)}, u32[]{:S(2)}, u32[]{:S(2)}) collective-permute-start(bf16[9,32,256]{2,1,0:T(8,128)(2,1)S(1)} %pad_maximum_fusion.8), channel_id=1, source_target_pairs={{4,0},{8,4},{12,8},{5,1},{9,5},{13,9},{6,2},{10,6},{14,10},{7,3},{... | collective-permute-start | bytes 442376 | tf_op jit(solution)/shard_map/ppermute | solution.py:414
  8.0 0.0 copy-start.8
  8.7 0.0 copy-done.8
  8.7 0.1 add_multiply_fusion
  8.8 0.0 copy-start.9
  8.8 0.1 stack.69.limits
  8.9 0.6 copy-done.9
  9.5 0.1 add_multiply_fusion.1
  9.5 0.1 collective-permute-done.above_ref
  9.6 4.3 %collective-permute-done.1.below_ref = bf16[9,32,256]{2,1,0:T(8,128)(2,1)S(1)} collective-permute-done((bf16[9,32,256]{2,1,0:T(8,128)(2,1)S(1)}, bf16[9,32,256]{2,1,0:T(8,128)(2,1)S(1)}, u32[]{:S(2)}, u32[]{:S(2)}) %collective-permute-start.1) | collective-permute-done | bytes 147488 | tf_op jit(solution)/shard_map/ppermute | solution.py:414
  14.0 0.0 copy-start.2
  14.0 0.7 copy-done.6
  14.7 0.0 copy-done.7
  14.7 1.6 %collective-permute-start.6 = (bf16[16,2048]{1,0:T(8,128)(2,1)S(1)}, bf16[16,2048]{1,0:T(8,128)(2,1)S(1)}, u32[]{:S(2)}, u32[]{:S(2)}) collective-permute-start(bf16[16,2048]{1,0:T(8,128)(2,1)S(1)} %pack_coarse.1), channel_id=1, source_target_pairs={{0,12},{4,8},{8,4},{12,0},{1,13},{5,9},{9,5},{13,1},{2,14},{6,10},... | collective-permute-start | bytes 196616 | tf_op jit(solution)/shard_map/ppermute | solution.py:418
  16.4 1.5 %collective-permute-start.5 = (bf16[16,2048]{1,0:T(8,128)(2,1)S(1)}, bf16[16,2048]{1,0:T(8,128)(2,1)S(1)}, u32[]{:S(2)}, u32[]{:S(2)}) collective-permute-start(bf16[16,2048]{1,0:T(8,128)(2,1)S(1)} %pack_coarse.1), channel_id=1, source_target_pairs={{0,8},{4,12},{8,0},{12,4},{1,9},{5,13},{9,1},{13,5},{2,10},{6,14},... | collective-permute-start | bytes 196616 | tf_op jit(solution)/shard_map/ppermute | solution.py:418
  17.8 1.4 %collective-permute-start.4 = (bf16[16,2048]{1,0:T(8,128)(2,1)S(1)}, bf16[16,2048]{1,0:T(8,128)(2,1)S(1)}, u32[]{:S(2)}, u32[]{:S(2)}) collective-permute-start(bf16[16,2048]{1,0:T(8,128)(2,1)S(1)} %pack_coarse.1), channel_id=1, source_target_pairs={{0,4},{4,0},{8,12},{12,8},{1,5},{5,1},{9,13},{13,9},{2,6},{6,2},{1... | collective-permute-start | bytes 196616 | tf_op jit(solution)/shard_map/ppermute | solution.py:418
  19.2 1.3 %collective-permute-start.2 = (bf16[34,6,256]{2,1,0:T(8,128)(2,1)S(1)}, bf16[34,6,256]{2,1,0:T(8,128)(2,1)S(1)}, u32[]{:S(2)}, u32[]{:S(2)}) collective-permute-start(bf16[34,6,256]{2,1,0:T(8,128)(2,1)S(1)} %get-tuple-element.51), channel_id=1, source_target_pairs={{0,1},{1,2},{2,3},{4,5},{5,6},{6,7},{8,9},{9,10},{10,11},{12,13},{... | collective-permute-start | bytes 313352 | tf_op jit(solution)/shard_map/ppermute | solution.py:414
  20.5 1.3 %collective-permute-start.3 = (bf16[34,6,256]{2,1,0:T(8,128)(2,1)S(1)}, bf16[34,6,256]{2,1,0:T(8,128)(2,1)S(1)}, u32[]{:S(2)}, u32[]{:S(2)}) collective-permute-start(bf16[34,6,256]{2,1,0:T(8,128)(2,1)S(1)} %get-tuple-element.52), channel_id=1, source_target_pairs={{1,0},{2,1},{3,2},{5,4},{6,5},{7,6},{9,8},{10,9},{11,10},{13,12},{... | collective-permute-start | bytes 313352 | tf_op jit(solution)/shard_map/ppermute | solution.py:414
  21.8 0.0 collective-permute-done.6
  21.8 1.0 %collective-permute-done.5 = bf16[16,2048]{1,0:T(8,128)(2,1)S(1)} collective-permute-done((bf16[16,2048]{1,0:T(8,128)(2,1)S(1)}, bf16[16,2048]{1,0:T(8,128)(2,1)S(1)}, u32[]{:S(2)}, u32[]{:S(2)}) %collective-permute-start.5) | collective-permute-done | bytes 65568 | tf_op jit(solution)/shard_map/ppermute | solution.py:418
  22.8 0.0 collective-permute-done.4
  22.8 0.0 collective-permute-done.2.left_ref
  22.8 2.6 %collective-permute-done.3.right_ref = bf16[34,6,256]{2,1,0:T(8,128)(2,1)S(1)} collective-permute-done((bf16[34,6,256]{2,1,0:T(8,128)(2,1)S(1)}, bf16[34,6,256]{2,1,0:T(8,128)(2,1)S(1)}, u32[]{:S(2)}, u32[]{:S(2)}) %collective-permute-start.3) | collective-permute-done | bytes 104480 | tf_op jit(solution)/shard_map/ppermute | solution.py:414
  25.5 3.4 %collective-permute-start.7 = (bf16[4,16,2048]{2,1,0:T(8,128)(2,1)S(1)}, bf16[4,16,2048]{2,1,0:T(8,128)(2,1)S(1)}, u32[]{:S(2)}, u32[]{:S(2)}) collective-permute-start(bf16[4,16,2048]{2,1,0:T(8,128)(2,1)S(1)} %pad_maximum_fusion.2), channel_id=1, source_target_pairs={{0,2},{1,3},{2,0},{3,1},{4,6},{5,7},{6,4},{7,5},{8,10},{9,11},{10,... | collective-permute-start | bytes 786440 | tf_op jit(solution)/shard_map/ppermute | solution.py:418
  28.8 6.6 %fine_block.1 = (bf16[8,32,256]{2,1,0:T(8,128)(2,1)}, f32[2,4,16,1024]{3,2,1,0:T(8,128)S(1)}, bf16[2,4,16,1024]{3,2,1,0:T(8,128)(2,1)S(1)}) custom-call(s32[6]{0:T(128)S(1)} %stack.69.limits, bf16[8,32,256]{2,1,0:T(8,128)(2,1)S(1)} %bitcast.66, bf16[8,32,256]{2,1,0:T(8,128)(2,1)S(1)} %bitcast.68, bf16[9,32,256]{2,1,0:T(8,128)(2,1)S(1)} %collective-permute-done.above_ref, ...), custom_call_target="tpu_custom_call" | custom-call | tf_op jit(solution)/shard_map/fine_block/pallas_call | solution.py:218
  35.4 0.0 collective-permute-done.7
  35.4 0.1 pad_maximum_fusion.1
  35.5 0.4 collective-permute-start.9
  35.9 0.1 collective-permute-start.8
  36.1 1.8 %collective-permute-done.8 = bf16[2,4,16,1024]{3,2,1,0:T(8,128)(2,1)S(1)} collective-permute-done((bf16[2,4,16,1024]{3,2,1,0:T(8,128)(2,1)S(1)}, bf16[2,4,16,1024]{3,2,1,0:T(8,128)(2,1)S(1)}, u32[]{:S(2)}, u32[]{:S(2)}) %collective-permute-start.8) | collective-permute-done | bytes 262176 | tf_op jit(solution)/shard_map/ppermute | solution.py:418
  37.8 0.1 convert_add_fusion.1
  37.9 0.0 collective-permute-done.9
  37.9 2.2 %collective-permute-start.10 = (bf16[4,16,1024]{2,1,0:T(8,128)(2,1)S(1)}, bf16[4,16,1024]{2,1,0:T(8,128)(2,1)S(1)}, u32[]{:S(2)}, u32[]{:S(2)}) collective-permute-start(bf16[4,16,1024]{2,1,0:T(8,128)(2,1)S(1)} %fusion.2), channel_id=1, source_target_pairs={{0,2},{1,3},{2,0},{3,1},{4,6},{5,7},{6,4},{7,5},{8,10},{9,11},{10,... | collective-permute-start | bytes 393224 | tf_op jit(solution)/shard_map/ppermute | solution.py:418
  40.1 0.1 pad_maximum_fusion
  40.2 0.0 copy-start.3
  40.2 0.0 copy-start.5
  40.3 0.1 fusion.5
  40.3 0.9 %copy-done.3 = bf16[3,64,1024]{2,1,0:T(8,128)(2,1)S(1)} copy-done((bf16[3,64,1024]{2,1,0:T(8,128)(2,1)S(1)}, bf16[3,64,1024]{2,1,0:T(8,128)(2,1)}, u32[]{:S(2)}) %copy-start.3) | copy-done | bytes 393240
  41.2 0.0 copy-done.5
  41.3 2.2 %coarse_block.1 = (bf16[256,1024]{1,0:T(8,128)(2,1)S(1)}, bf16[256,1024]{1,0:T(8,128)(2,1)S(1)}) custom-call(bf16[256,1024]{1,0:T(8,128)(2,1)S(1)} %get-tuple-element.91.x_ref, bf16[256,1024]{1,0:T(8,128)(2,1)S(1)} %get-tuple-element.90.dy_ref, f32[1,1024]{1,0:T(1,128)S(1)} %bitcast.72, bf16[3,64,1024]{2,1,0:T(8,128)(2,1)S(1)} %copy-done.3, ...), custom_call_target="tpu_custom_call" | custom-call | tf_op jit(solution)/shard_map/coarse_block/pallas_call | solution.py:294
  43.5 0.4 collective-permute-done.10
  44.0 1.6 %collective-permute-start.11 = (bf16[4,16,1024]{2,1,0:T(8,128)(2,1)S(1)}, bf16[4,16,1024]{2,1,0:T(8,128)(2,1)S(1)}, u32[]{:S(2)}, u32[]{:S(2)}) collective-permute-start(bf16[4,16,1024]{2,1,0:T(8,128)(2,1)S(1)} %fusion.1), channel_id=1, source_target_pairs={{0,16},{16,0},{1,17},{17,1},{2,18},{18,2},{3,19},{19,3},{4,20},{20... | collective-permute-start | bytes 393224 | tf_op jit(solution)/shard_map/ppermute | solution.py:418
  45.6 0.1 collective-permute-start.12
  45.7 3.4 %collective-permute-done.11 = bf16[4,16,1024]{2,1,0:T(8,128)(2,1)S(1)} collective-permute-done((bf16[4,16,1024]{2,1,0:T(8,128)(2,1)S(1)}, bf16[4,16,1024]{2,1,0:T(8,128)(2,1)S(1)}, u32[]{:S(2)}, u32[]{:S(2)}) %collective-permute-start.11) | collective-permute-done | bytes 131104 | tf_op jit(solution)/shard_map/ppermute | solution.py:418
  49.1 0.0 collective-permute-done.12
  49.1 0.1 convert_add_fusion
  49.2 0.7 collective-permute-start.13
  50.0 1.6 %collective-permute-start.14 = (bf16[128,1024]{1,0:T(8,128)(2,1)S(1)}, bf16[128,1024]{1,0:T(8,128)(2,1)S(1)}, u32[]{:S(2)}, u32[]{:S(2)}) collective-permute-start(bf16[128,1024]{1,0:T(8,128)(2,1)S(1)} %get-tuple-element.95), channel_id=1, source_target_pairs={{0,16},{16,0},{1,17},{17,1},{2,18},{18,2},{3,19},{19,3},{4,20},{20... | collective-permute-start | bytes 786440 | tf_op jit(solution)/shard_map/ppermute | solution.py:418
  51.6 4.6 %collective-permute-done.13 = bf16[128,1024]{1,0:T(8,128)(2,1)S(1)} collective-permute-done((bf16[128,1024]{1,0:T(8,128)(2,1)S(1)}, bf16[128,1024]{1,0:T(8,128)(2,1)S(1)}, u32[]{:S(2)}, u32[]{:S(2)}) %collective-permute-start.13) | collective-permute-done | bytes 262176 | tf_op jit(solution)/shard_map/ppermute | solution.py:418
  56.3 0.4 collective-permute-done.14.first
  56.8 1.5 %collective-permute-start.15 = (bf16[96,1024]{1,0:T(8,128)(2,1)S(1)}, bf16[96,1024]{1,0:T(8,128)(2,1)S(1)}, u32[]{:S(2)}, u32[]{:S(2)}) collective-permute-start(bf16[96,1024]{1,0:T(8,128)(2,1)S(1)} %pad_maximum_fusion.5), channel_id=1, source_target_pairs={{0,8},{4,12},{8,0},{12,4},{1,9},{5,13},{9,1},{13,5},{2,10},{6,14},... | collective-permute-start | bytes 589832 | tf_op jit(solution)/shard_map/ppermute | solution.py:418
  58.3 1.5 %collective-permute-start.16 = (bf16[128,1024]{1,0:T(8,128)(2,1)S(1)}, bf16[128,1024]{1,0:T(8,128)(2,1)S(1)}, u32[]{:S(2)}, u32[]{:S(2)}) collective-permute-start(bf16[128,1024]{1,0:T(8,128)(2,1)S(1)} %get-tuple-element.94), channel_id=1, source_target_pairs={{0,16},{16,0},{1,17},{17,1},{2,18},{18,2},{3,19},{19,3},{4,20},{20... | collective-permute-start | bytes 786440 | tf_op jit(solution)/shard_map/ppermute | solution.py:418
  59.8 6.5 %collective-permute-done.15 = bf16[96,1024]{1,0:T(8,128)(2,1)S(1)} collective-permute-done((bf16[96,1024]{1,0:T(8,128)(2,1)S(1)}, bf16[96,1024]{1,0:T(8,128)(2,1)S(1)}, u32[]{:S(2)}, u32[]{:S(2)}) %collective-permute-start.15) | collective-permute-done | bytes 196640 | tf_op jit(solution)/shard_map/ppermute | solution.py:418
  66.3 0.0 collective-permute-done.16.second
  66.4 1.1 %collective-permute-start.17 = (bf16[80,1024]{1,0:T(8,128)(2,1)S(1)}, bf16[80,1024]{1,0:T(8,128)(2,1)S(1)}, u32[]{:S(2)}, u32[]{:S(2)}) collective-permute-start(bf16[80,1024]{1,0:T(8,128)(2,1)S(1)} %pad_maximum_fusion.6), channel_id=1, source_target_pairs={{0,2},{1,3},{2,0},{3,1},{4,6},{5,7},{6,4},{7,5},{8,10},{9,11},{10,... | collective-permute-start | bytes 491528 | tf_op jit(solution)/shard_map/ppermute | solution.py:418
  67.5 0.9 %pair_sum.1 = (bf16[3,64,1024]{2,1,0:T(8,128)(2,1)}, bf16[64,1024]{1,0:T(8,128)(2,1)}) custom-call(bf16[256,1024]{1,0:T(8,128)(2,1)S(1)} %get-tuple-element.75.own, bf16[128,1024]{1,0:T(8,128)(2,1)S(1)} %collective-permute-done.14.first, bf16[128,1024]{1,0:T(8,128)(2,1)S(1)} %collective-permute-done.16.second), custom_call_target="tpu_custom_call" | custom-call | tf_op jit(solution)/shard_map/pair_sum/pallas_call | solution.py:342
  68.3 3.4 %collective-permute-done.17 = bf16[80,1024]{1,0:T(8,128)(2,1)S(1)} collective-permute-done((bf16[80,1024]{1,0:T(8,128)(2,1)S(1)}, bf16[80,1024]{1,0:T(8,128)(2,1)S(1)}, u32[]{:S(2)}, u32[]{:S(2)}) %collective-permute-start.17) | collective-permute-done | bytes 163872 | tf_op jit(solution)/shard_map/ppermute | solution.py:418
  71.8 0.1 collective-permute-start.18
  71.9 1.5 %collective-permute-done.18.far_ref = bf16[2,64,1024]{2,1,0:T(8,128)(2,1)S(1)} collective-permute-done((bf16[2,64,1024]{2,1,0:T(8,128)(2,1)S(1)}, bf16[2,64,1024]{2,1,0:T(8,128)(2,1)S(1)}, u32[]{:S(2)}, u32[]{:S(2)}) %collective-permute-start.18) | collective-permute-done | bytes 262176 | tf_op jit(solution)/shard_map/ppermute | solution.py:418
  73.4 1.5 %last_step.1 = (bf16[256,768]{1,0:T(8,128)(2,1)}, bf16[256,256]{1,0:T(8,128)(2,1)}, bf16[4,4,1024]{2,1,0:T(4,128)(2,1)}) custom-call(s32[1]{0:T(128)} %bitcast.8.place, bf16[2,64,1024]{2,1,0:T(8,128)(2,1)S(1)} %pad_maximum_fusion.4.near_ref, bf16[2,64,1024]{2,1,0:T(8,128)(2,1)S(1)} %collective-permute-done.18.far_ref, bf16[4,4,1024]{2,1,0:T(4,128)(2,1)S(1)} %bitcast.71, ...), custom_call_target="tpu_custom_call" | custom-call | tf_op jit(solution)/shard_map/last_step/pallas_call | solution.py:395
  (34 shorter events, 0.5 us)
Async XLA Ops:
  0.6 1.0 %copy-start = (bf16[1,8,32,256]{3,2,1,0:T(8,128)(2,1)S(1)}, bf16[1,8,32,256]{3,2,1,0:T(8,128)(2,1)}, u32[]{:S(2)}) copy-start(bf16[1,8,32,256]{3,2,1,0:T(8,128)(2,1)} %param.11) | copy-start | bytes 393220
  1.6 8.0 %collective-permute-start = (bf16[9,32,256]{2,1,0:T(8,128)(2,1)S(1)}, bf16[9,32,256]{2,1,0:T(8,128)(2,1)S(1)}, u32[]{:S(2)}, u32[]{:S(2)}) collective-permute-start(bf16[9,32,256]{2,1,0:T(8,128)(2,1)S(1)} %pad_maximum_fusion.7), channel_id=1, source_target_pairs={{0,4},{4,8},{8,12},{1,5},{5,9},{9,13},{2,6},{6,10},{10,14},{3,7},{... | collective-permute-start | bytes 442376 | tf_op jit(solution)/shard_map/ppermute | solution.py:414
  6.6 7.4 %copy-start.1 = (bf16[1,8,32,256]{3,2,1,0:T(8,128)(2,1)S(1)}, bf16[1,8,32,256]{3,2,1,0:T(8,128)(2,1)}, u32[]{:S(2)}) copy-start(bf16[1,8,32,256]{3,2,1,0:T(8,128)(2,1)} %param.12) | copy-start | bytes 393220
  6.6 7.3 %collective-permute-start.1 = (bf16[9,32,256]{2,1,0:T(8,128)(2,1)S(1)}, bf16[9,32,256]{2,1,0:T(8,128)(2,1)S(1)}, u32[]{:S(2)}, u32[]{:S(2)}) collective-permute-start(bf16[9,32,256]{2,1,0:T(8,128)(2,1)S(1)} %pad_maximum_fusion.8), channel_id=1, source_target_pairs={{4,0},{8,4},{12,8},{5,1},{9,5},{13,9},{6,2},{10,6},{14,10},{7,3},{... | collective-permute-start | bytes 442376 | tf_op jit(solution)/shard_map/ppermute | solution.py:414
  8.0 0.7 copy-start.8
  8.8 0.7 copy-start.9
  13.9 0.8 %copy-start.6 = (bf16[1,4,4,1024]{3,2,1,0:T(4,128)(2,1)S(1)}, bf16[1,4,4,1024]{3,2,1,0:T(4,128)(2,1)}, u32[]{:S(2)}) copy-start(bf16[1,4,4,1024]{3,2,1,0:T(4,128)(2,1)} %param.13) | copy-start | bytes 98308
  13.9 0.8 %copy-start.7 = (bf16[1,4,4,1024]{3,2,1,0:T(4,128)(2,1)S(1)}, bf16[1,4,4,1024]{3,2,1,0:T(4,128)(2,1)}, u32[]{:S(2)}) copy-start(bf16[1,4,4,1024]{3,2,1,0:T(4,128)(2,1)} %param.14) | copy-start | bytes 98308
  14.0 14.8 %copy-start.2 = (bf16[256,768]{1,0:T(8,128)(2,1)S(1)}, bf16[256,768]{1,0:T(8,128)(2,1)}, u32[]{:S(2)}) copy-start(bf16[256,768]{1,0:T(8,128)(2,1)} %qkv_ref.1) | copy-start | bytes 1179652
  14.7 7.1 %collective-permute-start.6 = (bf16[16,2048]{1,0:T(8,128)(2,1)S(1)}, bf16[16,2048]{1,0:T(8,128)(2,1)S(1)}, u32[]{:S(2)}, u32[]{:S(2)}) collective-permute-start(bf16[16,2048]{1,0:T(8,128)(2,1)S(1)} %pack_coarse.1), channel_id=1, source_target_pairs={{0,12},{4,8},{8,4},{12,0},{1,13},{5,9},{9,5},{13,1},{2,14},{6,10},... | collective-permute-start | bytes 196616 | tf_op jit(solution)/shard_map/ppermute | solution.py:418
  16.4 6.4 %collective-permute-start.5 = (bf16[16,2048]{1,0:T(8,128)(2,1)S(1)}, bf16[16,2048]{1,0:T(8,128)(2,1)S(1)}, u32[]{:S(2)}, u32[]{:S(2)}) collective-permute-start(bf16[16,2048]{1,0:T(8,128)(2,1)S(1)} %pack_coarse.1), channel_id=1, source_target_pairs={{0,8},{4,12},{8,0},{12,4},{1,9},{5,13},{9,1},{13,5},{2,10},{6,14},... | collective-permute-start | bytes 196616 | tf_op jit(solution)/shard_map/ppermute | solution.py:418
  17.8 4.9 %collective-permute-start.4 = (bf16[16,2048]{1,0:T(8,128)(2,1)S(1)}, bf16[16,2048]{1,0:T(8,128)(2,1)S(1)}, u32[]{:S(2)}, u32[]{:S(2)}) collective-permute-start(bf16[16,2048]{1,0:T(8,128)(2,1)S(1)} %pack_coarse.1), channel_id=1, source_target_pairs={{0,4},{4,0},{8,12},{12,8},{1,5},{5,1},{9,13},{13,9},{2,6},{6,2},{1... | collective-permute-start | bytes 196616 | tf_op jit(solution)/shard_map/ppermute | solution.py:418
  19.2 3.6 %collective-permute-start.2 = (bf16[34,6,256]{2,1,0:T(8,128)(2,1)S(1)}, bf16[34,6,256]{2,1,0:T(8,128)(2,1)S(1)}, u32[]{:S(2)}, u32[]{:S(2)}) collective-permute-start(bf16[34,6,256]{2,1,0:T(8,128)(2,1)S(1)} %get-tuple-element.51), channel_id=1, source_target_pairs={{0,1},{1,2},{2,3},{4,5},{5,6},{6,7},{8,9},{9,10},{10,11},{12,13},{... | collective-permute-start | bytes 313352 | tf_op jit(solution)/shard_map/ppermute | solution.py:414
  20.5 5.0 %collective-permute-start.3 = (bf16[34,6,256]{2,1,0:T(8,128)(2,1)S(1)}, bf16[34,6,256]{2,1,0:T(8,128)(2,1)S(1)}, u32[]{:S(2)}, u32[]{:S(2)}) collective-permute-start(bf16[34,6,256]{2,1,0:T(8,128)(2,1)S(1)} %get-tuple-element.52), channel_id=1, source_target_pairs={{1,0},{2,1},{3,2},{5,4},{6,5},{7,6},{9,8},{10,9},{11,10},{13,12},{... | collective-permute-start | bytes 313352 | tf_op jit(solution)/shard_map/ppermute | solution.py:414
  22.8 6.1 %copy-start.4 = (bf16[256,256]{1,0:T(8,128)(2,1)S(1)}, bf16[256,256]{1,0:T(8,128)(2,1)}, u32[]{:S(2)}) copy-start(bf16[256,256]{1,0:T(8,128)(2,1)} %out_ref.1) | copy-start | bytes 393220
  25.5 10.0 %collective-permute-start.7 = (bf16[4,16,2048]{2,1,0:T(8,128)(2,1)S(1)}, bf16[4,16,2048]{2,1,0:T(8,128)(2,1)S(1)}, u32[]{:S(2)}, u32[]{:S(2)}) collective-permute-start(bf16[4,16,2048]{2,1,0:T(8,128)(2,1)S(1)} %pad_maximum_fusion.2), channel_id=1, source_target_pairs={{0,2},{1,3},{2,0},{3,1},{4,6},{5,7},{6,4},{7,5},{8,10},{9,11},{10,... | collective-permute-start | bytes 786440 | tf_op jit(solution)/shard_map/ppermute | solution.py:418
  35.5 2.4 %collective-permute-start.9 = (bf16[2,4,16,2048]{3,2,1,0:T(8,128)(2,1)S(1)}, bf16[2,4,16,2048]{3,2,1,0:T(8,128)(2,1)S(1)}, u32[]{:S(2)}, u32[]{:S(2)}) collective-permute-start(bf16[2,4,16,2048]{3,2,1,0:T(8,128)(2,1)S(1)} %pad_maximum_fusion.1), channel_id=1, source_target_pairs={{0,1},{1,0},{2,3},{3,2},{4,5},{5,4},{6,7},{7,6},{8,9},{9,8},{10,11... | collective-permute-start | bytes 1572872 | tf_op jit(solution)/shard_map/ppermute | solution.py:418
  35.9 1.9 %collective-permute-start.8 = (bf16[2,4,16,1024]{3,2,1,0:T(8,128)(2,1)S(1)}, bf16[2,4,16,1024]{3,2,1,0:T(8,128)(2,1)S(1)}, u32[]{:S(2)}, u32[]{:S(2)}) collective-permute-start(bf16[2,4,16,1024]{3,2,1,0:T(8,128)(2,1)S(1)} %get-tuple-element.63), channel_id=1, source_target_pairs={{0,1},{1,0},{2,3},{3,2},{4,5},{5,4},{6,7},{7,6},{8,9},{9,8},{10,11... | collective-permute-start | bytes 786440 | tf_op jit(solution)/shard_map/ppermute | solution.py:418
  37.9 6.0 %collective-permute-start.10 = (bf16[4,16,1024]{2,1,0:T(8,128)(2,1)S(1)}, bf16[4,16,1024]{2,1,0:T(8,128)(2,1)S(1)}, u32[]{:S(2)}, u32[]{:S(2)}) collective-permute-start(bf16[4,16,1024]{2,1,0:T(8,128)(2,1)S(1)} %fusion.2), channel_id=1, source_target_pairs={{0,2},{1,3},{2,0},{3,1},{4,6},{5,7},{6,4},{7,5},{8,10},{9,11},{10,... | collective-permute-start | bytes 393224 | tf_op jit(solution)/shard_map/ppermute | solution.py:418
  40.2 1.0 %copy-start.3 = (bf16[3,64,1024]{2,1,0:T(8,128)(2,1)S(1)}, bf16[3,64,1024]{2,1,0:T(8,128)(2,1)}, u32[]{:S(2)}) copy-start(bf16[3,64,1024]{2,1,0:T(8,128)(2,1)} %qkv_hbm.1) | copy-start | bytes 1179652
  40.2 1.0 %copy-start.5 = (bf16[64,1024]{1,0:T(8,128)(2,1)S(1)}, bf16[64,1024]{1,0:T(8,128)(2,1)}, u32[]{:S(2)}) copy-start(bf16[64,1024]{1,0:T(8,128)(2,1)} %out_hbm.1) | copy-start | bytes 393220
  44.0 5.1 %collective-permute-start.11 = (bf16[4,16,1024]{2,1,0:T(8,128)(2,1)S(1)}, bf16[4,16,1024]{2,1,0:T(8,128)(2,1)S(1)}, u32[]{:S(2)}, u32[]{:S(2)}) collective-permute-start(bf16[4,16,1024]{2,1,0:T(8,128)(2,1)S(1)} %fusion.1), channel_id=1, source_target_pairs={{0,16},{16,0},{1,17},{17,1},{2,18},{18,2},{3,19},{19,3},{4,20},{20... | collective-permute-start | bytes 393224 | tf_op jit(solution)/shard_map/ppermute | solution.py:418
  45.6 3.5 %collective-permute-start.12 = (bf16[2,4,16,1024]{3,2,1,0:T(8,128)(2,1)S(1)}, bf16[2,4,16,1024]{3,2,1,0:T(8,128)(2,1)S(1)}, u32[]{:S(2)}, u32[]{:S(2)}) collective-permute-start(bf16[2,4,16,1024]{3,2,1,0:T(8,128)(2,1)S(1)} %bitcast.93), channel_id=1, source_target_pairs={{0,1},{1,0},{2,3},{3,2},{4,5},{5,4},{6,7},{7,6},{8,9},{9,8},{10,11... | collective-permute-start | bytes 786440 | tf_op jit(solution)/shard_map/ppermute | solution.py:418
  49.2 7.0 %collective-permute-start.13 = (bf16[128,1024]{1,0:T(8,128)(2,1)S(1)}, bf16[128,1024]{1,0:T(8,128)(2,1)S(1)}, u32[]{:S(2)}, u32[]{:S(2)}) collective-permute-start(bf16[128,1024]{1,0:T(8,128)(2,1)S(1)} %pad_maximum_fusion.3), channel_id=1, source_target_pairs={{0,4},{4,0},{8,12},{12,8},{1,5},{5,1},{9,13},{13,9},{2,6},{6,2},{1... | collective-permute-start | bytes 786440 | tf_op jit(solution)/shard_map/ppermute | solution.py:418
  50.0 6.7 %collective-permute-start.14 = (bf16[128,1024]{1,0:T(8,128)(2,1)S(1)}, bf16[128,1024]{1,0:T(8,128)(2,1)S(1)}, u32[]{:S(2)}, u32[]{:S(2)}) collective-permute-start(bf16[128,1024]{1,0:T(8,128)(2,1)S(1)} %get-tuple-element.95), channel_id=1, source_target_pairs={{0,16},{16,0},{1,17},{17,1},{2,18},{18,2},{3,19},{19,3},{4,20},{20... | collective-permute-start | bytes 786440 | tf_op jit(solution)/shard_map/ppermute | solution.py:418
  56.8 9.5 %collective-permute-start.15 = (bf16[96,1024]{1,0:T(8,128)(2,1)S(1)}, bf16[96,1024]{1,0:T(8,128)(2,1)S(1)}, u32[]{:S(2)}, u32[]{:S(2)}) collective-permute-start(bf16[96,1024]{1,0:T(8,128)(2,1)S(1)} %pad_maximum_fusion.5), channel_id=1, source_target_pairs={{0,8},{4,12},{8,0},{12,4},{1,9},{5,13},{9,1},{13,5},{2,10},{6,14},... | collective-permute-start | bytes 589832 | tf_op jit(solution)/shard_map/ppermute | solution.py:418
  58.3 8.1 %collective-permute-start.16 = (bf16[128,1024]{1,0:T(8,128)(2,1)S(1)}, bf16[128,1024]{1,0:T(8,128)(2,1)S(1)}, u32[]{:S(2)}, u32[]{:S(2)}) collective-permute-start(bf16[128,1024]{1,0:T(8,128)(2,1)S(1)} %get-tuple-element.94), channel_id=1, source_target_pairs={{0,16},{16,0},{1,17},{17,1},{2,18},{18,2},{3,19},{19,3},{4,20},{20... | collective-permute-start | bytes 786440 | tf_op jit(solution)/shard_map/ppermute | solution.py:418
  66.4 5.4 %collective-permute-start.17 = (bf16[80,1024]{1,0:T(8,128)(2,1)S(1)}, bf16[80,1024]{1,0:T(8,128)(2,1)S(1)}, u32[]{:S(2)}, u32[]{:S(2)}) collective-permute-start(bf16[80,1024]{1,0:T(8,128)(2,1)S(1)} %pad_maximum_fusion.6), channel_id=1, source_target_pairs={{0,2},{1,3},{2,0},{3,1},{4,6},{5,7},{6,4},{7,5},{8,10},{9,11},{10,... | collective-permute-start | bytes 491528 | tf_op jit(solution)/shard_map/ppermute | solution.py:418
  71.8 1.6 %collective-permute-start.18 = (bf16[2,64,1024]{2,1,0:T(8,128)(2,1)S(1)}, bf16[2,64,1024]{2,1,0:T(8,128)(2,1)S(1)}, u32[]{:S(2)}, u32[]{:S(2)}) collective-permute-start(bf16[2,64,1024]{2,1,0:T(8,128)(2,1)S(1)} %pad_maximum_fusion.4.near_ref), channel_id=1, source_target_pairs={{0,1},{1,0},{2,3},{3,2},{4,5},{5,4},{6,7},{7,6},{8,9},{9,8},{10,11... | collective-permute-start | bytes 786440 | tf_op jit(solution)/shard_map/ppermute | solution.py:418

commit v3 on v2

--- a/solution.py
+++ b/solution.py
@@ -309,22 +309,21 @@
     )(tokens, cotangents, factor, head_qkv, head_out)
 
 
-def pack_body(x_ref, dy_ref, own_ref):
+def pack_body(first, second, x_ref, dy_ref, own_ref):
     own_ref[:, :D_C] = x_ref[...].astype(jnp.float32).reshape(-1, D_C).astype(jnp.bfloat16)
     own_ref[:, D_C:] = dy_ref[...].astype(jnp.float32).reshape(-1, D_C).astype(jnp.bfloat16)
 
 
-def packed(tokens, cotangents):
+def packed(after, tokens, cotangents):
     vmem = pl.BlockSpec(memory_space=pltpu.VMEM)
     count = tokens.shape[0] * tokens.shape[1]
     return pl.pallas_call(
         pack_body,
         out_shape=jax.ShapeDtypeStruct((count, 2 * D_C), jnp.bfloat16),
-        in_specs=[vmem] * 2,
+        in_specs=[pl.BlockSpec(memory_space=pl.ANY)] * 2 + [vmem] * 2,
         out_specs=vmem,
-        compiler_params=pltpu.CompilerParams(vmem_limit_bytes=vmem_bytes),
         name="pack_coarse",
-    )(tokens, cotangents)
+    )(*after, tokens, cotangents)
 
 
 def pair_sum_body(own, first, second, qkv_ref, out_ref):
@@ -409,9 +408,13 @@
 
 def neighbours(low_edge, high_edge, axis):
     peers = lax.axis_size(axis)
-    up = [(i, i + 1) for i in range(peers - 1)]
-    down = [(i + 1, i) for i in range(peers - 1)]
-    return lax.ppermute(high_edge, axis, up), lax.ppermute(low_edge, axis, down)
+    odd = lax.axis_index(axis) & 1 == 1
+    near = [(i, i ^ 1) for i in range(peers)]
+    far = [(i, i + 1 if i % 2 else i - 1) for i in range(1, peers - 1)]
+    to_near, to_far = jnp.where(odd, low_edge, high_edge), jnp.where(odd, high_edge, low_edge)
+    second = lax.ppermute(to_far, axis, far)
+    first = lax.ppermute(to_near, axis, near)
+    return jnp.where(odd, first, second), jnp.where(odd, second, first), (to_near, to_far)
 
 
 def swapped(value, axis, mask):
@@ -463,7 +466,8 @@
 
     low = jnp.concatenate([picture[:HALO], cotangent[:RAD]], axis=0)
     high = jnp.concatenate([picture[height - HALO :], cotangent[height - RAD :]], axis=0)
-    above, below = neighbours(low, high, "gy")
+    above, below, payloads = neighbours(low, high, "gy")
+    own = packed(payloads, x_coarse[0], dy_coarse[0])
     row_first = gy * height - HALO
     col_first = gx * breadth - HALO
     limits = jnp.stack(
@@ -479,15 +483,12 @@
     factor = time_gain(fine_gain, step_value)[None]
     coarse_factor = time_gain(coarse_gain, step_value)[None]
     place = gx.astype(jnp.int32)[None]
-    coarse_picture, coarse_cot = x_coarse[0], dy_coarse[0]
     above, below, limits, place, factor, coarse_factor = tied(
         above, below, limits, place, factor, coarse_factor
     )
     column = jnp.concatenate([above, picture, cotangent, below], axis=0)
     first, final = column[:, :HALO], column[:, breadth - HALO :]
-    first, final, coarse_picture, coarse_cot = tied(first, final, coarse_picture, coarse_cot)
-    left, right = neighbours(first, final, "gx")
-    own = packed(coarse_picture, coarse_cot)
+    left, right, _ = neighbours(first, final, "gx")
     count = own.shape[0]
     row_group = all_rows(own)
     left, right, row_group = tied(left, right, row_group)
@@ -554,7 +555,7 @@
         place,
         fine_pair,
         swapped(fine_pair, "gx", 1),
-        coarse_picture,
+        x_coarse[0],
         coarse_factor,
         coarse_kept[0],
         come[rows:],

time: 75.2 us -> 69.5 us (0.924)
  waiting for transfers between devices: 30.1 us -> 24.4 us
  starting transfers between devices: 27.7 us -> 25.9 us
  Pallas kernels: 11.2 us -> 12.6 us
    ppermute x4, waiting for transfers between devices: 7.05 us -> 0.9 us  [the longest x2 0.9 us: neighbours(): first = lax.ppermute(to_near, axis, near)]
    ppermute x15, starting transfers between devices: 18.8 us -> 15.7 us  [swapped(): lax.ppermute(value, axis, [(i, i ^ mask) for i in range(lax.axis_size(axi...]
    pallas_call x1, Pallas kernels: 0.01 us -> 1.42 us  [packed(): pl.pallas_call(pack_body, out_shape=jax.ShapeDtypeStruct((count, 2 * D_C)...]
    ppermute x4, starting transfers between devices: 8.94 us -> 10.2 us  [the longest x2 8.81 us: neighbours(): first = lax.ppermute(to_near, axis, near)]
    unnamed x20 -> x24, local copies, waits for them, and re-layouts: 2.35 us -> 2.48 us
  transfers between devices with their start and end apart: 19 -> 19, of which waited for: 12 -> 8; matrix products, arithmetic and copies ran while one was open for 1% -> 1% of each run, Pallas kernels for 13% -> 16%
where the time goes in v3:
time: 69.5 us; the launch traced here: 69.1 us
  starting transfers between devices  25.9 us (37%)
  waiting for transfers between devices  24.4 us (35%)
  Pallas kernels  12.6 us (18%)
  local copies, waits for them, and re-layouts  3.68 us (5%)
  between operations  1.72 us (2%)
  other arithmetic  0.87 us (1%)
    ppermute x15, waiting for transfers between devices, swapped(): lax.ppermute(value, axis, [(i, i ^ mask) for i in range(lax.axis_size(axi...  23.5 us
    ppermute x15, starting transfers between devices, swapped(): lax.ppermute(value, axis, [(i, i ^ mask) for i in range(lax.axis_size(axi...  15.7 us
    ppermute x2, starting transfers between devices, neighbours(): first = lax.ppermute(to_near, axis, near)  8.81 us
    pallas_call x1, Pallas kernels, fine_block(): pl.pallas_call(fine_body, out_shape=(jax.ShapeDtypeStruct((height, breadt...  6.59 us
    unnamed x24, local copies, waits for them, and re-layouts  2.48 us
    pallas_call x1, Pallas kernels, coarse_block(): pl.pallas_call(coarse_body, out_shape=(jax.ShapeDtypeStruct((count, D_C),...  2.23 us
    pallas_call x1, Pallas kernels, last_step(): pl.pallas_call(last_body, out_shape=(jax.ShapeDtypeStruct((D_F, 3 * D_F),...  1.47 us
    pallas_call x1, Pallas kernels, packed(): pl.pallas_call(pack_body, out_shape=jax.ShapeDtypeStruct((count, 2 * D_C)...  1.42 us
  transfers between devices with their start and end apart: 19, of which 8 were waited for; matrix products, arithmetic and copies ran while one was open for 1% of the time, Pallas kernels for 16%

profile of v3, /device:TPU:0, one launch (start us, length us, event | category | flops | bytes accessed | tf_op | source)
XLA Modules:
  0.0 69.1 jit_solution(11208179087450449928)
XLA Ops:
  0.6 0.9 %slice_bitcast_fusion.6 = (bf16[3,32,256]{2,1,0:T(8,128)(2,1)S(1)}, bf16[3,32,256]{2,1,0:T(8,128)(2,1)S(1)}) fusion(bf16[1,8,32,256]{3,2,1,0:T(8,128)(2,1)} %param.12), kind=kLoop, calls=%fused_computation.42 | loop fusion | bytes 196608 | tf_op jit(solution)/shard_map/slice | solution.py:467
  1.5 0.1 copy-done
  1.6 0.0 copy-start.7
  1.7 0.0 copy-start.8
  1.7 0.7 collective-permute-start.1
  2.3 5.9 %collective-permute-start = (bf16[9,32,256]{2,1,0:T(8,128)(2,1)S(1)}, bf16[9,32,256]{2,1,0:T(8,128)(2,1)S(1)}, u32[]{:S(2)}, u32[]{:S(2)}) collective-permute-start(bf16[9,32,256]{2,1,0:T(8,128)(2,1)S(1)} %get-tuple-element.94.first), channel_id=1, source_target_pairs={{0,4},{4,0},{8,12},{12,8},{1,5},{5,1},{9,13},{13,9},{2,6},{6,2},{1... | collective-permute-start | bytes 442376 | tf_op jit(solution)/shard_map/ppermute | solution.py:416
  8.3 1.4 %pack_coarse.1 = bf16[16,2048]{1,0:T(8,128)(2,1)} custom-call(bf16[9,32,256]{2,1,0:T(8,128)(2,1)} %copy-done.7, bf16[9,32,256]{2,1,0:T(8,128)(2,1)} %copy-done.8, bf16[4,4,1024]{2,1,0:T(4,128)(2,1)} %bitcast.69, bf16[4,4,1024]{2,1,0:T(4,128)(2,1)} %bitcast.96), custom_call_target="tpu_custom_call" | custom-call | tf_op jit(solution)/shard_map/pack_coarse/pallas_call | solution.py:320
  9.7 1.3 %collective-permute-start.6 = (bf16[16,2048]{1,0:T(8,128)(2,1)}, bf16[16,2048]{1,0:T(8,128)(2,1)S(1)}, u32[]{:S(2)}, u32[]{:S(2)}) collective-permute-start(bf16[16,2048]{1,0:T(8,128)(2,1)} %pack_coarse.1), channel_id=1, source_target_pairs={{0,12},{4,8},{8,4},{12,0},{1,13},{5,9},{9,5},{13,1},{2,14},{6,10},... | collective-permute-start | bytes 196616 | tf_op jit(solution)/shard_map/ppermute | solution.py:421
  11.0 0.1 collective-permute-start.5
  11.2 2.9 %collective-permute-start.4 = (bf16[16,2048]{1,0:T(8,128)(2,1)}, bf16[16,2048]{1,0:T(8,128)(2,1)S(1)}, u32[]{:S(2)}, u32[]{:S(2)}) collective-permute-start(bf16[16,2048]{1,0:T(8,128)(2,1)} %pack_coarse.1), channel_id=1, source_target_pairs={{0,4},{4,0},{8,12},{12,8},{1,5},{5,1},{9,13},{13,9},{2,6},{6,2},{1... | collective-permute-start | bytes 196616 | tf_op jit(solution)/shard_map/ppermute | solution.py:421
  14.7 0.0 copy-done.10
  14.7 0.1 add_multiply_fusion
  14.8 0.0 copy-start.11
  14.8 0.1 stack.69.limits
  14.9 0.6 copy-done.11
  15.5 0.1 add_multiply_fusion.1
  15.5 0.0 copy-start.1
  15.6 0.0 collective-permute-done.1
  15.6 0.0 collective-permute-done
  15.6 0.8 %copy-done.1 = bf16[1,8,32,256]{3,2,1,0:T(8,128)(2,1)S(1)} copy-done((bf16[1,8,32,256]{3,2,1,0:T(8,128)(2,1)S(1)}, bf16[1,8,32,256]{3,2,1,0:T(8,128)(2,1)}, u32[]{:S(2)}) %copy-start.1) | copy-done | bytes 131096
  16.5 0.1 broadcast_select_fusion.6
  16.5 0.7 collective-permute-start.3
  17.2 0.0 copy-start.9
  17.2 2.9 %collective-permute-start.2 = (bf16[34,6,256]{2,1,0:T(8,128)(2,1)S(1)}, bf16[34,6,256]{2,1,0:T(8,128)(2,1)S(1)}, u32[]{:S(2)}, u32[]{:S(2)}) collective-permute-start(bf16[34,6,256]{2,1,0:T(8,128)(2,1)S(1)} %broadcast_select_fusion.7), channel_id=1, source_target_pairs={{0,1},{1,0},{2,3},{3,2},{4,5},{5,4},{6,7},{7,6},{8,9},{9,8},{10,11... | collective-permute-start | bytes 313352 | tf_op jit(solution)/shard_map/ppermute | solution.py:416
  20.2 0.0 collective-permute-done.6
  20.2 0.0 copy-start.2
  20.2 0.0 copy-start.4
  20.3 0.9 %collective-permute-done.2 = bf16[34,6,256]{2,1,0:T(8,128)(2,1)S(1)} collective-permute-done((bf16[34,6,256]{2,1,0:T(8,128)(2,1)S(1)}, bf16[34,6,256]{2,1,0:T(8,128)(2,1)S(1)}, u32[]{:S(2)}, u32[]{:S(2)}) %collective-permute-start.2) | collective-permute-done | bytes 104480 | tf_op jit(solution)/shard_map/ppermute | solution.py:416
  21.2 3.3 %collective-permute-start.7 = (bf16[4,16,2048]{2,1,0:T(8,128)(2,1)S(1)}, bf16[4,16,2048]{2,1,0:T(8,128)(2,1)S(1)}, u32[]{:S(2)}, u32[]{:S(2)}) collective-permute-start(bf16[4,16,2048]{2,1,0:T(8,128)(2,1)S(1)} %pad_maximum_fusion.2), channel_id=1, source_target_pairs={{0,2},{1,3},{2,0},{3,1},{4,6},{5,7},{6,4},{7,5},{8,10},{9,11},{10,... | collective-permute-start | bytes 786440 | tf_op jit(solution)/shard_map/ppermute | solution.py:421
  24.5 6.6 %fine_block.1 = (bf16[8,32,256]{2,1,0:T(8,128)(2,1)}, f32[2,4,16,1024]{3,2,1,0:T(8,128)S(1)}, bf16[2,4,16,1024]{3,2,1,0:T(8,128)(2,1)S(1)}) custom-call(s32[6]{0:T(128)S(1)} %stack.69.limits, bf16[8,32,256]{2,1,0:T(8,128)(2,1)S(1)} %bitcast.66, bf16[8,32,256]{2,1,0:T(8,128)(2,1)S(1)} %bitcast.68, bf16[9,32,256]{2,1,0:T(8,128)(2,1)S(1)} %get-tuple-element.45.above_ref, ...), custom_call_target="tpu_custom_call" | custom-call | tf_op jit(solution)/shard_map/fine_block/pallas_call | solution.py:218
  31.1 0.0 collective-permute-done.7
  31.1 0.1 pad_maximum_fusion.1
  31.2 0.1 collective-permute-start.9
  31.2 0.5 collective-permute-start.8
  31.7 1.8 %collective-permute-done.8 = bf16[2,4,16,1024]{3,2,1,0:T(8,128)(2,1)S(1)} collective-permute-done((bf16[2,4,16,1024]{3,2,1,0:T(8,128)(2,1)S(1)}, bf16[2,4,16,1024]{3,2,1,0:T(8,128)(2,1)S(1)}, u32[]{:S(2)}, u32[]{:S(2)}) %collective-permute-start.8) | collective-permute-done | bytes 262176 | tf_op jit(solution)/shard_map/ppermute | solution.py:421
  33.5 0.1 convert_add_fusion.1
  33.6 0.0 collective-permute-done.9
  33.6 0.3 collective-permute-start.10
  34.0 0.1 pad_maximum_fusion
  34.1 0.0 copy-start.3
  34.1 0.0 copy-start.5
  34.1 0.1 fusion.5
  34.2 0.9 %copy-done.3 = bf16[3,64,1024]{2,1,0:T(8,128)(2,1)S(1)} copy-done((bf16[3,64,1024]{2,1,0:T(8,128)(2,1)S(1)}, bf16[3,64,1024]{2,1,0:T(8,128)(2,1)}, u32[]{:S(2)}) %copy-start.3) | copy-done | bytes 393240
  35.1 0.0 copy-done.5
  35.1 2.2 %coarse_block.1 = (bf16[256,1024]{1,0:T(8,128)(2,1)S(1)}, bf16[256,1024]{1,0:T(8,128)(2,1)S(1)}) custom-call(bf16[256,1024]{1,0:T(8,128)(2,1)S(1)} %get-tuple-element.86.x_ref, bf16[256,1024]{1,0:T(8,128)(2,1)S(1)} %get-tuple-element.85.dy_ref, f32[1,1024]{1,0:T(1,128)S(1)} %bitcast.71, bf16[3,64,1024]{2,1,0:T(8,128)(2,1)S(1)} %copy-done.3, ...), custom_call_target="tpu_custom_call" | custom-call | tf_op jit(solution)/shard_map/coarse_block/pallas_call | solution.py:294
  37.3 1.9 %collective-permute-done.10 = bf16[4,16,1024]{2,1,0:T(8,128)(2,1)S(1)} collective-permute-done((bf16[4,16,1024]{2,1,0:T(8,128)(2,1)S(1)}, bf16[4,16,1024]{2,1,0:T(8,128)(2,1)S(1)}, u32[]{:S(2)}, u32[]{:S(2)}) %collective-permute-start.10) | collective-permute-done | bytes 131104 | tf_op jit(solution)/shard_map/ppermute | solution.py:421
  39.3 1.6 %collective-permute-start.11 = (bf16[4,16,1024]{2,1,0:T(8,128)(2,1)S(1)}, bf16[4,16,1024]{2,1,0:T(8,128)(2,1)S(1)}, u32[]{:S(2)}, u32[]{:S(2)}) collective-permute-start(bf16[4,16,1024]{2,1,0:T(8,128)(2,1)S(1)} %fusion.1), channel_id=1, source_target_pairs={{0,16},{16,0},{1,17},{17,1},{2,18},{18,2},{3,19},{19,3},{4,20},{20... | collective-permute-start | bytes 393224 | tf_op jit(solution)/shard_map/ppermute | solution.py:421
  40.9 0.1 collective-permute-start.12
  41.0 3.3 %collective-permute-done.11 = bf16[4,16,1024]{2,1,0:T(8,128)(2,1)S(1)} collective-permute-done((bf16[4,16,1024]{2,1,0:T(8,128)(2,1)S(1)}, bf16[4,16,1024]{2,1,0:T(8,128)(2,1)S(1)}, u32[]{:S(2)}, u32[]{:S(2)}) %collective-permute-start.11) | collective-permute-done | bytes 131104 | tf_op jit(solution)/shard_map/ppermute | solution.py:421
  44.3 0.1 convert_add_fusion
  44.5 0.1 collective-permute-start.13
  44.6 1.6 %collective-permute-start.14 = (bf16[128,1024]{1,0:T(8,128)(2,1)S(1)}, bf16[128,1024]{1,0:T(8,128)(2,1)S(1)}, u32[]{:S(2)}, u32[]{:S(2)}) collective-permute-start(bf16[128,1024]{1,0:T(8,128)(2,1)S(1)} %get-tuple-element.88), channel_id=1, source_target_pairs={{0,16},{16,0},{1,17},{17,1},{2,18},{18,2},{3,19},{19,3},{4,20},{20... | collective-permute-start | bytes 786440 | tf_op jit(solution)/shard_map/ppermute | solution.py:421
  46.2 4.8 %collective-permute-done.13 = bf16[128,1024]{1,0:T(8,128)(2,1)S(1)} collective-permute-done((bf16[128,1024]{1,0:T(8,128)(2,1)S(1)}, bf16[128,1024]{1,0:T(8,128)(2,1)S(1)}, u32[]{:S(2)}, u32[]{:S(2)}) %collective-permute-start.13) | collective-permute-done | bytes 262176 | tf_op jit(solution)/shard_map/ppermute | solution.py:421
  51.1 0.0 collective-permute-done.14.first
  51.2 1.8 %collective-permute-start.15 = (bf16[96,1024]{1,0:T(8,128)(2,1)S(1)}, bf16[96,1024]{1,0:T(8,128)(2,1)S(1)}, u32[]{:S(2)}, u32[]{:S(2)}) collective-permute-start(bf16[96,1024]{1,0:T(8,128)(2,1)S(1)} %pad_maximum_fusion.5), channel_id=1, source_target_pairs={{0,8},{4,12},{8,0},{12,4},{1,9},{5,13},{9,1},{13,5},{2,10},{6,14},... | collective-permute-start | bytes 589832 | tf_op jit(solution)/shard_map/ppermute | solution.py:421
  53.0 1.5 %collective-permute-start.16 = (bf16[128,1024]{1,0:T(8,128)(2,1)S(1)}, bf16[128,1024]{1,0:T(8,128)(2,1)S(1)}, u32[]{:S(2)}, u32[]{:S(2)}) collective-permute-start(bf16[128,1024]{1,0:T(8,128)(2,1)S(1)} %get-tuple-element.87), channel_id=1, source_target_pairs={{0,16},{16,0},{1,17},{17,1},{2,18},{18,2},{3,19},{19,3},{4,20},{20... | collective-permute-start | bytes 786440 | tf_op jit(solution)/shard_map/ppermute | solution.py:421
  54.5 6.0 %collective-permute-done.15 = bf16[96,1024]{1,0:T(8,128)(2,1)S(1)} collective-permute-done((bf16[96,1024]{1,0:T(8,128)(2,1)S(1)}, bf16[96,1024]{1,0:T(8,128)(2,1)S(1)}, u32[]{:S(2)}, u32[]{:S(2)}) %collective-permute-start.15) | collective-permute-done | bytes 196640 | tf_op jit(solution)/shard_map/ppermute | solution.py:421
  60.6 0.4 collective-permute-start.17
  61.0 0.9 %pair_sum.1 = (bf16[3,64,1024]{2,1,0:T(8,128)(2,1)}, bf16[64,1024]{1,0:T(8,128)(2,1)}) custom-call(bf16[256,1024]{1,0:T(8,128)(2,1)S(1)} %get-tuple-element.67.own, bf16[128,1024]{1,0:T(8,128)(2,1)S(1)} %collective-permute-done.14.first, bf16[128,1024]{1,0:T(8,128)(2,1)S(1)} %collective-permute-done.16.second), custom_call_target="tpu_custom_call" | custom-call | tf_op jit(solution)/shard_map/pair_sum/pallas_call | solution.py:341
  61.9 4.1 %collective-permute-done.17 = bf16[80,1024]{1,0:T(8,128)(2,1)S(1)} collective-permute-done((bf16[80,1024]{1,0:T(8,128)(2,1)S(1)}, bf16[80,1024]{1,0:T(8,128)(2,1)S(1)}, u32[]{:S(2)}, u32[]{:S(2)}) %collective-permute-start.17) | collective-permute-done | bytes 163872 | tf_op jit(solution)/shard_map/ppermute | solution.py:421
  66.1 0.1 collective-permute-start.18
  66.2 0.0 copy-start.6
  66.2 1.5 %collective-permute-done.18.far_ref = bf16[2,64,1024]{2,1,0:T(8,128)(2,1)S(1)} collective-permute-done((bf16[2,64,1024]{2,1,0:T(8,128)(2,1)S(1)}, bf16[2,64,1024]{2,1,0:T(8,128)(2,1)S(1)}, u32[]{:S(2)}, u32[]{:S(2)}) %collective-permute-start.18) | collective-permute-done | bytes 262176 | tf_op jit(solution)/shard_map/ppermute | solution.py:421
  67.7 1.5 %last_step.1 = (bf16[256,768]{1,0:T(8,128)(2,1)}, bf16[256,256]{1,0:T(8,128)(2,1)}, bf16[4,4,1024]{2,1,0:T(4,128)(2,1)}) custom-call(s32[1]{0:T(128)} %bitcast.8.place, bf16[2,64,1024]{2,1,0:T(8,128)(2,1)S(1)} %pad_maximum_fusion.4.near_ref, bf16[2,64,1024]{2,1,0:T(8,128)(2,1)S(1)} %collective-permute-done.18.far_ref, bf16[4,4,1024]{2,1,0:T(4,128)(2,1)S(1)} %bitcast.70, ...), custom_call_target="tpu_custom_call" | custom-call | tf_op jit(solution)/shard_map/last_step/pallas_call | solution.py:394
  (40 shorter events, 0.6 us)
Async XLA Ops:
  0.6 1.0 %copy-start = (bf16[1,8,32,256]{3,2,1,0:T(8,128)(2,1)S(1)}, bf16[1,8,32,256]{3,2,1,0:T(8,128)(2,1)}, u32[]{:S(2)}) copy-start(bf16[1,8,32,256]{3,2,1,0:T(8,128)(2,1)} %param.11) | copy-start | bytes 393220
  1.6 6.6 %copy-start.7 = (bf16[9,32,256]{2,1,0:T(8,128)(2,1)}, bf16[9,32,256]{2,1,0:T(8,128)(2,1)S(1)}, u32[]{:S(2)}) copy-start(bf16[9,32,256]{2,1,0:T(8,128)(2,1)S(1)} %get-tuple-element.94.first) | copy-start | bytes 442372
  1.7 6.6 %copy-start.8 = (bf16[9,32,256]{2,1,0:T(8,128)(2,1)}, bf16[9,32,256]{2,1,0:T(8,128)(2,1)S(1)}, u32[]{:S(2)}) copy-start(bf16[9,32,256]{2,1,0:T(8,128)(2,1)S(1)} %get-tuple-element.93.second) | copy-start | bytes 442372
  1.7 13.9 %collective-permute-start.1 = (bf16[9,32,256]{2,1,0:T(8,128)(2,1)S(1)}, bf16[9,32,256]{2,1,0:T(8,128)(2,1)S(1)}, u32[]{:S(2)}, u32[]{:S(2)}) collective-permute-start(bf16[9,32,256]{2,1,0:T(8,128)(2,1)S(1)} %get-tuple-element.93.second), channel_id=1, source_target_pairs={{4,8},{8,4},{5,9},{9,5},{6,10},{10,6},{7,11},{11,7},{20,24},{24,20... | collective-permute-start | bytes 442376 | tf_op jit(solution)/shard_map/ppermute | solution.py:415
  2.3 13.2 %collective-permute-start = (bf16[9,32,256]{2,1,0:T(8,128)(2,1)S(1)}, bf16[9,32,256]{2,1,0:T(8,128)(2,1)S(1)}, u32[]{:S(2)}, u32[]{:S(2)}) collective-permute-start(bf16[9,32,256]{2,1,0:T(8,128)(2,1)S(1)} %get-tuple-element.94.first), channel_id=1, source_target_pairs={{0,4},{4,0},{8,12},{12,8},{1,5},{5,1},{9,13},{13,9},{2,6},{6,2},{1... | collective-permute-start | bytes 442376 | tf_op jit(solution)/shard_map/ppermute | solution.py:416
  9.7 10.5 %collective-permute-start.6 = (bf16[16,2048]{1,0:T(8,128)(2,1)}, bf16[16,2048]{1,0:T(8,128)(2,1)S(1)}, u32[]{:S(2)}, u32[]{:S(2)}) collective-permute-start(bf16[16,2048]{1,0:T(8,128)(2,1)} %pack_coarse.1), channel_id=1, source_target_pairs={{0,12},{4,8},{8,4},{12,0},{1,13},{5,9},{9,5},{13,1},{2,14},{6,10},... | collective-permute-start | bytes 196616 | tf_op jit(solution)/shard_map/ppermute | solution.py:421
  11.0 9.1 %collective-permute-start.5 = (bf16[16,2048]{1,0:T(8,128)(2,1)}, bf16[16,2048]{1,0:T(8,128)(2,1)S(1)}, u32[]{:S(2)}, u32[]{:S(2)}) collective-permute-start(bf16[16,2048]{1,0:T(8,128)(2,1)} %pack_coarse.1), channel_id=1, source_target_pairs={{0,8},{4,12},{8,0},{12,4},{1,9},{5,13},{9,1},{13,5},{2,10},{6,14},... | collective-permute-start | bytes 196616 | tf_op jit(solution)/shard_map/ppermute | solution.py:421
  11.2 9.0 %collective-permute-start.4 = (bf16[16,2048]{1,0:T(8,128)(2,1)}, bf16[16,2048]{1,0:T(8,128)(2,1)S(1)}, u32[]{:S(2)}, u32[]{:S(2)}) collective-permute-start(bf16[16,2048]{1,0:T(8,128)(2,1)} %pack_coarse.1), channel_id=1, source_target_pairs={{0,4},{4,0},{8,12},{12,8},{1,5},{5,1},{9,13},{13,9},{2,6},{6,2},{1... | collective-permute-start | bytes 196616 | tf_op jit(solution)/shard_map/ppermute | solution.py:421
  14.1 0.7 copy-start.10
  14.8 0.7 copy-start.11
  15.5 0.9 %copy-start.1 = (bf16[1,8,32,256]{3,2,1,0:T(8,128)(2,1)S(1)}, bf16[1,8,32,256]{3,2,1,0:T(8,128)(2,1)}, u32[]{:S(2)}) copy-start(bf16[1,8,32,256]{3,2,1,0:T(8,128)(2,1)} %param.12) | copy-start | bytes 393220
  16.5 3.7 %collective-permute-start.3 = (bf16[34,6,256]{2,1,0:T(8,128)(2,1)S(1)}, bf16[34,6,256]{2,1,0:T(8,128)(2,1)S(1)}, u32[]{:S(2)}, u32[]{:S(2)}) collective-permute-start(bf16[34,6,256]{2,1,0:T(8,128)(2,1)S(1)} %get-tuple-element.82), channel_id=1, source_target_pairs={{1,2},{2,1},{5,6},{6,5},{9,10},{10,9},{13,14},{14,13},{17,18},{18,... | collective-permute-start | bytes 313352 | tf_op jit(solution)/shard_map/ppermute | solution.py:415
  17.2 3.0 %copy-start.9 = (bf16[16,2048]{1,0:T(8,128)(2,1)S(1)}, bf16[16,2048]{1,0:T(8,128)(2,1)}, u32[]{:S(2)}) copy-start(bf16[16,2048]{1,0:T(8,128)(2,1)} %pack_coarse.1) | copy-start | bytes 196612
  17.2 3.9 %collective-permute-start.2 = (bf16[34,6,256]{2,1,0:T(8,128)(2,1)S(1)}, bf16[34,6,256]{2,1,0:T(8,128)(2,1)S(1)}, u32[]{:S(2)}, u32[]{:S(2)}) collective-permute-start(bf16[34,6,256]{2,1,0:T(8,128)(2,1)S(1)} %broadcast_select_fusion.7), channel_id=1, source_target_pairs={{0,1},{1,0},{2,3},{3,2},{4,5},{5,4},{6,7},{7,6},{8,9},{9,8},{10,11... | collective-permute-start | bytes 313352 | tf_op jit(solution)/shard_map/ppermute | solution.py:416
  20.2 4.3 %copy-start.2 = (bf16[256,768]{1,0:T(8,128)(2,1)S(1)}, bf16[256,768]{1,0:T(8,128)(2,1)}, u32[]{:S(2)}) copy-start(bf16[256,768]{1,0:T(8,128)(2,1)} %qkv_ref.1) | copy-start | bytes 1179652
  20.2 4.3 %copy-start.4 = (bf16[256,256]{1,0:T(8,128)(2,1)S(1)}, bf16[256,256]{1,0:T(8,128)(2,1)}, u32[]{:S(2)}) copy-start(bf16[256,256]{1,0:T(8,128)(2,1)} %out_ref.1) | copy-start | bytes 393220
  21.2 9.9 %collective-permute-start.7 = (bf16[4,16,2048]{2,1,0:T(8,128)(2,1)S(1)}, bf16[4,16,2048]{2,1,0:T(8,128)(2,1)S(1)}, u32[]{:S(2)}, u32[]{:S(2)}) collective-permute-start(bf16[4,16,2048]{2,1,0:T(8,128)(2,1)S(1)} %pad_maximum_fusion.2), channel_id=1, source_target_pairs={{0,2},{1,3},{2,0},{3,1},{4,6},{5,7},{6,4},{7,5},{8,10},{9,11},{10,... | collective-permute-start | bytes 786440 | tf_op jit(solution)/shard_map/ppermute | solution.py:421
  31.2 2.4 %collective-permute-start.9 = (bf16[2,4,16,2048]{3,2,1,0:T(8,128)(2,1)S(1)}, bf16[2,4,16,2048]{3,2,1,0:T(8,128)(2,1)S(1)}, u32[]{:S(2)}, u32[]{:S(2)}) collective-permute-start(bf16[2,4,16,2048]{3,2,1,0:T(8,128)(2,1)S(1)} %pad_maximum_fusion.1), channel_id=1, source_target_pairs={{0,1},{1,0},{2,3},{3,2},{4,5},{5,4},{6,7},{7,6},{8,9},{9,8},{10,11... | collective-permute-start | bytes 1572872 | tf_op jit(solution)/shard_map/ppermute | solution.py:421
  31.2 2.3 %collective-permute-start.8 = (bf16[2,4,16,1024]{3,2,1,0:T(8,128)(2,1)S(1)}, bf16[2,4,16,1024]{3,2,1,0:T(8,128)(2,1)S(1)}, u32[]{:S(2)}, u32[]{:S(2)}) collective-permute-start(bf16[2,4,16,1024]{3,2,1,0:T(8,128)(2,1)S(1)} %get-tuple-element.55), channel_id=1, source_target_pairs={{0,1},{1,0},{2,3},{3,2},{4,5},{5,4},{6,7},{7,6},{8,9},{9,8},{10,11... | collective-permute-start | bytes 786440 | tf_op jit(solution)/shard_map/ppermute | solution.py:421
  33.6 5.6 %collective-permute-start.10 = (bf16[4,16,1024]{2,1,0:T(8,128)(2,1)S(1)}, bf16[4,16,1024]{2,1,0:T(8,128)(2,1)S(1)}, u32[]{:S(2)}, u32[]{:S(2)}) collective-permute-start(bf16[4,16,1024]{2,1,0:T(8,128)(2,1)S(1)} %fusion.2), channel_id=1, source_target_pairs={{0,2},{1,3},{2,0},{3,1},{4,6},{5,7},{6,4},{7,5},{8,10},{9,11},{10,... | collective-permute-start | bytes 393224 | tf_op jit(solution)/shard_map/ppermute | solution.py:421
  34.1 1.0 %copy-start.3 = (bf16[3,64,1024]{2,1,0:T(8,128)(2,1)S(1)}, bf16[3,64,1024]{2,1,0:T(8,128)(2,1)}, u32[]{:S(2)}) copy-start(bf16[3,64,1024]{2,1,0:T(8,128)(2,1)} %qkv_hbm.1) | copy-start | bytes 1179652
  34.1 1.0 %copy-start.5 = (bf16[64,1024]{1,0:T(8,128)(2,1)S(1)}, bf16[64,1024]{1,0:T(8,128)(2,1)}, u32[]{:S(2)}) copy-start(bf16[64,1024]{1,0:T(8,128)(2,1)} %out_hbm.1) | copy-start | bytes 393220
  39.3 5.0 %collective-permute-start.11 = (bf16[4,16,1024]{2,1,0:T(8,128)(2,1)S(1)}, bf16[4,16,1024]{2,1,0:T(8,128)(2,1)S(1)}, u32[]{:S(2)}, u32[]{:S(2)}) collective-permute-start(bf16[4,16,1024]{2,1,0:T(8,128)(2,1)S(1)} %fusion.1), channel_id=1, source_target_pairs={{0,16},{16,0},{1,17},{17,1},{2,18},{18,2},{3,19},{19,3},{4,20},{20... | collective-permute-start | bytes 393224 | tf_op jit(solution)/shard_map/ppermute | solution.py:421
  40.9 3.4 %collective-permute-start.12 = (bf16[2,4,16,1024]{3,2,1,0:T(8,128)(2,1)S(1)}, bf16[2,4,16,1024]{3,2,1,0:T(8,128)(2,1)S(1)}, u32[]{:S(2)}, u32[]{:S(2)}) collective-permute-start(bf16[2,4,16,1024]{3,2,1,0:T(8,128)(2,1)S(1)} %bitcast.91), channel_id=1, source_target_pairs={{0,1},{1,0},{2,3},{3,2},{4,5},{5,4},{6,7},{7,6},{8,9},{9,8},{10,11... | collective-permute-start | bytes 786440 | tf_op jit(solution)/shard_map/ppermute | solution.py:421
  44.5 6.6 %collective-permute-start.13 = (bf16[128,1024]{1,0:T(8,128)(2,1)S(1)}, bf16[128,1024]{1,0:T(8,128)(2,1)S(1)}, u32[]{:S(2)}, u32[]{:S(2)}) collective-permute-start(bf16[128,1024]{1,0:T(8,128)(2,1)S(1)} %pad_maximum_fusion.3), channel_id=1, source_target_pairs={{0,4},{4,0},{8,12},{12,8},{1,5},{5,1},{9,13},{13,9},{2,6},{6,2},{1... | collective-permute-start | bytes 786440 | tf_op jit(solution)/shard_map/ppermute | solution.py:421
  44.6 6.6 %collective-permute-start.14 = (bf16[128,1024]{1,0:T(8,128)(2,1)S(1)}, bf16[128,1024]{1,0:T(8,128)(2,1)S(1)}, u32[]{:S(2)}, u32[]{:S(2)}) collective-permute-start(bf16[128,1024]{1,0:T(8,128)(2,1)S(1)} %get-tuple-element.88), channel_id=1, source_target_pairs={{0,16},{16,0},{1,17},{17,1},{2,18},{18,2},{3,19},{19,3},{4,20},{20... | collective-permute-start | bytes 786440 | tf_op jit(solution)/shard_map/ppermute | solution.py:421
  51.2 9.3 %collective-permute-start.15 = (bf16[96,1024]{1,0:T(8,128)(2,1)S(1)}, bf16[96,1024]{1,0:T(8,128)(2,1)S(1)}, u32[]{:S(2)}, u32[]{:S(2)}) collective-permute-start(bf16[96,1024]{1,0:T(8,128)(2,1)S(1)} %pad_maximum_fusion.5), channel_id=1, source_target_pairs={{0,8},{4,12},{8,0},{12,4},{1,9},{5,13},{9,1},{13,5},{2,10},{6,14},... | collective-permute-start | bytes 589832 | tf_op jit(solution)/shard_map/ppermute | solution.py:421
  53.0 7.6 %collective-permute-start.16 = (bf16[128,1024]{1,0:T(8,128)(2,1)S(1)}, bf16[128,1024]{1,0:T(8,128)(2,1)S(1)}, u32[]{:S(2)}, u32[]{:S(2)}) collective-permute-start(bf16[128,1024]{1,0:T(8,128)(2,1)S(1)} %get-tuple-element.87), channel_id=1, source_target_pairs={{0,16},{16,0},{1,17},{17,1},{2,18},{18,2},{3,19},{19,3},{4,20},{20... | collective-permute-start | bytes 786440 | tf_op jit(solution)/shard_map/ppermute | solution.py:421
  60.6 5.4 %collective-permute-start.17 = (bf16[80,1024]{1,0:T(8,128)(2,1)S(1)}, bf16[80,1024]{1,0:T(8,128)(2,1)S(1)}, u32[]{:S(2)}, u32[]{:S(2)}) collective-permute-start(bf16[80,1024]{1,0:T(8,128)(2,1)S(1)} %pad_maximum_fusion.6), channel_id=1, source_target_pairs={{0,2},{1,3},{2,0},{3,1},{4,6},{5,7},{6,4},{7,5},{8,10},{9,11},{10,... | collective-permute-start | bytes 491528 | tf_op jit(solution)/shard_map/ppermute | solution.py:421
  66.1 1.6 %collective-permute-start.18 = (bf16[2,64,1024]{2,1,0:T(8,128)(2,1)S(1)}, bf16[2,64,1024]{2,1,0:T(8,128)(2,1)S(1)}, u32[]{:S(2)}, u32[]{:S(2)}) collective-permute-start(bf16[2,64,1024]{2,1,0:T(8,128)(2,1)S(1)} %pad_maximum_fusion.4.near_ref), channel_id=1, source_target_pairs={{0,1},{1,0},{2,3},{3,2},{4,5},{5,4},{6,7},{7,6},{8,9},{9,8},{10,11... | collective-permute-start | bytes 786440 | tf_op jit(solution)/shard_map/ppermute | solution.py:421
  66.2 1.5 %copy-start.6 = (bf16[1,4,4,1024]{3,2,1,0:T(4,128)(2,1)S(1)}, bf16[1,4,4,1024]{3,2,1,0:T(4,128)(2,1)}, u32[]{:S(2)}) copy-start(bf16[1,4,4,1024]{3,2,1,0:T(4,128)(2,1)} %param.13) | copy-start | bytes 98308

commit v4 on v3

--- a/solution.py
+++ b/solution.py
@@ -2,6 +2,7 @@
 
 import jax
 import jax.numpy as jnp
+import numpy as np
 from jax import lax
 from jax.experimental import pallas as pl
 from jax.experimental.pallas import tpu as pltpu
@@ -27,10 +28,13 @@
     return lax.dot_general(first, second, (dims, ((), ())), preferred_element_type=jnp.float32)
 
 
-def time_gain(gains, step_value):
-    channels = gains.shape[0]
-    frequency = jnp.exp(-log_span * jnp.arange(channels, dtype=jnp.float32) / channels)
-    return gains * (1.0 + 0.5 * jnp.cos(step_value.astype(jnp.float32) * frequency))
+def frequencies(channels):
+    steps = np.float32(-log_span) * np.arange(channels, dtype=np.float32) / np.float32(channels)
+    return np.exp(steps)[None]
+
+
+def odd_rank(axis):
+    return lax.axis_index(axis) & 1 == 1
 
 
 def inverse_rms(floats):
@@ -47,14 +51,19 @@
     return -(-value // multiple) * multiple
 
 
+def in_order(axis, near, far):
+    odd = odd_rank(axis)
+    first, second = near[...].astype(jnp.float32), far[...].astype(jnp.float32)
+    return jnp.where(odd, first, second), jnp.where(odd, second, first)
+
+
 def fine_body(
-    limits,
     x_ref,
     dy_ref,
-    above_ref,
-    below_ref,
-    left_ref,
-    right_ref,
+    row_near_ref,
+    row_far_ref,
+    col_near_ref,
+    col_far_ref,
     factor_ref,
     qkv_ref,
     out_ref,
@@ -85,13 +94,16 @@
     dk_grid[...] = jnp.zeros_like(dk_grid)
     dv_grid[...] = jnp.zeros_like(dv_grid)
     inner = slice(HALO, HALO + breadth)
-    x_grid[0:HALO, inner] = above_ref[0:HALO].astype(floats)
+    above, below = in_order("gy", row_near_ref, row_far_ref)
+    left, right = in_order("gx", col_near_ref, col_far_ref)
+    x_grid[0:HALO, inner] = above[0:HALO]
     x_grid[HALO : HALO + height, inner] = x_ref[...].astype(floats)
-    x_grid[HALO + height : HALO + height + HALO, inner] = below_ref[0:HALO].astype(floats)
-    dy_grid[0:RAD, inner] = above_ref[HALO : HALO + RAD].astype(floats)
+    x_grid[HALO + height : HALO + height + HALO, inner] = below[0:HALO]
+    dy_grid[0:RAD, inner] = above[HALO : HALO + RAD]
     dy_grid[RAD : RAD + height, inner] = dy_ref[...].astype(floats)
-    dy_grid[RAD + height : RAD + height + RAD, inner] = below_ref[HALO : HALO + RAD].astype(floats)
-    for strip, first in ((left_ref, 0), (right_ref, HALO + breadth)):
+    dy_grid[RAD + height : RAD + height + RAD, inner] = below[HALO : HALO + RAD]
+    left, right = left[:, left.shape[1] - HALO :], right[:, :HALO]
+    for strip, first in ((left, 0), (right, HALO + breadth)):
         span = slice(first, first + HALO)
         at = 0
         for grid, begin, count in (
@@ -102,7 +114,7 @@
             (x_grid, HALO + height, HALO),
             (dy_grid, RAD + height, RAD),
         ):
-            grid[begin : begin + count, span] = strip[at : at + count].astype(floats)
+            grid[begin : begin + count, span] = strip[at : at + count]
             at += count
 
     tokens = x_grid[...].reshape(grid_rows * grid_cols, D_F)
@@ -124,7 +136,10 @@
     col_gap = (key_at % lanes_wide) - (query_at % side)
     near = (row_gap >= 0) & (row_gap <= 2 * RAD) & (col_gap >= 0) & (col_gap <= 2 * RAD)
     bias_ref[...] = jnp.where(near, 0.0, -1e30)
-    row_low, row_high, col_low, col_high = limits[0], limits[1], limits[2], limits[3]
+    gx, gy = lax.axis_index("gx"), lax.axis_index("gy")
+    row_low, col_low = HALO - gy * height, HALO - gx * breadth
+    row_high = row_low + lax.axis_size("gy") * height
+    col_high = col_low + lax.axis_size("gx") * breadth
     lone = lax.broadcasted_iota(jnp.int32, (keys_count, 1), 0)
     head_of = lax.broadcasted_iota(jnp.int32, (side * side, D_F), 1) // HD
 
@@ -197,13 +212,13 @@
         target = (keep_ref, send_ref)[low]
         for high in range(half):
             for row in range(columns):
-                block = (limits[4] ^ (2 * high + low)) * columns + row
+                block = (gx ^ (2 * high + low)) * columns + row
                 target[high, row] = total_ref[block].astype(target.dtype)
     down = dot(grad_proj, qkv_ref[...], ((1,), (1,)))
     dx_ref[...] = norm_backward(picture, inverse, factor, down).reshape(height, breadth, D_F)
 
 
-def fine_block(peers, limits, picture, cotangent, above, below, left, right, factor, fine_qkv, fine_out):
+def fine_block(peers, picture, *operands):
     height, breadth = picture.shape[0], picture.shape[1]
     query_rows = round_up(height + 2 * RAD, side)
     query_cols = round_up(breadth + 2 * RAD, side)
@@ -222,7 +237,7 @@
             jax.ShapeDtypeStruct(halves, jnp.float32),
             jax.ShapeDtypeStruct(halves, jnp.bfloat16),
         ),
-        in_specs=[pl.BlockSpec(memory_space=pltpu.SMEM)] + [vmem] * 9,
+        in_specs=[vmem] * 9,
         out_specs=(vmem, vmem, vmem),
         scratch_shapes=[
             wide,
@@ -240,7 +255,7 @@
         ],
         compiler_params=pltpu.CompilerParams(vmem_limit_bytes=vmem_bytes),
         name="fine_block",
-    )(limits, picture, cotangent, above, below, left, right, factor, fine_qkv, fine_out)
+    )(picture, *operands)
 
 
 def coarse_body(
@@ -309,21 +324,110 @@
     )(tokens, cotangents, factor, head_qkv, head_out)
 
 
-def pack_body(first, second, x_ref, dy_ref, own_ref):
+def row_edges_body(x_ref, dy_ref, near_ref, far_ref):
+    height = x_ref.shape[0]
+    odd = odd_rank("gy")
+
+    def fill(low_ref, high_ref):
+        low_ref[:HALO], low_ref[HALO:] = x_ref[:HALO], dy_ref[:RAD]
+        high_ref[:HALO], high_ref[HALO:] = x_ref[height - HALO :], dy_ref[height - RAD :]
+
+    @pl.when(odd)
+    def _():
+        fill(near_ref, far_ref)
+
+    @pl.when(jnp.logical_not(odd))
+    def _():
+        fill(far_ref, near_ref)
+
+
+def row_edges(picture, cotangent):
+    vmem = pl.BlockSpec(memory_space=pltpu.VMEM)
+    shape = jax.ShapeDtypeStruct((HALO + RAD,) + picture.shape[1:], jnp.bfloat16)
+    return pl.pallas_call(
+        row_edges_body,
+        out_shape=(shape, shape),
+        in_specs=[vmem, vmem],
+        out_specs=(vmem, vmem),
+        compiler_params=pltpu.CompilerParams(vmem_limit_bytes=vmem_bytes),
+        name="row_edges",
+    )(picture, cotangent)
+
+
+def col_edges_body(x_ref, dy_ref, row_near_ref, row_far_ref, near_ref, far_ref):
+    above, below = in_order("gy", row_near_ref, row_far_ref)
+    breadth = x_ref.shape[1]
+    odd = odd_rank("gx")
+    at = 0
+    for rows in (above, x_ref[...].astype(jnp.float32), dy_ref[...].astype(jnp.float32), below):
+        first, final = rows[:, :side], rows[:, breadth - side :]
+        span = slice(at, at + rows.shape[0])
+        near_ref[span] = jnp.where(odd, first, final).astype(jnp.bfloat16)
+        far_ref[span] = jnp.where(odd, final, first).astype(jnp.bfloat16)
+        at += rows.shape[0]
+
+
+def col_edges(picture, cotangent, row_near, row_far):
+    vmem = pl.BlockSpec(memory_space=pltpu.VMEM)
+    rows = 2 * (picture.shape[0] + row_near.shape[0])
+    shape = jax.ShapeDtypeStruct((rows, side, D_F), jnp.bfloat16)
+    return pl.pallas_call(
+        col_edges_body,
+        out_shape=(shape, shape),
+        in_specs=[vmem] * 4,
+        out_specs=(vmem, vmem),
+        compiler_params=pltpu.CompilerParams(vmem_limit_bytes=vmem_bytes),
+        name="col_edges",
+    )(picture, cotangent, row_near, row_far)
+
+
+def pack_body(
+    first,
+    second,
+    step,
+    x_ref,
+    dy_ref,
+    fine_gain,
+    coarse_gain,
+    fine_freq,
+    coarse_freq,
+    own_ref,
+    fine_ref,
+    coarse_ref,
+):
     own_ref[:, :D_C] = x_ref[...].astype(jnp.float32).reshape(-1, D_C).astype(jnp.bfloat16)
     own_ref[:, D_C:] = dy_ref[...].astype(jnp.float32).reshape(-1, D_C).astype(jnp.bfloat16)
-
-
-def packed(after, tokens, cotangents):
+    time = step[0].astype(jnp.float32)
+    fine_ref[...] = fine_gain[...] * (1.0 + 0.5 * jnp.cos(time * fine_freq[...]))
+    coarse_ref[...] = coarse_gain[...] * (1.0 + 0.5 * jnp.cos(time * coarse_freq[...]))
+
+
+def packed(after, step, tokens, cotangents, fine_gain, coarse_gain):
     vmem = pl.BlockSpec(memory_space=pltpu.VMEM)
     count = tokens.shape[0] * tokens.shape[1]
     return pl.pallas_call(
         pack_body,
-        out_shape=jax.ShapeDtypeStruct((count, 2 * D_C), jnp.bfloat16),
-        in_specs=[pl.BlockSpec(memory_space=pl.ANY)] * 2 + [vmem] * 2,
-        out_specs=vmem,
+        out_shape=(
+            jax.ShapeDtypeStruct((count, 2 * D_C), jnp.bfloat16),
+            jax.ShapeDtypeStruct((1, D_F), jnp.float32),
+            jax.ShapeDtypeStruct((1, D_C), jnp.float32),
+        ),
+        in_specs=[pl.BlockSpec(memory_space=pl.ANY)] * 2
+        + [pl.BlockSpec(memory_space=pltpu.SMEM)]
+        + [vmem] * 6,
+        out_specs=(vmem, vmem, vmem),
+        compiler_params=pltpu.CompilerParams(vmem_limit_bytes=vmem_bytes),
         name="pack_coarse",
-    )(*after, tokens, cotangents)
+    )(
+        *after,
+        step,
+        tokens,
+        cotangents,
+        fine_gain[None],
+        coarse_gain[None],
+        frequencies(D_F),
+        frequencies(D_C),
+    )
 
 
 def pair_sum_body(own, first, second, qkv_ref, out_ref):
@@ -352,13 +456,11 @@
 
 
 def last_body(
-    place,
     near_ref,
     far_ref,
     x_ref,
     factor_ref,
-    kept_ref,
-    come_ref,
+    upstream_ref,
     qkv_hbm,
     out_hbm,
     dx_ref,
@@ -369,7 +471,7 @@
     for low in range(2):
         for high in range(highs):
             source = (near_ref, far_ref)[low].at[high]
-            block = place[0] ^ (2 * high + low)
+            block = lax.axis_index("gx") ^ (2 * high + low)
             at = pl.ds(pl.multiple_of(block * rows, rows), rows)
             for part, target in enumerate((qkv_hbm, out_hbm)):
                 lanes = (slice(0, 3 * D_F), slice(3 * D_F, 4 * D_F))[part]
@@ -381,14 +483,13 @@
     for copy in copies:
         copy.start()
     tokens = x_ref[...].astype(jnp.float32).reshape(-1, D_C)
-    upstream = kept_ref[...] + come_ref[...].astype(jnp.float32)
-    grads = norm_backward(tokens, inverse_rms(tokens), factor_ref[...], upstream)
+    grads = norm_backward(tokens, inverse_rms(tokens), factor_ref[...], upstream_ref[...])
     dx_ref[...] = grads.astype(jnp.float32).reshape(dx_ref.shape).astype(jnp.bfloat16)
     for copy in copies:
         copy.wait()
 
 
-def last_step(place, near, far, tokens, factor, kept, come):
+def last_step(near, far, tokens, factor, upstream):
     vmem = pl.BlockSpec(memory_space=pltpu.VMEM)
     hbm = pl.BlockSpec(memory_space=pltpu.HBM)
     return pl.pallas_call(
@@ -398,23 +499,20 @@
             jax.ShapeDtypeStruct((D_F, D_F), jnp.bfloat16),
             jax.ShapeDtypeStruct(tokens.shape, jnp.bfloat16),
         ),
-        in_specs=[pl.BlockSpec(memory_space=pltpu.SMEM)] + [vmem] * 6,
+        in_specs=[vmem] * 5,
         out_specs=(hbm, hbm, vmem),
         scratch_shapes=[pltpu.SemaphoreType.DMA((2, near.shape[0], 2))],
         compiler_params=pltpu.CompilerParams(vmem_limit_bytes=vmem_bytes),
         name="last_step",
-    )(place, near, far, tokens, factor, kept, come)
-
-
-def neighbours(low_edge, high_edge, axis):
+    )(near, far, tokens, factor, upstream)
+
+
+def neighbours(to_near, to_far, axis):
     peers = lax.axis_size(axis)
-    odd = lax.axis_index(axis) & 1 == 1
     near = [(i, i ^ 1) for i in range(peers)]
     far = [(i, i + 1 if i % 2 else i - 1) for i in range(1, peers - 1)]
-    to_near, to_far = jnp.where(odd, low_edge, high_edge), jnp.where(odd, high_edge, low_edge)
-    second = lax.ppermute(to_far, axis, far)
-    first = lax.ppermute(to_near, axis, near)
-    return jnp.where(odd, first, second), jnp.where(odd, second, first), (to_near, to_far)
+    from_far = lax.ppermute(to_far, axis, far)
+    return lax.ppermute(to_near, axis, near), from_far
 
 
 def swapped(value, axis, mask):
@@ -457,63 +555,40 @@
     coarse_qkv,
     coarse_out,
 ):
-    step_value = timestep[0]
     picture, cotangent = x_fine[0], dy_fine[0]
-    height, breadth = picture.shape[0], picture.shape[1]
     across, downs = lax.axis_size("gx"), lax.axis_size("gy")
     assert across == 4 and downs & (downs - 1) == 0
-    gx, gy = lax.axis_index("gx"), lax.axis_index("gy")
-
-    low = jnp.concatenate([picture[:HALO], cotangent[:RAD]], axis=0)
-    high = jnp.concatenate([picture[height - HALO :], cotangent[height - RAD :]], axis=0)
-    above, below, payloads = neighbours(low, high, "gy")
-    own = packed(payloads, x_coarse[0], dy_coarse[0])
-    row_first = gy * height - HALO
-    col_first = gx * breadth - HALO
-    limits = jnp.stack(
-        [
-            -row_first,
-            downs * height - row_first,
-            -col_first,
-            across * breadth - col_first,
-            gx,
-            gy,
-        ]
-    ).astype(jnp.int32)
-    factor = time_gain(fine_gain, step_value)[None]
-    coarse_factor = time_gain(coarse_gain, step_value)[None]
-    place = gx.astype(jnp.int32)[None]
-    above, below, limits, place, factor, coarse_factor = tied(
-        above, below, limits, place, factor, coarse_factor
-    )
-    column = jnp.concatenate([above, picture, cotangent, below], axis=0)
-    first, final = column[:, :HALO], column[:, breadth - HALO :]
-    left, right, _ = neighbours(first, final, "gx")
+
+    payloads = row_edges(picture, cotangent)
+    row_near, row_far = neighbours(*payloads, "gy")
+    own, factor, coarse_factor = packed(
+        payloads, timestep, x_coarse[0], dy_coarse[0], fine_gain, coarse_gain
+    )
     count = own.shape[0]
     row_group = all_rows(own)
-    left, right, row_group = tied(left, right, row_group)
-    pair = jnp.stack([row_group, swapped(row_group, "gx", 2)])
+    edges = col_edges(picture, cotangent, row_near, row_far)
+    col_near, col_far = neighbours(*edges, "gx")
+    col_near, col_far, row_group = tied(col_near, col_far, row_group)
+    cross = swapped(row_group, "gx", 2)
+    beside = swapped(row_group, "gx", 1)
     dx_picture, fine_keep, fine_send = fine_block(
         (across, downs),
-        limits,
         picture,
         cotangent,
-        above,
-        below,
-        left,
-        right,
+        row_near,
+        row_far,
+        col_near,
+        col_far,
         factor,
         fine_qkv,
         fine_out,
     )
-    fine_send, pair = tied(fine_send, pair)
-
     fine_half = fine_keep + wide(swapped(fine_send, "gx", 1))
-    other_pair = swapped(pair, "gx", 1)
-    fine_half, other_pair = tied(fine_half, other_pair)
+    opposite = swapped(cross, "gx", 1)
+    fine_half, opposite = tied(fine_half, opposite)
 
     fine_quarter = narrow(fine_half[0] + wide(swapped(narrow(fine_half[1]), "gx", 2)))
-    everyone = jnp.stack([pair, other_pair]).reshape(-1, 2 * D_C)
+    everyone = jnp.stack([row_group, cross, beside, opposite]).reshape(-1, 2 * D_C)
     parts, coarse_partial = coarse_block(
         everyone[:, :D_C], everyone[:, D_C:], coarse_factor, coarse_qkv, coarse_out
     )
@@ -523,6 +598,7 @@
     fine_quarter = narrow(batch_sum(fine_quarter)).reshape(rows, 4 * D_F)
     parts = parts.reshape(2, 2, downs, count, D_C)
     coarse_kept = wide(parts[0]) + wide(swapped(parts[1], "gx", 1))
+    coarse_kept = coarse_kept[0] + wide(swapped(narrow(coarse_kept[1]), "gx", 2))
     fine_quarter, coarse_kept, coarse_partial = tied(fine_quarter, coarse_kept, coarse_partial)
 
     pair_batch = lax.axis_size("batch") == 2
@@ -531,18 +607,17 @@
     mask = 1
     while mask < downs:
         last = 2 * mask == downs
-        coarse_kept = coarse_kept.reshape(2, -1, 2, count, D_C)
-        sent = narrow(coarse_kept[:, :, 1]).reshape(-1, D_C)
+        coarse_kept = coarse_kept.reshape(-1, 2, count, D_C)
+        sent = narrow(coarse_kept[:, 1]).reshape(-1, D_C)
         come = swapped(jnp.concatenate([fine_quarter, sent], axis=0), "gy", mask)
-        coarse_kept = coarse_kept[:, :, 0]
+        coarse_kept = coarse_kept[:, 0]
         coarse_kept = coarse_kept + wide(come[rows:]).reshape(coarse_kept.shape)
         fine_quarter = narrow(wide(fine_quarter) + wide(come[:rows]))
         at = int(last)
         fine_quarter, coarse_kept, others[at] = tied(fine_quarter, coarse_kept, others[at])
         mask *= 2
 
-    coarse_kept = coarse_kept.reshape(2, count, D_C)
-    come = swapped(jnp.concatenate([fine_quarter, narrow(coarse_kept[1])], axis=0), "gx", 2)
+    come = swapped(fine_quarter, "gx", 2)
     if pair_batch:
         grad_coarse_qkv, grad_coarse_out = pair_sum(coarse_partial, *others)
     else:
@@ -550,15 +625,13 @@
         grad_coarse_qkv = coarse_sum[: 3 * HD].reshape(coarse_qkv.shape)
         grad_coarse_out = coarse_sum[3 * HD :]
     come, grad_coarse_qkv, grad_coarse_out = tied(come, grad_coarse_qkv, grad_coarse_out)
-    fine_pair = jnp.stack([fine_quarter, come[:rows]])
+    fine_pair = jnp.stack([fine_quarter, come])
     grad_qkv, grad_out, dx_coarse = last_step(
-        place,
         fine_pair,
         swapped(fine_pair, "gx", 1),
         x_coarse[0],
         coarse_factor,
-        coarse_kept[0],
-        come[rows:],
+        coarse_kept.reshape(count, D_C),
     )
     return (
         dx_picture[None],

time: 69.5 us -> 72.7 us (1.046)
  waiting for transfers between devices: 24.4 us -> 30.3 us
  Pallas kernels: 12.6 us -> 10.9 us
    ppermute x15 -> x17, waiting for transfers between devices: 23.5 us -> 30.3 us  [swapped(): lax.ppermute(value, axis, [(i, i ^ mask) for i in range(lax.axis_size(axi...]
    ppermute x4, starting transfers between devices: 10.2 us -> 4.62 us  [the longest x2 3.16 us: neighbours(): return (lax.ppermute(to_near, axis, near), from_far)]
    ppermute x15 -> x17, starting transfers between devices: 15.7 us -> 20.8 us  [swapped(): lax.ppermute(value, axis, [(i, i ^ mask) for i in range(lax.axis_size(axi...]
    pallas_call x1 -> x3, Pallas kernels: 1.42 us -> 0.16 us  [the longest x1 0.08 us: col_edges(): pl.pallas_call(col_edges_body, out_shape=(shape, shape), in_specs=[vmem]...]
    unnamed x24 -> x28, local copies, waits for them, and re-layouts: 2.48 us -> 3.41 us
    slice x5 -> x1, local copies, waits for them, and re-layouts: 0.91 us -> 0.01 us  [local(): sent = narrow(coarse_kept[:, 1]).reshape(-1, D_C)]
    ppermute x4, waiting for transfers between devices: 0.9 us -> 0.01 us  [the longest x2 0.01 us: neighbours(): from_far = lax.ppermute(to_far, axis, far)]
  transfers between devices with their start and end apart: 19 -> 21, of which waited for: 8 -> 12; matrix products, arithmetic and copies ran while one was open for 1% -> 1% of each run, Pallas kernels for 16% -> 13%
where the time goes in v4:
time: 72.7 us; the launch traced here: 72.4 us
  waiting for transfers between devices  30.3 us (42%)
  starting transfers between devices  25.4 us (35%)
  Pallas kernels  10.9 us (15%)
  local copies, waits for them, and re-layouts  3.61 us (5%)
  between operations  1.63 us (2%)
    ppermute x17, waiting for transfers between devices, swapped(): lax.ppermute(value, axis, [(i, i ^ mask) for i in range(lax.axis_size(axi...  30.3 us
    ppermute x17, starting transfers between devices, swapped(): lax.ppermute(value, axis, [(i, i ^ mask) for i in range(lax.axis_size(axi...  20.8 us
    pallas_call x1, Pallas kernels, fine_block(): pl.pallas_call(fine_body, out_shape=(jax.ShapeDtypeStruct((height, breadt...  6.17 us
    unnamed x28, local copies, waits for them, and re-layouts  3.41 us
    ppermute x2, starting transfers between devices, neighbours(): return (lax.ppermute(to_near, axis, near), from_far)  3.16 us
    pallas_call x1, Pallas kernels, coarse_block(): pl.pallas_call(coarse_body, out_shape=(jax.ShapeDtypeStruct((count, D_C),...  2.23 us
    pallas_call x1, Pallas kernels, last_step(): pl.pallas_call(last_body, out_shape=(jax.ShapeDtypeStruct((D_F, 3 * D_F),...  1.48 us
    ppermute x2, starting transfers between devices, neighbours(): from_far = lax.ppermute(to_far, axis, far)  1.46 us
  transfers between devices with their start and end apart: 21, of which 12 were waited for; matrix products, arithmetic and copies ran while one was open for 1% of the time, Pallas kernels for 13%

profile of v4, /device:TPU:0, one launch (start us, length us, event | category | flops | bytes accessed | tf_op | source)
XLA Modules:
  0.0 72.4 jit_solution(11645225029312532162)
XLA Ops:
  0.6 0.0 copy-start
  0.6 0.9 %copy-done = bf16[1,8,32,256]{3,2,1,0:T(8,128)(2,1)S(1)} copy-done((bf16[1,8,32,256]{3,2,1,0:T(8,128)(2,1)S(1)}, bf16[1,8,32,256]{3,2,1,0:T(8,128)(2,1)}, u32[]{:S(2)}) %copy-start) | copy-done | bytes 131096
  1.5 0.9 %copy-done.2 = bf16[1,8,32,256]{3,2,1,0:T(8,128)(2,1)S(1)} copy-done((bf16[1,8,32,256]{3,2,1,0:T(8,128)(2,1)S(1)}, bf16[1,8,32,256]{3,2,1,0:T(8,128)(2,1)}, u32[]{:S(2)}) %copy-start.2) | copy-done | bytes 131096
  2.5 0.0 copy-start.13
  2.5 3.1 %collective-permute-start = (bf16[9,32,256]{2,1,0:T(8,128)(2,1)S(1)}, bf16[9,32,256]{2,1,0:T(8,128)(2,1)S(1)}, u32[]{:S(2)}, u32[]{:S(2)}) collective-permute-start(bf16[9,32,256]{2,1,0:T(8,128)(2,1)S(1)} %get-tuple-element.43.first), channel_id=1, source_target_pairs={{0,4},{4,0},{8,12},{12,8},{1,5},{5,1},{9,13},{13,9},{2,6},{6,2},{1... | collective-permute-start | bytes 442376 | tf_op jit(solution)/shard_map/ppermute | solution.py:515
  5.6 0.7 collective-permute-start.1
  6.2 0.0 copy-start.11
  6.9 0.0 copy-start.10
  6.9 0.0 copy-start.12
  7.0 0.6 copy-done.10
  7.6 0.0 copy-done.12
  7.6 0.1 pack_coarse.1
  7.7 2.5 %collective-permute-start.6 = (bf16[16,2048]{1,0:T(8,128)(2,1)S(1)}, bf16[16,2048]{1,0:T(8,128)(2,1)S(1)}, u32[]{:S(2)}, u32[]{:S(2)}) collective-permute-start(bf16[16,2048]{1,0:T(8,128)(2,1)S(1)} %get-tuple-element.47), channel_id=1, source_target_pairs={{0,12},{4,8},{8,4},{12,0},{1,13},{5,9},{9,5},{13,1},{2,14},{6,10},... | collective-permute-start | bytes 196616 | tf_op jit(solution)/shard_map/ppermute | solution.py:519
  10.2 3.4 %collective-permute-start.5 = (bf16[16,2048]{1,0:T(8,128)(2,1)S(1)}, bf16[16,2048]{1,0:T(8,128)(2,1)S(1)}, u32[]{:S(2)}, u32[]{:S(2)}) collective-permute-start(bf16[16,2048]{1,0:T(8,128)(2,1)S(1)} %get-tuple-element.47), channel_id=1, source_target_pairs={{0,8},{4,12},{8,0},{12,4},{1,9},{5,13},{9,1},{13,5},{2,10},{6,14},... | collective-permute-start | bytes 196616 | tf_op jit(solution)/shard_map/ppermute | solution.py:519
  13.6 0.0 collective-permute-start.4
  13.6 0.0 collective-permute-done.row_near_ref
  13.6 0.0 collective-permute-done.1.row_far_ref
  13.6 0.1 col_edges.1
  13.7 0.0 copy-start.4
  13.7 0.1 collective-permute-start.2
  13.8 0.8 %collective-permute-start.3 = (bf16[34,8,256]{2,1,0:T(8,128)(2,1)S(1)}, bf16[34,8,256]{2,1,0:T(8,128)(2,1)S(1)}, u32[]{:S(2)}, u32[]{:S(2)}) collective-permute-start(bf16[34,8,256]{2,1,0:T(8,128)(2,1)S(1)} %get-tuple-element.46), channel_id=1, source_target_pairs={{1,2},{2,1},{5,6},{6,5},{9,10},{10,9},{13,14},{14,13},{17,18},{18,... | collective-permute-start | bytes 417800 | tf_op jit(solution)/shard_map/ppermute | solution.py:514
  14.6 0.0 collective-permute-done.6
  14.6 4.6 %collective-permute-done.5 = bf16[16,2048]{1,0:T(8,128)(2,1)S(1)} collective-permute-done((bf16[16,2048]{1,0:T(8,128)(2,1)S(1)}, bf16[16,2048]{1,0:T(8,128)(2,1)S(1)}, u32[]{:S(2)}, u32[]{:S(2)}) %collective-permute-start.5) | collective-permute-done | bytes 65568 | tf_op jit(solution)/shard_map/ppermute | solution.py:519
  19.2 0.0 collective-permute-done.4
  19.3 0.0 collective-permute-done.3.col_far_ref
  19.3 2.5 %collective-permute-start.8 = (bf16[4,16,2048]{2,1,0:T(8,128)(2,1)S(1)}, bf16[4,16,2048]{2,1,0:T(8,128)(2,1)S(1)}, u32[]{:S(2)}, u32[]{:S(2)}) collective-permute-start(bf16[4,16,2048]{2,1,0:T(8,128)(2,1)S(1)} %pad_maximum_fusion.1), channel_id=1, source_target_pairs={{0,2},{1,3},{2,0},{3,1},{4,6},{5,7},{6,4},{7,5},{8,10},{9,11},{10,... | collective-permute-start | bytes 786440 | tf_op jit(solution)/shard_map/ppermute | solution.py:519
  21.8 6.2 %fine_block.1 = (bf16[8,32,256]{2,1,0:T(8,128)(2,1)}, f32[2,4,16,1024]{3,2,1,0:T(8,128)S(1)}, bf16[2,4,16,1024]{3,2,1,0:T(8,128)(2,1)S(1)}) custom-call(bf16[8,32,256]{2,1,0:T(8,128)(2,1)S(1)} %bitcast.59, bf16[8,32,256]{2,1,0:T(8,128)(2,1)S(1)} %bitcast.62, bf16[9,32,256]{2,1,0:T(8,128)(2,1)S(1)} %collective-permute-done.row_near_ref, ...), custom_call_target="tpu_custom_call" | custom-call | tf_op jit(solution)/shard_map/fine_block/pallas_call | solution.py:233
  28.0 0.9 %collective-permute-done.8 = bf16[4,16,2048]{2,1,0:T(8,128)(2,1)S(1)} collective-permute-done((bf16[4,16,2048]{2,1,0:T(8,128)(2,1)S(1)}, bf16[4,16,2048]{2,1,0:T(8,128)(2,1)S(1)}, u32[]{:S(2)}, u32[]{:S(2)}) %collective-permute-start.8) | collective-permute-done | bytes 262176 | tf_op jit(solution)/shard_map/ppermute | solution.py:519
  28.9 0.0 collective-permute-start.9
  28.9 0.5 collective-permute-start.11
  29.4 0.1 collective-permute-done.7
  29.5 0.1 convert_add_fusion.1
  29.6 0.8 %collective-permute-done.9 = bf16[4,16,2048]{2,1,0:T(8,128)(2,1)S(1)} collective-permute-done((bf16[4,16,2048]{2,1,0:T(8,128)(2,1)S(1)}, bf16[4,16,2048]{2,1,0:T(8,128)(2,1)S(1)}, u32[]{:S(2)}, u32[]{:S(2)}) %collective-permute-start.9) | collective-permute-done | bytes 262176 | tf_op jit(solution)/shard_map/ppermute | solution.py:519
  30.4 0.3 collective-permute-start.10
  30.8 0.0 collective-permute-done.11
  30.8 0.1 pad_maximum_fusion
  30.9 0.0 copy-start.5
  30.9 0.0 copy-start.7
  31.0 0.1 fusion.8
  31.0 0.9 %copy-done.5 = bf16[3,64,1024]{2,1,0:T(8,128)(2,1)S(1)} copy-done((bf16[3,64,1024]{2,1,0:T(8,128)(2,1)S(1)}, bf16[3,64,1024]{2,1,0:T(8,128)(2,1)}, u32[]{:S(2)}) %copy-start.5) | copy-done | bytes 393240
  31.9 0.0 copy-done.7
  32.0 2.2 %coarse_block.1 = (bf16[256,1024]{1,0:T(8,128)(2,1)S(1)}, bf16[256,1024]{1,0:T(8,128)(2,1)S(1)}) custom-call(bf16[256,1024]{1,0:T(8,128)(2,1)S(1)} %get-tuple-element.81.x_ref, bf16[256,1024]{1,0:T(8,128)(2,1)S(1)} %get-tuple-element.80.dy_ref, f32[1,1024]{1,0:T(1,128)S(1)} %get-tuple-element.57.factor_ref, bf16[3,64,1024]{2,1,0:T(8,128)(2,1)S(1)} %copy-done.5, ...), custom_call_target="tpu_custom_call" | custom-call | tf_op jit(solution)/shard_map/coarse_block/pallas_call | solution.py:309
  34.2 1.8 %collective-permute-done.10 = bf16[4,16,1024]{2,1,0:T(8,128)(2,1)S(1)} collective-permute-done((bf16[4,16,1024]{2,1,0:T(8,128)(2,1)S(1)}, bf16[4,16,1024]{2,1,0:T(8,128)(2,1)S(1)}, u32[]{:S(2)}, u32[]{:S(2)}) %collective-permute-start.10) | collective-permute-done | bytes 131104 | tf_op jit(solution)/shard_map/ppermute | solution.py:519
  36.1 0.1 collective-permute-start.13
  36.2 1.6 %collective-permute-start.12 = (bf16[4,16,1024]{2,1,0:T(8,128)(2,1)S(1)}, bf16[4,16,1024]{2,1,0:T(8,128)(2,1)S(1)}, u32[]{:S(2)}, u32[]{:S(2)}) collective-permute-start(bf16[4,16,1024]{2,1,0:T(8,128)(2,1)S(1)} %fusion.1), channel_id=1, source_target_pairs={{0,16},{16,0},{1,17},{17,1},{2,18},{18,2},{3,19},{19,3},{4,20},{20... | collective-permute-start | bytes 393224 | tf_op jit(solution)/shard_map/ppermute | solution.py:519
  37.8 0.0 collective-permute-done.13
  37.8 0.1 convert_add_fusion
  37.9 0.4 collective-permute-start.14
  38.2 3.9 %collective-permute-done.12 = bf16[4,16,1024]{2,1,0:T(8,128)(2,1)S(1)} collective-permute-done((bf16[4,16,1024]{2,1,0:T(8,128)(2,1)S(1)}, bf16[4,16,1024]{2,1,0:T(8,128)(2,1)S(1)}, u32[]{:S(2)}, u32[]{:S(2)}) %collective-permute-start.12) | collective-permute-done | bytes 131104 | tf_op jit(solution)/shard_map/ppermute | solution.py:519
  42.1 1.4 %collective-permute-done.14 = bf16[4,16,1024]{2,1,0:T(8,128)(2,1)S(1)} collective-permute-done((bf16[4,16,1024]{2,1,0:T(8,128)(2,1)S(1)}, bf16[4,16,1024]{2,1,0:T(8,128)(2,1)S(1)}, u32[]{:S(2)}, u32[]{:S(2)}) %collective-permute-start.14) | collective-permute-done | bytes 131104 | tf_op jit(solution)/shard_map/ppermute | solution.py:519
  43.6 4.5 %collective-permute-start.15 = (bf16[96,1024]{1,0:T(8,128)(2,1)S(1)}, bf16[96,1024]{1,0:T(8,128)(2,1)S(1)}, u32[]{:S(2)}, u32[]{:S(2)}) collective-permute-start(bf16[96,1024]{1,0:T(8,128)(2,1)S(1)} %pad_maximum_fusion.3), channel_id=1, source_target_pairs={{0,4},{4,0},{8,12},{12,8},{1,5},{5,1},{9,13},{13,9},{2,6},{6,2},{1... | collective-permute-start | bytes 589832 | tf_op jit(solution)/shard_map/ppermute | solution.py:519
  48.1 1.5 %collective-permute-start.16 = (bf16[128,1024]{1,0:T(8,128)(2,1)S(1)}, bf16[128,1024]{1,0:T(8,128)(2,1)S(1)}, u32[]{:S(2)}, u32[]{:S(2)}) collective-permute-start(bf16[128,1024]{1,0:T(8,128)(2,1)S(1)} %get-tuple-element.83), channel_id=1, source_target_pairs={{0,16},{16,0},{1,17},{17,1},{2,18},{18,2},{3,19},{19,3},{4,20},{20... | collective-permute-start | bytes 786440 | tf_op jit(solution)/shard_map/ppermute | solution.py:519
  49.6 2.9 %collective-permute-done.15 = bf16[96,1024]{1,0:T(8,128)(2,1)S(1)} collective-permute-done((bf16[96,1024]{1,0:T(8,128)(2,1)S(1)}, bf16[96,1024]{1,0:T(8,128)(2,1)S(1)}, u32[]{:S(2)}, u32[]{:S(2)}) %collective-permute-start.15) | collective-permute-done | bytes 196640 | tf_op jit(solution)/shard_map/ppermute | solution.py:519
  52.5 2.9 %collective-permute-done.16.first = bf16[128,1024]{1,0:T(8,128)(2,1)S(1)} collective-permute-done((bf16[128,1024]{1,0:T(8,128)(2,1)S(1)}, bf16[128,1024]{1,0:T(8,128)(2,1)S(1)}, u32[]{:S(2)}, u32[]{:S(2)}) %collective-permute-start.16) | collective-permute-done | bytes 262176 | tf_op jit(solution)/shard_map/ppermute | solution.py:519
  55.5 1.7 %collective-permute-start.17 = (bf16[80,1024]{1,0:T(8,128)(2,1)S(1)}, bf16[80,1024]{1,0:T(8,128)(2,1)S(1)}, u32[]{:S(2)}, u32[]{:S(2)}) collective-permute-start(bf16[80,1024]{1,0:T(8,128)(2,1)S(1)} %pad_maximum_fusion.4), channel_id=1, source_target_pairs={{0,8},{4,12},{8,0},{12,4},{1,9},{5,13},{9,1},{13,5},{2,10},{6,14},... | collective-permute-start | bytes 491528 | tf_op jit(solution)/shard_map/ppermute | solution.py:519
  57.2 1.4 %collective-permute-start.18 = (bf16[128,1024]{1,0:T(8,128)(2,1)S(1)}, bf16[128,1024]{1,0:T(8,128)(2,1)S(1)}, u32[]{:S(2)}, u32[]{:S(2)}) collective-permute-start(bf16[128,1024]{1,0:T(8,128)(2,1)S(1)} %get-tuple-element.82), channel_id=1, source_target_pairs={{0,16},{16,0},{1,17},{17,1},{2,18},{18,2},{3,19},{19,3},{4,20},{20... | collective-permute-start | bytes 786440 | tf_op jit(solution)/shard_map/ppermute | solution.py:519
  58.6 5.6 %collective-permute-done.17 = bf16[80,1024]{1,0:T(8,128)(2,1)S(1)} collective-permute-done((bf16[80,1024]{1,0:T(8,128)(2,1)S(1)}, bf16[80,1024]{1,0:T(8,128)(2,1)S(1)}, u32[]{:S(2)}, u32[]{:S(2)}) %collective-permute-start.17) | collective-permute-done | bytes 163872 | tf_op jit(solution)/shard_map/ppermute | solution.py:519
  64.2 0.0 collective-permute-done.18.second
  64.3 0.4 collective-permute-start.19
  64.6 0.9 %pair_sum.1 = (bf16[3,64,1024]{2,1,0:T(8,128)(2,1)}, bf16[64,1024]{1,0:T(8,128)(2,1)}) custom-call(bf16[256,1024]{1,0:T(8,128)(2,1)S(1)} %get-tuple-element.65.own, bf16[128,1024]{1,0:T(8,128)(2,1)S(1)} %collective-permute-done.16.first, bf16[128,1024]{1,0:T(8,128)(2,1)S(1)} %collective-permute-done.18.second), custom_call_target="tpu_custom_call" | custom-call | tf_op jit(solution)/shard_map/pair_sum/pallas_call | solution.py:445
  65.5 3.8 %collective-permute-done.19 = bf16[64,1024]{1,0:T(8,128)(2,1)S(1)} collective-permute-done((bf16[64,1024]{1,0:T(8,128)(2,1)S(1)}, bf16[64,1024]{1,0:T(8,128)(2,1)S(1)}, u32[]{:S(2)}, u32[]{:S(2)}) %collective-permute-start.19) | collective-permute-done | bytes 131104 | tf_op jit(solution)/shard_map/ppermute | solution.py:519
  69.3 0.1 collective-permute-start.20
  69.4 1.5 %collective-permute-done.20.far_ref = bf16[2,64,1024]{2,1,0:T(8,128)(2,1)S(1)} collective-permute-done((bf16[2,64,1024]{2,1,0:T(8,128)(2,1)S(1)}, bf16[2,64,1024]{2,1,0:T(8,128)(2,1)S(1)}, u32[]{:S(2)}, u32[]{:S(2)}) %collective-permute-start.20) | collective-permute-done | bytes 262176 | tf_op jit(solution)/shard_map/ppermute | solution.py:519
  70.9 1.5 %last_step.1 = (bf16[256,768]{1,0:T(8,128)(2,1)}, bf16[256,256]{1,0:T(8,128)(2,1)}, bf16[4,4,1024]{2,1,0:T(4,128)(2,1)}) custom-call(bf16[2,64,1024]{2,1,0:T(8,128)(2,1)S(1)} %pad_maximum_fusion.2.near_ref, bf16[2,64,1024]{2,1,0:T(8,128)(2,1)S(1)} %collective-permute-done.20.far_ref, bf16[4,4,1024]{2,1,0:T(4,128)(2,1)S(1)} %bitcast.65, ...), custom_call_target="tpu_custom_call" | custom-call | tf_op jit(solution)/shard_map/last_step/pallas_call | solution.py:495
  (35 shorter events, 0.4 us)
Async XLA Ops:
  0.6 0.9 %copy-start = (bf16[1,8,32,256]{3,2,1,0:T(8,128)(2,1)S(1)}, bf16[1,8,32,256]{3,2,1,0:T(8,128)(2,1)}, u32[]{:S(2)}) copy-start(bf16[1,8,32,256]{3,2,1,0:T(8,128)(2,1)} %param.13) | copy-start | bytes 393220
  1.5 0.9 %copy-start.2 = (bf16[1,8,32,256]{3,2,1,0:T(8,128)(2,1)S(1)}, bf16[1,8,32,256]{3,2,1,0:T(8,128)(2,1)}, u32[]{:S(2)}) copy-start(bf16[1,8,32,256]{3,2,1,0:T(8,128)(2,1)} %param.14) | copy-start | bytes 393220
  2.4 4.5 %copy-start.8 = (bf16[1,4,4,1024]{3,2,1,0:T(4,128)(2,1)S(1)}, bf16[1,4,4,1024]{3,2,1,0:T(4,128)(2,1)}, u32[]{:S(2)}) copy-start(bf16[1,4,4,1024]{3,2,1,0:T(4,128)(2,1)} %param.15) | copy-start | bytes 98308
  2.4 4.5 %copy-start.9 = (bf16[1,4,4,1024]{3,2,1,0:T(4,128)(2,1)S(1)}, bf16[1,4,4,1024]{3,2,1,0:T(4,128)(2,1)}, u32[]{:S(2)}) copy-start(bf16[1,4,4,1024]{3,2,1,0:T(4,128)(2,1)} %param.16) | copy-start | bytes 98308
  2.5 4.5 %copy-start.13 = (f32[1,256]{1,0:T(1,128)S(1)}, f32[1,256]{1,0:T(1,128)}, u32[]{:S(2)}) copy-start(f32[1,256]{1,0:T(1,128)} %constant.4.clone.fine_freq) | copy-start | bytes 3076
  2.5 11.1 %collective-permute-start = (bf16[9,32,256]{2,1,0:T(8,128)(2,1)S(1)}, bf16[9,32,256]{2,1,0:T(8,128)(2,1)S(1)}, u32[]{:S(2)}, u32[]{:S(2)}) collective-permute-start(bf16[9,32,256]{2,1,0:T(8,128)(2,1)S(1)} %get-tuple-element.43.first), channel_id=1, source_target_pairs={{0,4},{4,0},{8,12},{12,8},{1,5},{5,1},{9,13},{13,9},{2,6},{6,2},{1... | collective-permute-start | bytes 442376 | tf_op jit(solution)/shard_map/ppermute | solution.py:515
  5.6 8.0 %collective-permute-start.1 = (bf16[9,32,256]{2,1,0:T(8,128)(2,1)S(1)}, bf16[9,32,256]{2,1,0:T(8,128)(2,1)S(1)}, u32[]{:S(2)}, u32[]{:S(2)}) collective-permute-start(bf16[9,32,256]{2,1,0:T(8,128)(2,1)S(1)} %get-tuple-element.44.second), channel_id=1, source_target_pairs={{4,8},{8,4},{5,9},{9,5},{6,10},{10,6},{7,11},{11,7},{20,24},{24,20... | collective-permute-start | bytes 442376 | tf_op jit(solution)/shard_map/ppermute | solution.py:514
  6.2 0.7 %copy-start.11 = (f32[1,1024]{1,0:T(1,128)S(1)}, f32[1,1024]{1,0:T(1,128)}, u32[]{:S(2)}) copy-start(f32[1,1024]{1,0:T(1,128)} %constant.5.clone.coarse_freq) | copy-start | bytes 12292
  6.9 0.7 copy-start.10
  6.9 0.7 copy-start.12
  7.6 6.0 %copy-start.1 = (bf16[1,8,32,256]{3,2,1,0:T(8,128)(2,1)S(1)}, bf16[1,8,32,256]{3,2,1,0:T(8,128)(2,1)}, u32[]{:S(2)}) copy-start(bf16[1,8,32,256]{3,2,1,0:T(8,128)(2,1)} %param.13) | copy-start | bytes 393220
  7.6 6.0 %copy-start.3 = (bf16[1,8,32,256]{3,2,1,0:T(8,128)(2,1)S(1)}, bf16[1,8,32,256]{3,2,1,0:T(8,128)(2,1)}, u32[]{:S(2)}) copy-start(bf16[1,8,32,256]{3,2,1,0:T(8,128)(2,1)} %param.14) | copy-start | bytes 393220
  7.7 6.9 %collective-permute-start.6 = (bf16[16,2048]{1,0:T(8,128)(2,1)S(1)}, bf16[16,2048]{1,0:T(8,128)(2,1)S(1)}, u32[]{:S(2)}, u32[]{:S(2)}) collective-permute-start(bf16[16,2048]{1,0:T(8,128)(2,1)S(1)} %get-tuple-element.47), channel_id=1, source_target_pairs={{0,12},{4,8},{8,4},{12,0},{1,13},{5,9},{9,5},{13,1},{2,14},{6,10},... | collective-permute-start | bytes 196616 | tf_op jit(solution)/shard_map/ppermute | solution.py:519
  10.2 9.0 %collective-permute-start.5 = (bf16[16,2048]{1,0:T(8,128)(2,1)S(1)}, bf16[16,2048]{1,0:T(8,128)(2,1)S(1)}, u32[]{:S(2)}, u32[]{:S(2)}) collective-permute-start(bf16[16,2048]{1,0:T(8,128)(2,1)S(1)} %get-tuple-element.47), channel_id=1, source_target_pairs={{0,8},{4,12},{8,0},{12,4},{1,9},{5,13},{9,1},{13,5},{2,10},{6,14},... | collective-permute-start | bytes 196616 | tf_op jit(solution)/shard_map/ppermute | solution.py:519
  13.6 5.6 %collective-permute-start.4 = (bf16[16,2048]{1,0:T(8,128)(2,1)S(1)}, bf16[16,2048]{1,0:T(8,128)(2,1)S(1)}, u32[]{:S(2)}, u32[]{:S(2)}) collective-permute-start(bf16[16,2048]{1,0:T(8,128)(2,1)S(1)} %get-tuple-element.47), channel_id=1, source_target_pairs={{0,4},{4,0},{8,12},{12,8},{1,5},{5,1},{9,13},{13,9},{2,6},{6,2},{1... | collective-permute-start | bytes 196616 | tf_op jit(solution)/shard_map/ppermute | solution.py:519
  13.7 8.1 %copy-start.4 = (bf16[256,768]{1,0:T(8,128)(2,1)S(1)}, bf16[256,768]{1,0:T(8,128)(2,1)}, u32[]{:S(2)}) copy-start(bf16[256,768]{1,0:T(8,128)(2,1)} %qkv_ref.1) | copy-start | bytes 1179652
  13.7 5.6 %collective-permute-start.2 = (bf16[34,8,256]{2,1,0:T(8,128)(2,1)S(1)}, bf16[34,8,256]{2,1,0:T(8,128)(2,1)S(1)}, u32[]{:S(2)}, u32[]{:S(2)}) collective-permute-start(bf16[34,8,256]{2,1,0:T(8,128)(2,1)S(1)} %get-tuple-element.45), channel_id=1, source_target_pairs={{0,1},{1,0},{2,3},{3,2},{4,5},{5,4},{6,7},{7,6},{8,9},{9,8},{10,11... | collective-permute-start | bytes 417800 | tf_op jit(solution)/shard_map/ppermute | solution.py:515
  13.8 5.5 %collective-permute-start.3 = (bf16[34,8,256]{2,1,0:T(8,128)(2,1)S(1)}, bf16[34,8,256]{2,1,0:T(8,128)(2,1)S(1)}, u32[]{:S(2)}, u32[]{:S(2)}) collective-permute-start(bf16[34,8,256]{2,1,0:T(8,128)(2,1)S(1)} %get-tuple-element.46), channel_id=1, source_target_pairs={{1,2},{2,1},{5,6},{6,5},{9,10},{10,9},{13,14},{14,13},{17,18},{18,... | collective-permute-start | bytes 417800 | tf_op jit(solution)/shard_map/ppermute | solution.py:514
  19.2 2.6 %copy-start.6 = (bf16[256,256]{1,0:T(8,128)(2,1)S(1)}, bf16[256,256]{1,0:T(8,128)(2,1)}, u32[]{:S(2)}) copy-start(bf16[256,256]{1,0:T(8,128)(2,1)} %out_ref.1) | copy-start | bytes 393220
  19.3 9.6 %collective-permute-start.8 = (bf16[4,16,2048]{2,1,0:T(8,128)(2,1)S(1)}, bf16[4,16,2048]{2,1,0:T(8,128)(2,1)S(1)}, u32[]{:S(2)}, u32[]{:S(2)}) collective-permute-start(bf16[4,16,2048]{2,1,0:T(8,128)(2,1)S(1)} %pad_maximum_fusion.1), channel_id=1, source_target_pairs={{0,2},{1,3},{2,0},{3,1},{4,6},{5,7},{6,4},{7,5},{8,10},{9,11},{10,... | collective-permute-start | bytes 786440 | tf_op jit(solution)/shard_map/ppermute | solution.py:519
  28.0 1.5 %collective-permute-start.7 = (bf16[2,4,16,1024]{3,2,1,0:T(8,128)(2,1)S(1)}, bf16[2,4,16,1024]{3,2,1,0:T(8,128)(2,1)S(1)}, u32[]{:S(2)}, u32[]{:S(2)}) collective-permute-start(bf16[2,4,16,1024]{3,2,1,0:T(8,128)(2,1)S(1)} %get-tuple-element.53), channel_id=1, source_target_pairs={{0,1},{1,0},{2,3},{3,2},{4,5},{5,4},{6,7},{7,6},{8,9},{9,8},{10,11... | collective-permute-start | bytes 786440 | tf_op jit(solution)/shard_map/ppermute | solution.py:519
  28.9 1.5 %collective-permute-start.9 = (bf16[4,16,2048]{2,1,0:T(8,128)(2,1)S(1)}, bf16[4,16,2048]{2,1,0:T(8,128)(2,1)S(1)}, u32[]{:S(2)}, u32[]{:S(2)}) collective-permute-start(bf16[4,16,2048]{2,1,0:T(8,128)(2,1)S(1)} %collective-permute-done.8), channel_id=1, source_target_pairs={{0,1},{1,0},{2,3},{3,2},{4,5},{5,4},{6,7},{7,6},{8,9},{9,8},{10,11... | collective-permute-start | bytes 786440 | tf_op jit(solution)/shard_map/ppermute | solution.py:519
  28.9 1.9 %collective-permute-start.11 = (bf16[4,16,2048]{2,1,0:T(8,128)(2,1)S(1)}, bf16[4,16,2048]{2,1,0:T(8,128)(2,1)S(1)}, u32[]{:S(2)}, u32[]{:S(2)}) collective-permute-start(bf16[4,16,2048]{2,1,0:T(8,128)(2,1)S(1)} %pad_maximum_fusion.1), channel_id=1, source_target_pairs={{0,1},{1,0},{2,3},{3,2},{4,5},{5,4},{6,7},{7,6},{8,9},{9,8},{10,11... | collective-permute-start | bytes 786440 | tf_op jit(solution)/shard_map/ppermute | solution.py:519
  30.4 5.6 %collective-permute-start.10 = (bf16[4,16,1024]{2,1,0:T(8,128)(2,1)S(1)}, bf16[4,16,1024]{2,1,0:T(8,128)(2,1)S(1)}, u32[]{:S(2)}, u32[]{:S(2)}) collective-permute-start(bf16[4,16,1024]{2,1,0:T(8,128)(2,1)S(1)} %fusion.2), channel_id=1, source_target_pairs={{0,2},{1,3},{2,0},{3,1},{4,6},{5,7},{6,4},{7,5},{8,10},{9,11},{10,... | collective-permute-start | bytes 393224 | tf_op jit(solution)/shard_map/ppermute | solution.py:519
  30.9 1.0 %copy-start.5 = (bf16[3,64,1024]{2,1,0:T(8,128)(2,1)S(1)}, bf16[3,64,1024]{2,1,0:T(8,128)(2,1)}, u32[]{:S(2)}) copy-start(bf16[3,64,1024]{2,1,0:T(8,128)(2,1)} %qkv_hbm.1) | copy-start | bytes 1179652
  30.9 1.0 %copy-start.7 = (bf16[64,1024]{1,0:T(8,128)(2,1)S(1)}, bf16[64,1024]{1,0:T(8,128)(2,1)}, u32[]{:S(2)}) copy-start(bf16[64,1024]{1,0:T(8,128)(2,1)} %out_hbm.1) | copy-start | bytes 393220
  36.1 1.7 %collective-permute-start.13 = (bf16[2,4,16,1024]{3,2,1,0:T(8,128)(2,1)S(1)}, bf16[2,4,16,1024]{3,2,1,0:T(8,128)(2,1)S(1)}, u32[]{:S(2)}, u32[]{:S(2)}) collective-permute-start(bf16[2,4,16,1024]{3,2,1,0:T(8,128)(2,1)S(1)} %bitcast.82), channel_id=1, source_target_pairs={{0,1},{1,0},{2,3},{3,2},{4,5},{5,4},{6,7},{7,6},{8,9},{9,8},{10,11... | collective-permute-start | bytes 786440 | tf_op jit(solution)/shard_map/ppermute | solution.py:519
  36.2 5.9 %collective-permute-start.12 = (bf16[4,16,1024]{2,1,0:T(8,128)(2,1)S(1)}, bf16[4,16,1024]{2,1,0:T(8,128)(2,1)S(1)}, u32[]{:S(2)}, u32[]{:S(2)}) collective-permute-start(bf16[4,16,1024]{2,1,0:T(8,128)(2,1)S(1)} %fusion.1), channel_id=1, source_target_pairs={{0,16},{16,0},{1,17},{17,1},{2,18},{18,2},{3,19},{19,3},{4,20},{20... | collective-permute-start | bytes 393224 | tf_op jit(solution)/shard_map/ppermute | solution.py:519
  37.9 5.6 %collective-permute-start.14 = (bf16[4,16,1024]{2,1,0:T(8,128)(2,1)S(1)}, bf16[4,16,1024]{2,1,0:T(8,128)(2,1)S(1)}, u32[]{:S(2)}, u32[]{:S(2)}) collective-permute-start(bf16[4,16,1024]{2,1,0:T(8,128)(2,1)S(1)} %fusion.3), channel_id=1, source_target_pairs={{0,2},{1,3},{2,0},{3,1},{4,6},{5,7},{6,4},{7,5},{8,10},{9,11},{10,... | collective-permute-start | bytes 393224 | tf_op jit(solution)/shard_map/ppermute | solution.py:519
  43.6 8.9 %collective-permute-start.15 = (bf16[96,1024]{1,0:T(8,128)(2,1)S(1)}, bf16[96,1024]{1,0:T(8,128)(2,1)S(1)}, u32[]{:S(2)}, u32[]{:S(2)}) collective-permute-start(bf16[96,1024]{1,0:T(8,128)(2,1)S(1)} %pad_maximum_fusion.3), channel_id=1, source_target_pairs={{0,4},{4,0},{8,12},{12,8},{1,5},{5,1},{9,13},{13,9},{2,6},{6,2},{1... | collective-permute-start | bytes 589832 | tf_op jit(solution)/shard_map/ppermute | solution.py:519
  48.1 7.3 %collective-permute-start.16 = (bf16[128,1024]{1,0:T(8,128)(2,1)S(1)}, bf16[128,1024]{1,0:T(8,128)(2,1)S(1)}, u32[]{:S(2)}, u32[]{:S(2)}) collective-permute-start(bf16[128,1024]{1,0:T(8,128)(2,1)S(1)} %get-tuple-element.83), channel_id=1, source_target_pairs={{0,16},{16,0},{1,17},{17,1},{2,18},{18,2},{3,19},{19,3},{4,20},{20... | collective-permute-start | bytes 786440 | tf_op jit(solution)/shard_map/ppermute | solution.py:519
  55.5 8.7 %collective-permute-start.17 = (bf16[80,1024]{1,0:T(8,128)(2,1)S(1)}, bf16[80,1024]{1,0:T(8,128)(2,1)S(1)}, u32[]{:S(2)}, u32[]{:S(2)}) collective-permute-start(bf16[80,1024]{1,0:T(8,128)(2,1)S(1)} %pad_maximum_fusion.4), channel_id=1, source_target_pairs={{0,8},{4,12},{8,0},{12,4},{1,9},{5,13},{9,1},{13,5},{2,10},{6,14},... | collective-permute-start | bytes 491528 | tf_op jit(solution)/shard_map/ppermute | solution.py:519
  57.2 7.1 %collective-permute-start.18 = (bf16[128,1024]{1,0:T(8,128)(2,1)S(1)}, bf16[128,1024]{1,0:T(8,128)(2,1)S(1)}, u32[]{:S(2)}, u32[]{:S(2)}) collective-permute-start(bf16[128,1024]{1,0:T(8,128)(2,1)S(1)} %get-tuple-element.82), channel_id=1, source_target_pairs={{0,16},{16,0},{1,17},{17,1},{2,18},{18,2},{3,19},{19,3},{4,20},{20... | collective-permute-start | bytes 786440 | tf_op jit(solution)/shard_map/ppermute | solution.py:519
  64.3 5.0 %collective-permute-start.19 = (bf16[64,1024]{1,0:T(8,128)(2,1)S(1)}, bf16[64,1024]{1,0:T(8,128)(2,1)S(1)}, u32[]{:S(2)}, u32[]{:S(2)}) collective-permute-start(bf16[64,1024]{1,0:T(8,128)(2,1)S(1)} %add_convert_fusion), channel_id=1, source_target_pairs={{0,2},{1,3},{2,0},{3,1},{4,6},{5,7},{6,4},{7,5},{8,10},{9,11},{10,... | collective-permute-start | bytes 393224 | tf_op jit(solution)/shard_map/ppermute | solution.py:519
  69.3 1.6 %collective-permute-start.20 = (bf16[2,64,1024]{2,1,0:T(8,128)(2,1)S(1)}, bf16[2,64,1024]{2,1,0:T(8,128)(2,1)S(1)}, u32[]{:S(2)}, u32[]{:S(2)}) collective-permute-start(bf16[2,64,1024]{2,1,0:T(8,128)(2,1)S(1)} %pad_maximum_fusion.2.near_ref), channel_id=1, source_target_pairs={{0,1},{1,0},{2,3},{3,2},{4,5},{5,4},{6,7},{7,6},{8,9},{9,8},{10,11... | collective-permute-start | bytes 786440 | tf_op jit(solution)/shard_map/ppermute | solution.py:519

commit v5 on v4

--- a/solution.py
+++ b/solution.py
@@ -460,7 +460,8 @@
     far_ref,
     x_ref,
     factor_ref,
-    upstream_ref,
+    kept_ref,
+    come_ref,
     qkv_hbm,
     out_hbm,
     dx_ref,
@@ -483,13 +484,14 @@
     for copy in copies:
         copy.start()
     tokens = x_ref[...].astype(jnp.float32).reshape(-1, D_C)
-    grads = norm_backward(tokens, inverse_rms(tokens), factor_ref[...], upstream_ref[...])
+    upstream = kept_ref[...] + come_ref[...].astype(jnp.float32)
+    grads = norm_backward(tokens, inverse_rms(tokens), factor_ref[...], upstream)
     dx_ref[...] = grads.astype(jnp.float32).reshape(dx_ref.shape).astype(jnp.bfloat16)
     for copy in copies:
         copy.wait()
 
 
-def last_step(near, far, tokens, factor, upstream):
+def last_step(near, far, tokens, factor, kept, come):
     vmem = pl.BlockSpec(memory_space=pltpu.VMEM)
     hbm = pl.BlockSpec(memory_space=pltpu.HBM)
     return pl.pallas_call(
@@ -499,12 +501,12 @@
             jax.ShapeDtypeStruct((D_F, D_F), jnp.bfloat16),
             jax.ShapeDtypeStruct(tokens.shape, jnp.bfloat16),
         ),
-        in_specs=[vmem] * 5,
+        in_specs=[vmem] * 6,
         out_specs=(hbm, hbm, vmem),
         scratch_shapes=[pltpu.SemaphoreType.DMA((2, near.shape[0], 2))],
         compiler_params=pltpu.CompilerParams(vmem_limit_bytes=vmem_bytes),
         name="last_step",
-    )(near, far, tokens, factor, upstream)
+    )(near, far, tokens, factor, kept, come)
 
 
 def neighbours(to_near, to_far, axis):
@@ -564,11 +566,14 @@
     own, factor, coarse_factor = packed(
         payloads, timestep, x_coarse[0], dy_coarse[0], fine_gain, coarse_gain
     )
+    row_near, own, factor, coarse_factor = tied(row_near, own, factor, coarse_factor)
     count = own.shape[0]
-    row_group = all_rows(own)
     edges = col_edges(picture, cotangent, row_near, row_far)
     col_near, col_far = neighbours(*edges, "gx")
-    col_near, col_far, row_group = tied(col_near, col_far, row_group)
+    col_near, own = tied(col_near, own)
+    pieces = [own] + [swapped(own, "gy", row) for row in range(1, downs)]
+    col_near, col_far, *pieces = tied(col_near, col_far, *pieces)
+    row_group = jnp.stack(pieces)
     cross = swapped(row_group, "gx", 2)
     beside = swapped(row_group, "gx", 1)
     dx_picture, fine_keep, fine_send = fine_block(
@@ -598,7 +603,6 @@
     fine_quarter = narrow(batch_sum(fine_quarter)).reshape(rows, 4 * D_F)
     parts = parts.reshape(2, 2, downs, count, D_C)
     coarse_kept = wide(parts[0]) + wide(swapped(parts[1], "gx", 1))
-    coarse_kept = coarse_kept[0] + wide(swapped(narrow(coarse_kept[1]), "gx", 2))
     fine_quarter, coarse_kept, coarse_partial = tied(fine_quarter, coarse_kept, coarse_partial)
 
     pair_batch = lax.axis_size("batch") == 2
@@ -607,17 +611,18 @@
     mask = 1
     while mask < downs:
         last = 2 * mask == downs
-        coarse_kept = coarse_kept.reshape(-1, 2, count, D_C)
-        sent = narrow(coarse_kept[:, 1]).reshape(-1, D_C)
+        coarse_kept = coarse_kept.reshape(2, -1, 2, count, D_C)
+        sent = narrow(coarse_kept[:, :, 1]).reshape(-1, D_C)
         come = swapped(jnp.concatenate([fine_quarter, sent], axis=0), "gy", mask)
-        coarse_kept = coarse_kept[:, 0]
+        coarse_kept = coarse_kept[:, :, 0]
         coarse_kept = coarse_kept + wide(come[rows:]).reshape(coarse_kept.shape)
         fine_quarter = narrow(wide(fine_quarter) + wide(come[:rows]))
         at = int(last)
         fine_quarter, coarse_kept, others[at] = tied(fine_quarter, coarse_kept, others[at])
         mask *= 2
 
-    come = swapped(fine_quarter, "gx", 2)
+    coarse_kept = coarse_kept.reshape(2, count, D_C)
+    come = swapped(jnp.concatenate([fine_quarter, narrow(coarse_kept[1])], axis=0), "gx", 2)
     if pair_batch:
         grad_coarse_qkv, grad_coarse_out = pair_sum(coarse_partial, *others)
     else:
@@ -625,13 +630,14 @@
         grad_coarse_qkv = coarse_sum[: 3 * HD].reshape(coarse_qkv.shape)
         grad_coarse_out = coarse_sum[3 * HD :]
     come, grad_coarse_qkv, grad_coarse_out = tied(come, grad_coarse_qkv, grad_coarse_out)
-    fine_pair = jnp.stack([fine_quarter, come])
+    fine_pair = jnp.stack([fine_quarter, come[:rows]])
     grad_qkv, grad_out, dx_coarse = last_step(
         fine_pair,
         swapped(fine_pair, "gx", 1),
         x_coarse[0],
         coarse_factor,
-        coarse_kept.reshape(count, D_C),
+        coarse_kept[0],
+        come[rows:],
     )
     return (
         dx_picture[None],

time: 72.7 us -> 71.4 us (0.982)
  starting transfers between devices: 25.4 us -> 23.8 us
    ppermute x2, waiting for transfers between devices: 0.01 us -> 2.41 us  [neighbours(): return (lax.ppermute(to_near, axis, near), from_far)]
    ppermute x17 -> x16, waiting for transfers between devices: 30.3 us -> 28.1 us  [swapped(): lax.ppermute(value, axis, [(i, i ^ mask) for i in range(lax.axis_size(axi...]
    ppermute x17 -> x16, starting transfers between devices: 20.8 us -> 19.3 us  [swapped(): lax.ppermute(value, axis, [(i, i ^ mask) for i in range(lax.axis_size(axi...]
  transfers between devices with their start and end apart: 21 -> 20, of which waited for: 12 -> 14; matrix products, arithmetic and copies ran while one was open for 1% -> 1% of each run, Pallas kernels for 13% -> 13%
where the time goes in v5:
time: 71.4 us; the launch traced here: 71.1 us
  waiting for transfers between devices  30.5 us (43%)
  starting transfers between devices  23.8 us (33%)
  Pallas kernels  10.9 us (15%)
  local copies, waits for them, and re-layouts  3.63 us (5%)
  between operations  1.63 us (2%)
    ppermute x16, waiting for transfers between devices, swapped(): lax.ppermute(value, axis, [(i, i ^ mask) for i in range(lax.axis_size(axi...  28.1 us
    ppermute x16, starting transfers between devices, swapped(): lax.ppermute(value, axis, [(i, i ^ mask) for i in range(lax.axis_size(axi...  19.3 us
    pallas_call x1, Pallas kernels, fine_block(): pl.pallas_call(fine_body, out_shape=(jax.ShapeDtypeStruct((height, breadt...  6.17 us
    unnamed x28, local copies, waits for them, and re-layouts  3.4 us
    ppermute x2, starting transfers between devices, neighbours(): return (lax.ppermute(to_near, axis, near), from_far)  3.16 us
    ppermute x2, waiting for transfers between devices, neighbours(): return (lax.ppermute(to_near, axis, near), from_far)  2.41 us
    pallas_call x1, Pallas kernels, coarse_block(): pl.pallas_call(coarse_body, out_shape=(jax.ShapeDtypeStruct((count, D_C),...  2.23 us
    pallas_call x1, Pallas kernels, last_step(): pl.pallas_call(last_body, out_shape=(jax.ShapeDtypeStruct((D_F, 3 * D_F),...  1.48 us
  transfers between devices with their start and end apart: 20, of which 14 were waited for; matrix products, arithmetic and copies ran while one was open for 1% of the time, Pallas kernels for 13%

profile of v5, /device:TPU:0, one launch (start us, length us, event | category | flops | bytes accessed | tf_op | source)
XLA Modules:
  0.0 71.1 jit_solution(9444233497208841767)
XLA Ops:
  0.6 0.0 copy-start
  0.6 0.9 %copy-done = bf16[1,8,32,256]{3,2,1,0:T(8,128)(2,1)S(1)} copy-done((bf16[1,8,32,256]{3,2,1,0:T(8,128)(2,1)S(1)}, bf16[1,8,32,256]{3,2,1,0:T(8,128)(2,1)}, u32[]{:S(2)}) %copy-start) | copy-done | bytes 131096
  1.5 0.9 %copy-done.2 = bf16[1,8,32,256]{3,2,1,0:T(8,128)(2,1)S(1)} copy-done((bf16[1,8,32,256]{3,2,1,0:T(8,128)(2,1)S(1)}, bf16[1,8,32,256]{3,2,1,0:T(8,128)(2,1)}, u32[]{:S(2)}) %copy-start.2) | copy-done | bytes 131096
  2.5 0.0 copy-start.13
  2.5 3.1 %collective-permute-start = (bf16[9,32,256]{2,1,0:T(8,128)(2,1)S(1)}, bf16[9,32,256]{2,1,0:T(8,128)(2,1)S(1)}, u32[]{:S(2)}, u32[]{:S(2)}) collective-permute-start(bf16[9,32,256]{2,1,0:T(8,128)(2,1)S(1)} %get-tuple-element.52.first), channel_id=1, source_target_pairs={{0,4},{4,0},{8,12},{12,8},{1,5},{5,1},{9,13},{13,9},{2,6},{6,2},{1... | collective-permute-start | bytes 442376 | tf_op jit(solution)/shard_map/ppermute | solution.py:517
  5.6 0.7 collective-permute-start.1
  6.2 0.0 copy-start.11
  6.9 0.0 copy-start.10
  6.9 0.0 copy-start.12
  7.0 0.6 copy-done.10
  7.6 0.0 copy-done.12
  7.6 0.1 pack_coarse.1
  7.7 1.7 %collective-permute-done.row_near_ref = bf16[9,32,256]{2,1,0:T(8,128)(2,1)S(1)} collective-permute-done((bf16[9,32,256]{2,1,0:T(8,128)(2,1)S(1)}, bf16[9,32,256]{2,1,0:T(8,128)(2,1)S(1)}, u32[]{:S(2)}, u32[]{:S(2)}) %collective-permute-start) | collective-permute-done | bytes 147488 | tf_op jit(solution)/shard_map/ppermute | solution.py:517
  9.4 0.0 collective-permute-done.1.row_far_ref
  9.4 0.0 copy-done.3
  9.4 0.1 col_edges.1
  9.5 0.1 collective-permute-start.2
  9.6 0.7 collective-permute-start.3
  10.3 0.7 collective-permute-done.2.col_near_ref
  10.9 4.8 %collective-permute-start.4 = (bf16[16,2048]{1,0:T(8,128)(2,1)S(1)}, bf16[16,2048]{1,0:T(8,128)(2,1)S(1)}, u32[]{:S(2)}, u32[]{:S(2)}) collective-permute-start(bf16[16,2048]{1,0:T(8,128)(2,1)S(1)} %get-tuple-element.69), channel_id=1, source_target_pairs={{0,4},{4,0},{8,12},{12,8},{1,5},{5,1},{9,13},{13,9},{2,6},{6,2},{1... | collective-permute-start | bytes 196616 | tf_op jit(solution)/shard_map/ppermute | solution.py:521
  15.7 1.2 %collective-permute-start.5 = (bf16[16,2048]{1,0:T(8,128)(2,1)S(1)}, bf16[16,2048]{1,0:T(8,128)(2,1)S(1)}, u32[]{:S(2)}, u32[]{:S(2)}) collective-permute-start(bf16[16,2048]{1,0:T(8,128)(2,1)S(1)} %get-tuple-element.69), channel_id=1, source_target_pairs={{0,8},{4,12},{8,0},{12,4},{1,9},{5,13},{9,1},{13,5},{2,10},{6,14},... | collective-permute-start | bytes 196616 | tf_op jit(solution)/shard_map/ppermute | solution.py:521
  16.9 1.5 %collective-permute-start.6 = (bf16[16,2048]{1,0:T(8,128)(2,1)S(1)}, bf16[16,2048]{1,0:T(8,128)(2,1)S(1)}, u32[]{:S(2)}, u32[]{:S(2)}) collective-permute-start(bf16[16,2048]{1,0:T(8,128)(2,1)S(1)} %get-tuple-element.69), channel_id=1, source_target_pairs={{0,12},{4,8},{8,4},{12,0},{1,13},{5,9},{9,5},{13,1},{2,14},{6,10},... | collective-permute-start | bytes 196616 | tf_op jit(solution)/shard_map/ppermute | solution.py:521
  18.3 0.0 collective-permute-done.3.col_far_ref
  18.3 0.0 collective-permute-done.4
  18.3 3.4 %collective-permute-done.5 = bf16[16,2048]{1,0:T(8,128)(2,1)S(1)} collective-permute-done((bf16[16,2048]{1,0:T(8,128)(2,1)S(1)}, bf16[16,2048]{1,0:T(8,128)(2,1)S(1)}, u32[]{:S(2)}, u32[]{:S(2)}) %collective-permute-start.5) | collective-permute-done | bytes 65568 | tf_op jit(solution)/shard_map/ppermute | solution.py:521
  21.8 1.8 %collective-permute-done.6 = bf16[16,2048]{1,0:T(8,128)(2,1)S(1)} collective-permute-done((bf16[16,2048]{1,0:T(8,128)(2,1)S(1)}, bf16[16,2048]{1,0:T(8,128)(2,1)S(1)}, u32[]{:S(2)}, u32[]{:S(2)}) %collective-permute-start.6) | collective-permute-done | bytes 65568 | tf_op jit(solution)/shard_map/ppermute | solution.py:521
  23.6 2.3 %collective-permute-start.8 = (bf16[4,16,2048]{2,1,0:T(8,128)(2,1)S(1)}, bf16[4,16,2048]{2,1,0:T(8,128)(2,1)S(1)}, u32[]{:S(2)}, u32[]{:S(2)}) collective-permute-start(bf16[4,16,2048]{2,1,0:T(8,128)(2,1)S(1)} %get-tuple-element.105), channel_id=1, source_target_pairs={{0,2},{1,3},{2,0},{3,1},{4,6},{5,7},{6,4},{7,5},{8,10},{9,11},{10,... | collective-permute-start | bytes 786440 | tf_op jit(solution)/shard_map/ppermute | solution.py:521
  26.0 6.2 %fine_block.1 = (bf16[8,32,256]{2,1,0:T(8,128)(2,1)}, f32[2,4,16,1024]{3,2,1,0:T(8,128)S(1)}, bf16[2,4,16,1024]{3,2,1,0:T(8,128)(2,1)S(1)}) custom-call(bf16[8,32,256]{2,1,0:T(8,128)(2,1)S(1)} %bitcast.53, bf16[8,32,256]{2,1,0:T(8,128)(2,1)S(1)} %bitcast.56, bf16[9,32,256]{2,1,0:T(8,128)(2,1)S(1)} %collective-permute-done.row_near_ref, ...), custom_call_target="tpu_custom_call" | custom-call | tf_op jit(solution)/shard_map/fine_block/pallas_call | solution.py:233
  32.1 0.0 collective-permute-start.7
  32.1 0.8 %collective-permute-done.8 = bf16[4,16,2048]{2,1,0:T(8,128)(2,1)S(1)} collective-permute-done((bf16[4,16,2048]{2,1,0:T(8,128)(2,1)S(1)}, bf16[4,16,2048]{2,1,0:T(8,128)(2,1)S(1)}, u32[]{:S(2)}, u32[]{:S(2)}) %collective-permute-start.8) | collective-permute-done | bytes 262176 | tf_op jit(solution)/shard_map/ppermute | solution.py:521
  32.9 0.0 collective-permute-start.9
  32.9 0.5 collective-permute-start.11
  33.4 0.2 collective-permute-done.7
  33.7 0.1 convert_add_fusion.1
  33.7 0.7 collective-permute-done.9
  34.5 0.6 collective-permute-start.10
  35.0 0.0 collective-permute-done.11
  35.0 0.1 pad_maximum_fusion
  35.2 0.0 copy-start.5
  35.2 0.0 copy-start.7
  35.2 0.1 fusion.6
  35.3 0.9 %copy-done.5 = bf16[3,64,1024]{2,1,0:T(8,128)(2,1)S(1)} copy-done((bf16[3,64,1024]{2,1,0:T(8,128)(2,1)S(1)}, bf16[3,64,1024]{2,1,0:T(8,128)(2,1)}, u32[]{:S(2)}) %copy-start.5) | copy-done | bytes 393240
  36.2 0.0 copy-done.7
  36.2 2.2 %coarse_block.1 = (bf16[256,1024]{1,0:T(8,128)(2,1)S(1)}, bf16[256,1024]{1,0:T(8,128)(2,1)S(1)}) custom-call(bf16[256,1024]{1,0:T(8,128)(2,1)S(1)} %get-tuple-element.99.x_ref, bf16[256,1024]{1,0:T(8,128)(2,1)S(1)} %get-tuple-element.98.dy_ref, f32[1,1024]{1,0:T(1,128)S(1)} %get-tuple-element.75.factor_ref, bf16[3,64,1024]{2,1,0:T(8,128)(2,1)S(1)} %copy-done.5, ...), custom_call_target="tpu_custom_call" | custom-call | tf_op jit(solution)/shard_map/coarse_block/pallas_call | solution.py:309
  38.4 1.6 %collective-permute-done.10 = bf16[4,16,1024]{2,1,0:T(8,128)(2,1)S(1)} collective-permute-done((bf16[4,16,1024]{2,1,0:T(8,128)(2,1)S(1)}, bf16[4,16,1024]{2,1,0:T(8,128)(2,1)S(1)}, u32[]{:S(2)}, u32[]{:S(2)}) %collective-permute-start.10) | collective-permute-done | bytes 131104 | tf_op jit(solution)/shard_map/ppermute | solution.py:521
  40.1 1.6 %collective-permute-start.12 = (bf16[4,16,1024]{2,1,0:T(8,128)(2,1)S(1)}, bf16[4,16,1024]{2,1,0:T(8,128)(2,1)S(1)}, u32[]{:S(2)}, u32[]{:S(2)}) collective-permute-start(bf16[4,16,1024]{2,1,0:T(8,128)(2,1)S(1)} %fusion.1), channel_id=1, source_target_pairs={{0,16},{16,0},{1,17},{17,1},{2,18},{18,2},{3,19},{19,3},{4,20},{20... | collective-permute-start | bytes 393224 | tf_op jit(solution)/shard_map/ppermute | solution.py:521
  41.7 0.1 collective-permute-start.13
  41.8 3.3 %collective-permute-done.12 = bf16[4,16,1024]{2,1,0:T(8,128)(2,1)S(1)} collective-permute-done((bf16[4,16,1024]{2,1,0:T(8,128)(2,1)S(1)}, bf16[4,16,1024]{2,1,0:T(8,128)(2,1)S(1)}, u32[]{:S(2)}, u32[]{:S(2)}) %collective-permute-start.12) | collective-permute-done | bytes 131104 | tf_op jit(solution)/shard_map/ppermute | solution.py:521
  45.2 0.0 collective-permute-done.13
  45.2 0.1 convert_add_fusion
  45.3 1.7 %collective-permute-start.14 = (bf16[128,1024]{1,0:T(8,128)(2,1)S(1)}, bf16[128,1024]{1,0:T(8,128)(2,1)S(1)}, u32[]{:S(2)}, u32[]{:S(2)}) collective-permute-start(bf16[128,1024]{1,0:T(8,128)(2,1)S(1)} %pad_maximum_fusion.2), channel_id=1, source_target_pairs={{0,4},{4,0},{8,12},{12,8},{1,5},{5,1},{9,13},{13,9},{2,6},{6,2},{1... | collective-permute-start | bytes 786440 | tf_op jit(solution)/shard_map/ppermute | solution.py:521
  47.0 1.6 %collective-permute-start.15 = (bf16[128,1024]{1,0:T(8,128)(2,1)S(1)}, bf16[128,1024]{1,0:T(8,128)(2,1)S(1)}, u32[]{:S(2)}, u32[]{:S(2)}) collective-permute-start(bf16[128,1024]{1,0:T(8,128)(2,1)S(1)} %get-tuple-element.101), channel_id=1, source_target_pairs={{0,16},{16,0},{1,17},{17,1},{2,18},{18,2},{3,19},{19,3},{4,20},{20... | collective-permute-start | bytes 786440 | tf_op jit(solution)/shard_map/ppermute | solution.py:521
  48.6 3.3 %collective-permute-done.14 = bf16[128,1024]{1,0:T(8,128)(2,1)S(1)} collective-permute-done((bf16[128,1024]{1,0:T(8,128)(2,1)S(1)}, bf16[128,1024]{1,0:T(8,128)(2,1)S(1)}, u32[]{:S(2)}, u32[]{:S(2)}) %collective-permute-start.14) | collective-permute-done | bytes 262176 | tf_op jit(solution)/shard_map/ppermute | solution.py:521
  51.9 1.5 %collective-permute-done.15.first = bf16[128,1024]{1,0:T(8,128)(2,1)S(1)} collective-permute-done((bf16[128,1024]{1,0:T(8,128)(2,1)S(1)}, bf16[128,1024]{1,0:T(8,128)(2,1)S(1)}, u32[]{:S(2)}, u32[]{:S(2)}) %collective-permute-start.15) | collective-permute-done | bytes 262176 | tf_op jit(solution)/shard_map/ppermute | solution.py:521
  53.5 1.5 %collective-permute-start.16 = (bf16[96,1024]{1,0:T(8,128)(2,1)S(1)}, bf16[96,1024]{1,0:T(8,128)(2,1)S(1)}, u32[]{:S(2)}, u32[]{:S(2)}) collective-permute-start(bf16[96,1024]{1,0:T(8,128)(2,1)S(1)} %pad_maximum_fusion.4), channel_id=1, source_target_pairs={{0,8},{4,12},{8,0},{12,4},{1,9},{5,13},{9,1},{13,5},{2,10},{6,14},... | collective-permute-start | bytes 589832 | tf_op jit(solution)/shard_map/ppermute | solution.py:521
  55.0 1.5 %collective-permute-start.17 = (bf16[128,1024]{1,0:T(8,128)(2,1)S(1)}, bf16[128,1024]{1,0:T(8,128)(2,1)S(1)}, u32[]{:S(2)}, u32[]{:S(2)}) collective-permute-start(bf16[128,1024]{1,0:T(8,128)(2,1)S(1)} %get-tuple-element.100), channel_id=1, source_target_pairs={{0,16},{16,0},{1,17},{17,1},{2,18},{18,2},{3,19},{19,3},{4,20},{20... | collective-permute-start | bytes 786440 | tf_op jit(solution)/shard_map/ppermute | solution.py:521
  56.5 5.9 %collective-permute-done.16 = bf16[96,1024]{1,0:T(8,128)(2,1)S(1)} collective-permute-done((bf16[96,1024]{1,0:T(8,128)(2,1)S(1)}, bf16[96,1024]{1,0:T(8,128)(2,1)S(1)}, u32[]{:S(2)}, u32[]{:S(2)}) %collective-permute-start.16) | collective-permute-done | bytes 196640 | tf_op jit(solution)/shard_map/ppermute | solution.py:521
  62.5 0.0 collective-permute-done.17.second
  62.6 0.5 collective-permute-start.18
  63.1 0.9 %pair_sum.1 = (bf16[3,64,1024]{2,1,0:T(8,128)(2,1)}, bf16[64,1024]{1,0:T(8,128)(2,1)}) custom-call(bf16[256,1024]{1,0:T(8,128)(2,1)S(1)} %get-tuple-element.83.own, bf16[128,1024]{1,0:T(8,128)(2,1)S(1)} %collective-permute-done.15.first, bf16[128,1024]{1,0:T(8,128)(2,1)S(1)} %collective-permute-done.17.second), custom_call_target="tpu_custom_call" | custom-call | tf_op jit(solution)/shard_map/pair_sum/pallas_call | solution.py:445
  64.0 4.0 %collective-permute-done.18 = bf16[80,1024]{1,0:T(8,128)(2,1)S(1)} collective-permute-done((bf16[80,1024]{1,0:T(8,128)(2,1)S(1)}, bf16[80,1024]{1,0:T(8,128)(2,1)S(1)}, u32[]{:S(2)}, u32[]{:S(2)}) %collective-permute-start.18) | collective-permute-done | bytes 163872 | tf_op jit(solution)/shard_map/ppermute | solution.py:521
  68.0 0.1 collective-permute-start.19
  68.1 1.5 %collective-permute-done.19.far_ref = bf16[2,64,1024]{2,1,0:T(8,128)(2,1)S(1)} collective-permute-done((bf16[2,64,1024]{2,1,0:T(8,128)(2,1)S(1)}, bf16[2,64,1024]{2,1,0:T(8,128)(2,1)S(1)}, u32[]{:S(2)}, u32[]{:S(2)}) %collective-permute-start.19) | collective-permute-done | bytes 262176 | tf_op jit(solution)/shard_map/ppermute | solution.py:521
  69.6 1.5 %last_step.1 = (bf16[256,768]{1,0:T(8,128)(2,1)}, bf16[256,256]{1,0:T(8,128)(2,1)}, bf16[4,4,1024]{2,1,0:T(4,128)(2,1)}) custom-call(bf16[2,64,1024]{2,1,0:T(8,128)(2,1)S(1)} %pad_maximum_fusion.3.near_ref, bf16[2,64,1024]{2,1,0:T(8,128)(2,1)S(1)} %collective-permute-done.19.far_ref, bf16[4,4,1024]{2,1,0:T(4,128)(2,1)S(1)} %bitcast.58, ...), custom_call_target="tpu_custom_call" | custom-call | tf_op jit(solution)/shard_map/last_step/pallas_call | solution.py:497
  (37 shorter events, 0.5 us)
Async XLA Ops:
  0.6 0.9 %copy-start = (bf16[1,8,32,256]{3,2,1,0:T(8,128)(2,1)S(1)}, bf16[1,8,32,256]{3,2,1,0:T(8,128)(2,1)}, u32[]{:S(2)}) copy-start(bf16[1,8,32,256]{3,2,1,0:T(8,128)(2,1)} %param.13) | copy-start | bytes 393220
  1.5 0.9 %copy-start.2 = (bf16[1,8,32,256]{3,2,1,0:T(8,128)(2,1)S(1)}, bf16[1,8,32,256]{3,2,1,0:T(8,128)(2,1)}, u32[]{:S(2)}) copy-start(bf16[1,8,32,256]{3,2,1,0:T(8,128)(2,1)} %param.14) | copy-start | bytes 393220
  2.4 4.5 %copy-start.8 = (bf16[1,4,4,1024]{3,2,1,0:T(4,128)(2,1)S(1)}, bf16[1,4,4,1024]{3,2,1,0:T(4,128)(2,1)}, u32[]{:S(2)}) copy-start(bf16[1,4,4,1024]{3,2,1,0:T(4,128)(2,1)} %param.15) | copy-start | bytes 98308
  2.4 4.5 %copy-start.9 = (bf16[1,4,4,1024]{3,2,1,0:T(4,128)(2,1)S(1)}, bf16[1,4,4,1024]{3,2,1,0:T(4,128)(2,1)}, u32[]{:S(2)}) copy-start(bf16[1,4,4,1024]{3,2,1,0:T(4,128)(2,1)} %param.16) | copy-start | bytes 98308
  2.5 4.5 %copy-start.13 = (f32[1,256]{1,0:T(1,128)S(1)}, f32[1,256]{1,0:T(1,128)}, u32[]{:S(2)}) copy-start(f32[1,256]{1,0:T(1,128)} %constant.4.clone.fine_freq) | copy-start | bytes 3076
  2.5 6.9 %collective-permute-start = (bf16[9,32,256]{2,1,0:T(8,128)(2,1)S(1)}, bf16[9,32,256]{2,1,0:T(8,128)(2,1)S(1)}, u32[]{:S(2)}, u32[]{:S(2)}) collective-permute-start(bf16[9,32,256]{2,1,0:T(8,128)(2,1)S(1)} %get-tuple-element.52.first), channel_id=1, source_target_pairs={{0,4},{4,0},{8,12},{12,8},{1,5},{5,1},{9,13},{13,9},{2,6},{6,2},{1... | collective-permute-start | bytes 442376 | tf_op jit(solution)/shard_map/ppermute | solution.py:517
  5.6 3.9 %collective-permute-start.1 = (bf16[9,32,256]{2,1,0:T(8,128)(2,1)S(1)}, bf16[9,32,256]{2,1,0:T(8,128)(2,1)S(1)}, u32[]{:S(2)}, u32[]{:S(2)}) collective-permute-start(bf16[9,32,256]{2,1,0:T(8,128)(2,1)S(1)} %get-tuple-element.53.second), channel_id=1, source_target_pairs={{4,8},{8,4},{5,9},{9,5},{6,10},{10,6},{7,11},{11,7},{20,24},{24,20... | collective-permute-start | bytes 442376 | tf_op jit(solution)/shard_map/ppermute | solution.py:516
  6.2 0.7 %copy-start.11 = (f32[1,1024]{1,0:T(1,128)S(1)}, f32[1,1024]{1,0:T(1,128)}, u32[]{:S(2)}) copy-start(f32[1,1024]{1,0:T(1,128)} %constant.5.clone.coarse_freq) | copy-start | bytes 12292
  6.9 0.7 copy-start.10
  6.9 0.7 copy-start.12
  7.6 1.8 %copy-start.1 = (bf16[1,8,32,256]{3,2,1,0:T(8,128)(2,1)S(1)}, bf16[1,8,32,256]{3,2,1,0:T(8,128)(2,1)}, u32[]{:S(2)}) copy-start(bf16[1,8,32,256]{3,2,1,0:T(8,128)(2,1)} %param.13) | copy-start | bytes 393220
  7.6 1.8 %copy-start.3 = (bf16[1,8,32,256]{3,2,1,0:T(8,128)(2,1)S(1)}, bf16[1,8,32,256]{3,2,1,0:T(8,128)(2,1)}, u32[]{:S(2)}) copy-start(bf16[1,8,32,256]{3,2,1,0:T(8,128)(2,1)} %param.14) | copy-start | bytes 393220
  9.5 1.4 %collective-permute-start.2 = (bf16[34,8,256]{2,1,0:T(8,128)(2,1)S(1)}, bf16[34,8,256]{2,1,0:T(8,128)(2,1)S(1)}, u32[]{:S(2)}, u32[]{:S(2)}) collective-permute-start(bf16[34,8,256]{2,1,0:T(8,128)(2,1)S(1)} %get-tuple-element.58), channel_id=1, source_target_pairs={{0,1},{1,0},{2,3},{3,2},{4,5},{5,4},{6,7},{7,6},{8,9},{9,8},{10,11... | collective-permute-start | bytes 417800 | tf_op jit(solution)/shard_map/ppermute | solution.py:517
  9.6 8.7 %collective-permute-start.3 = (bf16[34,8,256]{2,1,0:T(8,128)(2,1)S(1)}, bf16[34,8,256]{2,1,0:T(8,128)(2,1)S(1)}, u32[]{:S(2)}, u32[]{:S(2)}) collective-permute-start(bf16[34,8,256]{2,1,0:T(8,128)(2,1)S(1)} %get-tuple-element.61), channel_id=1, source_target_pairs={{1,2},{2,1},{5,6},{6,5},{9,10},{10,9},{13,14},{14,13},{17,18},{18,... | collective-permute-start | bytes 417800 | tf_op jit(solution)/shard_map/ppermute | solution.py:516
  10.9 7.4 %collective-permute-start.4 = (bf16[16,2048]{1,0:T(8,128)(2,1)S(1)}, bf16[16,2048]{1,0:T(8,128)(2,1)S(1)}, u32[]{:S(2)}, u32[]{:S(2)}) collective-permute-start(bf16[16,2048]{1,0:T(8,128)(2,1)S(1)} %get-tuple-element.69), channel_id=1, source_target_pairs={{0,4},{4,0},{8,12},{12,8},{1,5},{5,1},{9,13},{13,9},{2,6},{6,2},{1... | collective-permute-start | bytes 196616 | tf_op jit(solution)/shard_map/ppermute | solution.py:521
  15.7 6.1 %collective-permute-start.5 = (bf16[16,2048]{1,0:T(8,128)(2,1)S(1)}, bf16[16,2048]{1,0:T(8,128)(2,1)S(1)}, u32[]{:S(2)}, u32[]{:S(2)}) collective-permute-start(bf16[16,2048]{1,0:T(8,128)(2,1)S(1)} %get-tuple-element.69), channel_id=1, source_target_pairs={{0,8},{4,12},{8,0},{12,4},{1,9},{5,13},{9,1},{13,5},{2,10},{6,14},... | collective-permute-start | bytes 196616 | tf_op jit(solution)/shard_map/ppermute | solution.py:521
  16.9 6.7 %collective-permute-start.6 = (bf16[16,2048]{1,0:T(8,128)(2,1)S(1)}, bf16[16,2048]{1,0:T(8,128)(2,1)S(1)}, u32[]{:S(2)}, u32[]{:S(2)}) collective-permute-start(bf16[16,2048]{1,0:T(8,128)(2,1)S(1)} %get-tuple-element.69), channel_id=1, source_target_pairs={{0,12},{4,8},{8,4},{12,0},{1,13},{5,9},{9,5},{13,1},{2,14},{6,10},... | collective-permute-start | bytes 196616 | tf_op jit(solution)/shard_map/ppermute | solution.py:521
  23.6 2.4 %copy-start.4 = (bf16[256,768]{1,0:T(8,128)(2,1)S(1)}, bf16[256,768]{1,0:T(8,128)(2,1)}, u32[]{:S(2)}) copy-start(bf16[256,768]{1,0:T(8,128)(2,1)} %qkv_ref.1) | copy-start | bytes 1179652
  23.6 2.4 %copy-start.6 = (bf16[256,256]{1,0:T(8,128)(2,1)S(1)}, bf16[256,256]{1,0:T(8,128)(2,1)}, u32[]{:S(2)}) copy-start(bf16[256,256]{1,0:T(8,128)(2,1)} %out_ref.1) | copy-start | bytes 393220
  23.6 9.3 %collective-permute-start.8 = (bf16[4,16,2048]{2,1,0:T(8,128)(2,1)S(1)}, bf16[4,16,2048]{2,1,0:T(8,128)(2,1)S(1)}, u32[]{:S(2)}, u32[]{:S(2)}) collective-permute-start(bf16[4,16,2048]{2,1,0:T(8,128)(2,1)S(1)} %get-tuple-element.105), channel_id=1, source_target_pairs={{0,2},{1,3},{2,0},{3,1},{4,6},{5,7},{6,4},{7,5},{8,10},{9,11},{10,... | collective-permute-start | bytes 786440 | tf_op jit(solution)/shard_map/ppermute | solution.py:521
  32.1 1.5 %collective-permute-start.7 = (bf16[2,4,16,1024]{3,2,1,0:T(8,128)(2,1)S(1)}, bf16[2,4,16,1024]{3,2,1,0:T(8,128)(2,1)S(1)}, u32[]{:S(2)}, u32[]{:S(2)}) collective-permute-start(bf16[2,4,16,1024]{3,2,1,0:T(8,128)(2,1)S(1)} %get-tuple-element.68), channel_id=1, source_target_pairs={{0,1},{1,0},{2,3},{3,2},{4,5},{5,4},{6,7},{7,6},{8,9},{9,8},{10,11... | collective-permute-start | bytes 786440 | tf_op jit(solution)/shard_map/ppermute | solution.py:521
  32.9 1.5 %collective-permute-start.9 = (bf16[4,16,2048]{2,1,0:T(8,128)(2,1)S(1)}, bf16[4,16,2048]{2,1,0:T(8,128)(2,1)S(1)}, u32[]{:S(2)}, u32[]{:S(2)}) collective-permute-start(bf16[4,16,2048]{2,1,0:T(8,128)(2,1)S(1)} %collective-permute-done.8), channel_id=1, source_target_pairs={{0,1},{1,0},{2,3},{3,2},{4,5},{5,4},{6,7},{7,6},{8,9},{9,8},{10,11... | collective-permute-start | bytes 786440 | tf_op jit(solution)/shard_map/ppermute | solution.py:521
  32.9 2.1 %collective-permute-start.11 = (bf16[4,16,2048]{2,1,0:T(8,128)(2,1)S(1)}, bf16[4,16,2048]{2,1,0:T(8,128)(2,1)S(1)}, u32[]{:S(2)}, u32[]{:S(2)}) collective-permute-start(bf16[4,16,2048]{2,1,0:T(8,128)(2,1)S(1)} %get-tuple-element.105), channel_id=1, source_target_pairs={{0,1},{1,0},{2,3},{3,2},{4,5},{5,4},{6,7},{7,6},{8,9},{9,8},{10,11... | collective-permute-start | bytes 786440 | tf_op jit(solution)/shard_map/ppermute | solution.py:521
  34.5 5.6 %collective-permute-start.10 = (bf16[4,16,1024]{2,1,0:T(8,128)(2,1)S(1)}, bf16[4,16,1024]{2,1,0:T(8,128)(2,1)S(1)}, u32[]{:S(2)}, u32[]{:S(2)}) collective-permute-start(bf16[4,16,1024]{2,1,0:T(8,128)(2,1)S(1)} %fusion.2), channel_id=1, source_target_pairs={{0,2},{1,3},{2,0},{3,1},{4,6},{5,7},{6,4},{7,5},{8,10},{9,11},{10,... | collective-permute-start | bytes 393224 | tf_op jit(solution)/shard_map/ppermute | solution.py:521
  35.2 1.0 %copy-start.5 = (bf16[3,64,1024]{2,1,0:T(8,128)(2,1)S(1)}, bf16[3,64,1024]{2,1,0:T(8,128)(2,1)}, u32[]{:S(2)}) copy-start(bf16[3,64,1024]{2,1,0:T(8,128)(2,1)} %qkv_hbm.1) | copy-start | bytes 1179652
  35.2 1.0 %copy-start.7 = (bf16[64,1024]{1,0:T(8,128)(2,1)S(1)}, bf16[64,1024]{1,0:T(8,128)(2,1)}, u32[]{:S(2)}) copy-start(bf16[64,1024]{1,0:T(8,128)(2,1)} %out_hbm.1) | copy-start | bytes 393220
  40.1 5.0 %collective-permute-start.12 = (bf16[4,16,1024]{2,1,0:T(8,128)(2,1)S(1)}, bf16[4,16,1024]{2,1,0:T(8,128)(2,1)S(1)}, u32[]{:S(2)}, u32[]{:S(2)}) collective-permute-start(bf16[4,16,1024]{2,1,0:T(8,128)(2,1)S(1)} %fusion.1), channel_id=1, source_target_pairs={{0,16},{16,0},{1,17},{17,1},{2,18},{18,2},{3,19},{19,3},{4,20},{20... | collective-permute-start | bytes 393224 | tf_op jit(solution)/shard_map/ppermute | solution.py:521
  41.7 3.5 %collective-permute-start.13 = (bf16[2,4,16,1024]{3,2,1,0:T(8,128)(2,1)S(1)}, bf16[2,4,16,1024]{3,2,1,0:T(8,128)(2,1)S(1)}, u32[]{:S(2)}, u32[]{:S(2)}) collective-permute-start(bf16[2,4,16,1024]{3,2,1,0:T(8,128)(2,1)S(1)} %bitcast.76), channel_id=1, source_target_pairs={{0,1},{1,0},{2,3},{3,2},{4,5},{5,4},{6,7},{7,6},{8,9},{9,8},{10,11... | collective-permute-start | bytes 786440 | tf_op jit(solution)/shard_map/ppermute | solution.py:521
  45.3 6.5 %collective-permute-start.14 = (bf16[128,1024]{1,0:T(8,128)(2,1)S(1)}, bf16[128,1024]{1,0:T(8,128)(2,1)S(1)}, u32[]{:S(2)}, u32[]{:S(2)}) collective-permute-start(bf16[128,1024]{1,0:T(8,128)(2,1)S(1)} %pad_maximum_fusion.2), channel_id=1, source_target_pairs={{0,4},{4,0},{8,12},{12,8},{1,5},{5,1},{9,13},{13,9},{2,6},{6,2},{1... | collective-permute-start | bytes 786440 | tf_op jit(solution)/shard_map/ppermute | solution.py:521
  47.0 6.4 %collective-permute-start.15 = (bf16[128,1024]{1,0:T(8,128)(2,1)S(1)}, bf16[128,1024]{1,0:T(8,128)(2,1)S(1)}, u32[]{:S(2)}, u32[]{:S(2)}) collective-permute-start(bf16[128,1024]{1,0:T(8,128)(2,1)S(1)} %get-tuple-element.101), channel_id=1, source_target_pairs={{0,16},{16,0},{1,17},{17,1},{2,18},{18,2},{3,19},{19,3},{4,20},{20... | collective-permute-start | bytes 786440 | tf_op jit(solution)/shard_map/ppermute | solution.py:521
  53.5 9.0 %collective-permute-start.16 = (bf16[96,1024]{1,0:T(8,128)(2,1)S(1)}, bf16[96,1024]{1,0:T(8,128)(2,1)S(1)}, u32[]{:S(2)}, u32[]{:S(2)}) collective-permute-start(bf16[96,1024]{1,0:T(8,128)(2,1)S(1)} %pad_maximum_fusion.4), channel_id=1, source_target_pairs={{0,8},{4,12},{8,0},{12,4},{1,9},{5,13},{9,1},{13,5},{2,10},{6,14},... | collective-permute-start | bytes 589832 | tf_op jit(solution)/shard_map/ppermute | solution.py:521
  55.0 7.5 %collective-permute-start.17 = (bf16[128,1024]{1,0:T(8,128)(2,1)S(1)}, bf16[128,1024]{1,0:T(8,128)(2,1)S(1)}, u32[]{:S(2)}, u32[]{:S(2)}) collective-permute-start(bf16[128,1024]{1,0:T(8,128)(2,1)S(1)} %get-tuple-element.100), channel_id=1, source_target_pairs={{0,16},{16,0},{1,17},{17,1},{2,18},{18,2},{3,19},{19,3},{4,20},{20... | collective-permute-start | bytes 786440 | tf_op jit(solution)/shard_map/ppermute | solution.py:521
  62.6 5.4 %collective-permute-start.18 = (bf16[80,1024]{1,0:T(8,128)(2,1)S(1)}, bf16[80,1024]{1,0:T(8,128)(2,1)S(1)}, u32[]{:S(2)}, u32[]{:S(2)}) collective-permute-start(bf16[80,1024]{1,0:T(8,128)(2,1)S(1)} %pad_maximum_fusion.5), channel_id=1, source_target_pairs={{0,2},{1,3},{2,0},{3,1},{4,6},{5,7},{6,4},{7,5},{8,10},{9,11},{10,... | collective-permute-start | bytes 491528 | tf_op jit(solution)/shard_map/ppermute | solution.py:521
  68.0 1.6 %collective-permute-start.19 = (bf16[2,64,1024]{2,1,0:T(8,128)(2,1)S(1)}, bf16[2,64,1024]{2,1,0:T(8,128)(2,1)S(1)}, u32[]{:S(2)}, u32[]{:S(2)}) collective-permute-start(bf16[2,64,1024]{2,1,0:T(8,128)(2,1)S(1)} %pad_maximum_fusion.3.near_ref), channel_id=1, source_target_pairs={{0,1},{1,0},{2,3},{3,2},{4,5},{5,4},{6,7},{7,6},{8,9},{9,8},{10,11... | collective-permute-start | bytes 786440 | tf_op jit(solution)/shard_map/ppermute | solution.py:521

commit v6 on v5

--- a/solution.py
+++ b/solution.py
@@ -60,10 +60,10 @@
 def fine_body(
     x_ref,
     dy_ref,
+    row_far_ref,
     row_near_ref,
-    row_far_ref,
+    col_far_ref,
     col_near_ref,
-    col_far_ref,
     factor_ref,
     qkv_ref,
     out_ref,
@@ -354,7 +354,7 @@
     )(picture, cotangent)
 
 
-def col_edges_body(x_ref, dy_ref, row_near_ref, row_far_ref, near_ref, far_ref):
+def col_edges_body(x_ref, dy_ref, row_far_ref, row_near_ref, near_ref, far_ref):
     above, below = in_order("gy", row_near_ref, row_far_ref)
     breadth = x_ref.shape[1]
     odd = odd_rank("gx")
@@ -367,7 +367,7 @@
         at += rows.shape[0]
 
 
-def col_edges(picture, cotangent, row_near, row_far):
+def col_edges(picture, cotangent, row_far, row_near):
     vmem = pl.BlockSpec(memory_space=pltpu.VMEM)
     rows = 2 * (picture.shape[0] + row_near.shape[0])
     shape = jax.ShapeDtypeStruct((rows, side, D_F), jnp.bfloat16)
@@ -378,7 +378,7 @@
         out_specs=(vmem, vmem),
         compiler_params=pltpu.CompilerParams(vmem_limit_bytes=vmem_bytes),
         name="col_edges",
-    )(picture, cotangent, row_near, row_far)
+    )(picture, cotangent, row_far, row_near)
 
 
 def pack_body(
@@ -566,24 +566,21 @@
     own, factor, coarse_factor = packed(
         payloads, timestep, x_coarse[0], dy_coarse[0], fine_gain, coarse_gain
     )
-    row_near, own, factor, coarse_factor = tied(row_near, own, factor, coarse_factor)
     count = own.shape[0]
-    edges = col_edges(picture, cotangent, row_near, row_far)
+    row_group = all_rows(own)
+    edges = col_edges(picture, cotangent, row_far, row_near)
     col_near, col_far = neighbours(*edges, "gx")
-    col_near, own = tied(col_near, own)
-    pieces = [own] + [swapped(own, "gy", row) for row in range(1, downs)]
-    col_near, col_far, *pieces = tied(col_near, col_far, *pieces)
-    row_group = jnp.stack(pieces)
+    col_far, col_near, row_group = tied(col_far, col_near, row_group)
     cross = swapped(row_group, "gx", 2)
     beside = swapped(row_group, "gx", 1)
     dx_picture, fine_keep, fine_send = fine_block(
         (across, downs),
         picture,
         cotangent,
+        row_far,
         row_near,
-        row_far,
+        col_far,
         col_near,
-        col_far,
         factor,
         fine_qkv,
         fine_out,

time: 71.4 us -> 67 us (0.938)
  waiting for transfers between devices: 30.5 us -> 23.9 us
  starting transfers between devices: 23.8 us -> 26.1 us
    ppermute x2, starting transfers between devices: 3.16 us -> 8.81 us  [neighbours(): return (lax.ppermute(to_near, axis, near), from_far)]
    ppermute x16, waiting for transfers between devices: 28.1 us -> 22.9 us  [swapped(): lax.ppermute(value, axis, [(i, i ^ mask) for i in range(lax.axis_size(axi...]
    ppermute x16, starting transfers between devices: 19.3 us -> 15.8 us  [swapped(): lax.ppermute(value, axis, [(i, i ^ mask) for i in range(lax.axis_size(axi...]
    ppermute x2, waiting for transfers between devices: 2.41 us -> 0.92 us  [neighbours(): return (lax.ppermute(to_near, axis, near), from_far)]
  transfers between devices with their start and end apart: 20 -> 20, of which waited for: 14 -> 10; matrix products, arithmetic and copies ran while one was open for 1% -> 1% of each run, Pallas kernels for 13% -> 14%
where the time goes in v6:
time: 67 us; the launch traced here: 66.7 us
  starting transfers between devices  26.1 us (39%)
  waiting for transfers between devices  23.9 us (36%)
  Pallas kernels  10.9 us (16%)
  local copies, waits for them, and re-layouts  3.64 us (5%)
  between operations  1.67 us (2%)
    ppermute x16, waiting for transfers between devices, swapped(): lax.ppermute(value, axis, [(i, i ^ mask) for i in range(lax.axis_size(axi...  22.9 us
    ppermute x16, starting transfers between devices, swapped(): lax.ppermute(value, axis, [(i, i ^ mask) for i in range(lax.axis_size(axi...  15.8 us
    ppermute x2, starting transfers between devices, neighbours(): return (lax.ppermute(to_near, axis, near), from_far)  8.81 us
    pallas_call x1, Pallas kernels, fine_block(): pl.pallas_call(fine_body, out_shape=(jax.ShapeDtypeStruct((height, breadt...  6.17 us
    unnamed x28, local copies, waits for them, and re-layouts  3.41 us
    pallas_call x1, Pallas kernels, coarse_block(): pl.pallas_call(coarse_body, out_shape=(jax.ShapeDtypeStruct((count, D_C),...  2.23 us
    pallas_call x1, Pallas kernels, last_step(): pl.pallas_call(last_body, out_shape=(jax.ShapeDtypeStruct((D_F, 3 * D_F),...  1.48 us
    ppermute x2, starting transfers between devices, neighbours(): from_far = lax.ppermute(to_far, axis, far)  1.47 us
  transfers between devices with their start and end apart: 20, of which 10 were waited for; matrix products, arithmetic and copies ran while one was open for 1% of the time, Pallas kernels for 14%

profile of v6, /device:TPU:0, one launch (start us, length us, event | category | flops | bytes accessed | tf_op | source)
XLA Modules:
  0.0 66.7 jit_solution(7434650556292622718)
XLA Ops:
  0.6 0.0 copy-start
  0.6 0.9 %copy-done = bf16[1,8,32,256]{3,2,1,0:T(8,128)(2,1)S(1)} copy-done((bf16[1,8,32,256]{3,2,1,0:T(8,128)(2,1)S(1)}, bf16[1,8,32,256]{3,2,1,0:T(8,128)(2,1)}, u32[]{:S(2)}) %copy-start) | copy-done | bytes 131096
  1.5 0.9 %copy-done.2 = bf16[1,8,32,256]{3,2,1,0:T(8,128)(2,1)S(1)} copy-done((bf16[1,8,32,256]{3,2,1,0:T(8,128)(2,1)S(1)}, bf16[1,8,32,256]{3,2,1,0:T(8,128)(2,1)}, u32[]{:S(2)}) %copy-start.2) | copy-done | bytes 131096
  2.5 0.0 copy-start.13
  2.5 0.7 %collective-permute-start = (bf16[9,32,256]{2,1,0:T(8,128)(2,1)S(1)}, bf16[9,32,256]{2,1,0:T(8,128)(2,1)S(1)}, u32[]{:S(2)}, u32[]{:S(2)}) collective-permute-start(bf16[9,32,256]{2,1,0:T(8,128)(2,1)S(1)} %get-tuple-element.43.second), channel_id=1, source_target_pairs={{4,8},{8,4},{5,9},{9,5},{6,10},{10,6},{7,11},{11,7},{20,24},{24,20... | collective-permute-start | bytes 442376 | tf_op jit(solution)/shard_map/ppermute | solution.py:516
  3.2 5.9 %collective-permute-start.1 = (bf16[9,32,256]{2,1,0:T(8,128)(2,1)S(1)}, bf16[9,32,256]{2,1,0:T(8,128)(2,1)S(1)}, u32[]{:S(2)}, u32[]{:S(2)}) collective-permute-start(bf16[9,32,256]{2,1,0:T(8,128)(2,1)S(1)} %get-tuple-element.44.first), channel_id=1, source_target_pairs={{0,4},{4,0},{8,12},{12,8},{1,5},{5,1},{9,13},{13,9},{2,6},{6,2},{1... | collective-permute-start | bytes 442376 | tf_op jit(solution)/shard_map/ppermute | solution.py:517
  9.7 0.0 copy-start.10
  9.7 0.0 copy-start.12
  9.8 0.6 copy-done.10
  10.4 0.0 copy-done.12
  10.4 0.1 pack_coarse.1
  10.5 1.4 %collective-permute-start.6 = (bf16[16,2048]{1,0:T(8,128)(2,1)S(1)}, bf16[16,2048]{1,0:T(8,128)(2,1)S(1)}, u32[]{:S(2)}, u32[]{:S(2)}) collective-permute-start(bf16[16,2048]{1,0:T(8,128)(2,1)S(1)} %get-tuple-element.47), channel_id=1, source_target_pairs={{0,12},{4,8},{8,4},{12,0},{1,13},{5,9},{9,5},{13,1},{2,14},{6,10},... | collective-permute-start | bytes 196616 | tf_op jit(solution)/shard_map/ppermute | solution.py:521
  11.9 0.1 collective-permute-start.5
  12.0 2.9 %collective-permute-start.4 = (bf16[16,2048]{1,0:T(8,128)(2,1)S(1)}, bf16[16,2048]{1,0:T(8,128)(2,1)S(1)}, u32[]{:S(2)}, u32[]{:S(2)}) collective-permute-start(bf16[16,2048]{1,0:T(8,128)(2,1)S(1)} %get-tuple-element.47), channel_id=1, source_target_pairs={{0,4},{4,0},{8,12},{12,8},{1,5},{5,1},{9,13},{13,9},{2,6},{6,2},{1... | collective-permute-start | bytes 196616 | tf_op jit(solution)/shard_map/ppermute | solution.py:521
  15.0 0.0 collective-permute-done.row_far_ref
  15.0 0.0 collective-permute-done.1.row_near_ref
  15.0 0.1 col_edges.1
  15.1 0.0 copy-start.4
  15.1 0.8 %collective-permute-start.2 = (bf16[34,8,256]{2,1,0:T(8,128)(2,1)S(1)}, bf16[34,8,256]{2,1,0:T(8,128)(2,1)S(1)}, u32[]{:S(2)}, u32[]{:S(2)}) collective-permute-start(bf16[34,8,256]{2,1,0:T(8,128)(2,1)S(1)} %get-tuple-element.45), channel_id=1, source_target_pairs={{1,2},{2,1},{5,6},{6,5},{9,10},{10,9},{13,14},{14,13},{17,18},{18,... | collective-permute-start | bytes 417800 | tf_op jit(solution)/shard_map/ppermute | solution.py:516
  15.9 2.9 %collective-permute-start.3 = (bf16[34,8,256]{2,1,0:T(8,128)(2,1)S(1)}, bf16[34,8,256]{2,1,0:T(8,128)(2,1)S(1)}, u32[]{:S(2)}, u32[]{:S(2)}) collective-permute-start(bf16[34,8,256]{2,1,0:T(8,128)(2,1)S(1)} %get-tuple-element.46), channel_id=1, source_target_pairs={{0,1},{1,0},{2,3},{3,2},{4,5},{5,4},{6,7},{7,6},{8,9},{9,8},{10,11... | collective-permute-start | bytes 417800 | tf_op jit(solution)/shard_map/ppermute | solution.py:517
  18.8 0.0 collective-permute-done.6
  18.8 0.0 collective-permute-done.5
  18.8 0.0 collective-permute-done.4
  18.8 0.0 copy-start.6
  18.9 0.0 collective-permute-done.2.col_far_ref
  18.9 0.9 %collective-permute-done.3.col_near_ref = bf16[34,8,256]{2,1,0:T(8,128)(2,1)S(1)} collective-permute-done((bf16[34,8,256]{2,1,0:T(8,128)(2,1)S(1)}, bf16[34,8,256]{2,1,0:T(8,128)(2,1)S(1)}, u32[]{:S(2)}, u32[]{:S(2)}) %collective-permute-start.3) | collective-permute-done | bytes 139296 | tf_op jit(solution)/shard_map/ppermute | solution.py:517
  19.8 3.3 %collective-permute-start.8 = (bf16[4,16,2048]{2,1,0:T(8,128)(2,1)S(1)}, bf16[4,16,2048]{2,1,0:T(8,128)(2,1)S(1)}, u32[]{:S(2)}, u32[]{:S(2)}) collective-permute-start(bf16[4,16,2048]{2,1,0:T(8,128)(2,1)S(1)} %pad_maximum_fusion.1), channel_id=1, source_target_pairs={{0,2},{1,3},{2,0},{3,1},{4,6},{5,7},{6,4},{7,5},{8,10},{9,11},{10,... | collective-permute-start | bytes 786440 | tf_op jit(solution)/shard_map/ppermute | solution.py:521
  23.1 6.2 %fine_block.1 = (bf16[8,32,256]{2,1,0:T(8,128)(2,1)}, f32[2,4,16,1024]{3,2,1,0:T(8,128)S(1)}, bf16[2,4,16,1024]{3,2,1,0:T(8,128)(2,1)S(1)}) custom-call(bf16[8,32,256]{2,1,0:T(8,128)(2,1)S(1)} %bitcast.52, bf16[8,32,256]{2,1,0:T(8,128)(2,1)S(1)} %bitcast.55, bf16[9,32,256]{2,1,0:T(8,128)(2,1)S(1)} %collective-permute-done.row_far_ref, ...), custom_call_target="tpu_custom_call" | custom-call | tf_op jit(solution)/shard_map/fine_block/pallas_call | solution.py:233
  29.3 0.0 collective-permute-start.7
  29.3 0.4 collective-permute-done.8
  29.7 0.1 collective-permute-start.9
  29.8 0.4 collective-permute-start.11
  30.2 0.6 collective-permute-done.7
  30.8 0.1 convert_add_fusion.1
  30.9 0.3 collective-permute-done.9
  31.2 0.3 collective-permute-start.10
  31.6 0.0 collective-permute-done.11
  31.6 0.1 pad_maximum_fusion
  31.7 0.0 copy-start.5
  31.7 0.0 copy-start.7
  31.7 0.1 fusion.5
  31.8 0.9 %copy-done.5 = bf16[3,64,1024]{2,1,0:T(8,128)(2,1)S(1)} copy-done((bf16[3,64,1024]{2,1,0:T(8,128)(2,1)S(1)}, bf16[3,64,1024]{2,1,0:T(8,128)(2,1)}, u32[]{:S(2)}) %copy-start.5) | copy-done | bytes 393240
  32.7 0.0 copy-done.7
  32.7 2.2 %coarse_block.1 = (bf16[256,1024]{1,0:T(8,128)(2,1)S(1)}, bf16[256,1024]{1,0:T(8,128)(2,1)S(1)}) custom-call(bf16[256,1024]{1,0:T(8,128)(2,1)S(1)} %get-tuple-element.81.x_ref, bf16[256,1024]{1,0:T(8,128)(2,1)S(1)} %get-tuple-element.80.dy_ref, f32[1,1024]{1,0:T(1,128)S(1)} %get-tuple-element.57.factor_ref, bf16[3,64,1024]{2,1,0:T(8,128)(2,1)S(1)} %copy-done.5, ...), custom_call_target="tpu_custom_call" | custom-call | tf_op jit(solution)/shard_map/coarse_block/pallas_call | solution.py:309
  35.0 1.8 %collective-permute-done.10 = bf16[4,16,1024]{2,1,0:T(8,128)(2,1)S(1)} collective-permute-done((bf16[4,16,1024]{2,1,0:T(8,128)(2,1)S(1)}, bf16[4,16,1024]{2,1,0:T(8,128)(2,1)S(1)}, u32[]{:S(2)}, u32[]{:S(2)}) %collective-permute-start.10) | collective-permute-done | bytes 131104 | tf_op jit(solution)/shard_map/ppermute | solution.py:521
  36.9 1.6 %collective-permute-start.12 = (bf16[4,16,1024]{2,1,0:T(8,128)(2,1)S(1)}, bf16[4,16,1024]{2,1,0:T(8,128)(2,1)S(1)}, u32[]{:S(2)}, u32[]{:S(2)}) collective-permute-start(bf16[4,16,1024]{2,1,0:T(8,128)(2,1)S(1)} %fusion.1), channel_id=1, source_target_pairs={{0,16},{16,0},{1,17},{17,1},{2,18},{18,2},{3,19},{19,3},{4,20},{20... | collective-permute-start | bytes 393224 | tf_op jit(solution)/shard_map/ppermute | solution.py:521
  38.5 0.1 collective-permute-start.13
  38.6 3.3 %collective-permute-done.12 = bf16[4,16,1024]{2,1,0:T(8,128)(2,1)S(1)} collective-permute-done((bf16[4,16,1024]{2,1,0:T(8,128)(2,1)S(1)}, bf16[4,16,1024]{2,1,0:T(8,128)(2,1)S(1)}, u32[]{:S(2)}, u32[]{:S(2)}) %collective-permute-start.12) | collective-permute-done | bytes 131104 | tf_op jit(solution)/shard_map/ppermute | solution.py:521
  41.9 0.0 collective-permute-done.13
  41.9 0.1 convert_add_fusion
  42.1 0.1 collective-permute-start.14
  42.2 1.6 %collective-permute-start.15 = (bf16[128,1024]{1,0:T(8,128)(2,1)S(1)}, bf16[128,1024]{1,0:T(8,128)(2,1)S(1)}, u32[]{:S(2)}, u32[]{:S(2)}) collective-permute-start(bf16[128,1024]{1,0:T(8,128)(2,1)S(1)} %get-tuple-element.83), channel_id=1, source_target_pairs={{0,16},{16,0},{1,17},{17,1},{2,18},{18,2},{3,19},{19,3},{4,20},{20... | collective-permute-start | bytes 786440 | tf_op jit(solution)/shard_map/ppermute | solution.py:521
  43.8 4.8 %collective-permute-done.14 = bf16[128,1024]{1,0:T(8,128)(2,1)S(1)} collective-permute-done((bf16[128,1024]{1,0:T(8,128)(2,1)S(1)}, bf16[128,1024]{1,0:T(8,128)(2,1)S(1)}, u32[]{:S(2)}, u32[]{:S(2)}) %collective-permute-start.14) | collective-permute-done | bytes 262176 | tf_op jit(solution)/shard_map/ppermute | solution.py:521
  48.7 0.0 collective-permute-done.15.first
  48.8 1.8 %collective-permute-start.16 = (bf16[96,1024]{1,0:T(8,128)(2,1)S(1)}, bf16[96,1024]{1,0:T(8,128)(2,1)S(1)}, u32[]{:S(2)}, u32[]{:S(2)}) collective-permute-start(bf16[96,1024]{1,0:T(8,128)(2,1)S(1)} %pad_maximum_fusion.4), channel_id=1, source_target_pairs={{0,8},{4,12},{8,0},{12,4},{1,9},{5,13},{9,1},{13,5},{2,10},{6,14},... | collective-permute-start | bytes 589832 | tf_op jit(solution)/shard_map/ppermute | solution.py:521
  50.6 1.5 %collective-permute-start.17 = (bf16[128,1024]{1,0:T(8,128)(2,1)S(1)}, bf16[128,1024]{1,0:T(8,128)(2,1)S(1)}, u32[]{:S(2)}, u32[]{:S(2)}) collective-permute-start(bf16[128,1024]{1,0:T(8,128)(2,1)S(1)} %get-tuple-element.82), channel_id=1, source_target_pairs={{0,16},{16,0},{1,17},{17,1},{2,18},{18,2},{3,19},{19,3},{4,20},{20... | collective-permute-start | bytes 786440 | tf_op jit(solution)/shard_map/ppermute | solution.py:521
  52.1 6.0 %collective-permute-done.16 = bf16[96,1024]{1,0:T(8,128)(2,1)S(1)} collective-permute-done((bf16[96,1024]{1,0:T(8,128)(2,1)S(1)}, bf16[96,1024]{1,0:T(8,128)(2,1)S(1)}, u32[]{:S(2)}, u32[]{:S(2)}) %collective-permute-start.16) | collective-permute-done | bytes 196640 | tf_op jit(solution)/shard_map/ppermute | solution.py:521
  58.2 0.0 collective-permute-done.17.second
  58.2 0.5 collective-permute-start.18
  58.7 0.9 %pair_sum.1 = (bf16[3,64,1024]{2,1,0:T(8,128)(2,1)}, bf16[64,1024]{1,0:T(8,128)(2,1)}) custom-call(bf16[256,1024]{1,0:T(8,128)(2,1)S(1)} %get-tuple-element.65.own, bf16[128,1024]{1,0:T(8,128)(2,1)S(1)} %collective-permute-done.15.first, bf16[128,1024]{1,0:T(8,128)(2,1)S(1)} %collective-permute-done.17.second), custom_call_target="tpu_custom_call" | custom-call | tf_op jit(solution)/shard_map/pair_sum/pallas_call | solution.py:445
  59.6 4.0 %collective-permute-done.18 = bf16[80,1024]{1,0:T(8,128)(2,1)S(1)} collective-permute-done((bf16[80,1024]{1,0:T(8,128)(2,1)S(1)}, bf16[80,1024]{1,0:T(8,128)(2,1)S(1)}, u32[]{:S(2)}, u32[]{:S(2)}) %collective-permute-start.18) | collective-permute-done | bytes 163872 | tf_op jit(solution)/shard_map/ppermute | solution.py:521
  63.7 0.1 collective-permute-start.19
  63.8 1.5 %collective-permute-done.19.far_ref = bf16[2,64,1024]{2,1,0:T(8,128)(2,1)S(1)} collective-permute-done((bf16[2,64,1024]{2,1,0:T(8,128)(2,1)S(1)}, bf16[2,64,1024]{2,1,0:T(8,128)(2,1)S(1)}, u32[]{:S(2)}, u32[]{:S(2)}) %collective-permute-start.19) | collective-permute-done | bytes 262176 | tf_op jit(solution)/shard_map/ppermute | solution.py:521
  65.3 1.5 %last_step.1 = (bf16[256,768]{1,0:T(8,128)(2,1)}, bf16[256,256]{1,0:T(8,128)(2,1)}, bf16[4,4,1024]{2,1,0:T(4,128)(2,1)}) custom-call(bf16[2,64,1024]{2,1,0:T(8,128)(2,1)S(1)} %pad_maximum_fusion.3.near_ref, bf16[2,64,1024]{2,1,0:T(8,128)(2,1)S(1)} %collective-permute-done.19.far_ref, bf16[4,4,1024]{2,1,0:T(4,128)(2,1)S(1)} %bitcast.57, ...), custom_call_target="tpu_custom_call" | custom-call | tf_op jit(solution)/shard_map/last_step/pallas_call | solution.py:497
  (37 shorter events, 0.5 us)
Async XLA Ops:
  0.6 0.9 %copy-start = (bf16[1,8,32,256]{3,2,1,0:T(8,128)(2,1)S(1)}, bf16[1,8,32,256]{3,2,1,0:T(8,128)(2,1)}, u32[]{:S(2)}) copy-start(bf16[1,8,32,256]{3,2,1,0:T(8,128)(2,1)} %param.13) | copy-start | bytes 393220
  1.5 0.9 %copy-start.2 = (bf16[1,8,32,256]{3,2,1,0:T(8,128)(2,1)S(1)}, bf16[1,8,32,256]{3,2,1,0:T(8,128)(2,1)}, u32[]{:S(2)}) copy-start(bf16[1,8,32,256]{3,2,1,0:T(8,128)(2,1)} %param.14) | copy-start | bytes 393220
  2.4 7.3 %copy-start.8 = (bf16[1,4,4,1024]{3,2,1,0:T(4,128)(2,1)S(1)}, bf16[1,4,4,1024]{3,2,1,0:T(4,128)(2,1)}, u32[]{:S(2)}) copy-start(bf16[1,4,4,1024]{3,2,1,0:T(4,128)(2,1)} %param.15) | copy-start | bytes 98308
  2.4 7.3 %copy-start.9 = (bf16[1,4,4,1024]{3,2,1,0:T(4,128)(2,1)S(1)}, bf16[1,4,4,1024]{3,2,1,0:T(4,128)(2,1)}, u32[]{:S(2)}) copy-start(bf16[1,4,4,1024]{3,2,1,0:T(4,128)(2,1)} %param.16) | copy-start | bytes 98308
  2.5 7.3 %copy-start.13 = (f32[1,256]{1,0:T(1,128)S(1)}, f32[1,256]{1,0:T(1,128)}, u32[]{:S(2)}) copy-start(f32[1,256]{1,0:T(1,128)} %constant.4.clone.fine_freq) | copy-start | bytes 3076
  2.5 12.5 %collective-permute-start = (bf16[9,32,256]{2,1,0:T(8,128)(2,1)S(1)}, bf16[9,32,256]{2,1,0:T(8,128)(2,1)S(1)}, u32[]{:S(2)}, u32[]{:S(2)}) collective-permute-start(bf16[9,32,256]{2,1,0:T(8,128)(2,1)S(1)} %get-tuple-element.43.second), channel_id=1, source_target_pairs={{4,8},{8,4},{5,9},{9,5},{6,10},{10,6},{7,11},{11,7},{20,24},{24,20... | collective-permute-start | bytes 442376 | tf_op jit(solution)/shard_map/ppermute | solution.py:516
  3.2 11.8 %collective-permute-start.1 = (bf16[9,32,256]{2,1,0:T(8,128)(2,1)S(1)}, bf16[9,32,256]{2,1,0:T(8,128)(2,1)S(1)}, u32[]{:S(2)}, u32[]{:S(2)}) collective-permute-start(bf16[9,32,256]{2,1,0:T(8,128)(2,1)S(1)} %get-tuple-element.44.first), channel_id=1, source_target_pairs={{0,4},{4,0},{8,12},{12,8},{1,5},{5,1},{9,13},{13,9},{2,6},{6,2},{1... | collective-permute-start | bytes 442376 | tf_op jit(solution)/shard_map/ppermute | solution.py:517
  9.1 0.7 %copy-start.11 = (f32[1,1024]{1,0:T(1,128)S(1)}, f32[1,1024]{1,0:T(1,128)}, u32[]{:S(2)}) copy-start(f32[1,1024]{1,0:T(1,128)} %constant.5.clone.coarse_freq) | copy-start | bytes 12292
  9.7 0.7 %copy-start.10 = (f32[1024]{0:T(1024)S(1)}, f32[1024]{0:T(1024)}, u32[]{:S(2)}) copy-start(f32[1024]{0:T(1024)} %param.19) | copy-start | bytes 12292
  9.7 0.7 %copy-start.12 = (f32[256]{0:T(256)S(1)}, f32[256]{0:T(256)}, u32[]{:S(2)}) copy-start(f32[256]{0:T(256)} %param.18) | copy-start | bytes 3076
  10.4 4.5 %copy-start.1 = (bf16[1,8,32,256]{3,2,1,0:T(8,128)(2,1)S(1)}, bf16[1,8,32,256]{3,2,1,0:T(8,128)(2,1)}, u32[]{:S(2)}) copy-start(bf16[1,8,32,256]{3,2,1,0:T(8,128)(2,1)} %param.13) | copy-start | bytes 393220
  10.4 4.5 %copy-start.3 = (bf16[1,8,32,256]{3,2,1,0:T(8,128)(2,1)S(1)}, bf16[1,8,32,256]{3,2,1,0:T(8,128)(2,1)}, u32[]{:S(2)}) copy-start(bf16[1,8,32,256]{3,2,1,0:T(8,128)(2,1)} %param.14) | copy-start | bytes 393220
  10.5 8.3 %collective-permute-start.6 = (bf16[16,2048]{1,0:T(8,128)(2,1)S(1)}, bf16[16,2048]{1,0:T(8,128)(2,1)S(1)}, u32[]{:S(2)}, u32[]{:S(2)}) collective-permute-start(bf16[16,2048]{1,0:T(8,128)(2,1)S(1)} %get-tuple-element.47), channel_id=1, source_target_pairs={{0,12},{4,8},{8,4},{12,0},{1,13},{5,9},{9,5},{13,1},{2,14},{6,10},... | collective-permute-start | bytes 196616 | tf_op jit(solution)/shard_map/ppermute | solution.py:521
  11.9 6.9 %collective-permute-start.5 = (bf16[16,2048]{1,0:T(8,128)(2,1)S(1)}, bf16[16,2048]{1,0:T(8,128)(2,1)S(1)}, u32[]{:S(2)}, u32[]{:S(2)}) collective-permute-start(bf16[16,2048]{1,0:T(8,128)(2,1)S(1)} %get-tuple-element.47), channel_id=1, source_target_pairs={{0,8},{4,12},{8,0},{12,4},{1,9},{5,13},{9,1},{13,5},{2,10},{6,14},... | collective-permute-start | bytes 196616 | tf_op jit(solution)/shard_map/ppermute | solution.py:521
  12.0 6.8 %collective-permute-start.4 = (bf16[16,2048]{1,0:T(8,128)(2,1)S(1)}, bf16[16,2048]{1,0:T(8,128)(2,1)S(1)}, u32[]{:S(2)}, u32[]{:S(2)}) collective-permute-start(bf16[16,2048]{1,0:T(8,128)(2,1)S(1)} %get-tuple-element.47), channel_id=1, source_target_pairs={{0,4},{4,0},{8,12},{12,8},{1,5},{5,1},{9,13},{13,9},{2,6},{6,2},{1... | collective-permute-start | bytes 196616 | tf_op jit(solution)/shard_map/ppermute | solution.py:521
  15.1 8.0 %copy-start.4 = (bf16[256,768]{1,0:T(8,128)(2,1)S(1)}, bf16[256,768]{1,0:T(8,128)(2,1)}, u32[]{:S(2)}) copy-start(bf16[256,768]{1,0:T(8,128)(2,1)} %qkv_ref.1) | copy-start | bytes 1179652
  15.1 3.8 %collective-permute-start.2 = (bf16[34,8,256]{2,1,0:T(8,128)(2,1)S(1)}, bf16[34,8,256]{2,1,0:T(8,128)(2,1)S(1)}, u32[]{:S(2)}, u32[]{:S(2)}) collective-permute-start(bf16[34,8,256]{2,1,0:T(8,128)(2,1)S(1)} %get-tuple-element.45), channel_id=1, source_target_pairs={{1,2},{2,1},{5,6},{6,5},{9,10},{10,9},{13,14},{14,13},{17,18},{18,... | collective-permute-start | bytes 417800 | tf_op jit(solution)/shard_map/ppermute | solution.py:516
  15.9 3.9 %collective-permute-start.3 = (bf16[34,8,256]{2,1,0:T(8,128)(2,1)S(1)}, bf16[34,8,256]{2,1,0:T(8,128)(2,1)S(1)}, u32[]{:S(2)}, u32[]{:S(2)}) collective-permute-start(bf16[34,8,256]{2,1,0:T(8,128)(2,1)S(1)} %get-tuple-element.46), channel_id=1, source_target_pairs={{0,1},{1,0},{2,3},{3,2},{4,5},{5,4},{6,7},{7,6},{8,9},{9,8},{10,11... | collective-permute-start | bytes 417800 | tf_op jit(solution)/shard_map/ppermute | solution.py:517
  18.8 4.3 %copy-start.6 = (bf16[256,256]{1,0:T(8,128)(2,1)S(1)}, bf16[256,256]{1,0:T(8,128)(2,1)}, u32[]{:S(2)}) copy-start(bf16[256,256]{1,0:T(8,128)(2,1)} %out_ref.1) | copy-start | bytes 393220
  19.8 9.9 %collective-permute-start.8 = (bf16[4,16,2048]{2,1,0:T(8,128)(2,1)S(1)}, bf16[4,16,2048]{2,1,0:T(8,128)(2,1)S(1)}, u32[]{:S(2)}, u32[]{:S(2)}) collective-permute-start(bf16[4,16,2048]{2,1,0:T(8,128)(2,1)S(1)} %pad_maximum_fusion.1), channel_id=1, source_target_pairs={{0,2},{1,3},{2,0},{3,1},{4,6},{5,7},{6,4},{7,5},{8,10},{9,11},{10,... | collective-permute-start | bytes 786440 | tf_op jit(solution)/shard_map/ppermute | solution.py:521
  29.3 1.5 %collective-permute-start.7 = (bf16[2,4,16,1024]{3,2,1,0:T(8,128)(2,1)S(1)}, bf16[2,4,16,1024]{3,2,1,0:T(8,128)(2,1)S(1)}, u32[]{:S(2)}, u32[]{:S(2)}) collective-permute-start(bf16[2,4,16,1024]{3,2,1,0:T(8,128)(2,1)S(1)} %get-tuple-element.53), channel_id=1, source_target_pairs={{0,1},{1,0},{2,3},{3,2},{4,5},{5,4},{6,7},{7,6},{8,9},{9,8},{10,11... | collective-permute-start | bytes 786440 | tf_op jit(solution)/shard_map/ppermute | solution.py:521
  29.7 1.5 %collective-permute-start.9 = (bf16[4,16,2048]{2,1,0:T(8,128)(2,1)S(1)}, bf16[4,16,2048]{2,1,0:T(8,128)(2,1)S(1)}, u32[]{:S(2)}, u32[]{:S(2)}) collective-permute-start(bf16[4,16,2048]{2,1,0:T(8,128)(2,1)S(1)} %collective-permute-done.8), channel_id=1, source_target_pairs={{0,1},{1,0},{2,3},{3,2},{4,5},{5,4},{6,7},{7,6},{8,9},{9,8},{10,11... | collective-permute-start | bytes 786440 | tf_op jit(solution)/shard_map/ppermute | solution.py:521
  29.8 1.8 %collective-permute-start.11 = (bf16[4,16,2048]{2,1,0:T(8,128)(2,1)S(1)}, bf16[4,16,2048]{2,1,0:T(8,128)(2,1)S(1)}, u32[]{:S(2)}, u32[]{:S(2)}) collective-permute-start(bf16[4,16,2048]{2,1,0:T(8,128)(2,1)S(1)} %pad_maximum_fusion.1), channel_id=1, source_target_pairs={{0,1},{1,0},{2,3},{3,2},{4,5},{5,4},{6,7},{7,6},{8,9},{9,8},{10,11... | collective-permute-start | bytes 786440 | tf_op jit(solution)/shard_map/ppermute | solution.py:521
  31.2 5.6 %collective-permute-start.10 = (bf16[4,16,1024]{2,1,0:T(8,128)(2,1)S(1)}, bf16[4,16,1024]{2,1,0:T(8,128)(2,1)S(1)}, u32[]{:S(2)}, u32[]{:S(2)}) collective-permute-start(bf16[4,16,1024]{2,1,0:T(8,128)(2,1)S(1)} %fusion.2), channel_id=1, source_target_pairs={{0,2},{1,3},{2,0},{3,1},{4,6},{5,7},{6,4},{7,5},{8,10},{9,11},{10,... | collective-permute-start | bytes 393224 | tf_op jit(solution)/shard_map/ppermute | solution.py:521
  31.7 1.0 %copy-start.5 = (bf16[3,64,1024]{2,1,0:T(8,128)(2,1)S(1)}, bf16[3,64,1024]{2,1,0:T(8,128)(2,1)}, u32[]{:S(2)}) copy-start(bf16[3,64,1024]{2,1,0:T(8,128)(2,1)} %qkv_hbm.1) | copy-start | bytes 1179652
  31.7 1.0 %copy-start.7 = (bf16[64,1024]{1,0:T(8,128)(2,1)S(1)}, bf16[64,1024]{1,0:T(8,128)(2,1)}, u32[]{:S(2)}) copy-start(bf16[64,1024]{1,0:T(8,128)(2,1)} %out_hbm.1) | copy-start | bytes 393220
  36.9 5.0 %collective-permute-start.12 = (bf16[4,16,1024]{2,1,0:T(8,128)(2,1)S(1)}, bf16[4,16,1024]{2,1,0:T(8,128)(2,1)S(1)}, u32[]{:S(2)}, u32[]{:S(2)}) collective-permute-start(bf16[4,16,1024]{2,1,0:T(8,128)(2,1)S(1)} %fusion.1), channel_id=1, source_target_pairs={{0,16},{16,0},{1,17},{17,1},{2,18},{18,2},{3,19},{19,3},{4,20},{20... | collective-permute-start | bytes 393224 | tf_op jit(solution)/shard_map/ppermute | solution.py:521
  38.5 3.5 %collective-permute-start.13 = (bf16[2,4,16,1024]{3,2,1,0:T(8,128)(2,1)S(1)}, bf16[2,4,16,1024]{3,2,1,0:T(8,128)(2,1)S(1)}, u32[]{:S(2)}, u32[]{:S(2)}) collective-permute-start(bf16[2,4,16,1024]{3,2,1,0:T(8,128)(2,1)S(1)} %bitcast.76), channel_id=1, source_target_pairs={{0,1},{1,0},{2,3},{3,2},{4,5},{5,4},{6,7},{7,6},{8,9},{9,8},{10,11... | collective-permute-start | bytes 786440 | tf_op jit(solution)/shard_map/ppermute | solution.py:521
  42.1 6.5 %collective-permute-start.14 = (bf16[128,1024]{1,0:T(8,128)(2,1)S(1)}, bf16[128,1024]{1,0:T(8,128)(2,1)S(1)}, u32[]{:S(2)}, u32[]{:S(2)}) collective-permute-start(bf16[128,1024]{1,0:T(8,128)(2,1)S(1)} %pad_maximum_fusion.2), channel_id=1, source_target_pairs={{0,4},{4,0},{8,12},{12,8},{1,5},{5,1},{9,13},{13,9},{2,6},{6,2},{1... | collective-permute-start | bytes 786440 | tf_op jit(solution)/shard_map/ppermute | solution.py:521
  42.2 6.5 %collective-permute-start.15 = (bf16[128,1024]{1,0:T(8,128)(2,1)S(1)}, bf16[128,1024]{1,0:T(8,128)(2,1)S(1)}, u32[]{:S(2)}, u32[]{:S(2)}) collective-permute-start(bf16[128,1024]{1,0:T(8,128)(2,1)S(1)} %get-tuple-element.83), channel_id=1, source_target_pairs={{0,16},{16,0},{1,17},{17,1},{2,18},{18,2},{3,19},{19,3},{4,20},{20... | collective-permute-start | bytes 786440 | tf_op jit(solution)/shard_map/ppermute | solution.py:521
  48.8 9.3 %collective-permute-start.16 = (bf16[96,1024]{1,0:T(8,128)(2,1)S(1)}, bf16[96,1024]{1,0:T(8,128)(2,1)S(1)}, u32[]{:S(2)}, u32[]{:S(2)}) collective-permute-start(bf16[96,1024]{1,0:T(8,128)(2,1)S(1)} %pad_maximum_fusion.4), channel_id=1, source_target_pairs={{0,8},{4,12},{8,0},{12,4},{1,9},{5,13},{9,1},{13,5},{2,10},{6,14},... | collective-permute-start | bytes 589832 | tf_op jit(solution)/shard_map/ppermute | solution.py:521
  50.6 7.6 %collective-permute-start.17 = (bf16[128,1024]{1,0:T(8,128)(2,1)S(1)}, bf16[128,1024]{1,0:T(8,128)(2,1)S(1)}, u32[]{:S(2)}, u32[]{:S(2)}) collective-permute-start(bf16[128,1024]{1,0:T(8,128)(2,1)S(1)} %get-tuple-element.82), channel_id=1, source_target_pairs={{0,16},{16,0},{1,17},{17,1},{2,18},{18,2},{3,19},{19,3},{4,20},{20... | collective-permute-start | bytes 786440 | tf_op jit(solution)/shard_map/ppermute | solution.py:521
  58.2 5.4 %collective-permute-start.18 = (bf16[80,1024]{1,0:T(8,128)(2,1)S(1)}, bf16[80,1024]{1,0:T(8,128)(2,1)S(1)}, u32[]{:S(2)}, u32[]{:S(2)}) collective-permute-start(bf16[80,1024]{1,0:T(8,128)(2,1)S(1)} %pad_maximum_fusion.5), channel_id=1, source_target_pairs={{0,2},{1,3},{2,0},{3,1},{4,6},{5,7},{6,4},{7,5},{8,10},{9,11},{10,... | collective-permute-start | bytes 491528 | tf_op jit(solution)/shard_map/ppermute | solution.py:521
  63.7 1.6 %collective-permute-start.19 = (bf16[2,64,1024]{2,1,0:T(8,128)(2,1)S(1)}, bf16[2,64,1024]{2,1,0:T(8,128)(2,1)S(1)}, u32[]{:S(2)}, u32[]{:S(2)}) collective-permute-start(bf16[2,64,1024]{2,1,0:T(8,128)(2,1)S(1)} %pad_maximum_fusion.3.near_ref), channel_id=1, source_target_pairs={{0,1},{1,0},{2,3},{3,2},{4,5},{5,4},{6,7},{7,6},{8,9},{9,8},{10,11... | collective-permute-start | bytes 786440 | tf_op jit(solution)/shard_map/ppermute | solution.py:521

commit v7 on v6

--- a/solution.py
+++ b/solution.py
@@ -381,66 +381,58 @@
     )(picture, cotangent, row_far, row_near)
 
 
-def pack_body(
-    first,
-    second,
-    step,
-    x_ref,
-    dy_ref,
-    fine_gain,
-    coarse_gain,
-    fine_freq,
-    coarse_freq,
-    own_ref,
-    fine_ref,
-    coarse_ref,
-):
+def pack_body(first, second, x_ref, dy_ref, own_ref):
     own_ref[:, :D_C] = x_ref[...].astype(jnp.float32).reshape(-1, D_C).astype(jnp.bfloat16)
     own_ref[:, D_C:] = dy_ref[...].astype(jnp.float32).reshape(-1, D_C).astype(jnp.bfloat16)
+
+
+def packed(after, tokens, cotangents):
+    vmem = pl.BlockSpec(memory_space=pltpu.VMEM)
+    count = tokens.shape[0] * tokens.shape[1]
+    return pl.pallas_call(
+        pack_body,
+        out_shape=jax.ShapeDtypeStruct((count, 2 * D_C), jnp.bfloat16),
+        in_specs=[pl.BlockSpec(memory_space=pl.ANY)] * 2 + [vmem] * 2,
+        out_specs=vmem,
+        compiler_params=pltpu.CompilerParams(vmem_limit_bytes=vmem_bytes),
+        name="pack_coarse",
+    )(*after, tokens, cotangents)
+
+
+def factors_body(step, fine_gain, coarse_gain, fine_freq, coarse_freq, fine_ref, coarse_ref):
     time = step[0].astype(jnp.float32)
     fine_ref[...] = fine_gain[...] * (1.0 + 0.5 * jnp.cos(time * fine_freq[...]))
     coarse_ref[...] = coarse_gain[...] * (1.0 + 0.5 * jnp.cos(time * coarse_freq[...]))
 
 
-def packed(after, step, tokens, cotangents, fine_gain, coarse_gain):
-    vmem = pl.BlockSpec(memory_space=pltpu.VMEM)
-    count = tokens.shape[0] * tokens.shape[1]
-    return pl.pallas_call(
-        pack_body,
+def time_factors(step, fine_gain, coarse_gain):
+    vmem = pl.BlockSpec(memory_space=pltpu.VMEM)
+    return pl.pallas_call(
+        factors_body,
         out_shape=(
-            jax.ShapeDtypeStruct((count, 2 * D_C), jnp.bfloat16),
             jax.ShapeDtypeStruct((1, D_F), jnp.float32),
             jax.ShapeDtypeStruct((1, D_C), jnp.float32),
         ),
-        in_specs=[pl.BlockSpec(memory_space=pl.ANY)] * 2
-        + [pl.BlockSpec(memory_space=pltpu.SMEM)]
-        + [vmem] * 6,
-        out_specs=(vmem, vmem, vmem),
-        compiler_params=pltpu.CompilerParams(vmem_limit_bytes=vmem_bytes),
-        name="pack_coarse",
-    )(
-        *after,
-        step,
-        tokens,
-        cotangents,
-        fine_gain[None],
-        coarse_gain[None],
-        frequencies(D_F),
-        frequencies(D_C),
-    )
-
-
-def pair_sum_body(own, first, second, qkv_ref, out_ref):
+        in_specs=[pl.BlockSpec(memory_space=pltpu.SMEM)] + [vmem] * 4,
+        out_specs=(vmem, vmem),
+        compiler_params=pltpu.CompilerParams(vmem_limit_bytes=vmem_bytes),
+        name="time_factors",
+    )(step, fine_gain[None], coarse_gain[None], frequencies(D_F), frequencies(D_C))
+
+
+def pair_sum_body(own, *refs):
+    qkv_ref, out_ref = refs[-2:]
+    come = jnp.concatenate([ref[...] for ref in refs[:-2]], axis=0)
     for part in range(4):
-        come = (first, second)[part // 2][(part % 2) * HD : (part % 2 + 1) * HD]
-        total = own[part * HD : (part + 1) * HD].astype(jnp.float32) + come.astype(jnp.float32)
+        rows = slice(part * HD, (part + 1) * HD)
+        total = own[rows].astype(jnp.float32) + come[rows].astype(jnp.float32)
         if part < 3:
             qkv_ref[part] = total.astype(jnp.bfloat16)
         else:
             out_ref[...] = total.astype(jnp.bfloat16)
 
 
-def pair_sum(own, first, second):
+def pair_sum(own, *come):
     vmem = pl.BlockSpec(memory_space=pltpu.VMEM)
     return pl.pallas_call(
         pair_sum_body,
@@ -448,11 +440,11 @@
             jax.ShapeDtypeStruct((3, HD, D_C), jnp.bfloat16),
             jax.ShapeDtypeStruct((HD, D_C), jnp.bfloat16),
         ),
-        in_specs=[vmem] * 3,
+        in_specs=[vmem] * (1 + len(come)),
         out_specs=(vmem, vmem),
         compiler_params=pltpu.CompilerParams(vmem_limit_bytes=vmem_bytes),
         name="pair_sum",
-    )(own, first, second)
+    )(own, *come)
 
 
 def last_body(
@@ -544,6 +536,13 @@
     return jnp.stack([piece] + [swapped(piece, "gy", row) for row in range(1, downs)])
 
 
+def row_halved(kept, mask):
+    columns, count = kept.shape[0], kept.shape[-2]
+    kept = kept.reshape(columns, -1, 2, count, D_C)
+    come = swapped(narrow(kept[:, :, 1]), "gy", mask)
+    return kept[:, :, 0] + wide(come)
+
+
 def local(
     x_fine,
     dy_fine,
@@ -563,14 +562,14 @@
 
     payloads = row_edges(picture, cotangent)
     row_near, row_far = neighbours(*payloads, "gy")
-    own, factor, coarse_factor = packed(
-        payloads, timestep, x_coarse[0], dy_coarse[0], fine_gain, coarse_gain
-    )
+    own = packed(payloads, x_coarse[0], dy_coarse[0])
     count = own.shape[0]
     row_group = all_rows(own)
     edges = col_edges(picture, cotangent, row_far, row_near)
+    *edges, step, gain_f, gain_c = tied(*edges, timestep, fine_gain, coarse_gain)
     col_near, col_far = neighbours(*edges, "gx")
-    col_far, col_near, row_group = tied(col_far, col_near, row_group)
+    factor, coarse_factor = time_factors(step, gain_f, gain_c)
+    col_far, col_near, row_group, factor = tied(col_far, col_near, row_group, factor)
     cross = swapped(row_group, "gx", 2)
     beside = swapped(row_group, "gx", 1)
     dx_picture, fine_keep, fine_send = fine_block(
@@ -594,29 +593,34 @@
     parts, coarse_partial = coarse_block(
         everyone[:, :D_C], everyone[:, D_C:], coarse_factor, coarse_qkv, coarse_out
     )
-    fine_quarter, parts, coarse_partial = tied(fine_quarter, parts, coarse_partial)
-
-    rows = D_F // across
-    fine_quarter = narrow(batch_sum(fine_quarter)).reshape(rows, 4 * D_F)
     parts = parts.reshape(2, 2, downs, count, D_C)
     coarse_kept = wide(parts[0]) + wide(swapped(parts[1], "gx", 1))
     fine_quarter, coarse_kept, coarse_partial = tied(fine_quarter, coarse_kept, coarse_partial)
 
+    rows = D_F // across
+    fine_quarter = narrow(batch_sum(fine_quarter)).reshape(rows, 4 * D_F)
+    masks = [1 << bit for bit in range(downs.bit_length() - 1)]
+    coarse_kept = row_halved(coarse_kept, masks[0])
+    fine_quarter, coarse_kept, coarse_partial = tied(fine_quarter, coarse_kept, coarse_partial)
+
     pair_batch = lax.axis_size("batch") == 2
-    halves = (coarse_partial[: 2 * HD], coarse_partial[2 * HD :])
+    cut = 5 * HD // 4
+    halves = (coarse_partial[:cut], coarse_partial[cut:])
     others = [swapped(half, "batch", 1) if pair_batch else half for half in halves]
-    mask = 1
-    while mask < downs:
-        last = 2 * mask == downs
-        coarse_kept = coarse_kept.reshape(2, -1, 2, count, D_C)
-        sent = narrow(coarse_kept[:, :, 1]).reshape(-1, D_C)
-        come = swapped(jnp.concatenate([fine_quarter, sent], axis=0), "gy", mask)
-        coarse_kept = coarse_kept[:, :, 0]
-        coarse_kept = coarse_kept + wide(come[rows:]).reshape(coarse_kept.shape)
+    for turn, mask in enumerate(masks):
+        last = turn + 1 == len(masks)
+        sent = fine_quarter
+        if turn:
+            coarse_kept = coarse_kept.reshape(2, -1, 2, count, D_C)
+            extra = narrow(coarse_kept[:, :, 1]).reshape(-1, D_C)
+            sent = jnp.concatenate([fine_quarter, extra], axis=0)
+        come = swapped(sent, "gy", mask)
         fine_quarter = narrow(wide(fine_quarter) + wide(come[:rows]))
+        if turn:
+            coarse_kept = coarse_kept[:, :, 0]
+            coarse_kept = coarse_kept + wide(come[rows:]).reshape(coarse_kept.shape)
         at = int(last)
         fine_quarter, coarse_kept, others[at] = tied(fine_quarter, coarse_kept, others[at])
-        mask *= 2
 
     coarse_kept = coarse_kept.reshape(2, count, D_C)
     come = swapped(jnp.concatenate([fine_quarter, narrow(coarse_kept[1])], axis=0), "gx", 2)

time: 67 us -> 68.3 us (1.019)
  starting transfers between devices: 26.1 us -> 28.6 us
  waiting for transfers between devices: 23.9 us -> 22.7 us
    ppermute x16 -> x17, starting transfers between devices: 15.8 us -> 18.3 us  [swapped(): lax.ppermute(value, axis, [(i, i ^ mask) for i in range(lax.axis_size(axi...]
    ppermute x2, waiting for transfers between devices: 0.92 us -> 0.11 us  [neighbours(): return (lax.ppermute(to_near, axis, near), from_far)]
    ppermute x16 -> x17, waiting for transfers between devices: 22.9 us -> 22.6 us  [swapped(): lax.ppermute(value, axis, [(i, i ^ mask) for i in range(lax.axis_size(axi...]
  transfers between devices with their start and end apart: 20 -> 21, of which waited for: 10 -> 12; matrix products, arithmetic and copies ran while one was open for 1% -> 1% of each run, Pallas kernels for 14% -> 14%
where the time goes in v7:
time: 68.3 us; the launch traced here: 68.1 us
  starting transfers between devices  28.6 us (42%)
  waiting for transfers between devices  22.7 us (33%)
  Pallas kernels  10.9 us (16%)
  local copies, waits for them, and re-layouts  3.69 us (5%)
  between operations  1.63 us (2%)
    ppermute x17, waiting for transfers between devices, swapped(): lax.ppermute(value, axis, [(i, i ^ mask) for i in range(lax.axis_size(axi...  22.6 us
    ppermute x17, starting transfers between devices, swapped(): lax.ppermute(value, axis, [(i, i ^ mask) for i in range(lax.axis_size(axi...  18.3 us
    ppermute x2, starting transfers between devices, neighbours(): return (lax.ppermute(to_near, axis, near), from_far)  8.81 us
    pallas_call x1, Pallas kernels, fine_block(): pl.pallas_call(fine_body, out_shape=(jax.ShapeDtypeStruct((height, breadt...  6.17 us
    unnamed x28, local copies, waits for them, and re-layouts  3.47 us
    pallas_call x1, Pallas kernels, coarse_block(): pl.pallas_call(coarse_body, out_shape=(jax.ShapeDtypeStruct((count, D_C),...  2.23 us
    pallas_call x1, Pallas kernels, last_step(): pl.pallas_call(last_body, out_shape=(jax.ShapeDtypeStruct((D_F, 3 * D_F),...  1.48 us
    ppermute x2, starting transfers between devices, neighbours(): from_far = lax.ppermute(to_far, axis, far)  1.47 us
  transfers between devices with their start and end apart: 21, of which 12 were waited for; matrix products, arithmetic and copies ran while one was open for 1% of the time, Pallas kernels for 14%

profile of v7, /device:TPU:0, one launch (start us, length us, event | category | flops | bytes accessed | tf_op | source)
XLA Modules:
  0.0 68.1 jit_solution(17419384375670691418)
XLA Ops:
  0.6 0.0 copy-start
  0.6 0.9 %copy-done = bf16[1,8,32,256]{3,2,1,0:T(8,128)(2,1)S(1)} copy-done((bf16[1,8,32,256]{3,2,1,0:T(8,128)(2,1)S(1)}, bf16[1,8,32,256]{3,2,1,0:T(8,128)(2,1)}, u32[]{:S(2)}) %copy-start) | copy-done | bytes 131096
  1.5 0.9 %copy-done.2 = bf16[1,8,32,256]{3,2,1,0:T(8,128)(2,1)S(1)} copy-done((bf16[1,8,32,256]{3,2,1,0:T(8,128)(2,1)S(1)}, bf16[1,8,32,256]{3,2,1,0:T(8,128)(2,1)}, u32[]{:S(2)}) %copy-start.2) | copy-done | bytes 131096
  2.5 0.7 collective-permute-start
  3.1 5.9 %collective-permute-start.1 = (bf16[9,32,256]{2,1,0:T(8,128)(2,1)S(1)}, bf16[9,32,256]{2,1,0:T(8,128)(2,1)S(1)}, u32[]{:S(2)}, u32[]{:S(2)}) collective-permute-start(bf16[9,32,256]{2,1,0:T(8,128)(2,1)S(1)} %get-tuple-element.49.first), channel_id=1, source_target_pairs={{0,4},{4,0},{8,12},{12,8},{1,5},{5,1},{9,13},{13,9},{2,6},{6,2},{1... | collective-permute-start | bytes 442376 | tf_op jit(solution)/shard_map/ppermute | solution.py:509
  9.1 1.4 %collective-permute-start.6 = (bf16[16,2048]{1,0:T(8,128)(2,1)S(1)}, bf16[16,2048]{1,0:T(8,128)(2,1)S(1)}, u32[]{:S(2)}, u32[]{:S(2)}) collective-permute-start(bf16[16,2048]{1,0:T(8,128)(2,1)S(1)} %pack_coarse.1), channel_id=1, source_target_pairs={{0,12},{4,8},{8,4},{12,0},{1,13},{5,9},{9,5},{13,1},{2,14},{6,10},... | collective-permute-start | bytes 196616 | tf_op jit(solution)/shard_map/ppermute | solution.py:513
  10.5 0.2 collective-permute-start.5
  10.7 2.9 %collective-permute-start.4 = (bf16[16,2048]{1,0:T(8,128)(2,1)S(1)}, bf16[16,2048]{1,0:T(8,128)(2,1)S(1)}, u32[]{:S(2)}, u32[]{:S(2)}) collective-permute-start(bf16[16,2048]{1,0:T(8,128)(2,1)S(1)} %pack_coarse.1), channel_id=1, source_target_pairs={{0,4},{4,0},{8,12},{12,8},{1,5},{5,1},{9,13},{13,9},{2,6},{6,2},{1... | collective-permute-start | bytes 196616 | tf_op jit(solution)/shard_map/ppermute | solution.py:513
  14.2 0.0 collective-permute-done.row_far_ref
  14.2 0.1 col_edges.1
  14.3 0.0 copy-start.4
  14.3 0.8 %collective-permute-start.2 = (bf16[34,8,256]{2,1,0:T(8,128)(2,1)S(1)}, bf16[34,8,256]{2,1,0:T(8,128)(2,1)S(1)}, u32[]{:S(2)}, u32[]{:S(2)}) collective-permute-start(bf16[34,8,256]{2,1,0:T(8,128)(2,1)S(1)} %get-tuple-element.52), channel_id=1, source_target_pairs={{1,2},{2,1},{5,6},{6,5},{9,10},{10,9},{13,14},{14,13},{17,18},{18,... | collective-permute-start | bytes 417800 | tf_op jit(solution)/shard_map/ppermute | solution.py:508
  15.1 2.9 %collective-permute-start.3 = (bf16[34,8,256]{2,1,0:T(8,128)(2,1)S(1)}, bf16[34,8,256]{2,1,0:T(8,128)(2,1)S(1)}, u32[]{:S(2)}, u32[]{:S(2)}) collective-permute-start(bf16[34,8,256]{2,1,0:T(8,128)(2,1)S(1)} %get-tuple-element.53), channel_id=1, source_target_pairs={{0,1},{1,0},{2,3},{3,2},{4,5},{5,4},{6,7},{7,6},{8,9},{9,8},{10,11... | collective-permute-start | bytes 417800 | tf_op jit(solution)/shard_map/ppermute | solution.py:509
  18.1 0.0 collective-permute-done.6
  18.1 0.0 collective-permute-done.5
  18.1 0.0 collective-permute-done.4
  18.1 0.0 copy-start.10
  18.1 0.0 copy-start.11
  18.1 0.0 copy-start.13
  18.1 0.0 copy-start.6
  18.2 0.0 copy-start.12
  18.2 0.6 copy-done.10
  18.8 0.0 copy-done.11
  18.8 0.0 copy-done.13
  18.8 0.1 copy-done.12
  18.9 0.1 time_factors.1
  18.9 0.1 collective-permute-done.3.col_near_ref
  19.1 3.3 %collective-permute-start.8 = (bf16[4,16,2048]{2,1,0:T(8,128)(2,1)S(1)}, bf16[4,16,2048]{2,1,0:T(8,128)(2,1)S(1)}, u32[]{:S(2)}, u32[]{:S(2)}) collective-permute-start(bf16[4,16,2048]{2,1,0:T(8,128)(2,1)S(1)} %pad_maximum_fusion.1), channel_id=1, source_target_pairs={{0,2},{1,3},{2,0},{3,1},{4,6},{5,7},{6,4},{7,5},{8,10},{9,11},{10,... | collective-permute-start | bytes 786440 | tf_op jit(solution)/shard_map/ppermute | solution.py:513
  22.3 6.2 %fine_block.1 = (bf16[8,32,256]{2,1,0:T(8,128)(2,1)}, f32[2,4,16,1024]{3,2,1,0:T(8,128)S(1)}, bf16[2,4,16,1024]{3,2,1,0:T(8,128)(2,1)S(1)}) custom-call(bf16[8,32,256]{2,1,0:T(8,128)(2,1)S(1)} %bitcast.51, bf16[8,32,256]{2,1,0:T(8,128)(2,1)S(1)} %bitcast.54, bf16[9,32,256]{2,1,0:T(8,128)(2,1)S(1)} %collective-permute-done.row_far_ref, ...), custom_call_target="tpu_custom_call" | custom-call | tf_op jit(solution)/shard_map/fine_block/pallas_call | solution.py:233
  28.5 0.4 collective-permute-done.8
  28.9 0.1 collective-permute-start.9
  29.0 0.4 collective-permute-start.11
  29.4 0.6 collective-permute-done.7
  30.1 0.1 convert_add_fusion.1
  30.1 0.3 collective-permute-done.9
  30.5 0.3 collective-permute-start.10
  30.8 0.0 collective-permute-done.11
  30.8 0.1 pad_maximum_fusion
  31.0 0.0 copy-start.5
  31.0 0.0 copy-start.7
  31.0 0.1 fusion.6
  31.1 0.9 %copy-done.5 = bf16[3,64,1024]{2,1,0:T(8,128)(2,1)S(1)} copy-done((bf16[3,64,1024]{2,1,0:T(8,128)(2,1)S(1)}, bf16[3,64,1024]{2,1,0:T(8,128)(2,1)}, u32[]{:S(2)}) %copy-start.5) | copy-done | bytes 393240
  32.0 0.0 copy-done.7
  32.0 2.2 %coarse_block.1 = (bf16[256,1024]{1,0:T(8,128)(2,1)S(1)}, bf16[256,1024]{1,0:T(8,128)(2,1)S(1)}) custom-call(bf16[256,1024]{1,0:T(8,128)(2,1)S(1)} %get-tuple-element.91.x_ref, bf16[256,1024]{1,0:T(8,128)(2,1)S(1)} %get-tuple-element.90.dy_ref, f32[1,1024]{1,0:T(1,128)S(1)} %get-tuple-element.67.factor_ref, bf16[3,64,1024]{2,1,0:T(8,128)(2,1)S(1)} %copy-done.5, ...), custom_call_target="tpu_custom_call" | custom-call | tf_op jit(solution)/shard_map/coarse_block/pallas_call | solution.py:309
  34.3 0.2 collective-permute-start.12
  34.5 1.6 %collective-permute-done.10 = bf16[4,16,1024]{2,1,0:T(8,128)(2,1)S(1)} collective-permute-done((bf16[4,16,1024]{2,1,0:T(8,128)(2,1)S(1)}, bf16[4,16,1024]{2,1,0:T(8,128)(2,1)S(1)}, u32[]{:S(2)}, u32[]{:S(2)}) %collective-permute-start.10) | collective-permute-done | bytes 131104 | tf_op jit(solution)/shard_map/ppermute | solution.py:513
  36.1 0.1 convert_add_fusion
  36.2 1.6 %collective-permute-start.13 = (bf16[4,16,1024]{2,1,0:T(8,128)(2,1)S(1)}, bf16[4,16,1024]{2,1,0:T(8,128)(2,1)S(1)}, u32[]{:S(2)}, u32[]{:S(2)}) collective-permute-start(bf16[4,16,1024]{2,1,0:T(8,128)(2,1)S(1)} %fusion.1), channel_id=1, source_target_pairs={{0,16},{16,0},{1,17},{17,1},{2,18},{18,2},{3,19},{19,3},{4,20},{20... | collective-permute-start | bytes 393224 | tf_op jit(solution)/shard_map/ppermute | solution.py:513
  37.8 1.7 %collective-permute-start.14 = (bf16[2,2,16,1024]{3,2,0,1:T(8,128)(2,1)S(1)}, bf16[2,2,16,1024]{3,2,0,1:T(8,128)(2,1)S(1)}, u32[]{:S(2)}, u32[]{:S(2)}) collective-permute-start(bf16[2,2,16,1024]{3,2,0,1:T(8,128)(2,1)S(1)} %fusion.3), channel_id=1, source_target_pairs={{0,4},{4,0},{8,12},{12,8},{1,5},{5,1},{9,13},{13,9},{2,6},{6,2},{1... | collective-permute-start | bytes 393224 | tf_op jit(solution)/shard_map/ppermute | solution.py:513
  39.5 2.1 %collective-permute-done.13 = bf16[4,16,1024]{2,1,0:T(8,128)(2,1)S(1)} collective-permute-done((bf16[4,16,1024]{2,1,0:T(8,128)(2,1)S(1)}, bf16[4,16,1024]{2,1,0:T(8,128)(2,1)S(1)}, u32[]{:S(2)}, u32[]{:S(2)}) %collective-permute-start.13) | collective-permute-done | bytes 131104 | tf_op jit(solution)/shard_map/ppermute | solution.py:513
  41.6 1.3 %collective-permute-done.14 = bf16[2,2,16,1024]{3,2,0,1:T(8,128)(2,1)S(1)} collective-permute-done((bf16[2,2,16,1024]{3,2,0,1:T(8,128)(2,1)S(1)}, bf16[2,2,16,1024]{3,2,0,1:T(8,128)(2,1)S(1)}, u32[]{:S(2)}, u32[]{:S(2)}) %collective-permute-start.14) | collective-permute-done | bytes 131104 | tf_op jit(solution)/shard_map/ppermute | solution.py:513
  42.9 1.7 %collective-permute-start.15 = (bf16[64,1024]{1,0:T(8,128)(2,1)S(1)}, bf16[64,1024]{1,0:T(8,128)(2,1)S(1)}, u32[]{:S(2)}, u32[]{:S(2)}) collective-permute-start(bf16[64,1024]{1,0:T(8,128)(2,1)S(1)} %bitcast.69), channel_id=1, source_target_pairs={{0,4},{4,0},{8,12},{12,8},{1,5},{5,1},{9,13},{13,9},{2,6},{6,2},{1... | collective-permute-start | bytes 393224 | tf_op jit(solution)/shard_map/ppermute | solution.py:513
  44.6 0.6 collective-permute-start.16
  45.2 2.8 %collective-permute-done.15 = bf16[64,1024]{1,0:T(8,128)(2,1)S(1)} collective-permute-done((bf16[64,1024]{1,0:T(8,128)(2,1)S(1)}, bf16[64,1024]{1,0:T(8,128)(2,1)S(1)}, u32[]{:S(2)}, u32[]{:S(2)}) %collective-permute-start.15) | collective-permute-done | bytes 131104 | tf_op jit(solution)/shard_map/ppermute | solution.py:513
  48.0 2.0 %collective-permute-done.16.refs_0_ = bf16[80,1024]{1,0:T(8,128)(2,1)S(1)} collective-permute-done((bf16[80,1024]{1,0:T(8,128)(2,1)S(1)}, bf16[80,1024]{1,0:T(8,128)(2,1)S(1)}, u32[]{:S(2)}, u32[]{:S(2)}) %collective-permute-start.16) | collective-permute-done | bytes 163872 | tf_op jit(solution)/shard_map/ppermute | solution.py:513
  50.0 1.0 %collective-permute-start.17 = (bf16[96,1024]{1,0:T(8,128)(2,1)S(1)}, bf16[96,1024]{1,0:T(8,128)(2,1)S(1)}, u32[]{:S(2)}, u32[]{:S(2)}) collective-permute-start(bf16[96,1024]{1,0:T(8,128)(2,1)S(1)} %pad_maximum_fusion.3), channel_id=1, source_target_pairs={{0,8},{4,12},{8,0},{12,4},{1,9},{5,13},{9,1},{13,5},{2,10},{6,14},... | collective-permute-start | bytes 589832 | tf_op jit(solution)/shard_map/ppermute | solution.py:513
  51.0 0.6 collective-permute-start.18
  51.6 7.5 %collective-permute-done.17 = bf16[96,1024]{1,0:T(8,128)(2,1)S(1)} collective-permute-done((bf16[96,1024]{1,0:T(8,128)(2,1)S(1)}, bf16[96,1024]{1,0:T(8,128)(2,1)S(1)}, u32[]{:S(2)}, u32[]{:S(2)}) %collective-permute-start.17) | collective-permute-done | bytes 196640 | tf_op jit(solution)/shard_map/ppermute | solution.py:513
  59.3 2.4 %collective-permute-start.19 = (bf16[80,1024]{1,0:T(8,128)(2,1)S(1)}, bf16[80,1024]{1,0:T(8,128)(2,1)S(1)}, u32[]{:S(2)}, u32[]{:S(2)}) collective-permute-start(bf16[80,1024]{1,0:T(8,128)(2,1)S(1)} %pad_maximum_fusion.4), channel_id=1, source_target_pairs={{0,2},{1,3},{2,0},{3,1},{4,6},{5,7},{6,4},{7,5},{8,10},{9,11},{10,... | collective-permute-start | bytes 491528 | tf_op jit(solution)/shard_map/ppermute | solution.py:513
  61.6 0.9 %pair_sum.1 = (bf16[3,64,1024]{2,1,0:T(8,128)(2,1)}, bf16[64,1024]{1,0:T(8,128)(2,1)}) custom-call(bf16[256,1024]{1,0:T(8,128)(2,1)S(1)} %get-tuple-element.75.own, bf16[80,1024]{1,0:T(8,128)(2,1)S(1)} %collective-permute-done.16.refs_0_, bf16[176,1024]{1,0:T(8,128)(2,1)S(1)} %collective-permute-done.18.refs_1_), custom_call_target="tpu_custom_call" | custom-call | tf_op jit(solution)/shard_map/pair_sum/pallas_call | solution.py:437
  62.5 2.4 %collective-permute-done.19 = bf16[80,1024]{1,0:T(8,128)(2,1)S(1)} collective-permute-done((bf16[80,1024]{1,0:T(8,128)(2,1)S(1)}, bf16[80,1024]{1,0:T(8,128)(2,1)S(1)}, u32[]{:S(2)}, u32[]{:S(2)}) %collective-permute-start.19) | collective-permute-done | bytes 163872 | tf_op jit(solution)/shard_map/ppermute | solution.py:513
  65.0 0.1 collective-permute-start.20
  65.1 1.5 %collective-permute-done.20.far_ref = bf16[2,64,1024]{2,1,0:T(8,128)(2,1)S(1)} collective-permute-done((bf16[2,64,1024]{2,1,0:T(8,128)(2,1)S(1)}, bf16[2,64,1024]{2,1,0:T(8,128)(2,1)S(1)}, u32[]{:S(2)}, u32[]{:S(2)}) %collective-permute-start.20) | collective-permute-done | bytes 262176 | tf_op jit(solution)/shard_map/ppermute | solution.py:513
  66.6 1.5 %last_step.1 = (bf16[256,768]{1,0:T(8,128)(2,1)}, bf16[256,256]{1,0:T(8,128)(2,1)}, bf16[4,4,1024]{2,1,0:T(4,128)(2,1)}) custom-call(bf16[2,64,1024]{2,1,0:T(8,128)(2,1)S(1)} %pad_maximum_fusion.2.near_ref, bf16[2,64,1024]{2,1,0:T(8,128)(2,1)S(1)} %collective-permute-done.20.far_ref, bf16[4,4,1024]{2,1,0:T(4,128)(2,1)S(1)} %bitcast.57, ...), custom_call_target="tpu_custom_call" | custom-call | tf_op jit(solution)/shard_map/last_step/pallas_call | solution.py:489
  (39 shorter events, 0.5 us)
Async XLA Ops:
  0.6 0.9 %copy-start = (bf16[1,8,32,256]{3,2,1,0:T(8,128)(2,1)S(1)}, bf16[1,8,32,256]{3,2,1,0:T(8,128)(2,1)}, u32[]{:S(2)}) copy-start(bf16[1,8,32,256]{3,2,1,0:T(8,128)(2,1)} %param.13) | copy-start | bytes 393220
  1.5 0.9 %copy-start.2 = (bf16[1,8,32,256]{3,2,1,0:T(8,128)(2,1)S(1)}, bf16[1,8,32,256]{3,2,1,0:T(8,128)(2,1)}, u32[]{:S(2)}) copy-start(bf16[1,8,32,256]{3,2,1,0:T(8,128)(2,1)} %param.14) | copy-start | bytes 393220
  2.4 6.6 %copy-start.8 = (bf16[1,4,4,1024]{3,2,1,0:T(4,128)(2,1)S(1)}, bf16[1,4,4,1024]{3,2,1,0:T(4,128)(2,1)}, u32[]{:S(2)}) copy-start(bf16[1,4,4,1024]{3,2,1,0:T(4,128)(2,1)} %param.15) | copy-start | bytes 98308
  2.4 6.6 %copy-start.9 = (bf16[1,4,4,1024]{3,2,1,0:T(4,128)(2,1)S(1)}, bf16[1,4,4,1024]{3,2,1,0:T(4,128)(2,1)}, u32[]{:S(2)}) copy-start(bf16[1,4,4,1024]{3,2,1,0:T(4,128)(2,1)} %param.16) | copy-start | bytes 98308
  2.5 11.7 %collective-permute-start = (bf16[9,32,256]{2,1,0:T(8,128)(2,1)S(1)}, bf16[9,32,256]{2,1,0:T(8,128)(2,1)S(1)}, u32[]{:S(2)}, u32[]{:S(2)}) collective-permute-start(bf16[9,32,256]{2,1,0:T(8,128)(2,1)S(1)} %get-tuple-element.48.second), channel_id=1, source_target_pairs={{4,8},{8,4},{5,9},{9,5},{6,10},{10,6},{7,11},{11,7},{20,24},{24,20... | collective-permute-start | bytes 442376 | tf_op jit(solution)/shard_map/ppermute | solution.py:508
  3.1 11.1 %collective-permute-start.1 = (bf16[9,32,256]{2,1,0:T(8,128)(2,1)S(1)}, bf16[9,32,256]{2,1,0:T(8,128)(2,1)S(1)}, u32[]{:S(2)}, u32[]{:S(2)}) collective-permute-start(bf16[9,32,256]{2,1,0:T(8,128)(2,1)S(1)} %get-tuple-element.49.first), channel_id=1, source_target_pairs={{0,4},{4,0},{8,12},{12,8},{1,5},{5,1},{9,13},{13,9},{2,6},{6,2},{1... | collective-permute-start | bytes 442376 | tf_op jit(solution)/shard_map/ppermute | solution.py:509
  9.1 5.2 %copy-start.1 = (bf16[1,8,32,256]{3,2,1,0:T(8,128)(2,1)S(1)}, bf16[1,8,32,256]{3,2,1,0:T(8,128)(2,1)}, u32[]{:S(2)}) copy-start(bf16[1,8,32,256]{3,2,1,0:T(8,128)(2,1)} %param.13) | copy-start | bytes 393220
  9.1 5.2 %copy-start.3 = (bf16[1,8,32,256]{3,2,1,0:T(8,128)(2,1)S(1)}, bf16[1,8,32,256]{3,2,1,0:T(8,128)(2,1)}, u32[]{:S(2)}) copy-start(bf16[1,8,32,256]{3,2,1,0:T(8,128)(2,1)} %param.14) | copy-start | bytes 393220
  9.1 9.0 %collective-permute-start.6 = (bf16[16,2048]{1,0:T(8,128)(2,1)S(1)}, bf16[16,2048]{1,0:T(8,128)(2,1)S(1)}, u32[]{:S(2)}, u32[]{:S(2)}) collective-permute-start(bf16[16,2048]{1,0:T(8,128)(2,1)S(1)} %pack_coarse.1), channel_id=1, source_target_pairs={{0,12},{4,8},{8,4},{12,0},{1,13},{5,9},{9,5},{13,1},{2,14},{6,10},... | collective-permute-start | bytes 196616 | tf_op jit(solution)/shard_map/ppermute | solution.py:513
  10.5 7.6 %collective-permute-start.5 = (bf16[16,2048]{1,0:T(8,128)(2,1)S(1)}, bf16[16,2048]{1,0:T(8,128)(2,1)S(1)}, u32[]{:S(2)}, u32[]{:S(2)}) collective-permute-start(bf16[16,2048]{1,0:T(8,128)(2,1)S(1)} %pack_coarse.1), channel_id=1, source_target_pairs={{0,8},{4,12},{8,0},{12,4},{1,9},{5,13},{9,1},{13,5},{2,10},{6,14},... | collective-permute-start | bytes 196616 | tf_op jit(solution)/shard_map/ppermute | solution.py:513
  10.7 7.4 %collective-permute-start.4 = (bf16[16,2048]{1,0:T(8,128)(2,1)S(1)}, bf16[16,2048]{1,0:T(8,128)(2,1)S(1)}, u32[]{:S(2)}, u32[]{:S(2)}) collective-permute-start(bf16[16,2048]{1,0:T(8,128)(2,1)S(1)} %pack_coarse.1), channel_id=1, source_target_pairs={{0,4},{4,0},{8,12},{12,8},{1,5},{5,1},{9,13},{13,9},{2,6},{6,2},{1... | collective-permute-start | bytes 196616 | tf_op jit(solution)/shard_map/ppermute | solution.py:513
  14.3 8.0 %copy-start.4 = (bf16[256,768]{1,0:T(8,128)(2,1)S(1)}, bf16[256,768]{1,0:T(8,128)(2,1)}, u32[]{:S(2)}) copy-start(bf16[256,768]{1,0:T(8,128)(2,1)} %qkv_ref.1) | copy-start | bytes 1179652
  14.3 4.6 %collective-permute-start.2 = (bf16[34,8,256]{2,1,0:T(8,128)(2,1)S(1)}, bf16[34,8,256]{2,1,0:T(8,128)(2,1)S(1)}, u32[]{:S(2)}, u32[]{:S(2)}) collective-permute-start(bf16[34,8,256]{2,1,0:T(8,128)(2,1)S(1)} %get-tuple-element.52), channel_id=1, source_target_pairs={{1,2},{2,1},{5,6},{6,5},{9,10},{10,9},{13,14},{14,13},{17,18},{18,... | collective-permute-start | bytes 417800 | tf_op jit(solution)/shard_map/ppermute | solution.py:508
  15.1 3.9 %collective-permute-start.3 = (bf16[34,8,256]{2,1,0:T(8,128)(2,1)S(1)}, bf16[34,8,256]{2,1,0:T(8,128)(2,1)S(1)}, u32[]{:S(2)}, u32[]{:S(2)}) collective-permute-start(bf16[34,8,256]{2,1,0:T(8,128)(2,1)S(1)} %get-tuple-element.53), channel_id=1, source_target_pairs={{0,1},{1,0},{2,3},{3,2},{4,5},{5,4},{6,7},{7,6},{8,9},{9,8},{10,11... | collective-permute-start | bytes 417800 | tf_op jit(solution)/shard_map/ppermute | solution.py:509
  18.1 0.7 %copy-start.10 = (f32[1024]{0:T(1024)S(1)}, f32[1024]{0:T(1024)}, u32[]{:S(2)}) copy-start(f32[1024]{0:T(1024)} %param.19) | copy-start | bytes 12292
  18.1 0.7 %copy-start.11 = (f32[1,1024]{1,0:T(1,128)S(1)}, f32[1,1024]{1,0:T(1,128)}, u32[]{:S(2)}) copy-start(f32[1,1024]{1,0:T(1,128)} %constant.5.clone.coarse_freq) | copy-start | bytes 12292
  18.1 0.7 %copy-start.13 = (f32[1,256]{1,0:T(1,128)S(1)}, f32[1,256]{1,0:T(1,128)}, u32[]{:S(2)}) copy-start(f32[1,256]{1,0:T(1,128)} %constant.4.clone.fine_freq) | copy-start | bytes 3076
  18.1 4.2 %copy-start.6 = (bf16[256,256]{1,0:T(8,128)(2,1)S(1)}, bf16[256,256]{1,0:T(8,128)(2,1)}, u32[]{:S(2)}) copy-start(bf16[256,256]{1,0:T(8,128)(2,1)} %out_ref.1) | copy-start | bytes 393220
  18.2 0.7 %copy-start.12 = (f32[256]{0:T(256)S(1)}, f32[256]{0:T(256)}, u32[]{:S(2)}) copy-start(f32[256]{0:T(256)} %param.18) | copy-start | bytes 3076
  19.1 9.9 %collective-permute-start.8 = (bf16[4,16,2048]{2,1,0:T(8,128)(2,1)S(1)}, bf16[4,16,2048]{2,1,0:T(8,128)(2,1)S(1)}, u32[]{:S(2)}, u32[]{:S(2)}) collective-permute-start(bf16[4,16,2048]{2,1,0:T(8,128)(2,1)S(1)} %pad_maximum_fusion.1), channel_id=1, source_target_pairs={{0,2},{1,3},{2,0},{3,1},{4,6},{5,7},{6,4},{7,5},{8,10},{9,11},{10,... | collective-permute-start | bytes 786440 | tf_op jit(solution)/shard_map/ppermute | solution.py:513
  28.5 1.5 %collective-permute-start.7 = (bf16[2,4,16,1024]{3,2,1,0:T(8,128)(2,1)S(1)}, bf16[2,4,16,1024]{3,2,1,0:T(8,128)(2,1)S(1)}, u32[]{:S(2)}, u32[]{:S(2)}) collective-permute-start(bf16[2,4,16,1024]{3,2,1,0:T(8,128)(2,1)S(1)} %get-tuple-element.63), channel_id=1, source_target_pairs={{0,1},{1,0},{2,3},{3,2},{4,5},{5,4},{6,7},{7,6},{8,9},{9,8},{10,11... | collective-permute-start | bytes 786440 | tf_op jit(solution)/shard_map/ppermute | solution.py:513
  28.9 1.5 %collective-permute-start.9 = (bf16[4,16,2048]{2,1,0:T(8,128)(2,1)S(1)}, bf16[4,16,2048]{2,1,0:T(8,128)(2,1)S(1)}, u32[]{:S(2)}, u32[]{:S(2)}) collective-permute-start(bf16[4,16,2048]{2,1,0:T(8,128)(2,1)S(1)} %collective-permute-done.8), channel_id=1, source_target_pairs={{0,1},{1,0},{2,3},{3,2},{4,5},{5,4},{6,7},{7,6},{8,9},{9,8},{10,11... | collective-permute-start | bytes 786440 | tf_op jit(solution)/shard_map/ppermute | solution.py:513
  29.0 1.8 %collective-permute-start.11 = (bf16[4,16,2048]{2,1,0:T(8,128)(2,1)S(1)}, bf16[4,16,2048]{2,1,0:T(8,128)(2,1)S(1)}, u32[]{:S(2)}, u32[]{:S(2)}) collective-permute-start(bf16[4,16,2048]{2,1,0:T(8,128)(2,1)S(1)} %pad_maximum_fusion.1), channel_id=1, source_target_pairs={{0,1},{1,0},{2,3},{3,2},{4,5},{5,4},{6,7},{7,6},{8,9},{9,8},{10,11... | collective-permute-start | bytes 786440 | tf_op jit(solution)/shard_map/ppermute | solution.py:513
  30.5 5.6 %collective-permute-start.10 = (bf16[4,16,1024]{2,1,0:T(8,128)(2,1)S(1)}, bf16[4,16,1024]{2,1,0:T(8,128)(2,1)S(1)}, u32[]{:S(2)}, u32[]{:S(2)}) collective-permute-start(bf16[4,16,1024]{2,1,0:T(8,128)(2,1)S(1)} %fusion.2), channel_id=1, source_target_pairs={{0,2},{1,3},{2,0},{3,1},{4,6},{5,7},{6,4},{7,5},{8,10},{9,11},{10,... | collective-permute-start | bytes 393224 | tf_op jit(solution)/shard_map/ppermute | solution.py:513
  31.0 1.0 %copy-start.5 = (bf16[3,64,1024]{2,1,0:T(8,128)(2,1)S(1)}, bf16[3,64,1024]{2,1,0:T(8,128)(2,1)}, u32[]{:S(2)}) copy-start(bf16[3,64,1024]{2,1,0:T(8,128)(2,1)} %qkv_hbm.1) | copy-start | bytes 1179652
  31.0 1.0 %copy-start.7 = (bf16[64,1024]{1,0:T(8,128)(2,1)S(1)}, bf16[64,1024]{1,0:T(8,128)(2,1)}, u32[]{:S(2)}) copy-start(bf16[64,1024]{1,0:T(8,128)(2,1)} %out_hbm.1) | copy-start | bytes 393220
  34.3 1.8 %collective-permute-start.12 = (bf16[2,4,16,1024]{3,2,1,0:T(8,128)(2,1)S(1)}, bf16[2,4,16,1024]{3,2,1,0:T(8,128)(2,1)S(1)}, u32[]{:S(2)}, u32[]{:S(2)}) collective-permute-start(bf16[2,4,16,1024]{3,2,1,0:T(8,128)(2,1)S(1)} %bitcast.73), channel_id=1, source_target_pairs={{0,1},{1,0},{2,3},{3,2},{4,5},{5,4},{6,7},{7,6},{8,9},{9,8},{10,11... | collective-permute-start | bytes 786440 | tf_op jit(solution)/shard_map/ppermute | solution.py:513
  36.2 5.4 %collective-permute-start.13 = (bf16[4,16,1024]{2,1,0:T(8,128)(2,1)S(1)}, bf16[4,16,1024]{2,1,0:T(8,128)(2,1)S(1)}, u32[]{:S(2)}, u32[]{:S(2)}) collective-permute-start(bf16[4,16,1024]{2,1,0:T(8,128)(2,1)S(1)} %fusion.1), channel_id=1, source_target_pairs={{0,16},{16,0},{1,17},{17,1},{2,18},{18,2},{3,19},{19,3},{4,20},{20... | collective-permute-start | bytes 393224 | tf_op jit(solution)/shard_map/ppermute | solution.py:513
  37.8 5.1 %collective-permute-start.14 = (bf16[2,2,16,1024]{3,2,0,1:T(8,128)(2,1)S(1)}, bf16[2,2,16,1024]{3,2,0,1:T(8,128)(2,1)S(1)}, u32[]{:S(2)}, u32[]{:S(2)}) collective-permute-start(bf16[2,2,16,1024]{3,2,0,1:T(8,128)(2,1)S(1)} %fusion.3), channel_id=1, source_target_pairs={{0,4},{4,0},{8,12},{12,8},{1,5},{5,1},{9,13},{13,9},{2,6},{6,2},{1... | collective-permute-start | bytes 393224 | tf_op jit(solution)/shard_map/ppermute | solution.py:513
  42.9 5.0 %collective-permute-start.15 = (bf16[64,1024]{1,0:T(8,128)(2,1)S(1)}, bf16[64,1024]{1,0:T(8,128)(2,1)S(1)}, u32[]{:S(2)}, u32[]{:S(2)}) collective-permute-start(bf16[64,1024]{1,0:T(8,128)(2,1)S(1)} %bitcast.69), channel_id=1, source_target_pairs={{0,4},{4,0},{8,12},{12,8},{1,5},{5,1},{9,13},{13,9},{2,6},{6,2},{1... | collective-permute-start | bytes 393224 | tf_op jit(solution)/shard_map/ppermute | solution.py:513
  44.6 5.4 %collective-permute-start.16 = (bf16[80,1024]{1,0:T(8,128)(2,1)S(1)}, bf16[80,1024]{1,0:T(8,128)(2,1)S(1)}, u32[]{:S(2)}, u32[]{:S(2)}) collective-permute-start(bf16[80,1024]{1,0:T(8,128)(2,1)S(1)} %slice.70), channel_id=1, source_target_pairs={{0,16},{16,0},{1,17},{17,1},{2,18},{18,2},{3,19},{19,3},{4,20},{20... | collective-permute-start | bytes 491528 | tf_op jit(solution)/shard_map/ppermute | solution.py:513
  50.0 9.1 %collective-permute-start.17 = (bf16[96,1024]{1,0:T(8,128)(2,1)S(1)}, bf16[96,1024]{1,0:T(8,128)(2,1)S(1)}, u32[]{:S(2)}, u32[]{:S(2)}) collective-permute-start(bf16[96,1024]{1,0:T(8,128)(2,1)S(1)} %pad_maximum_fusion.3), channel_id=1, source_target_pairs={{0,8},{4,12},{8,0},{12,4},{1,9},{5,13},{9,1},{13,5},{2,10},{6,14},... | collective-permute-start | bytes 589832 | tf_op jit(solution)/shard_map/ppermute | solution.py:513
  51.0 8.2 %collective-permute-start.18 = (bf16[176,1024]{1,0:T(8,128)(2,1)S(1)}, bf16[176,1024]{1,0:T(8,128)(2,1)S(1)}, u32[]{:S(2)}, u32[]{:S(2)}) collective-permute-start(bf16[176,1024]{1,0:T(8,128)(2,1)S(1)} %slice.75), channel_id=1, source_target_pairs={{0,16},{16,0},{1,17},{17,1},{2,18},{18,2},{3,19},{19,3},{4,20},{20... | collective-permute-start | bytes 1081352 | tf_op jit(solution)/shard_map/ppermute | solution.py:513
  59.3 5.7 %collective-permute-start.19 = (bf16[80,1024]{1,0:T(8,128)(2,1)S(1)}, bf16[80,1024]{1,0:T(8,128)(2,1)S(1)}, u32[]{:S(2)}, u32[]{:S(2)}) collective-permute-start(bf16[80,1024]{1,0:T(8,128)(2,1)S(1)} %pad_maximum_fusion.4), channel_id=1, source_target_pairs={{0,2},{1,3},{2,0},{3,1},{4,6},{5,7},{6,4},{7,5},{8,10},{9,11},{10,... | collective-permute-start | bytes 491528 | tf_op jit(solution)/shard_map/ppermute | solution.py:513
  65.0 1.6 %collective-permute-start.20 = (bf16[2,64,1024]{2,1,0:T(8,128)(2,1)S(1)}, bf16[2,64,1024]{2,1,0:T(8,128)(2,1)S(1)}, u32[]{:S(2)}, u32[]{:S(2)}) collective-permute-start(bf16[2,64,1024]{2,1,0:T(8,128)(2,1)S(1)} %pad_maximum_fusion.2.near_ref), channel_id=1, source_target_pairs={{0,1},{1,0},{2,3},{3,2},{4,5},{5,4},{6,7},{7,6},{8,9},{9,8},{10,11... | collective-permute-start | bytes 786440 | tf_op jit(solution)/shard_map/ppermute | solution.py:513

commit v8 on v7

--- a/solution.py
+++ b/solution.py
@@ -324,13 +324,12 @@
     )(tokens, cotangents, factor, head_qkv, head_out)
 
 
-def row_edges_body(x_ref, dy_ref, near_ref, far_ref):
-    height = x_ref.shape[0]
+def row_edges_body(x_low, x_high, dy_low, dy_high, near_ref, far_ref):
     odd = odd_rank("gy")
 
     def fill(low_ref, high_ref):
-        low_ref[:HALO], low_ref[HALO:] = x_ref[:HALO], dy_ref[:RAD]
-        high_ref[:HALO], high_ref[HALO:] = x_ref[height - HALO :], dy_ref[height - RAD :]
+        low_ref[:HALO], low_ref[HALO:] = x_low[...], dy_low[...]
+        high_ref[:HALO], high_ref[HALO:] = x_high[...], dy_high[...]
 
     @pl.when(odd)
     def _():
@@ -343,15 +342,16 @@
 
 def row_edges(picture, cotangent):
     vmem = pl.BlockSpec(memory_space=pltpu.VMEM)
+    height = picture.shape[0]
     shape = jax.ShapeDtypeStruct((HALO + RAD,) + picture.shape[1:], jnp.bfloat16)
     return pl.pallas_call(
         row_edges_body,
         out_shape=(shape, shape),
-        in_specs=[vmem, vmem],
+        in_specs=[vmem] * 4,
         out_specs=(vmem, vmem),
         compiler_params=pltpu.CompilerParams(vmem_limit_bytes=vmem_bytes),
         name="row_edges",
-    )(picture, cotangent)
+    )(picture[:HALO], picture[height - HALO :], cotangent[:RAD], cotangent[height - RAD :])
 
 
 def col_edges_body(x_ref, dy_ref, row_far_ref, row_near_ref, near_ref, far_ref):
@@ -420,19 +420,17 @@
     )(step, fine_gain[None], coarse_gain[None], frequencies(D_F), frequencies(D_C))
 
 
-def pair_sum_body(own, *refs):
-    qkv_ref, out_ref = refs[-2:]
-    come = jnp.concatenate([ref[...] for ref in refs[:-2]], axis=0)
+def pair_sum_body(own, first, second, qkv_ref, out_ref):
     for part in range(4):
-        rows = slice(part * HD, (part + 1) * HD)
-        total = own[rows].astype(jnp.float32) + come[rows].astype(jnp.float32)
+        come = (first, second)[part // 2][(part % 2) * HD : (part % 2 + 1) * HD]
+        total = own[part * HD : (part + 1) * HD].astype(jnp.float32) + come.astype(jnp.float32)
         if part < 3:
             qkv_ref[part] = total.astype(jnp.bfloat16)
         else:
             out_ref[...] = total.astype(jnp.bfloat16)
 
 
-def pair_sum(own, *come):
+def pair_sum(own, first, second):
     vmem = pl.BlockSpec(memory_space=pltpu.VMEM)
     return pl.pallas_call(
         pair_sum_body,
@@ -440,41 +438,33 @@
             jax.ShapeDtypeStruct((3, HD, D_C), jnp.bfloat16),
             jax.ShapeDtypeStruct((HD, D_C), jnp.bfloat16),
         ),
-        in_specs=[vmem] * (1 + len(come)),
+        in_specs=[vmem] * 3,
         out_specs=(vmem, vmem),
         compiler_params=pltpu.CompilerParams(vmem_limit_bytes=vmem_bytes),
         name="pair_sum",
-    )(own, *come)
-
-
-def last_body(
-    near_ref,
-    far_ref,
-    x_ref,
-    factor_ref,
-    kept_ref,
-    come_ref,
-    qkv_hbm,
-    out_hbm,
-    dx_ref,
-    sems,
-):
+    )(own, first, second)
+
+
+def block_copies(near_ref, low, qkv_hbm, out_hbm, sems):
     highs, rows = near_ref.shape[0], near_ref.shape[1]
     copies = []
-    for low in range(2):
-        for high in range(highs):
-            source = (near_ref, far_ref)[low].at[high]
-            block = lax.axis_index("gx") ^ (2 * high + low)
-            at = pl.ds(pl.multiple_of(block * rows, rows), rows)
-            for part, target in enumerate((qkv_hbm, out_hbm)):
-                lanes = (slice(0, 3 * D_F), slice(3 * D_F, 4 * D_F))[part]
-                copies.append(
-                    pltpu.make_async_copy(
-                        source.at[:, lanes], target.at[at, :], sems.at[low, high, part]
-                    )
+    for high in range(highs):
+        block = lax.axis_index("gx") ^ (2 * high + low)
+        at = pl.ds(pl.multiple_of(block * rows, rows), rows)
+        for part, target in enumerate((qkv_hbm, out_hbm)):
+            lanes = (slice(0, 3 * D_F), slice(3 * D_F, 4 * D_F))[part]
+            copies.append(
+                pltpu.make_async_copy(
+                    near_ref.at[high, :, lanes], target.at[at, :], sems.at[high, part]
                 )
+            )
     for copy in copies:
         copy.start()
+    return copies
+
+
+def near_body(near_ref, x_ref, factor_ref, kept_ref, come_ref, qkv_hbm, out_hbm, dx_ref, sems):
+    copies = block_copies(near_ref, 0, qkv_hbm, out_hbm, sems)
     tokens = x_ref[...].astype(jnp.float32).reshape(-1, D_C)
     upstream = kept_ref[...] + come_ref[...].astype(jnp.float32)
     grads = norm_backward(tokens, inverse_rms(tokens), factor_ref[...], upstream)
@@ -483,22 +473,45 @@
         copy.wait()
 
 
-def last_step(near, far, tokens, factor, kept, come):
+def far_body(far_ref, qkv_in, out_in, qkv_hbm, out_hbm, sems):
+    for copy in block_copies(far_ref, 1, qkv_hbm, out_hbm, sems):
+        copy.wait()
+
+
+def near_step(near, tokens, *operands):
     vmem = pl.BlockSpec(memory_space=pltpu.VMEM)
     hbm = pl.BlockSpec(memory_space=pltpu.HBM)
     return pl.pallas_call(
-        last_body,
+        near_body,
         out_shape=(
             jax.ShapeDtypeStruct((D_F, 3 * D_F), jnp.bfloat16),
             jax.ShapeDtypeStruct((D_F, D_F), jnp.bfloat16),
             jax.ShapeDtypeStruct(tokens.shape, jnp.bfloat16),
         ),
-        in_specs=[vmem] * 6,
+        in_specs=[vmem] * 5,
         out_specs=(hbm, hbm, vmem),
-        scratch_shapes=[pltpu.SemaphoreType.DMA((2, near.shape[0], 2))],
-        compiler_params=pltpu.CompilerParams(vmem_limit_bytes=vmem_bytes),
-        name="last_step",
-    )(near, far, tokens, factor, kept, come)
+        scratch_shapes=[pltpu.SemaphoreType.DMA((near.shape[0], 2))],
+        compiler_params=pltpu.CompilerParams(vmem_limit_bytes=vmem_bytes),
+        name="near_step",
+    )(near, tokens, *operands)
+
+
+def far_step(far, qkv, out):
+    vmem = pl.BlockSpec(memory_space=pltpu.VMEM)
+    hbm = pl.BlockSpec(memory_space=pltpu.HBM)
+    return pl.pallas_call(
+        far_body,
+        out_shape=(
+            jax.ShapeDtypeStruct(qkv.shape, qkv.dtype),
+            jax.ShapeDtypeStruct(out.shape, out.dtype),
+        ),
+        in_specs=[vmem, hbm, hbm],
+        out_specs=(hbm, hbm),
+        input_output_aliases={1: 0, 2: 1},
+        scratch_shapes=[pltpu.SemaphoreType.DMA((far.shape[0], 2))],
+        compiler_params=pltpu.CompilerParams(vmem_limit_bytes=vmem_bytes),
+        name="far_step",
+    )(far, qkv, out)
 
 
 def neighbours(to_near, to_far, axis):
@@ -534,13 +547,6 @@
 def all_rows(piece):
     downs = lax.axis_size("gy")
     return jnp.stack([piece] + [swapped(piece, "gy", row) for row in range(1, downs)])
-
-
-def row_halved(kept, mask):
-    columns, count = kept.shape[0], kept.shape[-2]
-    kept = kept.reshape(columns, -1, 2, count, D_C)
-    come = swapped(narrow(kept[:, :, 1]), "gy", mask)
-    return kept[:, :, 0] + wide(come)
 
 
 def local(
@@ -569,9 +575,9 @@
     *edges, step, gain_f, gain_c = tied(*edges, timestep, fine_gain, coarse_gain)
     col_near, col_far = neighbours(*edges, "gx")
     factor, coarse_factor = time_factors(step, gain_f, gain_c)
-    col_far, col_near, row_group, factor = tied(col_far, col_near, row_group, factor)
     cross = swapped(row_group, "gx", 2)
     beside = swapped(row_group, "gx", 1)
+    col_far, col_near, row_group, factor = tied(col_far, col_near, row_group, factor)
     dx_picture, fine_keep, fine_send = fine_block(
         (across, downs),
         picture,
@@ -593,34 +599,29 @@
     parts, coarse_partial = coarse_block(
         everyone[:, :D_C], everyone[:, D_C:], coarse_factor, coarse_qkv, coarse_out
     )
+    fine_quarter, parts, coarse_partial = tied(fine_quarter, parts, coarse_partial)
+
+    rows = D_F // across
+    fine_quarter = narrow(batch_sum(fine_quarter)).reshape(rows, 4 * D_F)
     parts = parts.reshape(2, 2, downs, count, D_C)
     coarse_kept = wide(parts[0]) + wide(swapped(parts[1], "gx", 1))
     fine_quarter, coarse_kept, coarse_partial = tied(fine_quarter, coarse_kept, coarse_partial)
 
-    rows = D_F // across
-    fine_quarter = narrow(batch_sum(fine_quarter)).reshape(rows, 4 * D_F)
-    masks = [1 << bit for bit in range(downs.bit_length() - 1)]
-    coarse_kept = row_halved(coarse_kept, masks[0])
-    fine_quarter, coarse_kept, coarse_partial = tied(fine_quarter, coarse_kept, coarse_partial)
-
     pair_batch = lax.axis_size("batch") == 2
-    cut = 5 * HD // 4
-    halves = (coarse_partial[:cut], coarse_partial[cut:])
+    halves = (coarse_partial[: 2 * HD], coarse_partial[2 * HD :])
     others = [swapped(half, "batch", 1) if pair_batch else half for half in halves]
-    for turn, mask in enumerate(masks):
-        last = turn + 1 == len(masks)
-        sent = fine_quarter
-        if turn:
-            coarse_kept = coarse_kept.reshape(2, -1, 2, count, D_C)
-            extra = narrow(coarse_kept[:, :, 1]).reshape(-1, D_C)
-            sent = jnp.concatenate([fine_quarter, extra], axis=0)
-        come = swapped(sent, "gy", mask)
+    mask = 1
+    while mask < downs:
+        last = 2 * mask == downs
+        coarse_kept = coarse_kept.reshape(2, -1, 2, count, D_C)
+        sent = narrow(coarse_kept[:, :, 1]).reshape(-1, D_C)
+        come = swapped(jnp.concatenate([fine_quarter, sent], axis=0), "gy", mask)
+        coarse_kept = coarse_kept[:, :, 0]
+        coarse_kept = coarse_kept + wide(come[rows:]).reshape(coarse_kept.shape)
         fine_quarter = narrow(wide(fine_quarter) + wide(come[:rows]))
-        if turn:
-            coarse_kept = coarse_kept[:, :, 0]
-            coarse_kept = coarse_kept + wide(come[rows:]).reshape(coarse_kept.shape)
         at = int(last)
         fine_quarter, coarse_kept, others[at] = tied(fine_quarter, coarse_kept, others[at])
+        mask *= 2
 
     coarse_kept = coarse_kept.reshape(2, count, D_C)
     come = swapped(jnp.concatenate([fine_quarter, narrow(coarse_kept[1])], axis=0), "gx", 2)
@@ -632,14 +633,12 @@
         grad_coarse_out = coarse_sum[3 * HD :]
     come, grad_coarse_qkv, grad_coarse_out = tied(come, grad_coarse_qkv, grad_coarse_out)
     fine_pair = jnp.stack([fine_quarter, come[:rows]])
-    grad_qkv, grad_out, dx_coarse = last_step(
-        fine_pair,
-        swapped(fine_pair, "gx", 1),
-        x_coarse[0],
-        coarse_factor,
-        coarse_kept[0],
-        come[rows:],
+    near_qkv, near_out, dx_coarse = near_step(
+        fine_pair, x_coarse[0], coarse_factor, coarse_kept[0], come[rows:]
     )
+    far_pair = swapped(fine_pair, "gx", 1)
+    far_pair, near_qkv, near_out = tied(far_pair, near_qkv, near_out)
+    grad_qkv, grad_out = far_step(far_pair, near_qkv, near_out)
     return (
         dx_picture[None],
         dx_coarse[None],

time: 68.3 us -> 65.1 us (0.953)
  starting transfers between devices: 28.6 us -> 26 us
  local copies, waits for them, and re-layouts: 3.69 us -> 2.84 us
  Pallas kernels: 10.9 us -> 11.6 us
    ppermute x17 -> x16, starting transfers between devices: 18.3 us -> 15.7 us  [swapped(): lax.ppermute(value, axis, [(i, i ^ mask) for i in range(lax.axis_size(axi...]
    unnamed x28 -> x24, local copies, waits for them, and re-layouts: 3.47 us -> 1.61 us
    slice x3 -> x5, local copies, waits for them, and re-layouts: 0.04 us -> 1.06 us  [the longest x1 0.99 us: row_edges(): picture[height - HALO:]]
    pallas_call x2 -> x3, Pallas kernels: 1.5 us -> 2.12 us  [the longest x1 1.36 us: near_step(): pl.pallas_call(near_body, out_shape=(jax.ShapeDtypeStruct((D_F, 3 * D_F),...]
    ppermute x17 -> x16, waiting for transfers between devices: 22.6 us -> 22.2 us  [swapped(): lax.ppermute(value, axis, [(i, i ^ mask) for i in range(lax.axis_size(axi...]
  transfers between devices with their start and end apart: 21 -> 20, of which waited for: 12 -> 10; matrix products, arithmetic and copies ran while one was open for 1% -> 1% of each run, Pallas kernels for 14% -> 17%
where the time goes in v8:
time: 65.1 us; the launch traced here: 64.8 us
  starting transfers between devices  26 us (40%)
  waiting for transfers between devices  22.2 us (34%)
  Pallas kernels  11.6 us (18%)
  local copies, waits for them, and re-layouts  2.84 us (4%)
  between operations  1.69 us (3%)
    ppermute x16, waiting for transfers between devices, swapped(): lax.ppermute(value, axis, [(i, i ^ mask) for i in range(lax.axis_size(axi...  22.2 us
    ppermute x16, starting transfers between devices, swapped(): lax.ppermute(value, axis, [(i, i ^ mask) for i in range(lax.axis_size(axi...  15.7 us
    ppermute x2, starting transfers between devices, neighbours(): return (lax.ppermute(to_near, axis, near), from_far)  8.81 us
    pallas_call x1, Pallas kernels, fine_block(): pl.pallas_call(fine_body, out_shape=(jax.ShapeDtypeStruct((height, breadt...  6.17 us
    pallas_call x1, Pallas kernels, coarse_block(): pl.pallas_call(coarse_body, out_shape=(jax.ShapeDtypeStruct((count, D_C),...  2.23 us
    unnamed x24, local copies, waits for them, and re-layouts  1.61 us
    ppermute x2, starting transfers between devices, neighbours(): from_far = lax.ppermute(to_far, axis, far)  1.47 us
    pallas_call x1, Pallas kernels, near_step(): pl.pallas_call(near_body, out_shape=(jax.ShapeDtypeStruct((D_F, 3 * D_F),...  1.36 us
  transfers between devices with their start and end apart: 20, of which 10 were waited for; matrix products, arithmetic and copies ran while one was open for 1% of the time, Pallas kernels for 17%

profile of v8, /device:TPU:0, one launch (start us, length us, event | category | flops | bytes accessed | tf_op | source)
XLA Modules:
  0.0 64.8 jit_solution(5348954590704362053)
XLA Ops:
  0.6 1.0 %slice_bitcast_fusion.2 = (bf16[6,32,256]{2,1,0:T(8,128)(2,1)S(1)}, bf16[6,32,256]{2,1,0:T(8,128)(2,1)S(1)}) fusion(bf16[1,8,32,256]{3,2,1,0:T(8,128)(2,1)} %param.13), kind=kLoop, calls=%fused_computation.22 | loop fusion | bytes 393216 | tf_op jit(solution)/shard_map/slice | solution.py:354
  1.7 0.0 copy-start.6
  1.7 0.0 copy-start.7
  1.7 0.7 %collective-permute-start = (bf16[9,32,256]{2,1,0:T(8,128)(2,1)S(1)}, bf16[9,32,256]{2,1,0:T(8,128)(2,1)S(1)}, u32[]{:S(2)}, u32[]{:S(2)}) collective-permute-start(bf16[9,32,256]{2,1,0:T(8,128)(2,1)S(1)} %get-tuple-element.53.second), channel_id=1, source_target_pairs={{4,8},{8,4},{5,9},{9,5},{6,10},{10,6},{7,11},{11,7},{20,24},{24,20... | collective-permute-start | bytes 442376 | tf_op jit(solution)/shard_map/ppermute | solution.py:521
  2.4 5.9 %collective-permute-start.1 = (bf16[9,32,256]{2,1,0:T(8,128)(2,1)S(1)}, bf16[9,32,256]{2,1,0:T(8,128)(2,1)S(1)}, u32[]{:S(2)}, u32[]{:S(2)}) collective-permute-start(bf16[9,32,256]{2,1,0:T(8,128)(2,1)S(1)} %get-tuple-element.54.first), channel_id=1, source_target_pairs={{0,4},{4,0},{8,12},{12,8},{1,5},{5,1},{9,13},{13,9},{2,6},{6,2},{1... | collective-permute-start | bytes 442376 | tf_op jit(solution)/shard_map/ppermute | solution.py:522
  8.3 1.4 %collective-permute-start.6 = (bf16[16,2048]{1,0:T(8,128)(2,1)S(1)}, bf16[16,2048]{1,0:T(8,128)(2,1)S(1)}, u32[]{:S(2)}, u32[]{:S(2)}) collective-permute-start(bf16[16,2048]{1,0:T(8,128)(2,1)S(1)} %pack_coarse.1), channel_id=1, source_target_pairs={{0,12},{4,8},{8,4},{12,0},{1,13},{5,9},{9,5},{13,1},{2,14},{6,10},... | collective-permute-start | bytes 196616 | tf_op jit(solution)/shard_map/ppermute | solution.py:526
  9.8 0.2 collective-permute-start.5
  9.9 2.9 %collective-permute-start.4 = (bf16[16,2048]{1,0:T(8,128)(2,1)S(1)}, bf16[16,2048]{1,0:T(8,128)(2,1)S(1)}, u32[]{:S(2)}, u32[]{:S(2)}) collective-permute-start(bf16[16,2048]{1,0:T(8,128)(2,1)S(1)} %pack_coarse.1), channel_id=1, source_target_pairs={{0,4},{4,0},{8,12},{12,8},{1,5},{5,1},{9,13},{13,9},{2,6},{6,2},{1... | collective-permute-start | bytes 196616 | tf_op jit(solution)/shard_map/ppermute | solution.py:526
  12.8 0.0 collective-permute-done.row_far_ref
  12.8 0.0 collective-permute-done.1.row_near_ref
  12.8 0.0 copy-done
  12.8 0.1 col_edges.1
  12.9 0.0 copy-start.2
  12.9 0.8 %collective-permute-start.2 = (bf16[34,8,256]{2,1,0:T(8,128)(2,1)S(1)}, bf16[34,8,256]{2,1,0:T(8,128)(2,1)S(1)}, u32[]{:S(2)}, u32[]{:S(2)}) collective-permute-start(bf16[34,8,256]{2,1,0:T(8,128)(2,1)S(1)} %get-tuple-element.57), channel_id=1, source_target_pairs={{1,2},{2,1},{5,6},{6,5},{9,10},{10,9},{13,14},{14,13},{17,18},{18,... | collective-permute-start | bytes 417800 | tf_op jit(solution)/shard_map/ppermute | solution.py:521
  13.7 2.9 %collective-permute-start.3 = (bf16[34,8,256]{2,1,0:T(8,128)(2,1)S(1)}, bf16[34,8,256]{2,1,0:T(8,128)(2,1)S(1)}, u32[]{:S(2)}, u32[]{:S(2)}) collective-permute-start(bf16[34,8,256]{2,1,0:T(8,128)(2,1)S(1)} %get-tuple-element.58), channel_id=1, source_target_pairs={{0,1},{1,0},{2,3},{3,2},{4,5},{5,4},{6,7},{7,6},{8,9},{9,8},{10,11... | collective-permute-start | bytes 417800 | tf_op jit(solution)/shard_map/ppermute | solution.py:522
  16.6 0.0 collective-permute-done.6
  16.6 0.7 %collective-permute-done.5 = bf16[16,2048]{1,0:T(8,128)(2,1)S(1)} collective-permute-done((bf16[16,2048]{1,0:T(8,128)(2,1)S(1)}, bf16[16,2048]{1,0:T(8,128)(2,1)S(1)}, u32[]{:S(2)}, u32[]{:S(2)}) %collective-permute-start.5) | collective-permute-done | bytes 65568 | tf_op jit(solution)/shard_map/ppermute | solution.py:526
  17.3 0.0 collective-permute-done.4
  17.4 0.0 copy-start.8
  17.4 1.6 %collective-permute-start.8 = (bf16[4,16,2048]{2,1,0:T(8,128)(2,1)S(1)}, bf16[4,16,2048]{2,1,0:T(8,128)(2,1)S(1)}, u32[]{:S(2)}, u32[]{:S(2)}) collective-permute-start(bf16[4,16,2048]{2,1,0:T(8,128)(2,1)S(1)} %pad_maximum_fusion.1), channel_id=1, source_target_pairs={{0,2},{1,3},{2,0},{3,1},{4,6},{5,7},{6,4},{7,5},{8,10},{9,11},{10,... | collective-permute-start | bytes 786440 | tf_op jit(solution)/shard_map/ppermute | solution.py:526
  19.6 0.0 copy-start.10
  19.6 0.0 copy-done.9
  19.6 0.6 copy-done.10
  20.3 0.1 time_factors.1
  20.3 0.0 collective-permute-done.2.col_far_ref
  20.3 0.0 collective-permute-done.3.col_near_ref
  20.4 6.2 %fine_block.1 = (bf16[8,32,256]{2,1,0:T(8,128)(2,1)}, f32[2,4,16,1024]{3,2,1,0:T(8,128)S(1)}, bf16[2,4,16,1024]{3,2,1,0:T(8,128)(2,1)S(1)}) custom-call(bf16[8,32,256]{2,1,0:T(8,128)(2,1)S(1)} %bitcast.59, bf16[8,32,256]{2,1,0:T(8,128)(2,1)S(1)} %bitcast.61, bf16[9,32,256]{2,1,0:T(8,128)(2,1)S(1)} %collective-permute-done.row_far_ref, ...), custom_call_target="tpu_custom_call" | custom-call | tf_op jit(solution)/shard_map/fine_block/pallas_call | solution.py:233
  26.5 0.0 collective-permute-start.7
  26.5 0.0 collective-permute-done.8
  26.5 0.5 collective-permute-start.9
  27.0 0.0 collective-permute-start.11
  27.0 1.0 %collective-permute-done.7 = bf16[2,4,16,1024]{3,2,1,0:T(8,128)(2,1)S(1)} collective-permute-done((bf16[2,4,16,1024]{3,2,1,0:T(8,128)(2,1)S(1)}, bf16[2,4,16,1024]{3,2,1,0:T(8,128)(2,1)S(1)}, u32[]{:S(2)}, u32[]{:S(2)}) %collective-permute-start.7) | collective-permute-done | bytes 262176 | tf_op jit(solution)/shard_map/ppermute | solution.py:526
  28.1 0.1 convert_add_fusion.1
  28.1 0.3 collective-permute-done.9
  28.5 0.6 collective-permute-start.10
  29.1 0.0 collective-permute-done.11
  29.1 0.1 pad_maximum_fusion
  29.2 0.0 copy-start.3
  29.2 0.0 copy-start.5
  29.2 0.1 fusion.5
  29.3 0.9 %copy-done.3 = bf16[3,64,1024]{2,1,0:T(8,128)(2,1)S(1)} copy-done((bf16[3,64,1024]{2,1,0:T(8,128)(2,1)S(1)}, bf16[3,64,1024]{2,1,0:T(8,128)(2,1)}, u32[]{:S(2)}) %copy-start.3) | copy-done | bytes 393240
  30.2 0.0 copy-done.5
  30.2 2.2 %coarse_block.1 = (bf16[256,1024]{1,0:T(8,128)(2,1)S(1)}, bf16[256,1024]{1,0:T(8,128)(2,1)S(1)}) custom-call(bf16[256,1024]{1,0:T(8,128)(2,1)S(1)} %get-tuple-element.101.x_ref, bf16[256,1024]{1,0:T(8,128)(2,1)S(1)} %get-tuple-element.100.dy_ref, f32[1,1024]{1,0:T(1,128)S(1)} %get-tuple-element.72.factor_ref, bf16[3,64,1024]{2,1,0:T(8,128)(2,1)S(1)} %copy-done.3, ...), custom_call_target="tpu_custom_call" | custom-call | tf_op jit(solution)/shard_map/coarse_block/pallas_call | solution.py:309
  32.5 1.6 %collective-permute-done.10 = bf16[4,16,1024]{2,1,0:T(8,128)(2,1)S(1)} collective-permute-done((bf16[4,16,1024]{2,1,0:T(8,128)(2,1)S(1)}, bf16[4,16,1024]{2,1,0:T(8,128)(2,1)S(1)}, u32[]{:S(2)}, u32[]{:S(2)}) %collective-permute-start.10) | collective-permute-done | bytes 131104 | tf_op jit(solution)/shard_map/ppermute | solution.py:526
  34.1 1.6 %collective-permute-start.12 = (bf16[4,16,1024]{2,1,0:T(8,128)(2,1)S(1)}, bf16[4,16,1024]{2,1,0:T(8,128)(2,1)S(1)}, u32[]{:S(2)}, u32[]{:S(2)}) collective-permute-start(bf16[4,16,1024]{2,1,0:T(8,128)(2,1)S(1)} %fusion.1), channel_id=1, source_target_pairs={{0,16},{16,0},{1,17},{17,1},{2,18},{18,2},{3,19},{19,3},{4,20},{20... | collective-permute-start | bytes 393224 | tf_op jit(solution)/shard_map/ppermute | solution.py:526
  35.7 0.1 collective-permute-start.13
  35.8 3.3 %collective-permute-done.12 = bf16[4,16,1024]{2,1,0:T(8,128)(2,1)S(1)} collective-permute-done((bf16[4,16,1024]{2,1,0:T(8,128)(2,1)S(1)}, bf16[4,16,1024]{2,1,0:T(8,128)(2,1)S(1)}, u32[]{:S(2)}, u32[]{:S(2)}) %collective-permute-start.12) | collective-permute-done | bytes 131104 | tf_op jit(solution)/shard_map/ppermute | solution.py:526
  39.2 0.0 collective-permute-done.13
  39.2 0.1 convert_add_fusion
  39.3 1.3 %collective-permute-start.14 = (bf16[128,1024]{1,0:T(8,128)(2,1)S(1)}, bf16[128,1024]{1,0:T(8,128)(2,1)S(1)}, u32[]{:S(2)}, u32[]{:S(2)}) collective-permute-start(bf16[128,1024]{1,0:T(8,128)(2,1)S(1)} %pad_maximum_fusion.2), channel_id=1, source_target_pairs={{0,4},{4,0},{8,12},{12,8},{1,5},{5,1},{9,13},{13,9},{2,6},{6,2},{1... | collective-permute-start | bytes 786440 | tf_op jit(solution)/shard_map/ppermute | solution.py:526
  40.7 1.6 %collective-permute-start.15 = (bf16[128,1024]{1,0:T(8,128)(2,1)S(1)}, bf16[128,1024]{1,0:T(8,128)(2,1)S(1)}, u32[]{:S(2)}, u32[]{:S(2)}) collective-permute-start(bf16[128,1024]{1,0:T(8,128)(2,1)S(1)} %get-tuple-element.103), channel_id=1, source_target_pairs={{0,16},{16,0},{1,17},{17,1},{2,18},{18,2},{3,19},{19,3},{4,20},{20... | collective-permute-start | bytes 786440 | tf_op jit(solution)/shard_map/ppermute | solution.py:526
  42.3 3.6 %collective-permute-done.14 = bf16[128,1024]{1,0:T(8,128)(2,1)S(1)} collective-permute-done((bf16[128,1024]{1,0:T(8,128)(2,1)S(1)}, bf16[128,1024]{1,0:T(8,128)(2,1)S(1)}, u32[]{:S(2)}, u32[]{:S(2)}) %collective-permute-start.14) | collective-permute-done | bytes 262176 | tf_op jit(solution)/shard_map/ppermute | solution.py:526
  45.9 1.5 %collective-permute-done.15.first = bf16[128,1024]{1,0:T(8,128)(2,1)S(1)} collective-permute-done((bf16[128,1024]{1,0:T(8,128)(2,1)S(1)}, bf16[128,1024]{1,0:T(8,128)(2,1)S(1)}, u32[]{:S(2)}, u32[]{:S(2)}) %collective-permute-start.15) | collective-permute-done | bytes 262176 | tf_op jit(solution)/shard_map/ppermute | solution.py:526
  47.4 1.5 %collective-permute-start.16 = (bf16[96,1024]{1,0:T(8,128)(2,1)S(1)}, bf16[96,1024]{1,0:T(8,128)(2,1)S(1)}, u32[]{:S(2)}, u32[]{:S(2)}) collective-permute-start(bf16[96,1024]{1,0:T(8,128)(2,1)S(1)} %pad_maximum_fusion.4), channel_id=1, source_target_pairs={{0,8},{4,12},{8,0},{12,4},{1,9},{5,13},{9,1},{13,5},{2,10},{6,14},... | collective-permute-start | bytes 589832 | tf_op jit(solution)/shard_map/ppermute | solution.py:526
  49.0 1.5 %collective-permute-start.17 = (bf16[128,1024]{1,0:T(8,128)(2,1)S(1)}, bf16[128,1024]{1,0:T(8,128)(2,1)S(1)}, u32[]{:S(2)}, u32[]{:S(2)}) collective-permute-start(bf16[128,1024]{1,0:T(8,128)(2,1)S(1)} %get-tuple-element.102), channel_id=1, source_target_pairs={{0,16},{16,0},{1,17},{17,1},{2,18},{18,2},{3,19},{19,3},{4,20},{20... | collective-permute-start | bytes 786440 | tf_op jit(solution)/shard_map/ppermute | solution.py:526
  50.5 6.5 %collective-permute-done.16 = bf16[96,1024]{1,0:T(8,128)(2,1)S(1)} collective-permute-done((bf16[96,1024]{1,0:T(8,128)(2,1)S(1)}, bf16[96,1024]{1,0:T(8,128)(2,1)S(1)}, u32[]{:S(2)}, u32[]{:S(2)}) %collective-permute-start.16) | collective-permute-done | bytes 196640 | tf_op jit(solution)/shard_map/ppermute | solution.py:526
  57.0 0.0 collective-permute-done.17.second
  57.1 0.9 %collective-permute-start.18 = (bf16[80,1024]{1,0:T(8,128)(2,1)S(1)}, bf16[80,1024]{1,0:T(8,128)(2,1)S(1)}, u32[]{:S(2)}, u32[]{:S(2)}) collective-permute-start(bf16[80,1024]{1,0:T(8,128)(2,1)S(1)} %pad_maximum_fusion.5), channel_id=1, source_target_pairs={{0,2},{1,3},{2,0},{3,1},{4,6},{5,7},{6,4},{7,5},{8,10},{9,11},{10,... | collective-permute-start | bytes 491528 | tf_op jit(solution)/shard_map/ppermute | solution.py:526
  57.9 0.9 %pair_sum.1 = (bf16[3,64,1024]{2,1,0:T(8,128)(2,1)}, bf16[64,1024]{1,0:T(8,128)(2,1)}) custom-call(bf16[256,1024]{1,0:T(8,128)(2,1)S(1)} %get-tuple-element.80.own, bf16[128,1024]{1,0:T(8,128)(2,1)S(1)} %collective-permute-done.15.first, bf16[128,1024]{1,0:T(8,128)(2,1)S(1)} %collective-permute-done.17.second), custom_call_target="tpu_custom_call" | custom-call | tf_op jit(solution)/shard_map/pair_sum/pallas_call | solution.py:435
  58.8 3.6 %collective-permute-done.18 = bf16[80,1024]{1,0:T(8,128)(2,1)S(1)} collective-permute-done((bf16[80,1024]{1,0:T(8,128)(2,1)S(1)}, bf16[80,1024]{1,0:T(8,128)(2,1)S(1)}, u32[]{:S(2)}, u32[]{:S(2)}) %collective-permute-start.18) | collective-permute-done | bytes 163872 | tf_op jit(solution)/shard_map/ppermute | solution.py:526
  62.5 0.1 collective-permute-start.19
  62.6 1.4 %near_step.1 = (bf16[256,768]{1,0:T(8,128)(2,1)}, bf16[256,256]{1,0:T(8,128)(2,1)}, bf16[4,4,1024]{2,1,0:T(4,128)(2,1)}) custom-call(bf16[2,64,1024]{2,1,0:T(8,128)(2,1)S(1)} %pad_maximum_fusion.3.near_ref, bf16[4,4,1024]{2,1,0:T(4,128)(2,1)S(1)} %bitcast.64, f32[1,1024]{1,0:T(1,128)S(1)} %get-tuple-element.72.factor_ref, ...), custom_call_target="tpu_custom_call" | custom-call | tf_op jit(solution)/shard_map/near_step/pallas_call | solution.py:484
  64.0 0.1 collective-permute-done.19.far_ref
  64.1 0.7 %far_step.1 = (bf16[256,768]{1,0:T(8,128)(2,1)}, bf16[256,256]{1,0:T(8,128)(2,1)}) custom-call(bf16[2,64,1024]{2,1,0:T(8,128)(2,1)S(1)} %collective-permute-done.19.far_ref, bf16[256,768]{1,0:T(8,128)(2,1)} %get-tuple-element.94.qkv_in, bf16[256,256]{1,0:T(8,128)(2,1)} %get-tuple-element.95.out_in), custom_call_target="tpu_custom_call", output_to_operand_aliasing={{0}: (1, {}), {1}: (2, {})} | custom-call | tf_op jit(solution)/shard_map/far_step/pallas_call | solution.py:502
  (37 shorter events, 0.5 us)
Async XLA Ops:
  0.6 1.0 %copy-start.1 = (bf16[1,8,32,256]{3,2,1,0:T(8,128)(2,1)S(1)}, bf16[1,8,32,256]{3,2,1,0:T(8,128)(2,1)}, u32[]{:S(2)}) copy-start(bf16[1,8,32,256]{3,2,1,0:T(8,128)(2,1)} %param.14) | copy-start | bytes 393220
  1.7 6.7 %copy-start.6 = (bf16[1,4,4,1024]{3,2,1,0:T(4,128)(2,1)S(1)}, bf16[1,4,4,1024]{3,2,1,0:T(4,128)(2,1)}, u32[]{:S(2)}) copy-start(bf16[1,4,4,1024]{3,2,1,0:T(4,128)(2,1)} %param.15) | copy-start | bytes 98308
  1.7 6.6 %copy-start.7 = (bf16[1,4,4,1024]{3,2,1,0:T(4,128)(2,1)S(1)}, bf16[1,4,4,1024]{3,2,1,0:T(4,128)(2,1)}, u32[]{:S(2)}) copy-start(bf16[1,4,4,1024]{3,2,1,0:T(4,128)(2,1)} %param.16) | copy-start | bytes 98308
  1.7 11.1 %collective-permute-start = (bf16[9,32,256]{2,1,0:T(8,128)(2,1)S(1)}, bf16[9,32,256]{2,1,0:T(8,128)(2,1)S(1)}, u32[]{:S(2)}, u32[]{:S(2)}) collective-permute-start(bf16[9,32,256]{2,1,0:T(8,128)(2,1)S(1)} %get-tuple-element.53.second), channel_id=1, source_target_pairs={{4,8},{8,4},{5,9},{9,5},{6,10},{10,6},{7,11},{11,7},{20,24},{24,20... | collective-permute-start | bytes 442376 | tf_op jit(solution)/shard_map/ppermute | solution.py:521
  2.4 10.4 %collective-permute-start.1 = (bf16[9,32,256]{2,1,0:T(8,128)(2,1)S(1)}, bf16[9,32,256]{2,1,0:T(8,128)(2,1)S(1)}, u32[]{:S(2)}, u32[]{:S(2)}) collective-permute-start(bf16[9,32,256]{2,1,0:T(8,128)(2,1)S(1)} %get-tuple-element.54.first), channel_id=1, source_target_pairs={{0,4},{4,0},{8,12},{12,8},{1,5},{5,1},{9,13},{13,9},{2,6},{6,2},{1... | collective-permute-start | bytes 442376 | tf_op jit(solution)/shard_map/ppermute | solution.py:522
  8.3 4.5 %copy-start = (bf16[1,8,32,256]{3,2,1,0:T(8,128)(2,1)S(1)}, bf16[1,8,32,256]{3,2,1,0:T(8,128)(2,1)}, u32[]{:S(2)}) copy-start(bf16[1,8,32,256]{3,2,1,0:T(8,128)(2,1)} %param.13) | copy-start | bytes 393220
  8.3 8.3 %collective-permute-start.6 = (bf16[16,2048]{1,0:T(8,128)(2,1)S(1)}, bf16[16,2048]{1,0:T(8,128)(2,1)S(1)}, u32[]{:S(2)}, u32[]{:S(2)}) collective-permute-start(bf16[16,2048]{1,0:T(8,128)(2,1)S(1)} %pack_coarse.1), channel_id=1, source_target_pairs={{0,12},{4,8},{8,4},{12,0},{1,13},{5,9},{9,5},{13,1},{2,14},{6,10},... | collective-permute-start | bytes 196616 | tf_op jit(solution)/shard_map/ppermute | solution.py:526
  9.8 7.5 %collective-permute-start.5 = (bf16[16,2048]{1,0:T(8,128)(2,1)S(1)}, bf16[16,2048]{1,0:T(8,128)(2,1)S(1)}, u32[]{:S(2)}, u32[]{:S(2)}) collective-permute-start(bf16[16,2048]{1,0:T(8,128)(2,1)S(1)} %pack_coarse.1), channel_id=1, source_target_pairs={{0,8},{4,12},{8,0},{12,4},{1,9},{5,13},{9,1},{13,5},{2,10},{6,14},... | collective-permute-start | bytes 196616 | tf_op jit(solution)/shard_map/ppermute | solution.py:526
  9.9 7.4 %collective-permute-start.4 = (bf16[16,2048]{1,0:T(8,128)(2,1)S(1)}, bf16[16,2048]{1,0:T(8,128)(2,1)S(1)}, u32[]{:S(2)}, u32[]{:S(2)}) collective-permute-start(bf16[16,2048]{1,0:T(8,128)(2,1)S(1)} %pack_coarse.1), channel_id=1, source_target_pairs={{0,4},{4,0},{8,12},{12,8},{1,5},{5,1},{9,13},{13,9},{2,6},{6,2},{1... | collective-permute-start | bytes 196616 | tf_op jit(solution)/shard_map/ppermute | solution.py:526
  12.9 7.4 %copy-start.2 = (bf16[256,768]{1,0:T(8,128)(2,1)S(1)}, bf16[256,768]{1,0:T(8,128)(2,1)}, u32[]{:S(2)}) copy-start(bf16[256,768]{1,0:T(8,128)(2,1)} %qkv_ref.1) | copy-start | bytes 1179652
  12.9 7.4 %collective-permute-start.2 = (bf16[34,8,256]{2,1,0:T(8,128)(2,1)S(1)}, bf16[34,8,256]{2,1,0:T(8,128)(2,1)S(1)}, u32[]{:S(2)}, u32[]{:S(2)}) collective-permute-start(bf16[34,8,256]{2,1,0:T(8,128)(2,1)S(1)} %get-tuple-element.57), channel_id=1, source_target_pairs={{1,2},{2,1},{5,6},{6,5},{9,10},{10,9},{13,14},{14,13},{17,18},{18,... | collective-permute-start | bytes 417800 | tf_op jit(solution)/shard_map/ppermute | solution.py:521
  13.7 6.6 %collective-permute-start.3 = (bf16[34,8,256]{2,1,0:T(8,128)(2,1)S(1)}, bf16[34,8,256]{2,1,0:T(8,128)(2,1)S(1)}, u32[]{:S(2)}, u32[]{:S(2)}) collective-permute-start(bf16[34,8,256]{2,1,0:T(8,128)(2,1)S(1)} %get-tuple-element.58), channel_id=1, source_target_pairs={{0,1},{1,0},{2,3},{3,2},{4,5},{5,4},{6,7},{7,6},{8,9},{9,8},{10,11... | collective-permute-start | bytes 417800 | tf_op jit(solution)/shard_map/ppermute | solution.py:522
  17.3 2.3 %copy-start.9 = (f32[1,1024]{1,0:T(1,128)S(1)}, f32[1,1024]{1,0:T(1,128)}, u32[]{:S(2)}) copy-start(f32[1,1024]{1,0:T(1,128)} %constant.5.clone.coarse_freq) | copy-start | bytes 12292
  17.3 2.3 %copy-start.11 = (f32[1,256]{1,0:T(1,128)S(1)}, f32[1,256]{1,0:T(1,128)}, u32[]{:S(2)}) copy-start(f32[1,256]{1,0:T(1,128)} %constant.4.clone.fine_freq) | copy-start | bytes 3076
  17.3 3.0 %copy-start.4 = (bf16[256,256]{1,0:T(8,128)(2,1)S(1)}, bf16[256,256]{1,0:T(8,128)(2,1)}, u32[]{:S(2)}) copy-start(bf16[256,256]{1,0:T(8,128)(2,1)} %out_ref.1) | copy-start | bytes 393220
  17.4 2.3 %copy-start.8 = (f32[1024]{0:T(1024)S(1)}, f32[1024]{0:T(1024)}, u32[]{:S(2)}) copy-start(f32[1024]{0:T(1024)} %param.19) | copy-start | bytes 12292
  17.4 9.2 %collective-permute-start.8 = (bf16[4,16,2048]{2,1,0:T(8,128)(2,1)S(1)}, bf16[4,16,2048]{2,1,0:T(8,128)(2,1)S(1)}, u32[]{:S(2)}, u32[]{:S(2)}) collective-permute-start(bf16[4,16,2048]{2,1,0:T(8,128)(2,1)S(1)} %pad_maximum_fusion.1), channel_id=1, source_target_pairs={{0,2},{1,3},{2,0},{3,1},{4,6},{5,7},{6,4},{7,5},{8,10},{9,11},{10,... | collective-permute-start | bytes 786440 | tf_op jit(solution)/shard_map/ppermute | solution.py:526
  19.6 0.7 %copy-start.10 = (f32[256]{0:T(256)S(1)}, f32[256]{0:T(256)}, u32[]{:S(2)}) copy-start(f32[256]{0:T(256)} %param.18) | copy-start | bytes 3076
  26.5 1.5 %collective-permute-start.7 = (bf16[2,4,16,1024]{3,2,1,0:T(8,128)(2,1)S(1)}, bf16[2,4,16,1024]{3,2,1,0:T(8,128)(2,1)S(1)}, u32[]{:S(2)}, u32[]{:S(2)}) collective-permute-start(bf16[2,4,16,1024]{3,2,1,0:T(8,128)(2,1)S(1)} %get-tuple-element.68), channel_id=1, source_target_pairs={{0,1},{1,0},{2,3},{3,2},{4,5},{5,4},{6,7},{7,6},{8,9},{9,8},{10,11... | collective-permute-start | bytes 786440 | tf_op jit(solution)/shard_map/ppermute | solution.py:526
  26.5 1.9 %collective-permute-start.9 = (bf16[4,16,2048]{2,1,0:T(8,128)(2,1)S(1)}, bf16[4,16,2048]{2,1,0:T(8,128)(2,1)S(1)}, u32[]{:S(2)}, u32[]{:S(2)}) collective-permute-start(bf16[4,16,2048]{2,1,0:T(8,128)(2,1)S(1)} %collective-permute-done.8), channel_id=1, source_target_pairs={{0,1},{1,0},{2,3},{3,2},{4,5},{5,4},{6,7},{7,6},{8,9},{9,8},{10,11... | collective-permute-start | bytes 786440 | tf_op jit(solution)/shard_map/ppermute | solution.py:526
  27.0 2.0 %collective-permute-start.11 = (bf16[4,16,2048]{2,1,0:T(8,128)(2,1)S(1)}, bf16[4,16,2048]{2,1,0:T(8,128)(2,1)S(1)}, u32[]{:S(2)}, u32[]{:S(2)}) collective-permute-start(bf16[4,16,2048]{2,1,0:T(8,128)(2,1)S(1)} %pad_maximum_fusion.1), channel_id=1, source_target_pairs={{0,1},{1,0},{2,3},{3,2},{4,5},{5,4},{6,7},{7,6},{8,9},{9,8},{10,11... | collective-permute-start | bytes 786440 | tf_op jit(solution)/shard_map/ppermute | solution.py:526
  28.5 5.6 %collective-permute-start.10 = (bf16[4,16,1024]{2,1,0:T(8,128)(2,1)S(1)}, bf16[4,16,1024]{2,1,0:T(8,128)(2,1)S(1)}, u32[]{:S(2)}, u32[]{:S(2)}) collective-permute-start(bf16[4,16,1024]{2,1,0:T(8,128)(2,1)S(1)} %fusion.2), channel_id=1, source_target_pairs={{0,2},{1,3},{2,0},{3,1},{4,6},{5,7},{6,4},{7,5},{8,10},{9,11},{10,... | collective-permute-start | bytes 393224 | tf_op jit(solution)/shard_map/ppermute | solution.py:526
  29.2 1.0 %copy-start.3 = (bf16[3,64,1024]{2,1,0:T(8,128)(2,1)S(1)}, bf16[3,64,1024]{2,1,0:T(8,128)(2,1)}, u32[]{:S(2)}) copy-start(bf16[3,64,1024]{2,1,0:T(8,128)(2,1)} %qkv_hbm.1) | copy-start | bytes 1179652
  29.2 1.0 %copy-start.5 = (bf16[64,1024]{1,0:T(8,128)(2,1)S(1)}, bf16[64,1024]{1,0:T(8,128)(2,1)}, u32[]{:S(2)}) copy-start(bf16[64,1024]{1,0:T(8,128)(2,1)} %out_hbm.1) | copy-start | bytes 393220
  34.1 5.0 %collective-permute-start.12 = (bf16[4,16,1024]{2,1,0:T(8,128)(2,1)S(1)}, bf16[4,16,1024]{2,1,0:T(8,128)(2,1)S(1)}, u32[]{:S(2)}, u32[]{:S(2)}) collective-permute-start(bf16[4,16,1024]{2,1,0:T(8,128)(2,1)S(1)} %fusion.1), channel_id=1, source_target_pairs={{0,16},{16,0},{1,17},{17,1},{2,18},{18,2},{3,19},{19,3},{4,20},{20... | collective-permute-start | bytes 393224 | tf_op jit(solution)/shard_map/ppermute | solution.py:526
  35.7 3.5 %collective-permute-start.13 = (bf16[2,4,16,1024]{3,2,1,0:T(8,128)(2,1)S(1)}, bf16[2,4,16,1024]{3,2,1,0:T(8,128)(2,1)S(1)}, u32[]{:S(2)}, u32[]{:S(2)}) collective-permute-start(bf16[2,4,16,1024]{3,2,1,0:T(8,128)(2,1)S(1)} %bitcast.82), channel_id=1, source_target_pairs={{0,1},{1,0},{2,3},{3,2},{4,5},{5,4},{6,7},{7,6},{8,9},{9,8},{10,11... | collective-permute-start | bytes 786440 | tf_op jit(solution)/shard_map/ppermute | solution.py:526
  39.3 6.6 %collective-permute-start.14 = (bf16[128,1024]{1,0:T(8,128)(2,1)S(1)}, bf16[128,1024]{1,0:T(8,128)(2,1)S(1)}, u32[]{:S(2)}, u32[]{:S(2)}) collective-permute-start(bf16[128,1024]{1,0:T(8,128)(2,1)S(1)} %pad_maximum_fusion.2), channel_id=1, source_target_pairs={{0,4},{4,0},{8,12},{12,8},{1,5},{5,1},{9,13},{13,9},{2,6},{6,2},{1... | collective-permute-start | bytes 786440 | tf_op jit(solution)/shard_map/ppermute | solution.py:526
  40.7 6.7 %collective-permute-start.15 = (bf16[128,1024]{1,0:T(8,128)(2,1)S(1)}, bf16[128,1024]{1,0:T(8,128)(2,1)S(1)}, u32[]{:S(2)}, u32[]{:S(2)}) collective-permute-start(bf16[128,1024]{1,0:T(8,128)(2,1)S(1)} %get-tuple-element.103), channel_id=1, source_target_pairs={{0,16},{16,0},{1,17},{17,1},{2,18},{18,2},{3,19},{19,3},{4,20},{20... | collective-permute-start | bytes 786440 | tf_op jit(solution)/shard_map/ppermute | solution.py:526
  47.4 9.5 %collective-permute-start.16 = (bf16[96,1024]{1,0:T(8,128)(2,1)S(1)}, bf16[96,1024]{1,0:T(8,128)(2,1)S(1)}, u32[]{:S(2)}, u32[]{:S(2)}) collective-permute-start(bf16[96,1024]{1,0:T(8,128)(2,1)S(1)} %pad_maximum_fusion.4), channel_id=1, source_target_pairs={{0,8},{4,12},{8,0},{12,4},{1,9},{5,13},{9,1},{13,5},{2,10},{6,14},... | collective-permute-start | bytes 589832 | tf_op jit(solution)/shard_map/ppermute | solution.py:526
  49.0 8.0 %collective-permute-start.17 = (bf16[128,1024]{1,0:T(8,128)(2,1)S(1)}, bf16[128,1024]{1,0:T(8,128)(2,1)S(1)}, u32[]{:S(2)}, u32[]{:S(2)}) collective-permute-start(bf16[128,1024]{1,0:T(8,128)(2,1)S(1)} %get-tuple-element.102), channel_id=1, source_target_pairs={{0,16},{16,0},{1,17},{17,1},{2,18},{18,2},{3,19},{19,3},{4,20},{20... | collective-permute-start | bytes 786440 | tf_op jit(solution)/shard_map/ppermute | solution.py:526
  57.1 5.4 %collective-permute-start.18 = (bf16[80,1024]{1,0:T(8,128)(2,1)S(1)}, bf16[80,1024]{1,0:T(8,128)(2,1)S(1)}, u32[]{:S(2)}, u32[]{:S(2)}) collective-permute-start(bf16[80,1024]{1,0:T(8,128)(2,1)S(1)} %pad_maximum_fusion.5), channel_id=1, source_target_pairs={{0,2},{1,3},{2,0},{3,1},{4,6},{5,7},{6,4},{7,5},{8,10},{9,11},{10,... | collective-permute-start | bytes 491528 | tf_op jit(solution)/shard_map/ppermute | solution.py:526
  62.5 1.6 %collective-permute-start.19 = (bf16[2,64,1024]{2,1,0:T(8,128)(2,1)S(1)}, bf16[2,64,1024]{2,1,0:T(8,128)(2,1)S(1)}, u32[]{:S(2)}, u32[]{:S(2)}) collective-permute-start(bf16[2,64,1024]{2,1,0:T(8,128)(2,1)S(1)} %pad_maximum_fusion.3.near_ref), channel_id=1, source_target_pairs={{0,1},{1,0},{2,3},{3,2},{4,5},{5,4},{6,7},{7,6},{8,9},{9,8},{10,11... | collective-permute-start | bytes 786440 | tf_op jit(solution)/shard_map/ppermute | solution.py:526

commit v9 on v8

--- a/solution.py
+++ b/solution.py
@@ -20,6 +20,7 @@
 side = 8
 extent = side + 2 * RAD
 lanes_wide = 16
+thin = 4
 scale = 1.0 / math.sqrt(HD)
 vmem_bytes = 48 * 1024 * 1024
 
@@ -31,6 +32,10 @@
 def frequencies(channels):
     steps = np.float32(-log_span) * np.arange(channels, dtype=np.float32) / np.float32(channels)
     return np.exp(steps)[None]
+
+
+def time_gain(step_ref, gain_ref, freq_ref):
+    return gain_ref[...] * (1.0 + 0.5 * jnp.cos(step_ref[...].astype(jnp.float32) * freq_ref[...]))
 
 
 def odd_rank(axis):
@@ -64,7 +69,9 @@
     row_near_ref,
     col_far_ref,
     col_near_ref,
-    factor_ref,
+    step_ref,
+    gain_ref,
+    freq_ref,
     qkv_ref,
     out_ref,
     dx_ref,
@@ -81,16 +88,19 @@
     dq_grid,
     a_grid,
     bias_ref,
+    thin_bias_ref,
     total_ref,
 ):
     height, breadth = x_ref.shape[0], x_ref.shape[1]
     grid_rows, grid_cols = x_grid.shape[0], x_grid.shape[1]
     query_rows = dy_grid.shape[0]
     floats = jnp.float32
-    factor = factor_ref[...]
-
-    x_grid[...] = jnp.zeros_like(x_grid)
-    dy_grid[...] = jnp.zeros_like(dy_grid)
+    factor = time_gain(step_ref, gain_ref, freq_ref)
+
+    for grid, rows in ((x_grid, height + 2 * HALO), (dy_grid, height + 2 * RAD)):
+        grid[rows:] = jnp.zeros((grid.shape[0] - rows,) + grid.shape[1:], floats)
+        cols = breadth + 2 * HALO
+        grid[:rows, cols:] = jnp.zeros((rows, grid_cols - cols, D_F), floats)
     dk_grid[...] = jnp.zeros_like(dk_grid)
     dv_grid[...] = jnp.zeros_like(dv_grid)
     inner = slice(HALO, HALO + breadth)
@@ -129,67 +139,85 @@
     ups = dot(cotangents, out_ref[...], ((1,), (1,))).astype(jnp.bfloat16).astype(floats)
     u_grid[...] = ups.reshape(query_rows, grid_cols, D_F)
 
-    keys_count, heads_count = extent * lanes_wide, H_F * side * side
-    key_at = lax.broadcasted_iota(jnp.int32, (keys_count, heads_count), 0)
-    query_at = lax.broadcasted_iota(jnp.int32, (keys_count, heads_count), 1)
-    row_gap = (key_at // lanes_wide) - ((query_at // side) % side)
-    col_gap = (key_at % lanes_wide) - (query_at % side)
-    near = (row_gap >= 0) & (row_gap <= 2 * RAD) & (col_gap >= 0) & (col_gap <= 2 * RAD)
-    bias_ref[...] = jnp.where(near, 0.0, -1e30)
     gx, gy = lax.axis_index("gx"), lax.axis_index("gy")
     row_low, col_low = HALO - gy * height, HALO - gx * breadth
     row_high = row_low + lax.axis_size("gy") * height
     col_high = col_low + lax.axis_size("gx") * breadth
-    lone = lax.broadcasted_iota(jnp.int32, (keys_count, 1), 0)
-    head_of = lax.broadcasted_iota(jnp.int32, (side * side, D_F), 1) // HD
+
+    def window_bias(query_rows):
+        shape = ((query_rows + 2 * RAD) * lanes_wide, H_F * query_rows * side)
+        key_at = lax.broadcasted_iota(jnp.int32, shape, 0)
+        query_at = lax.broadcasted_iota(jnp.int32, shape, 1)
+        row_gap = (key_at // lanes_wide) - ((query_at // side) % query_rows)
+        col_gap = (key_at % lanes_wide) - (query_at % side)
+        near = (row_gap >= 0) & (row_gap <= 2 * RAD) & (col_gap >= 0) & (col_gap <= 2 * RAD)
+        return jnp.where(near, 0.0, -1e30)
+
+    bias_ref[...] = window_bias(side)
+    thin_bias_ref[...] = window_bias(thin)
+
+    def head_of(rows):
+        return lax.broadcasted_iota(jnp.int32, (rows, D_F), 1) // HD
 
     def spread(block):
+        block = block.reshape(-1, D_F)
+        heads = head_of(block.shape[0])
         return jnp.concatenate(
-            [jnp.where(head_of == h, block, 0.0).astype(jnp.bfloat16) for h in range(H_F)], axis=0
+            [jnp.where(heads == h, block, 0.0).astype(jnp.bfloat16) for h in range(H_F)], axis=0
         )
 
     def collect(full):
-        total = jnp.where(head_of == 0, full[: side * side], 0.0)
+        rows = full.shape[0] // H_F
+        heads = head_of(rows)
+        total = jnp.where(heads == 0, full[:rows], 0.0)
         for h in range(1, H_F):
-            piece = full[h * side * side : (h + 1) * side * side]
-            total = jnp.where(head_of == h, piece, total)
-        return total.reshape(side, side, D_F)
-
-    for block_row in range(query_rows // side):
-        top = block_row * side
-        for block_col in range((grid_cols - side) // side):
-            start = block_col * side
-            window = (slice(top, top + extent), slice(start, start + lanes_wide))
-            keys = k_grid[window].reshape(keys_count, D_F).astype(jnp.bfloat16)
-            values = v_grid[window].reshape(keys_count, D_F).astype(jnp.bfloat16)
-            place = (slice(top, top + side), slice(start + RAD, start + RAD + side))
-            wide_queries = spread(q_grid[place].reshape(side * side, D_F))
-            wide_ups = spread(u_grid[place].reshape(side * side, D_F))
-            key_row = lone // lanes_wide + top
-            key_col = lone % lanes_wide + start
-            inside = (
-                (key_row >= row_low)
-                & (key_row < row_high)
-                & (key_col >= col_low)
-                & (key_col < col_high)
-            )
-            scores = dot(keys, wide_queries, ((1,), (1,)))
-            scores = scores + (bias_ref[...] + jnp.where(inside, 0.0, -1e30))
-            raised = jnp.exp(scores - jnp.max(scores, axis=0, keepdims=True))
-            shares = raised * (1.0 / jnp.sum(raised, axis=0, keepdims=True))
-            products = dot(values, wide_ups, ((1,), (1,)))
-            centre = jnp.sum(shares * products, axis=0, keepdims=True)
-            slopes = (shares * (products - centre)).astype(jnp.bfloat16)
-            weights = shares.astype(jnp.bfloat16)
-            dv_grid[window] += dot(weights, wide_ups).reshape(extent, lanes_wide, D_F)
-            dk_grid[window] += dot(slopes, wide_queries).reshape(extent, lanes_wide, D_F)
-            block = (slice(top, top + side), slice(start, start + side))
+            total = jnp.where(heads == h, full[h * rows : (h + 1) * rows], total)
+        return total.reshape(rows // side, side, D_F)
+
+    def attend(top, start, query_rows, near_bias, live):
+        key_rows = query_rows + 2 * RAD
+        window = (slice(top, top + key_rows), slice(start, start + lanes_wide))
+        keys = k_grid[window].reshape(-1, D_F).astype(jnp.bfloat16)
+        values = v_grid[window].reshape(-1, D_F).astype(jnp.bfloat16)
+        place = (slice(top, top + query_rows), slice(start + RAD, start + RAD + side))
+        wide_queries = spread(q_grid[place])
+        ups = u_grid[place]
+        if live < query_rows:
+            row = lax.broadcasted_iota(jnp.int32, ups.shape, 0)
+            ups = jnp.where(row < live, ups, 0.0)
+        wide_ups = spread(ups)
+        lone = lax.broadcasted_iota(jnp.int32, (key_rows * lanes_wide, 1), 0)
+        key_row, key_col = lone // lanes_wide + top, lone % lanes_wide + start
+        inside = (key_row >= row_low) & (key_row < row_high)
+        inside = inside & (key_col >= col_low) & (key_col < col_high)
+        scores = dot(keys, wide_queries, ((1,), (1,)))
+        scores = scores + (near_bias[...] + jnp.where(inside, 0.0, -1e30))
+        raised = jnp.exp(scores - jnp.max(scores, axis=0, keepdims=True))
+        shares = raised * (1.0 / jnp.sum(raised, axis=0, keepdims=True))
+        products = dot(values, wide_ups, ((1,), (1,)))
+        centre = jnp.sum(shares * products, axis=0, keepdims=True)
+        slopes = (shares * (products - centre)).astype(jnp.bfloat16)
+        weights = shares.astype(jnp.bfloat16)
+        first, final = max(top, HALO), min(top + key_rows, HALO + height)
+        kept = slice((first - top) * lanes_wide, (final - top) * lanes_wide)
+        target = (slice(first - HALO, final - HALO), slice(start, start + lanes_wide))
+        shape = (final - first, lanes_wide, D_F)
+        dv_grid[target] += dot(weights[kept], wide_ups).reshape(shape)
+        dk_grid[target] += dot(slopes[kept], wide_queries).reshape(shape)
+        return keys, values, slopes, weights
+
+    for start in range(0, grid_cols - side, side):
+        for top in range(RAD, RAD + height, side):
+            keys, values, slopes, weights = attend(top, start, side, bias_ref, side)
+            block = (slice(top - RAD, top - RAD + side), slice(start, start + side))
             a_grid[block] = collect(dot(weights, values, ((0,), (0,))))
             dq_grid[block] = collect(dot(slopes, keys, ((0,), (0,))))
+        attend(0, start, thin, thin_bias_ref, RAD)
+        attend(RAD + height, start, thin, thin_bias_ref, RAD)
 
     count = height * breadth
-    own_queries = (slice(RAD, RAD + height), slice(RAD, RAD + breadth))
-    own_keys = (slice(HALO, HALO + height), inner)
+    own_queries = (slice(0, height), slice(RAD, RAD + breadth))
+    own_keys = (slice(0, height), inner)
     attended = a_grid[own_queries].reshape(count, D_F).astype(jnp.bfloat16)
     grad_q = (dq_grid[own_queries].reshape(count, D_F) * scale).astype(jnp.bfloat16)
     grad_k = dk_grid[own_keys].reshape(count, D_F).astype(jnp.bfloat16)
@@ -220,7 +248,7 @@
 
 def fine_block(peers, picture, *operands):
     height, breadth = picture.shape[0], picture.shape[1]
-    query_rows = round_up(height + 2 * RAD, side)
+    query_rows = RAD + height + thin
     query_cols = round_up(breadth + 2 * RAD, side)
     grid_rows, grid_cols = query_rows + 2 * RAD, query_cols + side
     across, down = peers
@@ -229,7 +257,8 @@
     vmem = pl.BlockSpec(memory_space=pltpu.VMEM)
     wide = pltpu.VMEM((grid_rows, grid_cols, D_F), jnp.float32)
     middle = pltpu.VMEM((query_rows, grid_cols, D_F), jnp.float32)
-    small = pltpu.VMEM((query_rows, query_cols, D_F), jnp.float32)
+    small = pltpu.VMEM((height, query_cols, D_F), jnp.float32)
+    strip = pltpu.VMEM((height, grid_cols, D_F), jnp.float32)
     return pl.pallas_call(
         fine_body,
         out_shape=(
@@ -237,7 +266,7 @@
             jax.ShapeDtypeStruct(halves, jnp.float32),
             jax.ShapeDtypeStruct(halves, jnp.bfloat16),
         ),
-        in_specs=[vmem] * 9,
+        in_specs=[vmem] * 11,
         out_specs=(vmem, vmem, vmem),
         scratch_shapes=[
             wide,
@@ -246,11 +275,12 @@
             wide,
             middle,
             middle,
-            wide,
-            wide,
+            strip,
+            strip,
             small,
             small,
             pltpu.VMEM((extent * lanes_wide, H_F * side * side), jnp.float32),
+            pltpu.VMEM(((thin + 2 * RAD) * lanes_wide, H_F * thin * side), jnp.float32),
             pltpu.VMEM((across * down, rows, 4 * D_F), jnp.float32),
         ],
         compiler_params=pltpu.CompilerParams(vmem_limit_bytes=vmem_bytes),
@@ -261,11 +291,14 @@
 def coarse_body(
     x_ref,
     dy_ref,
-    factor_ref,
+    step_ref,
+    gain_ref,
+    freq_ref,
     qkv_hbm,
     out_hbm,
     parts_ref,
     grads_ref,
+    factor_ref,
     qkv_ref,
     out_ref,
     arrived,
@@ -277,6 +310,7 @@
     for fetch in fetches:
         fetch.start()
     tokens = x_ref[...].astype(jnp.float32)
+    factor_ref[...] = time_gain(step_ref, gain_ref, freq_ref)
     normed = (tokens * inverse_rms(tokens) * factor_ref[...]).astype(jnp.bfloat16)
     cot = dy_ref[...]
     for fetch in fetches:
@@ -303,7 +337,7 @@
     grads_ref[3 * HD :] = dot(mixed, cot, ((0,), (0,))).astype(grads_ref.dtype)
 
 
-def coarse_block(tokens, cotangents, factor, head_qkv, head_out):
+def coarse_block(tokens, cotangents, step, gain, head_qkv, head_out):
     count = tokens.shape[0]
     vmem = pl.BlockSpec(memory_space=pltpu.VMEM)
     return pl.pallas_call(
@@ -311,9 +345,10 @@
         out_shape=(
             jax.ShapeDtypeStruct((count, D_C), jnp.bfloat16),
             jax.ShapeDtypeStruct((4 * HD, D_C), jnp.bfloat16),
+            jax.ShapeDtypeStruct((1, D_C), jnp.float32),
         ),
-        in_specs=[vmem] * 3 + [pl.BlockSpec(memory_space=pltpu.HBM)] * 2,
-        out_specs=(vmem, vmem),
+        in_specs=[vmem] * 5 + [pl.BlockSpec(memory_space=pltpu.HBM)] * 2,
+        out_specs=(vmem, vmem, vmem),
         scratch_shapes=[
             pltpu.VMEM(head_qkv.shape, jnp.bfloat16),
             pltpu.VMEM(head_out.shape, jnp.bfloat16),
@@ -321,7 +356,7 @@
         ],
         compiler_params=pltpu.CompilerParams(vmem_limit_bytes=vmem_bytes),
         name="coarse_block",
-    )(tokens, cotangents, factor, head_qkv, head_out)
+    )(tokens, cotangents, step, gain[None], frequencies(D_C), head_qkv, head_out)
 
 
 def row_edges_body(x_low, x_high, dy_low, dy_high, near_ref, far_ref):
@@ -399,38 +434,19 @@
     )(*after, tokens, cotangents)
 
 
-def factors_body(step, fine_gain, coarse_gain, fine_freq, coarse_freq, fine_ref, coarse_ref):
-    time = step[0].astype(jnp.float32)
-    fine_ref[...] = fine_gain[...] * (1.0 + 0.5 * jnp.cos(time * fine_freq[...]))
-    coarse_ref[...] = coarse_gain[...] * (1.0 + 0.5 * jnp.cos(time * coarse_freq[...]))
-
-
-def time_factors(step, fine_gain, coarse_gain):
-    vmem = pl.BlockSpec(memory_space=pltpu.VMEM)
-    return pl.pallas_call(
-        factors_body,
-        out_shape=(
-            jax.ShapeDtypeStruct((1, D_F), jnp.float32),
-            jax.ShapeDtypeStruct((1, D_C), jnp.float32),
-        ),
-        in_specs=[pl.BlockSpec(memory_space=pltpu.SMEM)] + [vmem] * 4,
-        out_specs=(vmem, vmem),
-        compiler_params=pltpu.CompilerParams(vmem_limit_bytes=vmem_bytes),
-        name="time_factors",
-    )(step, fine_gain[None], coarse_gain[None], frequencies(D_F), frequencies(D_C))
-
-
-def pair_sum_body(own, first, second, qkv_ref, out_ref):
+def pair_sum_body(own, *refs):
+    qkv_ref, out_ref = refs[-2:]
+    come = jnp.concatenate([ref[...] for ref in refs[:-2]], axis=0)
     for part in range(4):
-        come = (first, second)[part // 2][(part % 2) * HD : (part % 2 + 1) * HD]
-        total = own[part * HD : (part + 1) * HD].astype(jnp.float32) + come.astype(jnp.float32)
+        rows = slice(part * HD, (part + 1) * HD)
+        total = own[rows].astype(jnp.float32) + come[rows].astype(jnp.float32)
         if part < 3:
             qkv_ref[part] = total.astype(jnp.bfloat16)
         else:
             out_ref[...] = total.astype(jnp.bfloat16)
 
 
-def pair_sum(own, first, second):
+def pair_sum(own, *come):
     vmem = pl.BlockSpec(memory_space=pltpu.VMEM)
     return pl.pallas_call(
         pair_sum_body,
@@ -438,11 +454,11 @@
             jax.ShapeDtypeStruct((3, HD, D_C), jnp.bfloat16),
             jax.ShapeDtypeStruct((HD, D_C), jnp.bfloat16),
         ),
-        in_specs=[vmem] * 3,
+        in_specs=[vmem] * (1 + len(come)),
         out_specs=(vmem, vmem),
         compiler_params=pltpu.CompilerParams(vmem_limit_bytes=vmem_bytes),
         name="pair_sum",
-    )(own, first, second)
+    )(own, *come)
 
 
 def block_copies(near_ref, low, qkv_hbm, out_hbm, sems):
@@ -572,12 +588,11 @@
     count = own.shape[0]
     row_group = all_rows(own)
     edges = col_edges(picture, cotangent, row_far, row_near)
-    *edges, step, gain_f, gain_c = tied(*edges, timestep, fine_gain, coarse_gain)
     col_near, col_far = neighbours(*edges, "gx")
-    factor, coarse_factor = time_factors(step, gain_f, gain_c)
+    step = timestep[None]
     cross = swapped(row_group, "gx", 2)
     beside = swapped(row_group, "gx", 1)
-    col_far, col_near, row_group, factor = tied(col_far, col_near, row_group, factor)
+    col_far, col_near, row_group = tied(col_far, col_near, row_group)
     dx_picture, fine_keep, fine_send = fine_block(
         (across, downs),
         picture,
@@ -586,7 +601,9 @@
         row_near,
         col_far,
         col_near,
-        factor,
+        step,
+        fine_gain[None],
+        frequencies(D_F),
         fine_qkv,
         fine_out,
     )
@@ -596,8 +613,8 @@
 
     fine_quarter = narrow(fine_half[0] + wide(swapped(narrow(fine_half[1]), "gx", 2)))
     everyone = jnp.stack([row_group, cross, beside, opposite]).reshape(-1, 2 * D_C)
-    parts, coarse_partial = coarse_block(
-        everyone[:, :D_C], everyone[:, D_C:], coarse_factor, coarse_qkv, coarse_out
+    parts, coarse_partial, coarse_factor = coarse_block(
+        everyone[:, :D_C], everyone[:, D_C:], step, coarse_gain, coarse_qkv, coarse_out
     )
     fine_quarter, parts, coarse_partial = tied(fine_quarter, parts, coarse_partial)
 
@@ -608,7 +625,8 @@
     fine_quarter, coarse_kept, coarse_partial = tied(fine_quarter, coarse_kept, coarse_partial)
 
     pair_batch = lax.axis_size("batch") == 2
-    halves = (coarse_partial[: 2 * HD], coarse_partial[2 * HD :])
+    cut = 7 * HD // 4
+    halves = (coarse_partial[:cut], coarse_partial[cut:])
     others = [swapped(half, "batch", 1) if pair_batch else half for half in halves]
     mask = 1
     while mask < downs:

time: 65.1 us -> 65.8 us (1.011)
  starting transfers between devices: 26 us -> 28.5 us
  waiting for transfers between devices: 22.2 us -> 19.8 us
    ppermute x16, starting transfers between devices: 15.7 us -> 18.2 us  [swapped(): lax.ppermute(value, axis, [(i, i ^ mask) for i in range(lax.axis_size(axi...]
    ppermute x16, waiting for transfers between devices: 22.2 us -> 19.8 us  [swapped(): lax.ppermute(value, axis, [(i, i ^ mask) for i in range(lax.axis_size(axi...]
where the time goes in v9:
time: 65.8 us; the launch traced here: 65.5 us
  starting transfers between devices  28.5 us (43%)
  waiting for transfers between devices  19.8 us (30%)
  Pallas kernels  12.1 us (18%)
  local copies, waits for them, and re-layouts  2.82 us (4%)
  between operations  1.67 us (3%)
    ppermute x16, waiting for transfers between devices, swapped(): lax.ppermute(value, axis, [(i, i ^ mask) for i in range(lax.axis_size(axi...  19.8 us
    ppermute x16, starting transfers between devices, swapped(): lax.ppermute(value, axis, [(i, i ^ mask) for i in range(lax.axis_size(axi...  18.2 us
    ppermute x2, starting transfers between devices, neighbours(): return (lax.ppermute(to_near, axis, near), from_far)  8.81 us
    pallas_call x1, Pallas kernels, fine_block(): pl.pallas_call(fine_body, out_shape=(jax.ShapeDtypeStruct((height, breadt...  6.76 us
    pallas_call x1, Pallas kernels, coarse_block(): pl.pallas_call(coarse_body, out_shape=(jax.ShapeDtypeStruct((count, D_C),...  2.25 us
    unnamed x24, local copies, waits for them, and re-layouts  1.6 us
    ppermute x2, starting transfers between devices, neighbours(): from_far = lax.ppermute(to_far, axis, far)  1.47 us
    pallas_call x1, Pallas kernels, near_step(): pl.pallas_call(near_body, out_shape=(jax.ShapeDtypeStruct((D_F, 3 * D_F),...  1.36 us
  transfers between devices with their start and end apart: 20, of which 10 were waited for; matrix products, arithmetic and copies ran while one was open for 1% of the time, Pallas kernels for 17%

profile of v9, /device:TPU:0, one launch (start us, length us, event | category | flops | bytes accessed | tf_op | source)
XLA Modules:
  0.0 65.5 jit_solution(17747410593269814769)
XLA Ops:
  0.6 0.0 copy-start.1
  0.6 1.0 %slice_bitcast_fusion.2 = (bf16[6,32,256]{2,1,0:T(8,128)(2,1)S(1)}, bf16[6,32,256]{2,1,0:T(8,128)(2,1)S(1)}) fusion(bf16[1,8,32,256]{3,2,1,0:T(8,128)(2,1)} %param.13), kind=kLoop, calls=%fused_computation.22 | loop fusion | bytes 393216 | tf_op jit(solution)/shard_map/slice | solution.py:389
  1.7 0.0 copy-start.6
  1.7 0.0 copy-start.7
  1.7 0.7 %collective-permute-start = (bf16[9,32,256]{2,1,0:T(8,128)(2,1)S(1)}, bf16[9,32,256]{2,1,0:T(8,128)(2,1)S(1)}, u32[]{:S(2)}, u32[]{:S(2)}) collective-permute-start(bf16[9,32,256]{2,1,0:T(8,128)(2,1)S(1)} %get-tuple-element.46.second), channel_id=1, source_target_pairs={{4,8},{8,4},{5,9},{9,5},{6,10},{10,6},{7,11},{11,7},{20,24},{24,20... | collective-permute-start | bytes 442376 | tf_op jit(solution)/shard_map/ppermute | solution.py:537
  2.4 5.9 %collective-permute-start.1 = (bf16[9,32,256]{2,1,0:T(8,128)(2,1)S(1)}, bf16[9,32,256]{2,1,0:T(8,128)(2,1)S(1)}, u32[]{:S(2)}, u32[]{:S(2)}) collective-permute-start(bf16[9,32,256]{2,1,0:T(8,128)(2,1)S(1)} %get-tuple-element.47.first), channel_id=1, source_target_pairs={{0,4},{4,0},{8,12},{12,8},{1,5},{5,1},{9,13},{13,9},{2,6},{6,2},{1... | collective-permute-start | bytes 442376 | tf_op jit(solution)/shard_map/ppermute | solution.py:538
  8.3 1.4 %collective-permute-start.6 = (bf16[16,2048]{1,0:T(8,128)(2,1)S(1)}, bf16[16,2048]{1,0:T(8,128)(2,1)S(1)}, u32[]{:S(2)}, u32[]{:S(2)}) collective-permute-start(bf16[16,2048]{1,0:T(8,128)(2,1)S(1)} %pack_coarse.1), channel_id=1, source_target_pairs={{0,12},{4,8},{8,4},{12,0},{1,13},{5,9},{9,5},{13,1},{2,14},{6,10},... | collective-permute-start | bytes 196616 | tf_op jit(solution)/shard_map/ppermute | solution.py:542
  9.8 0.2 collective-permute-start.5
  9.9 2.9 %collective-permute-start.4 = (bf16[16,2048]{1,0:T(8,128)(2,1)S(1)}, bf16[16,2048]{1,0:T(8,128)(2,1)S(1)}, u32[]{:S(2)}, u32[]{:S(2)}) collective-permute-start(bf16[16,2048]{1,0:T(8,128)(2,1)S(1)} %pack_coarse.1), channel_id=1, source_target_pairs={{0,4},{4,0},{8,12},{12,8},{1,5},{5,1},{9,13},{13,9},{2,6},{6,2},{1... | collective-permute-start | bytes 196616 | tf_op jit(solution)/shard_map/ppermute | solution.py:542
  12.8 0.0 collective-permute-done.row_far_ref
  12.8 0.0 collective-permute-done.1.row_near_ref
  12.8 0.0 copy-done
  12.8 0.1 col_edges.1
  12.9 0.0 copy-start.2
  12.9 0.8 %collective-permute-start.2 = (bf16[34,8,256]{2,1,0:T(8,128)(2,1)S(1)}, bf16[34,8,256]{2,1,0:T(8,128)(2,1)S(1)}, u32[]{:S(2)}, u32[]{:S(2)}) collective-permute-start(bf16[34,8,256]{2,1,0:T(8,128)(2,1)S(1)} %get-tuple-element.48), channel_id=1, source_target_pairs={{1,2},{2,1},{5,6},{6,5},{9,10},{10,9},{13,14},{14,13},{17,18},{18,... | collective-permute-start | bytes 417800 | tf_op jit(solution)/shard_map/ppermute | solution.py:537
  13.7 2.9 %collective-permute-start.3 = (bf16[34,8,256]{2,1,0:T(8,128)(2,1)S(1)}, bf16[34,8,256]{2,1,0:T(8,128)(2,1)S(1)}, u32[]{:S(2)}, u32[]{:S(2)}) collective-permute-start(bf16[34,8,256]{2,1,0:T(8,128)(2,1)S(1)} %get-tuple-element.49), channel_id=1, source_target_pairs={{0,1},{1,0},{2,3},{3,2},{4,5},{5,4},{6,7},{7,6},{8,9},{9,8},{10,11... | collective-permute-start | bytes 417800 | tf_op jit(solution)/shard_map/ppermute | solution.py:538
  16.6 0.0 collective-permute-done.6
  16.6 0.7 %collective-permute-done.5 = bf16[16,2048]{1,0:T(8,128)(2,1)S(1)} collective-permute-done((bf16[16,2048]{1,0:T(8,128)(2,1)S(1)}, bf16[16,2048]{1,0:T(8,128)(2,1)S(1)}, u32[]{:S(2)}, u32[]{:S(2)}) %collective-permute-start.5) | collective-permute-done | bytes 65568 | tf_op jit(solution)/shard_map/ppermute | solution.py:542
  17.3 0.0 collective-permute-done.4
  17.3 1.6 %collective-permute-start.8 = (bf16[4,16,2048]{2,1,0:T(8,128)(2,1)S(1)}, bf16[4,16,2048]{2,1,0:T(8,128)(2,1)S(1)}, u32[]{:S(2)}, u32[]{:S(2)}) collective-permute-start(bf16[4,16,2048]{2,1,0:T(8,128)(2,1)S(1)} %pad_maximum_fusion.1), channel_id=1, source_target_pairs={{0,2},{1,3},{2,0},{3,1},{4,6},{5,7},{6,4},{7,5},{8,10},{9,11},{10,... | collective-permute-start | bytes 786440 | tf_op jit(solution)/shard_map/ppermute | solution.py:542
  19.5 0.0 collective-permute-done.2.col_far_ref
  19.6 0.0 collective-permute-done.3.col_near_ref
  19.6 0.0 copy-start.10
  19.6 0.6 copy-done.10
  20.3 6.8 %fine_block.1 = (bf16[8,32,256]{2,1,0:T(8,128)(2,1)}, f32[2,4,16,1024]{3,2,1,0:T(8,128)S(1)}, bf16[2,4,16,1024]{3,2,1,0:T(8,128)(2,1)S(1)}) custom-call(bf16[8,32,256]{2,1,0:T(8,128)(2,1)S(1)} %bitcast.62, bf16[8,32,256]{2,1,0:T(8,128)(2,1)S(1)} %bitcast.64, bf16[9,32,256]{2,1,0:T(8,128)(2,1)S(1)} %collective-permute-done.row_far_ref, ...), custom_call_target="tpu_custom_call" | custom-call | tf_op jit(solution)/shard_map/fine_block/pallas_call | solution.py:262
  27.0 0.0 collective-permute-start.7
  27.0 0.0 collective-permute-done.8
  27.0 0.5 collective-permute-start.9
  27.5 0.0 collective-permute-start.11
  27.5 1.0 %collective-permute-done.7 = bf16[2,4,16,1024]{3,2,1,0:T(8,128)(2,1)S(1)} collective-permute-done((bf16[2,4,16,1024]{3,2,1,0:T(8,128)(2,1)S(1)}, bf16[2,4,16,1024]{3,2,1,0:T(8,128)(2,1)S(1)}, u32[]{:S(2)}, u32[]{:S(2)}) %collective-permute-start.7) | collective-permute-done | bytes 262176 | tf_op jit(solution)/shard_map/ppermute | solution.py:542
  28.5 0.1 convert_add_fusion.1
  28.6 0.3 collective-permute-done.9
  28.9 1.4 %collective-permute-start.10 = (bf16[4,16,1024]{2,1,0:T(8,128)(2,1)S(1)}, bf16[4,16,1024]{2,1,0:T(8,128)(2,1)S(1)}, u32[]{:S(2)}, u32[]{:S(2)}) collective-permute-start(bf16[4,16,1024]{2,1,0:T(8,128)(2,1)S(1)} %fusion.2), channel_id=1, source_target_pairs={{0,2},{1,3},{2,0},{3,1},{4,6},{5,7},{6,4},{7,5},{8,10},{9,11},{10,... | collective-permute-start | bytes 393224 | tf_op jit(solution)/shard_map/ppermute | solution.py:542
  30.3 0.0 collective-permute-done.11
  30.3 0.1 pad_maximum_fusion
  30.5 0.0 copy-start.3
  30.5 0.0 copy-start.5
  30.5 0.0 copy-start.9
  30.5 0.1 fusion.5
  30.6 0.0 copy-start.8
  30.6 0.9 %copy-done.3 = bf16[3,64,1024]{2,1,0:T(8,128)(2,1)S(1)} copy-done((bf16[3,64,1024]{2,1,0:T(8,128)(2,1)S(1)}, bf16[3,64,1024]{2,1,0:T(8,128)(2,1)}, u32[]{:S(2)}) %copy-start.3) | copy-done | bytes 393240
  31.5 0.0 copy-done.5
  31.5 2.3 %coarse_block.1 = (bf16[256,1024]{1,0:T(8,128)(2,1)S(1)}, bf16[256,1024]{1,0:T(8,128)(2,1)S(1)}, f32[1,1024]{1,0:T(1,128)S(1)}) custom-call(bf16[256,1024]{1,0:T(8,128)(2,1)S(1)} %get-tuple-element.87.x_ref, bf16[256,1024]{1,0:T(8,128)(2,1)S(1)} %get-tuple-element.86.dy_ref, s32[1,1]{1,0:T(1,128)} %bitcast.60.step_ref, f32[1,1024]{1,0:T(1,128)S(1)} %bitcast.69, ...), custom_call_target="tpu_custom_call" | custom-call | tf_op jit(solution)/shard_map/coarse_block/pallas_call | solution.py:343
  33.8 0.8 %collective-permute-done.10 = bf16[4,16,1024]{2,1,0:T(8,128)(2,1)S(1)} collective-permute-done((bf16[4,16,1024]{2,1,0:T(8,128)(2,1)S(1)}, bf16[4,16,1024]{2,1,0:T(8,128)(2,1)S(1)}, u32[]{:S(2)}, u32[]{:S(2)}) %collective-permute-start.10) | collective-permute-done | bytes 131104 | tf_op jit(solution)/shard_map/ppermute | solution.py:542
  34.6 1.6 %collective-permute-start.12 = (bf16[4,16,1024]{2,1,0:T(8,128)(2,1)S(1)}, bf16[4,16,1024]{2,1,0:T(8,128)(2,1)S(1)}, u32[]{:S(2)}, u32[]{:S(2)}) collective-permute-start(bf16[4,16,1024]{2,1,0:T(8,128)(2,1)S(1)} %fusion.1), channel_id=1, source_target_pairs={{0,16},{16,0},{1,17},{17,1},{2,18},{18,2},{3,19},{19,3},{4,20},{20... | collective-permute-start | bytes 393224 | tf_op jit(solution)/shard_map/ppermute | solution.py:542
  36.2 0.1 collective-permute-start.13
  36.3 3.3 %collective-permute-done.12 = bf16[4,16,1024]{2,1,0:T(8,128)(2,1)S(1)} collective-permute-done((bf16[4,16,1024]{2,1,0:T(8,128)(2,1)S(1)}, bf16[4,16,1024]{2,1,0:T(8,128)(2,1)S(1)}, u32[]{:S(2)}, u32[]{:S(2)}) %collective-permute-start.12) | collective-permute-done | bytes 131104 | tf_op jit(solution)/shard_map/ppermute | solution.py:542
  39.7 0.0 collective-permute-done.13
  39.7 0.1 convert_add_fusion
  39.8 2.1 %collective-permute-start.14 = (bf16[128,1024]{1,0:T(8,128)(2,1)S(1)}, bf16[128,1024]{1,0:T(8,128)(2,1)S(1)}, u32[]{:S(2)}, u32[]{:S(2)}) collective-permute-start(bf16[128,1024]{1,0:T(8,128)(2,1)S(1)} %pad_maximum_fusion.2), channel_id=1, source_target_pairs={{0,4},{4,0},{8,12},{12,8},{1,5},{5,1},{9,13},{13,9},{2,6},{6,2},{1... | collective-permute-start | bytes 786440 | tf_op jit(solution)/shard_map/ppermute | solution.py:542
  41.9 1.6 %collective-permute-start.15 = (bf16[112,1024]{1,0:T(8,128)(2,1)S(1)}, bf16[112,1024]{1,0:T(8,128)(2,1)S(1)}, u32[]{:S(2)}, u32[]{:S(2)}) collective-permute-start(bf16[112,1024]{1,0:T(8,128)(2,1)S(1)} %slice.110), channel_id=1, source_target_pairs={{0,16},{16,0},{1,17},{17,1},{2,18},{18,2},{3,19},{19,3},{4,20},{20... | collective-permute-start | bytes 688136 | tf_op jit(solution)/shard_map/ppermute | solution.py:542
  43.5 3.6 %collective-permute-done.14 = bf16[128,1024]{1,0:T(8,128)(2,1)S(1)} collective-permute-done((bf16[128,1024]{1,0:T(8,128)(2,1)S(1)}, bf16[128,1024]{1,0:T(8,128)(2,1)S(1)}, u32[]{:S(2)}, u32[]{:S(2)}) %collective-permute-start.14) | collective-permute-done | bytes 262176 | tf_op jit(solution)/shard_map/ppermute | solution.py:542
  47.2 0.8 %collective-permute-done.15.refs_0_ = bf16[112,1024]{1,0:T(8,128)(2,1)S(1)} collective-permute-done((bf16[112,1024]{1,0:T(8,128)(2,1)S(1)}, bf16[112,1024]{1,0:T(8,128)(2,1)S(1)}, u32[]{:S(2)}, u32[]{:S(2)}) %collective-permute-start.15) | collective-permute-done | bytes 229408 | tf_op jit(solution)/shard_map/ppermute | solution.py:542
  48.1 2.0 %collective-permute-start.16 = (bf16[96,1024]{1,0:T(8,128)(2,1)S(1)}, bf16[96,1024]{1,0:T(8,128)(2,1)S(1)}, u32[]{:S(2)}, u32[]{:S(2)}) collective-permute-start(bf16[96,1024]{1,0:T(8,128)(2,1)S(1)} %pad_maximum_fusion.4), channel_id=1, source_target_pairs={{0,8},{4,12},{8,0},{12,4},{1,9},{5,13},{9,1},{13,5},{2,10},{6,14},... | collective-permute-start | bytes 589832 | tf_op jit(solution)/shard_map/ppermute | solution.py:542
  50.1 1.6 %collective-permute-start.17 = (bf16[144,1024]{1,0:T(8,128)(2,1)S(1)}, bf16[144,1024]{1,0:T(8,128)(2,1)S(1)}, u32[]{:S(2)}, u32[]{:S(2)}) collective-permute-start(bf16[144,1024]{1,0:T(8,128)(2,1)S(1)} %slice.115), channel_id=1, source_target_pairs={{0,16},{16,0},{1,17},{17,1},{2,18},{18,2},{3,19},{19,3},{4,20},{20... | collective-permute-start | bytes 884744 | tf_op jit(solution)/shard_map/ppermute | solution.py:542
  51.7 6.0 %collective-permute-done.16 = bf16[96,1024]{1,0:T(8,128)(2,1)S(1)} collective-permute-done((bf16[96,1024]{1,0:T(8,128)(2,1)S(1)}, bf16[96,1024]{1,0:T(8,128)(2,1)S(1)}, u32[]{:S(2)}, u32[]{:S(2)}) %collective-permute-start.16) | collective-permute-done | bytes 196640 | tf_op jit(solution)/shard_map/ppermute | solution.py:542
  57.7 0.0 collective-permute-done.17.refs_1_
  57.7 1.3 %collective-permute-start.18 = (bf16[80,1024]{1,0:T(8,128)(2,1)S(1)}, bf16[80,1024]{1,0:T(8,128)(2,1)S(1)}, u32[]{:S(2)}, u32[]{:S(2)}) collective-permute-start(bf16[80,1024]{1,0:T(8,128)(2,1)S(1)} %pad_maximum_fusion.5), channel_id=1, source_target_pairs={{0,2},{1,3},{2,0},{3,1},{4,6},{5,7},{6,4},{7,5},{8,10},{9,11},{10,... | collective-permute-start | bytes 491528 | tf_op jit(solution)/shard_map/ppermute | solution.py:542
  59.0 0.9 %pair_sum.1 = (bf16[3,64,1024]{2,1,0:T(8,128)(2,1)}, bf16[64,1024]{1,0:T(8,128)(2,1)}) custom-call(bf16[256,1024]{1,0:T(8,128)(2,1)S(1)} %get-tuple-element.65.own, bf16[112,1024]{1,0:T(8,128)(2,1)S(1)} %collective-permute-done.15.refs_0_, bf16[144,1024]{1,0:T(8,128)(2,1)S(1)} %collective-permute-done.17.refs_1_), custom_call_target="tpu_custom_call" | custom-call | tf_op jit(solution)/shard_map/pair_sum/pallas_call | solution.py:451
  59.9 3.2 %collective-permute-done.18 = bf16[80,1024]{1,0:T(8,128)(2,1)S(1)} collective-permute-done((bf16[80,1024]{1,0:T(8,128)(2,1)S(1)}, bf16[80,1024]{1,0:T(8,128)(2,1)S(1)}, u32[]{:S(2)}, u32[]{:S(2)}) %collective-permute-start.18) | collective-permute-done | bytes 163872 | tf_op jit(solution)/shard_map/ppermute | solution.py:542
  63.2 0.1 collective-permute-start.19
  63.3 1.4 %near_step.1 = (bf16[256,768]{1,0:T(8,128)(2,1)}, bf16[256,256]{1,0:T(8,128)(2,1)}, bf16[4,4,1024]{2,1,0:T(4,128)(2,1)}) custom-call(bf16[2,64,1024]{2,1,0:T(8,128)(2,1)S(1)} %pad_maximum_fusion.3.near_ref, bf16[4,4,1024]{2,1,0:T(4,128)(2,1)S(1)} %bitcast.67, f32[1,1024]{1,0:T(1,128)S(1)} %get-tuple-element.75.factor_ref, ...), custom_call_target="tpu_custom_call" | custom-call | tf_op jit(solution)/shard_map/near_step/pallas_call | solution.py:500
  64.7 0.1 collective-permute-done.19.far_ref
  64.8 0.7 %far_step.1 = (bf16[256,768]{1,0:T(8,128)(2,1)}, bf16[256,256]{1,0:T(8,128)(2,1)}) custom-call(bf16[2,64,1024]{2,1,0:T(8,128)(2,1)S(1)} %collective-permute-done.19.far_ref, bf16[256,768]{1,0:T(8,128)(2,1)} %get-tuple-element.80.qkv_in, bf16[256,256]{1,0:T(8,128)(2,1)} %get-tuple-element.81.out_in), custom_call_target="tpu_custom_call", output_to_operand_aliasing={{0}: (1, {}), {1}: (2, {})} | custom-call | tf_op jit(solution)/shard_map/far_step/pallas_call | solution.py:518
  (37 shorter events, 0.5 us)
Async XLA Ops:
  0.6 1.0 %copy-start.1 = (bf16[1,8,32,256]{3,2,1,0:T(8,128)(2,1)S(1)}, bf16[1,8,32,256]{3,2,1,0:T(8,128)(2,1)}, u32[]{:S(2)}) copy-start(bf16[1,8,32,256]{3,2,1,0:T(8,128)(2,1)} %param.14) | copy-start | bytes 393220
  1.7 6.7 %copy-start.6 = (bf16[1,4,4,1024]{3,2,1,0:T(4,128)(2,1)S(1)}, bf16[1,4,4,1024]{3,2,1,0:T(4,128)(2,1)}, u32[]{:S(2)}) copy-start(bf16[1,4,4,1024]{3,2,1,0:T(4,128)(2,1)} %param.15) | copy-start | bytes 98308
  1.7 6.6 %copy-start.7 = (bf16[1,4,4,1024]{3,2,1,0:T(4,128)(2,1)S(1)}, bf16[1,4,4,1024]{3,2,1,0:T(4,128)(2,1)}, u32[]{:S(2)}) copy-start(bf16[1,4,4,1024]{3,2,1,0:T(4,128)(2,1)} %param.16) | copy-start | bytes 98308
  1.7 11.1 %collective-permute-start = (bf16[9,32,256]{2,1,0:T(8,128)(2,1)S(1)}, bf16[9,32,256]{2,1,0:T(8,128)(2,1)S(1)}, u32[]{:S(2)}, u32[]{:S(2)}) collective-permute-start(bf16[9,32,256]{2,1,0:T(8,128)(2,1)S(1)} %get-tuple-element.46.second), channel_id=1, source_target_pairs={{4,8},{8,4},{5,9},{9,5},{6,10},{10,6},{7,11},{11,7},{20,24},{24,20... | collective-permute-start | bytes 442376 | tf_op jit(solution)/shard_map/ppermute | solution.py:537
  2.4 10.4 %collective-permute-start.1 = (bf16[9,32,256]{2,1,0:T(8,128)(2,1)S(1)}, bf16[9,32,256]{2,1,0:T(8,128)(2,1)S(1)}, u32[]{:S(2)}, u32[]{:S(2)}) collective-permute-start(bf16[9,32,256]{2,1,0:T(8,128)(2,1)S(1)} %get-tuple-element.47.first), channel_id=1, source_target_pairs={{0,4},{4,0},{8,12},{12,8},{1,5},{5,1},{9,13},{13,9},{2,6},{6,2},{1... | collective-permute-start | bytes 442376 | tf_op jit(solution)/shard_map/ppermute | solution.py:538
  8.3 4.5 %copy-start = (bf16[1,8,32,256]{3,2,1,0:T(8,128)(2,1)S(1)}, bf16[1,8,32,256]{3,2,1,0:T(8,128)(2,1)}, u32[]{:S(2)}) copy-start(bf16[1,8,32,256]{3,2,1,0:T(8,128)(2,1)} %param.13) | copy-start | bytes 393220
  8.3 8.3 %collective-permute-start.6 = (bf16[16,2048]{1,0:T(8,128)(2,1)S(1)}, bf16[16,2048]{1,0:T(8,128)(2,1)S(1)}, u32[]{:S(2)}, u32[]{:S(2)}) collective-permute-start(bf16[16,2048]{1,0:T(8,128)(2,1)S(1)} %pack_coarse.1), channel_id=1, source_target_pairs={{0,12},{4,8},{8,4},{12,0},{1,13},{5,9},{9,5},{13,1},{2,14},{6,10},... | collective-permute-start | bytes 196616 | tf_op jit(solution)/shard_map/ppermute | solution.py:542
  9.8 7.5 %collective-permute-start.5 = (bf16[16,2048]{1,0:T(8,128)(2,1)S(1)}, bf16[16,2048]{1,0:T(8,128)(2,1)S(1)}, u32[]{:S(2)}, u32[]{:S(2)}) collective-permute-start(bf16[16,2048]{1,0:T(8,128)(2,1)S(1)} %pack_coarse.1), channel_id=1, source_target_pairs={{0,8},{4,12},{8,0},{12,4},{1,9},{5,13},{9,1},{13,5},{2,10},{6,14},... | collective-permute-start | bytes 196616 | tf_op jit(solution)/shard_map/ppermute | solution.py:542
  9.9 7.4 %collective-permute-start.4 = (bf16[16,2048]{1,0:T(8,128)(2,1)S(1)}, bf16[16,2048]{1,0:T(8,128)(2,1)S(1)}, u32[]{:S(2)}, u32[]{:S(2)}) collective-permute-start(bf16[16,2048]{1,0:T(8,128)(2,1)S(1)} %pack_coarse.1), channel_id=1, source_target_pairs={{0,4},{4,0},{8,12},{12,8},{1,5},{5,1},{9,13},{13,9},{2,6},{6,2},{1... | collective-permute-start | bytes 196616 | tf_op jit(solution)/shard_map/ppermute | solution.py:542
  12.9 6.7 %copy-start.2 = (bf16[256,768]{1,0:T(8,128)(2,1)S(1)}, bf16[256,768]{1,0:T(8,128)(2,1)}, u32[]{:S(2)}) copy-start(bf16[256,768]{1,0:T(8,128)(2,1)} %qkv_ref.1) | copy-start | bytes 1179652
  12.9 6.6 %collective-permute-start.2 = (bf16[34,8,256]{2,1,0:T(8,128)(2,1)S(1)}, bf16[34,8,256]{2,1,0:T(8,128)(2,1)S(1)}, u32[]{:S(2)}, u32[]{:S(2)}) collective-permute-start(bf16[34,8,256]{2,1,0:T(8,128)(2,1)S(1)} %get-tuple-element.48), channel_id=1, source_target_pairs={{1,2},{2,1},{5,6},{6,5},{9,10},{10,9},{13,14},{14,13},{17,18},{18,... | collective-permute-start | bytes 417800 | tf_op jit(solution)/shard_map/ppermute | solution.py:537
  13.7 5.9 %collective-permute-start.3 = (bf16[34,8,256]{2,1,0:T(8,128)(2,1)S(1)}, bf16[34,8,256]{2,1,0:T(8,128)(2,1)S(1)}, u32[]{:S(2)}, u32[]{:S(2)}) collective-permute-start(bf16[34,8,256]{2,1,0:T(8,128)(2,1)S(1)} %get-tuple-element.49), channel_id=1, source_target_pairs={{0,1},{1,0},{2,3},{3,2},{4,5},{5,4},{6,7},{7,6},{8,9},{9,8},{10,11... | collective-permute-start | bytes 417800 | tf_op jit(solution)/shard_map/ppermute | solution.py:538
  17.3 2.3 %copy-start.4 = (bf16[256,256]{1,0:T(8,128)(2,1)S(1)}, bf16[256,256]{1,0:T(8,128)(2,1)}, u32[]{:S(2)}) copy-start(bf16[256,256]{1,0:T(8,128)(2,1)} %out_ref.1) | copy-start | bytes 393220
  17.3 2.3 %copy-start.11 = (f32[1,256]{1,0:T(1,128)S(1)}, f32[1,256]{1,0:T(1,128)}, u32[]{:S(2)}) copy-start(f32[1,256]{1,0:T(1,128)} %constant.4.clone.freq_ref) | copy-start | bytes 3076
  17.3 9.7 %collective-permute-start.8 = (bf16[4,16,2048]{2,1,0:T(8,128)(2,1)S(1)}, bf16[4,16,2048]{2,1,0:T(8,128)(2,1)S(1)}, u32[]{:S(2)}, u32[]{:S(2)}) collective-permute-start(bf16[4,16,2048]{2,1,0:T(8,128)(2,1)S(1)} %pad_maximum_fusion.1), channel_id=1, source_target_pairs={{0,2},{1,3},{2,0},{3,1},{4,6},{5,7},{6,4},{7,5},{8,10},{9,11},{10,... | collective-permute-start | bytes 786440 | tf_op jit(solution)/shard_map/ppermute | solution.py:542
  19.6 0.7 %copy-start.10 = (f32[256]{0:T(256)S(1)}, f32[256]{0:T(256)}, u32[]{:S(2)}) copy-start(f32[256]{0:T(256)} %param.18) | copy-start | bytes 3076
  27.0 1.5 %collective-permute-start.7 = (bf16[2,4,16,1024]{3,2,1,0:T(8,128)(2,1)S(1)}, bf16[2,4,16,1024]{3,2,1,0:T(8,128)(2,1)S(1)}, u32[]{:S(2)}, u32[]{:S(2)}) collective-permute-start(bf16[2,4,16,1024]{3,2,1,0:T(8,128)(2,1)S(1)} %get-tuple-element.54), channel_id=1, source_target_pairs={{0,1},{1,0},{2,3},{3,2},{4,5},{5,4},{6,7},{7,6},{8,9},{9,8},{10,11... | collective-permute-start | bytes 786440 | tf_op jit(solution)/shard_map/ppermute | solution.py:542
  27.0 1.9 %collective-permute-start.9 = (bf16[4,16,2048]{2,1,0:T(8,128)(2,1)S(1)}, bf16[4,16,2048]{2,1,0:T(8,128)(2,1)S(1)}, u32[]{:S(2)}, u32[]{:S(2)}) collective-permute-start(bf16[4,16,2048]{2,1,0:T(8,128)(2,1)S(1)} %collective-permute-done.8), channel_id=1, source_target_pairs={{0,1},{1,0},{2,3},{3,2},{4,5},{5,4},{6,7},{7,6},{8,9},{9,8},{10,11... | collective-permute-start | bytes 786440 | tf_op jit(solution)/shard_map/ppermute | solution.py:542
  27.5 2.8 %collective-permute-start.11 = (bf16[4,16,2048]{2,1,0:T(8,128)(2,1)S(1)}, bf16[4,16,2048]{2,1,0:T(8,128)(2,1)S(1)}, u32[]{:S(2)}, u32[]{:S(2)}) collective-permute-start(bf16[4,16,2048]{2,1,0:T(8,128)(2,1)S(1)} %pad_maximum_fusion.1), channel_id=1, source_target_pairs={{0,1},{1,0},{2,3},{3,2},{4,5},{5,4},{6,7},{7,6},{8,9},{9,8},{10,11... | collective-permute-start | bytes 786440 | tf_op jit(solution)/shard_map/ppermute | solution.py:542
  28.9 5.6 %collective-permute-start.10 = (bf16[4,16,1024]{2,1,0:T(8,128)(2,1)S(1)}, bf16[4,16,1024]{2,1,0:T(8,128)(2,1)S(1)}, u32[]{:S(2)}, u32[]{:S(2)}) collective-permute-start(bf16[4,16,1024]{2,1,0:T(8,128)(2,1)S(1)} %fusion.2), channel_id=1, source_target_pairs={{0,2},{1,3},{2,0},{3,1},{4,6},{5,7},{6,4},{7,5},{8,10},{9,11},{10,... | collective-permute-start | bytes 393224 | tf_op jit(solution)/shard_map/ppermute | solution.py:542
  30.5 1.0 %copy-start.3 = (bf16[3,64,1024]{2,1,0:T(8,128)(2,1)S(1)}, bf16[3,64,1024]{2,1,0:T(8,128)(2,1)}, u32[]{:S(2)}) copy-start(bf16[3,64,1024]{2,1,0:T(8,128)(2,1)} %qkv_hbm.1) | copy-start | bytes 1179652
  30.5 1.0 %copy-start.5 = (bf16[64,1024]{1,0:T(8,128)(2,1)S(1)}, bf16[64,1024]{1,0:T(8,128)(2,1)}, u32[]{:S(2)}) copy-start(bf16[64,1024]{1,0:T(8,128)(2,1)} %out_hbm.1) | copy-start | bytes 393220
  30.5 1.0 %copy-start.9 = (f32[1,1024]{1,0:T(1,128)S(1)}, f32[1,1024]{1,0:T(1,128)}, u32[]{:S(2)}) copy-start(f32[1,1024]{1,0:T(1,128)} %constant.5.clone.freq_ref) | copy-start | bytes 12292
  30.6 0.9 %copy-start.8 = (f32[1024]{0:T(1024)S(1)}, f32[1024]{0:T(1024)}, u32[]{:S(2)}) copy-start(f32[1024]{0:T(1024)} %param.19) | copy-start | bytes 12292
  34.6 5.0 %collective-permute-start.12 = (bf16[4,16,1024]{2,1,0:T(8,128)(2,1)S(1)}, bf16[4,16,1024]{2,1,0:T(8,128)(2,1)S(1)}, u32[]{:S(2)}, u32[]{:S(2)}) collective-permute-start(bf16[4,16,1024]{2,1,0:T(8,128)(2,1)S(1)} %fusion.1), channel_id=1, source_target_pairs={{0,16},{16,0},{1,17},{17,1},{2,18},{18,2},{3,19},{19,3},{4,20},{20... | collective-permute-start | bytes 393224 | tf_op jit(solution)/shard_map/ppermute | solution.py:542
  36.2 3.5 %collective-permute-start.13 = (bf16[2,4,16,1024]{3,2,1,0:T(8,128)(2,1)S(1)}, bf16[2,4,16,1024]{3,2,1,0:T(8,128)(2,1)S(1)}, u32[]{:S(2)}, u32[]{:S(2)}) collective-permute-start(bf16[2,4,16,1024]{3,2,1,0:T(8,128)(2,1)S(1)} %bitcast.85), channel_id=1, source_target_pairs={{0,1},{1,0},{2,3},{3,2},{4,5},{5,4},{6,7},{7,6},{8,9},{9,8},{10,11... | collective-permute-start | bytes 786440 | tf_op jit(solution)/shard_map/ppermute | solution.py:542
  39.8 7.3 %collective-permute-start.14 = (bf16[128,1024]{1,0:T(8,128)(2,1)S(1)}, bf16[128,1024]{1,0:T(8,128)(2,1)S(1)}, u32[]{:S(2)}, u32[]{:S(2)}) collective-permute-start(bf16[128,1024]{1,0:T(8,128)(2,1)S(1)} %pad_maximum_fusion.2), channel_id=1, source_target_pairs={{0,4},{4,0},{8,12},{12,8},{1,5},{5,1},{9,13},{13,9},{2,6},{6,2},{1... | collective-permute-start | bytes 786440 | tf_op jit(solution)/shard_map/ppermute | solution.py:542
  41.9 6.1 %collective-permute-start.15 = (bf16[112,1024]{1,0:T(8,128)(2,1)S(1)}, bf16[112,1024]{1,0:T(8,128)(2,1)S(1)}, u32[]{:S(2)}, u32[]{:S(2)}) collective-permute-start(bf16[112,1024]{1,0:T(8,128)(2,1)S(1)} %slice.110), channel_id=1, source_target_pairs={{0,16},{16,0},{1,17},{17,1},{2,18},{18,2},{3,19},{19,3},{4,20},{20... | collective-permute-start | bytes 688136 | tf_op jit(solution)/shard_map/ppermute | solution.py:542
  48.1 9.6 %collective-permute-start.16 = (bf16[96,1024]{1,0:T(8,128)(2,1)S(1)}, bf16[96,1024]{1,0:T(8,128)(2,1)S(1)}, u32[]{:S(2)}, u32[]{:S(2)}) collective-permute-start(bf16[96,1024]{1,0:T(8,128)(2,1)S(1)} %pad_maximum_fusion.4), channel_id=1, source_target_pairs={{0,8},{4,12},{8,0},{12,4},{1,9},{5,13},{9,1},{13,5},{2,10},{6,14},... | collective-permute-start | bytes 589832 | tf_op jit(solution)/shard_map/ppermute | solution.py:542
  50.1 7.6 %collective-permute-start.17 = (bf16[144,1024]{1,0:T(8,128)(2,1)S(1)}, bf16[144,1024]{1,0:T(8,128)(2,1)S(1)}, u32[]{:S(2)}, u32[]{:S(2)}) collective-permute-start(bf16[144,1024]{1,0:T(8,128)(2,1)S(1)} %slice.115), channel_id=1, source_target_pairs={{0,16},{16,0},{1,17},{17,1},{2,18},{18,2},{3,19},{19,3},{4,20},{20... | collective-permute-start | bytes 884744 | tf_op jit(solution)/shard_map/ppermute | solution.py:542
  57.7 5.4 %collective-permute-start.18 = (bf16[80,1024]{1,0:T(8,128)(2,1)S(1)}, bf16[80,1024]{1,0:T(8,128)(2,1)S(1)}, u32[]{:S(2)}, u32[]{:S(2)}) collective-permute-start(bf16[80,1024]{1,0:T(8,128)(2,1)S(1)} %pad_maximum_fusion.5), channel_id=1, source_target_pairs={{0,2},{1,3},{2,0},{3,1},{4,6},{5,7},{6,4},{7,5},{8,10},{9,11},{10,... | collective-permute-start | bytes 491528 | tf_op jit(solution)/shard_map/ppermute | solution.py:542
  63.2 1.6 %collective-permute-start.19 = (bf16[2,64,1024]{2,1,0:T(8,128)(2,1)S(1)}, bf16[2,64,1024]{2,1,0:T(8,128)(2,1)S(1)}, u32[]{:S(2)}, u32[]{:S(2)}) collective-permute-start(bf16[2,64,1024]{2,1,0:T(8,128)(2,1)S(1)} %pad_maximum_fusion.3.near_ref), channel_id=1, source_target_pairs={{0,1},{1,0},{2,3},{3,2},{4,5},{5,4},{6,7},{7,6},{8,9},{9,8},{10,11... | collective-permute-start | bytes 786440 | tf_op jit(solution)/shard_map/ppermute | solution.py:542

commit v10 on v9

--- a/solution.py
+++ b/solution.py
@@ -21,6 +21,7 @@
 extent = side + 2 * RAD
 lanes_wide = 16
 thin = 4
+lag = 1
 scale = 1.0 / math.sqrt(HD)
 vmem_bytes = 48 * 1024 * 1024
 
@@ -32,10 +33,6 @@
 def frequencies(channels):
     steps = np.float32(-log_span) * np.arange(channels, dtype=np.float32) / np.float32(channels)
     return np.exp(steps)[None]
-
-
-def time_gain(step_ref, gain_ref, freq_ref):
-    return gain_ref[...] * (1.0 + 0.5 * jnp.cos(step_ref[...].astype(jnp.float32) * freq_ref[...]))
 
 
 def odd_rank(axis):
@@ -69,9 +66,7 @@
     row_near_ref,
     col_far_ref,
     col_near_ref,
-    step_ref,
-    gain_ref,
-    freq_ref,
+    factor_ref,
     qkv_ref,
     out_ref,
     dx_ref,
@@ -87,15 +82,14 @@
     dv_grid,
     dq_grid,
     a_grid,
-    bias_ref,
-    thin_bias_ref,
     total_ref,
+    *scratch,
 ):
     height, breadth = x_ref.shape[0], x_ref.shape[1]
     grid_rows, grid_cols = x_grid.shape[0], x_grid.shape[1]
     query_rows = dy_grid.shape[0]
     floats = jnp.float32
-    factor = time_gain(step_ref, gain_ref, freq_ref)
+    factor = factor_ref[...]
 
     for grid, rows in ((x_grid, height + 2 * HALO), (dy_grid, height + 2 * RAD)):
         grid[rows:] = jnp.zeros((grid.shape[0] - rows,) + grid.shape[1:], floats)
@@ -153,8 +147,9 @@
         near = (row_gap >= 0) & (row_gap <= 2 * RAD) & (col_gap >= 0) & (col_gap <= 2 * RAD)
         return jnp.where(near, 0.0, -1e30)
 
-    bias_ref[...] = window_bias(side)
-    thin_bias_ref[...] = window_bias(thin)
+    own_scratch, thin_scratch = scratch[:7], scratch[7:]
+    own_scratch[-1][...] = window_bias(side)
+    thin_scratch[-1][...] = window_bias(thin)
 
     def head_of(rows):
         return lax.broadcasted_iota(jnp.int32, (rows, D_F), 1) // HD
@@ -174,11 +169,16 @@
             total = jnp.where(heads == h, full[h * rows : (h + 1) * rows], total)
         return total.reshape(rows // side, side, D_F)
 
-    def attend(top, start, query_rows, near_bias, live):
-        key_rows = query_rows + 2 * RAD
-        window = (slice(top, top + key_rows), slice(start, start + lanes_wide))
+    def windows(task):
+        top, start, query_rows = task[:3]
+        window = (slice(top, top + query_rows + 2 * RAD), slice(start, start + lanes_wide))
         keys = k_grid[window].reshape(-1, D_F).astype(jnp.bfloat16)
-        values = v_grid[window].reshape(-1, D_F).astype(jnp.bfloat16)
+        return keys, v_grid[window].reshape(-1, D_F).astype(jnp.bfloat16)
+
+    def begin(task):
+        top, start, query_rows, live, scratch, index = task
+        score_ref, product_ref, query_ref, up_ref = scratch[:4]
+        keys, values = windows(task)
         place = (slice(top, top + query_rows), slice(start + RAD, start + RAD + side))
         wide_queries = spread(q_grid[place])
         ups = u_grid[place]
@@ -186,34 +186,54 @@
             row = lax.broadcasted_iota(jnp.int32, ups.shape, 0)
             ups = jnp.where(row < live, ups, 0.0)
         wide_ups = spread(ups)
-        lone = lax.broadcasted_iota(jnp.int32, (key_rows * lanes_wide, 1), 0)
+        query_ref[index], up_ref[index] = wide_queries, wide_ups
+        score_ref[index] = dot(keys, wide_queries, ((1,), (1,)))
+        product_ref[index] = dot(values, wide_ups, ((1,), (1,)))
+
+    def share(task):
+        top, start, query_rows, live, scratch, index = task
+        score_ref, product_ref, _, _, weight_ref, slope_ref, near_bias = scratch
+        lone = lax.broadcasted_iota(jnp.int32, ((query_rows + 2 * RAD) * lanes_wide, 1), 0)
         key_row, key_col = lone // lanes_wide + top, lone % lanes_wide + start
         inside = (key_row >= row_low) & (key_row < row_high)
         inside = inside & (key_col >= col_low) & (key_col < col_high)
-        scores = dot(keys, wide_queries, ((1,), (1,)))
-        scores = scores + (near_bias[...] + jnp.where(inside, 0.0, -1e30))
+        scores = score_ref[index] + (near_bias[...] + jnp.where(inside, 0.0, -1e30))
         raised = jnp.exp(scores - jnp.max(scores, axis=0, keepdims=True))
         shares = raised * (1.0 / jnp.sum(raised, axis=0, keepdims=True))
-        products = dot(values, wide_ups, ((1,), (1,)))
+        products = product_ref[index]
         centre = jnp.sum(shares * products, axis=0, keepdims=True)
-        slopes = (shares * (products - centre)).astype(jnp.bfloat16)
-        weights = shares.astype(jnp.bfloat16)
-        first, final = max(top, HALO), min(top + key_rows, HALO + height)
+        slope_ref[index] = (shares * (products - centre)).astype(jnp.bfloat16)
+        weight_ref[index] = shares.astype(jnp.bfloat16)
+
+    def finish(task):
+        top, start, query_rows, live, scratch, index = task
+        query_ref, up_ref, weight_ref, slope_ref = scratch[2:6]
+        first, final = max(top, HALO), min(top + query_rows + 2 * RAD, HALO + height)
         kept = slice((first - top) * lanes_wide, (final - top) * lanes_wide)
         target = (slice(first - HALO, final - HALO), slice(start, start + lanes_wide))
         shape = (final - first, lanes_wide, D_F)
-        dv_grid[target] += dot(weights[kept], wide_ups).reshape(shape)
-        dk_grid[target] += dot(slopes[kept], wide_queries).reshape(shape)
-        return keys, values, slopes, weights
-
+        dv_grid[target] += dot(weight_ref[index, kept], up_ref[index]).reshape(shape)
+        dk_grid[target] += dot(slope_ref[index, kept], query_ref[index]).reshape(shape)
+        if live == side:
+            keys, values = windows(task)
+            block = (slice(top - RAD, top - RAD + side), slice(start, start + side))
+            a_grid[block] = collect(dot(weight_ref[index], values, ((0,), (0,))))
+            dq_grid[block] = collect(dot(slope_ref[index], keys, ((0,), (0,))))
+
+    tasks = []
     for start in range(0, grid_cols - side, side):
         for top in range(RAD, RAD + height, side):
-            keys, values, slopes, weights = attend(top, start, side, bias_ref, side)
-            block = (slice(top - RAD, top - RAD + side), slice(start, start + side))
-            a_grid[block] = collect(dot(weights, values, ((0,), (0,))))
-            dq_grid[block] = collect(dot(slopes, keys, ((0,), (0,))))
-        attend(0, start, thin, thin_bias_ref, RAD)
-        attend(RAD + height, start, thin, thin_bias_ref, RAD)
+            tasks.append((top, start, side, side, own_scratch, len(tasks)))
+    for index, start in enumerate(range(0, grid_cols - side, side)):
+        tasks.append((0, start, thin, RAD, thin_scratch, 2 * index))
+        tasks.append((RAD + height, start, thin, thin, thin_scratch, 2 * index + 1))
+    for turn in range(len(tasks) + 2 * lag):
+        if turn < len(tasks):
+            begin(tasks[turn])
+        if 0 <= turn - lag < len(tasks):
+            share(tasks[turn - lag])
+        if turn >= 2 * lag:
+            finish(tasks[turn - 2 * lag])
 
     count = height * breadth
     own_queries = (slice(0, height), slice(RAD, RAD + breadth))
@@ -246,6 +266,21 @@
     dx_ref[...] = norm_backward(picture, inverse, factor, down).reshape(height, breadth, D_F)
 
 
+def block_scratch(blocks, query_rows):
+    keys_count, heads_count = (query_rows + 2 * RAD) * lanes_wide, H_F * query_rows * side
+    square = (blocks, keys_count, heads_count)
+    wide = (blocks, heads_count, D_F)
+    return [
+        pltpu.VMEM(square, jnp.float32),
+        pltpu.VMEM(square, jnp.float32),
+        pltpu.VMEM(wide, jnp.bfloat16),
+        pltpu.VMEM(wide, jnp.bfloat16),
+        pltpu.VMEM(square, jnp.bfloat16),
+        pltpu.VMEM(square, jnp.bfloat16),
+        pltpu.VMEM((keys_count, heads_count), jnp.float32),
+    ]
+
+
 def fine_block(peers, picture, *operands):
     height, breadth = picture.shape[0], picture.shape[1]
     query_rows = RAD + height + thin
@@ -266,7 +301,7 @@
             jax.ShapeDtypeStruct(halves, jnp.float32),
             jax.ShapeDtypeStruct(halves, jnp.bfloat16),
         ),
-        in_specs=[vmem] * 11,
+        in_specs=[vmem] * 9,
         out_specs=(vmem, vmem, vmem),
         scratch_shapes=[
             wide,
@@ -279,9 +314,9 @@
             strip,
             small,
             small,
-            pltpu.VMEM((extent * lanes_wide, H_F * side * side), jnp.float32),
-            pltpu.VMEM(((thin + 2 * RAD) * lanes_wide, H_F * thin * side), jnp.float32),
             pltpu.VMEM((across * down, rows, 4 * D_F), jnp.float32),
+            *block_scratch(query_cols // side * (height // side), side),
+            *block_scratch(2 * (query_cols // side), thin),
         ],
         compiler_params=pltpu.CompilerParams(vmem_limit_bytes=vmem_bytes),
         name="fine_block",
@@ -291,14 +326,11 @@
 def coarse_body(
     x_ref,
     dy_ref,
-    step_ref,
-    gain_ref,
-    freq_ref,
+    factor_ref,
     qkv_hbm,
     out_hbm,
     parts_ref,
     grads_ref,
-    factor_ref,
     qkv_ref,
     out_ref,
     arrived,
@@ -310,7 +342,6 @@
     for fetch in fetches:
         fetch.start()
     tokens = x_ref[...].astype(jnp.float32)
-    factor_ref[...] = time_gain(step_ref, gain_ref, freq_ref)
     normed = (tokens * inverse_rms(tokens) * factor_ref[...]).astype(jnp.bfloat16)
     cot = dy_ref[...]
     for fetch in fetches:
@@ -337,7 +368,7 @@
     grads_ref[3 * HD :] = dot(mixed, cot, ((0,), (0,))).astype(grads_ref.dtype)
 
 
-def coarse_block(tokens, cotangents, step, gain, head_qkv, head_out):
+def coarse_block(tokens, cotangents, factor, head_qkv, head_out):
     count = tokens.shape[0]
     vmem = pl.BlockSpec(memory_space=pltpu.VMEM)
     return pl.pallas_call(
@@ -345,10 +376,9 @@
         out_shape=(
             jax.ShapeDtypeStruct((count, D_C), jnp.bfloat16),
             jax.ShapeDtypeStruct((4 * HD, D_C), jnp.bfloat16),
-            jax.ShapeDtypeStruct((1, D_C), jnp.float32),
         ),
-        in_specs=[vmem] * 5 + [pl.BlockSpec(memory_space=pltpu.HBM)] * 2,
-        out_specs=(vmem, vmem, vmem),
+        in_specs=[vmem] * 3 + [pl.BlockSpec(memory_space=pltpu.HBM)] * 2,
+        out_specs=(vmem, vmem),
         scratch_shapes=[
             pltpu.VMEM(head_qkv.shape, jnp.bfloat16),
             pltpu.VMEM(head_out.shape, jnp.bfloat16),
@@ -356,7 +386,7 @@
         ],
         compiler_params=pltpu.CompilerParams(vmem_limit_bytes=vmem_bytes),
         name="coarse_block",
-    )(tokens, cotangents, step, gain[None], frequencies(D_C), head_qkv, head_out)
+    )(tokens, cotangents, factor, head_qkv, head_out)
 
 
 def row_edges_body(x_low, x_high, dy_low, dy_high, near_ref, far_ref):
@@ -432,6 +462,27 @@
         compiler_params=pltpu.CompilerParams(vmem_limit_bytes=vmem_bytes),
         name="pack_coarse",
     )(*after, tokens, cotangents)
+
+
+def factors_body(step, fine_gain, coarse_gain, fine_freq, coarse_freq, fine_ref, coarse_ref):
+    time = step[0].astype(jnp.float32)
+    fine_ref[...] = fine_gain[...] * (1.0 + 0.5 * jnp.cos(time * fine_freq[...]))
+    coarse_ref[...] = coarse_gain[...] * (1.0 + 0.5 * jnp.cos(time * coarse_freq[...]))
+
+
+def time_factors(step, fine_gain, coarse_gain):
+    vmem = pl.BlockSpec(memory_space=pltpu.VMEM)
+    return pl.pallas_call(
+        factors_body,
+        out_shape=(
+            jax.ShapeDtypeStruct((1, D_F), jnp.float32),
+            jax.ShapeDtypeStruct((1, D_C), jnp.float32),
+        ),
+        in_specs=[pl.BlockSpec(memory_space=pltpu.SMEM)] + [vmem] * 4,
+        out_specs=(vmem, vmem),
+        compiler_params=pltpu.CompilerParams(vmem_limit_bytes=vmem_bytes),
+        name="time_factors",
+    )(step, fine_gain[None], coarse_gain[None], frequencies(D_F), frequencies(D_C))
 
 
 def pair_sum_body(own, *refs):
@@ -588,11 +639,12 @@
     count = own.shape[0]
     row_group = all_rows(own)
     edges = col_edges(picture, cotangent, row_far, row_near)
+    *edges, step, gain_f, gain_c = tied(*edges, timestep, fine_gain, coarse_gain)
     col_near, col_far = neighbours(*edges, "gx")
-    step = timestep[None]
+    factor, coarse_factor = time_factors(step, gain_f, gain_c)
     cross = swapped(row_group, "gx", 2)
     beside = swapped(row_group, "gx", 1)
-    col_far, col_near, row_group = tied(col_far, col_near, row_group)
+    col_far, col_near, row_group, factor = tied(col_far, col_near, row_group, factor)
     dx_picture, fine_keep, fine_send = fine_block(
         (across, downs),
         picture,
@@ -601,9 +653,7 @@
         row_near,
         col_far,
         col_near,
-        step,
-        fine_gain[None],
-        frequencies(D_F),
+        factor,
         fine_qkv,
         fine_out,
     )
@@ -613,8 +663,8 @@
 
     fine_quarter = narrow(fine_half[0] + wide(swapped(narrow(fine_half[1]), "gx", 2)))
     everyone = jnp.stack([row_group, cross, beside, opposite]).reshape(-1, 2 * D_C)
-    parts, coarse_partial, coarse_factor = coarse_block(
-        everyone[:, :D_C], everyone[:, D_C:], step, coarse_gain, coarse_qkv, coarse_out
+    parts, coarse_partial = coarse_block(
+        everyone[:, :D_C], everyone[:, D_C:], coarse_factor, coarse_qkv, coarse_out
     )
     fine_quarter, parts, coarse_partial = tied(fine_quarter, parts, coarse_partial)
 

time: 65.8 us -> 63.2 us (0.960)
  Pallas kernels: 12.1 us -> 9.73 us
    pallas_call x1, Pallas kernels: 6.76 us -> 4.33 us  [fine_block(): pl.pallas_call(fine_body, out_shape=(jax.ShapeDtypeStruct((height, breadt...]
  transfers between devices with their start and end apart: 20 -> 20, of which waited for: 10 -> 11; matrix products, arithmetic and copies ran while one was open for 1% -> 1% of each run, Pallas kernels for 17% -> 14%
where the time goes in v10:
time: 63.2 us; the launch traced here: 63 us
  starting transfers between devices  28 us (44%)
  waiting for transfers between devices  20.1 us (32%)
  Pallas kernels  9.73 us (15%)
  local copies, waits for them, and re-layouts  2.84 us (4%)
  between operations  1.69 us (3%)
    ppermute x16, waiting for transfers between devices, swapped(): lax.ppermute(value, axis, [(i, i ^ mask) for i in range(lax.axis_size(axi...  20.1 us
    ppermute x16, starting transfers between devices, swapped(): lax.ppermute(value, axis, [(i, i ^ mask) for i in range(lax.axis_size(axi...  17.7 us
    ppermute x2, starting transfers between devices, neighbours(): return (lax.ppermute(to_near, axis, near), from_far)  8.81 us
    pallas_call x1, Pallas kernels, fine_block(): pl.pallas_call(fine_body, out_shape=(jax.ShapeDtypeStruct((height, breadt...  4.33 us
    pallas_call x1, Pallas kernels, coarse_block(): pl.pallas_call(coarse_body, out_shape=(jax.ShapeDtypeStruct((count, D_C),...  2.23 us
    unnamed x24, local copies, waits for them, and re-layouts  1.61 us
    ppermute x2, starting transfers between devices, neighbours(): from_far = lax.ppermute(to_far, axis, far)  1.47 us
    pallas_call x1, Pallas kernels, near_step(): pl.pallas_call(near_body, out_shape=(jax.ShapeDtypeStruct((D_F, 3 * D_F),...  1.36 us
  transfers between devices with their start and end apart: 20, of which 11 were waited for; matrix products, arithmetic and copies ran while one was open for 1% of the time, Pallas kernels for 14%

profile of v10, /device:TPU:0, one launch (start us, length us, event | category | flops | bytes accessed | tf_op | source)
XLA Modules:
  0.0 63.0 jit_solution(14372343519719928589)
XLA Ops:
  0.6 1.0 %slice_bitcast_fusion.2 = (bf16[6,32,256]{2,1,0:T(8,128)(2,1)S(1)}, bf16[6,32,256]{2,1,0:T(8,128)(2,1)S(1)}) fusion(bf16[1,8,32,256]{3,2,1,0:T(8,128)(2,1)} %param.13), kind=kLoop, calls=%fused_computation.22 | loop fusion | bytes 393216 | tf_op jit(solution)/shard_map/slice | solution.py:419
  1.6 0.0 copy-done.1
  1.7 0.0 copy-start.6
  1.7 0.0 copy-start.7
  1.7 0.7 %collective-permute-start = (bf16[9,32,256]{2,1,0:T(8,128)(2,1)S(1)}, bf16[9,32,256]{2,1,0:T(8,128)(2,1)S(1)}, u32[]{:S(2)}, u32[]{:S(2)}) collective-permute-start(bf16[9,32,256]{2,1,0:T(8,128)(2,1)S(1)} %get-tuple-element.53.second), channel_id=1, source_target_pairs={{4,8},{8,4},{5,9},{9,5},{6,10},{10,6},{7,11},{11,7},{20,24},{24,20... | collective-permute-start | bytes 442376 | tf_op jit(solution)/shard_map/ppermute | solution.py:588
  2.4 5.9 %collective-permute-start.1 = (bf16[9,32,256]{2,1,0:T(8,128)(2,1)S(1)}, bf16[9,32,256]{2,1,0:T(8,128)(2,1)S(1)}, u32[]{:S(2)}, u32[]{:S(2)}) collective-permute-start(bf16[9,32,256]{2,1,0:T(8,128)(2,1)S(1)} %get-tuple-element.54.first), channel_id=1, source_target_pairs={{0,4},{4,0},{8,12},{12,8},{1,5},{5,1},{9,13},{13,9},{2,6},{6,2},{1... | collective-permute-start | bytes 442376 | tf_op jit(solution)/shard_map/ppermute | solution.py:589
  8.3 0.0 copy-done.6
  8.3 1.4 %collective-permute-start.6 = (bf16[16,2048]{1,0:T(8,128)(2,1)S(1)}, bf16[16,2048]{1,0:T(8,128)(2,1)S(1)}, u32[]{:S(2)}, u32[]{:S(2)}) collective-permute-start(bf16[16,2048]{1,0:T(8,128)(2,1)S(1)} %pack_coarse.1), channel_id=1, source_target_pairs={{0,12},{4,8},{8,4},{12,0},{1,13},{5,9},{9,5},{13,1},{2,14},{6,10},... | collective-permute-start | bytes 196616 | tf_op jit(solution)/shard_map/ppermute | solution.py:593
  9.8 0.2 collective-permute-start.5
  9.9 2.9 %collective-permute-start.4 = (bf16[16,2048]{1,0:T(8,128)(2,1)S(1)}, bf16[16,2048]{1,0:T(8,128)(2,1)S(1)}, u32[]{:S(2)}, u32[]{:S(2)}) collective-permute-start(bf16[16,2048]{1,0:T(8,128)(2,1)S(1)} %pack_coarse.1), channel_id=1, source_target_pairs={{0,4},{4,0},{8,12},{12,8},{1,5},{5,1},{9,13},{13,9},{2,6},{6,2},{1... | collective-permute-start | bytes 196616 | tf_op jit(solution)/shard_map/ppermute | solution.py:593
  12.8 0.0 collective-permute-done.row_far_ref
  12.8 0.0 collective-permute-done.1.row_near_ref
  12.8 0.1 col_edges.1
  12.9 0.0 copy-start.2
  12.9 0.8 %collective-permute-start.2 = (bf16[34,8,256]{2,1,0:T(8,128)(2,1)S(1)}, bf16[34,8,256]{2,1,0:T(8,128)(2,1)S(1)}, u32[]{:S(2)}, u32[]{:S(2)}) collective-permute-start(bf16[34,8,256]{2,1,0:T(8,128)(2,1)S(1)} %get-tuple-element.57), channel_id=1, source_target_pairs={{1,2},{2,1},{5,6},{6,5},{9,10},{10,9},{13,14},{14,13},{17,18},{18,... | collective-permute-start | bytes 417800 | tf_op jit(solution)/shard_map/ppermute | solution.py:588
  13.7 2.9 %collective-permute-start.3 = (bf16[34,8,256]{2,1,0:T(8,128)(2,1)S(1)}, bf16[34,8,256]{2,1,0:T(8,128)(2,1)S(1)}, u32[]{:S(2)}, u32[]{:S(2)}) collective-permute-start(bf16[34,8,256]{2,1,0:T(8,128)(2,1)S(1)} %get-tuple-element.58), channel_id=1, source_target_pairs={{0,1},{1,0},{2,3},{3,2},{4,5},{5,4},{6,7},{7,6},{8,9},{9,8},{10,11... | collective-permute-start | bytes 417800 | tf_op jit(solution)/shard_map/ppermute | solution.py:589
  16.6 0.0 collective-permute-done.6
  16.6 0.7 %collective-permute-done.5 = bf16[16,2048]{1,0:T(8,128)(2,1)S(1)} collective-permute-done((bf16[16,2048]{1,0:T(8,128)(2,1)S(1)}, bf16[16,2048]{1,0:T(8,128)(2,1)S(1)}, u32[]{:S(2)}, u32[]{:S(2)}) %collective-permute-start.5) | collective-permute-done | bytes 65568 | tf_op jit(solution)/shard_map/ppermute | solution.py:593
  17.3 0.0 collective-permute-done.4
  17.4 0.0 copy-start.8
  17.4 1.6 %collective-permute-start.8 = (bf16[4,16,2048]{2,1,0:T(8,128)(2,1)S(1)}, bf16[4,16,2048]{2,1,0:T(8,128)(2,1)S(1)}, u32[]{:S(2)}, u32[]{:S(2)}) collective-permute-start(bf16[4,16,2048]{2,1,0:T(8,128)(2,1)S(1)} %pad_maximum_fusion.1), channel_id=1, source_target_pairs={{0,2},{1,3},{2,0},{3,1},{4,6},{5,7},{6,4},{7,5},{8,10},{9,11},{10,... | collective-permute-start | bytes 786440 | tf_op jit(solution)/shard_map/ppermute | solution.py:593
  19.6 0.0 copy-start.10
  19.6 0.6 %copy-done.10 = f32[256]{0:T(256)S(1)} copy-done((f32[256]{0:T(256)S(1)}, f32[256]{0:T(256)}, u32[]{:S(2)}) %copy-start.10) | copy-done | bytes 1048
  20.3 0.1 time_factors.1
  20.3 0.0 collective-permute-done.2.col_far_ref
  20.3 0.0 collective-permute-done.3.col_near_ref
  20.4 4.3 %fine_block.1 = (bf16[8,32,256]{2,1,0:T(8,128)(2,1)}, f32[2,4,16,1024]{3,2,1,0:T(8,128)S(1)}, bf16[2,4,16,1024]{3,2,1,0:T(8,128)(2,1)S(1)}) custom-call(bf16[8,32,256]{2,1,0:T(8,128)(2,1)S(1)} %bitcast.59, bf16[8,32,256]{2,1,0:T(8,128)(2,1)S(1)} %bitcast.61, bf16[9,32,256]{2,1,0:T(8,128)(2,1)S(1)} %collective-permute-done.row_far_ref, ...), custom_call_target="tpu_custom_call" | custom-call | tf_op jit(solution)/shard_map/fine_block/pallas_call | solution.py:297
  24.7 0.0 collective-permute-start.7
  24.7 0.4 collective-permute-done.8
  25.1 0.1 collective-permute-start.9
  25.2 0.4 collective-permute-start.11
  25.6 0.6 collective-permute-done.7
  26.2 0.1 convert_add_fusion.1
  26.3 0.3 collective-permute-done.9
  26.6 1.5 %collective-permute-start.10 = (bf16[4,16,1024]{2,1,0:T(8,128)(2,1)S(1)}, bf16[4,16,1024]{2,1,0:T(8,128)(2,1)S(1)}, u32[]{:S(2)}, u32[]{:S(2)}) collective-permute-start(bf16[4,16,1024]{2,1,0:T(8,128)(2,1)S(1)} %fusion.2), channel_id=1, source_target_pairs={{0,2},{1,3},{2,0},{3,1},{4,6},{5,7},{6,4},{7,5},{8,10},{9,11},{10,... | collective-permute-start | bytes 393224 | tf_op jit(solution)/shard_map/ppermute | solution.py:593
  28.1 0.0 collective-permute-done.11
  28.1 0.1 pad_maximum_fusion
  28.3 0.0 copy-start.3
  28.3 0.0 copy-start.5
  28.3 0.1 fusion.5
  28.4 0.9 %copy-done.3 = bf16[3,64,1024]{2,1,0:T(8,128)(2,1)S(1)} copy-done((bf16[3,64,1024]{2,1,0:T(8,128)(2,1)S(1)}, bf16[3,64,1024]{2,1,0:T(8,128)(2,1)}, u32[]{:S(2)}) %copy-start.3) | copy-done | bytes 393240
  29.3 0.0 copy-done.5
  29.3 2.2 %coarse_block.1 = (bf16[256,1024]{1,0:T(8,128)(2,1)S(1)}, bf16[256,1024]{1,0:T(8,128)(2,1)S(1)}) custom-call(bf16[256,1024]{1,0:T(8,128)(2,1)S(1)} %get-tuple-element.101.x_ref, bf16[256,1024]{1,0:T(8,128)(2,1)S(1)} %get-tuple-element.100.dy_ref, f32[1,1024]{1,0:T(1,128)S(1)} %get-tuple-element.72.factor_ref, bf16[3,64,1024]{2,1,0:T(8,128)(2,1)S(1)} %copy-done.3, ...), custom_call_target="tpu_custom_call" | custom-call | tf_op jit(solution)/shard_map/coarse_block/pallas_call | solution.py:374
  31.5 0.7 %collective-permute-done.10 = bf16[4,16,1024]{2,1,0:T(8,128)(2,1)S(1)} collective-permute-done((bf16[4,16,1024]{2,1,0:T(8,128)(2,1)S(1)}, bf16[4,16,1024]{2,1,0:T(8,128)(2,1)S(1)}, u32[]{:S(2)}, u32[]{:S(2)}) %collective-permute-start.10) | collective-permute-done | bytes 131104 | tf_op jit(solution)/shard_map/ppermute | solution.py:593
  32.3 1.6 %collective-permute-start.12 = (bf16[4,16,1024]{2,1,0:T(8,128)(2,1)S(1)}, bf16[4,16,1024]{2,1,0:T(8,128)(2,1)S(1)}, u32[]{:S(2)}, u32[]{:S(2)}) collective-permute-start(bf16[4,16,1024]{2,1,0:T(8,128)(2,1)S(1)} %fusion.1), channel_id=1, source_target_pairs={{0,16},{16,0},{1,17},{17,1},{2,18},{18,2},{3,19},{19,3},{4,20},{20... | collective-permute-start | bytes 393224 | tf_op jit(solution)/shard_map/ppermute | solution.py:593
  33.9 0.1 collective-permute-start.13
  34.0 3.3 %collective-permute-done.12 = bf16[4,16,1024]{2,1,0:T(8,128)(2,1)S(1)} collective-permute-done((bf16[4,16,1024]{2,1,0:T(8,128)(2,1)S(1)}, bf16[4,16,1024]{2,1,0:T(8,128)(2,1)S(1)}, u32[]{:S(2)}, u32[]{:S(2)}) %collective-permute-start.12) | collective-permute-done | bytes 131104 | tf_op jit(solution)/shard_map/ppermute | solution.py:593
  37.3 0.0 collective-permute-done.13
  37.4 0.1 convert_add_fusion
  37.5 2.3 %collective-permute-start.14 = (bf16[128,1024]{1,0:T(8,128)(2,1)S(1)}, bf16[128,1024]{1,0:T(8,128)(2,1)S(1)}, u32[]{:S(2)}, u32[]{:S(2)}) collective-permute-start(bf16[128,1024]{1,0:T(8,128)(2,1)S(1)} %pad_maximum_fusion.2), channel_id=1, source_target_pairs={{0,4},{4,0},{8,12},{12,8},{1,5},{5,1},{9,13},{13,9},{2,6},{6,2},{1... | collective-permute-start | bytes 786440 | tf_op jit(solution)/shard_map/ppermute | solution.py:593
  39.8 1.6 %collective-permute-start.15 = (bf16[112,1024]{1,0:T(8,128)(2,1)S(1)}, bf16[112,1024]{1,0:T(8,128)(2,1)S(1)}, u32[]{:S(2)}, u32[]{:S(2)}) collective-permute-start(bf16[112,1024]{1,0:T(8,128)(2,1)S(1)} %slice.110), channel_id=1, source_target_pairs={{0,16},{16,0},{1,17},{17,1},{2,18},{18,2},{3,19},{19,3},{4,20},{20... | collective-permute-start | bytes 688136 | tf_op jit(solution)/shard_map/ppermute | solution.py:593
  41.4 3.1 %collective-permute-done.14 = bf16[128,1024]{1,0:T(8,128)(2,1)S(1)} collective-permute-done((bf16[128,1024]{1,0:T(8,128)(2,1)S(1)}, bf16[128,1024]{1,0:T(8,128)(2,1)S(1)}, u32[]{:S(2)}, u32[]{:S(2)}) %collective-permute-start.14) | collective-permute-done | bytes 262176 | tf_op jit(solution)/shard_map/ppermute | solution.py:593
  44.7 1.3 %collective-permute-done.15.refs_0_ = bf16[112,1024]{1,0:T(8,128)(2,1)S(1)} collective-permute-done((bf16[112,1024]{1,0:T(8,128)(2,1)S(1)}, bf16[112,1024]{1,0:T(8,128)(2,1)S(1)}, u32[]{:S(2)}, u32[]{:S(2)}) %collective-permute-start.15) | collective-permute-done | bytes 229408 | tf_op jit(solution)/shard_map/ppermute | solution.py:593
  46.0 1.2 %collective-permute-start.16 = (bf16[96,1024]{1,0:T(8,128)(2,1)S(1)}, bf16[96,1024]{1,0:T(8,128)(2,1)S(1)}, u32[]{:S(2)}, u32[]{:S(2)}) collective-permute-start(bf16[96,1024]{1,0:T(8,128)(2,1)S(1)} %pad_maximum_fusion.4), channel_id=1, source_target_pairs={{0,8},{4,12},{8,0},{12,4},{1,9},{5,13},{9,1},{13,5},{2,10},{6,14},... | collective-permute-start | bytes 589832 | tf_op jit(solution)/shard_map/ppermute | solution.py:593
  47.2 1.5 %collective-permute-start.17 = (bf16[144,1024]{1,0:T(8,128)(2,1)S(1)}, bf16[144,1024]{1,0:T(8,128)(2,1)S(1)}, u32[]{:S(2)}, u32[]{:S(2)}) collective-permute-start(bf16[144,1024]{1,0:T(8,128)(2,1)S(1)} %slice.115), channel_id=1, source_target_pairs={{0,16},{16,0},{1,17},{17,1},{2,18},{18,2},{3,19},{19,3},{4,20},{20... | collective-permute-start | bytes 884744 | tf_op jit(solution)/shard_map/ppermute | solution.py:593
  48.7 6.4 %collective-permute-done.16 = bf16[96,1024]{1,0:T(8,128)(2,1)S(1)} collective-permute-done((bf16[96,1024]{1,0:T(8,128)(2,1)S(1)}, bf16[96,1024]{1,0:T(8,128)(2,1)S(1)}, u32[]{:S(2)}, u32[]{:S(2)}) %collective-permute-start.16) | collective-permute-done | bytes 196640 | tf_op jit(solution)/shard_map/ppermute | solution.py:593
  55.2 0.0 collective-permute-done.17.refs_1_
  55.2 1.4 %collective-permute-start.18 = (bf16[80,1024]{1,0:T(8,128)(2,1)S(1)}, bf16[80,1024]{1,0:T(8,128)(2,1)S(1)}, u32[]{:S(2)}, u32[]{:S(2)}) collective-permute-start(bf16[80,1024]{1,0:T(8,128)(2,1)S(1)} %pad_maximum_fusion.5), channel_id=1, source_target_pairs={{0,2},{1,3},{2,0},{3,1},{4,6},{5,7},{6,4},{7,5},{8,10},{9,11},{10,... | collective-permute-start | bytes 491528 | tf_op jit(solution)/shard_map/ppermute | solution.py:593
  56.6 0.9 %pair_sum.1 = (bf16[3,64,1024]{2,1,0:T(8,128)(2,1)}, bf16[64,1024]{1,0:T(8,128)(2,1)}) custom-call(bf16[256,1024]{1,0:T(8,128)(2,1)S(1)} %get-tuple-element.80.own, bf16[112,1024]{1,0:T(8,128)(2,1)S(1)} %collective-permute-done.15.refs_0_, bf16[144,1024]{1,0:T(8,128)(2,1)S(1)} %collective-permute-done.17.refs_1_), custom_call_target="tpu_custom_call" | custom-call | tf_op jit(solution)/shard_map/pair_sum/pallas_call | solution.py:502
  57.5 3.1 %collective-permute-done.18 = bf16[80,1024]{1,0:T(8,128)(2,1)S(1)} collective-permute-done((bf16[80,1024]{1,0:T(8,128)(2,1)S(1)}, bf16[80,1024]{1,0:T(8,128)(2,1)S(1)}, u32[]{:S(2)}, u32[]{:S(2)}) %collective-permute-start.18) | collective-permute-done | bytes 163872 | tf_op jit(solution)/shard_map/ppermute | solution.py:593
  60.6 0.1 collective-permute-start.19
  60.7 1.4 %near_step.1 = (bf16[256,768]{1,0:T(8,128)(2,1)}, bf16[256,256]{1,0:T(8,128)(2,1)}, bf16[4,4,1024]{2,1,0:T(4,128)(2,1)}) custom-call(bf16[2,64,1024]{2,1,0:T(8,128)(2,1)S(1)} %pad_maximum_fusion.3.near_ref, bf16[4,4,1024]{2,1,0:T(4,128)(2,1)S(1)} %bitcast.64, f32[1,1024]{1,0:T(1,128)S(1)} %get-tuple-element.72.factor_ref, ...), custom_call_target="tpu_custom_call" | custom-call | tf_op jit(solution)/shard_map/near_step/pallas_call | solution.py:551
  62.1 0.1 collective-permute-done.19.far_ref
  62.2 0.7 %far_step.1 = (bf16[256,768]{1,0:T(8,128)(2,1)}, bf16[256,256]{1,0:T(8,128)(2,1)}) custom-call(bf16[2,64,1024]{2,1,0:T(8,128)(2,1)S(1)} %collective-permute-done.19.far_ref, bf16[256,768]{1,0:T(8,128)(2,1)} %get-tuple-element.94.qkv_in, bf16[256,256]{1,0:T(8,128)(2,1)} %get-tuple-element.95.out_in), custom_call_target="tpu_custom_call", output_to_operand_aliasing={{0}: (1, {}), {1}: (2, {})} | custom-call | tf_op jit(solution)/shard_map/far_step/pallas_call | solution.py:569
  (38 shorter events, 0.5 us)
Async XLA Ops:
  0.6 1.0 %copy-start.1 = (bf16[1,8,32,256]{3,2,1,0:T(8,128)(2,1)S(1)}, bf16[1,8,32,256]{3,2,1,0:T(8,128)(2,1)}, u32[]{:S(2)}) copy-start(bf16[1,8,32,256]{3,2,1,0:T(8,128)(2,1)} %param.14) | copy-start | bytes 393220
  1.7 6.7 %copy-start.6 = (bf16[1,4,4,1024]{3,2,1,0:T(4,128)(2,1)S(1)}, bf16[1,4,4,1024]{3,2,1,0:T(4,128)(2,1)}, u32[]{:S(2)}) copy-start(bf16[1,4,4,1024]{3,2,1,0:T(4,128)(2,1)} %param.15) | copy-start | bytes 98308
  1.7 6.6 %copy-start.7 = (bf16[1,4,4,1024]{3,2,1,0:T(4,128)(2,1)S(1)}, bf16[1,4,4,1024]{3,2,1,0:T(4,128)(2,1)}, u32[]{:S(2)}) copy-start(bf16[1,4,4,1024]{3,2,1,0:T(4,128)(2,1)} %param.16) | copy-start | bytes 98308
  1.7 11.1 %collective-permute-start = (bf16[9,32,256]{2,1,0:T(8,128)(2,1)S(1)}, bf16[9,32,256]{2,1,0:T(8,128)(2,1)S(1)}, u32[]{:S(2)}, u32[]{:S(2)}) collective-permute-start(bf16[9,32,256]{2,1,0:T(8,128)(2,1)S(1)} %get-tuple-element.53.second), channel_id=1, source_target_pairs={{4,8},{8,4},{5,9},{9,5},{6,10},{10,6},{7,11},{11,7},{20,24},{24,20... | collective-permute-start | bytes 442376 | tf_op jit(solution)/shard_map/ppermute | solution.py:588
  2.4 10.4 %collective-permute-start.1 = (bf16[9,32,256]{2,1,0:T(8,128)(2,1)S(1)}, bf16[9,32,256]{2,1,0:T(8,128)(2,1)S(1)}, u32[]{:S(2)}, u32[]{:S(2)}) collective-permute-start(bf16[9,32,256]{2,1,0:T(8,128)(2,1)S(1)} %get-tuple-element.54.first), channel_id=1, source_target_pairs={{0,4},{4,0},{8,12},{12,8},{1,5},{5,1},{9,13},{13,9},{2,6},{6,2},{1... | collective-permute-start | bytes 442376 | tf_op jit(solution)/shard_map/ppermute | solution.py:589
  8.3 4.5 %copy-start = (bf16[1,8,32,256]{3,2,1,0:T(8,128)(2,1)S(1)}, bf16[1,8,32,256]{3,2,1,0:T(8,128)(2,1)}, u32[]{:S(2)}) copy-start(bf16[1,8,32,256]{3,2,1,0:T(8,128)(2,1)} %param.13) | copy-start | bytes 393220
  8.3 8.3 %collective-permute-start.6 = (bf16[16,2048]{1,0:T(8,128)(2,1)S(1)}, bf16[16,2048]{1,0:T(8,128)(2,1)S(1)}, u32[]{:S(2)}, u32[]{:S(2)}) collective-permute-start(bf16[16,2048]{1,0:T(8,128)(2,1)S(1)} %pack_coarse.1), channel_id=1, source_target_pairs={{0,12},{4,8},{8,4},{12,0},{1,13},{5,9},{9,5},{13,1},{2,14},{6,10},... | collective-permute-start | bytes 196616 | tf_op jit(solution)/shard_map/ppermute | solution.py:593
  9.8 7.5 %collective-permute-start.5 = (bf16[16,2048]{1,0:T(8,128)(2,1)S(1)}, bf16[16,2048]{1,0:T(8,128)(2,1)S(1)}, u32[]{:S(2)}, u32[]{:S(2)}) collective-permute-start(bf16[16,2048]{1,0:T(8,128)(2,1)S(1)} %pack_coarse.1), channel_id=1, source_target_pairs={{0,8},{4,12},{8,0},{12,4},{1,9},{5,13},{9,1},{13,5},{2,10},{6,14},... | collective-permute-start | bytes 196616 | tf_op jit(solution)/shard_map/ppermute | solution.py:593
  9.9 7.4 %collective-permute-start.4 = (bf16[16,2048]{1,0:T(8,128)(2,1)S(1)}, bf16[16,2048]{1,0:T(8,128)(2,1)S(1)}, u32[]{:S(2)}, u32[]{:S(2)}) collective-permute-start(bf16[16,2048]{1,0:T(8,128)(2,1)S(1)} %pack_coarse.1), channel_id=1, source_target_pairs={{0,4},{4,0},{8,12},{12,8},{1,5},{5,1},{9,13},{13,9},{2,6},{6,2},{1... | collective-permute-start | bytes 196616 | tf_op jit(solution)/shard_map/ppermute | solution.py:593
  12.9 7.4 %copy-start.2 = (bf16[256,768]{1,0:T(8,128)(2,1)S(1)}, bf16[256,768]{1,0:T(8,128)(2,1)}, u32[]{:S(2)}) copy-start(bf16[256,768]{1,0:T(8,128)(2,1)} %qkv_ref.1) | copy-start | bytes 1179652
  12.9 7.4 %collective-permute-start.2 = (bf16[34,8,256]{2,1,0:T(8,128)(2,1)S(1)}, bf16[34,8,256]{2,1,0:T(8,128)(2,1)S(1)}, u32[]{:S(2)}, u32[]{:S(2)}) collective-permute-start(bf16[34,8,256]{2,1,0:T(8,128)(2,1)S(1)} %get-tuple-element.57), channel_id=1, source_target_pairs={{1,2},{2,1},{5,6},{6,5},{9,10},{10,9},{13,14},{14,13},{17,18},{18,... | collective-permute-start | bytes 417800 | tf_op jit(solution)/shard_map/ppermute | solution.py:588
  13.7 6.6 %collective-permute-start.3 = (bf16[34,8,256]{2,1,0:T(8,128)(2,1)S(1)}, bf16[34,8,256]{2,1,0:T(8,128)(2,1)S(1)}, u32[]{:S(2)}, u32[]{:S(2)}) collective-permute-start(bf16[34,8,256]{2,1,0:T(8,128)(2,1)S(1)} %get-tuple-element.58), channel_id=1, source_target_pairs={{0,1},{1,0},{2,3},{3,2},{4,5},{5,4},{6,7},{7,6},{8,9},{9,8},{10,11... | collective-permute-start | bytes 417800 | tf_op jit(solution)/shard_map/ppermute | solution.py:589
  17.3 2.3 %copy-start.9 = (f32[1,1024]{1,0:T(1,128)S(1)}, f32[1,1024]{1,0:T(1,128)}, u32[]{:S(2)}) copy-start(f32[1,1024]{1,0:T(1,128)} %constant.5.clone.coarse_freq) | copy-start | bytes 12292
  17.3 2.3 %copy-start.11 = (f32[1,256]{1,0:T(1,128)S(1)}, f32[1,256]{1,0:T(1,128)}, u32[]{:S(2)}) copy-start(f32[1,256]{1,0:T(1,128)} %constant.4.clone.fine_freq) | copy-start | bytes 3076
  17.3 3.0 %copy-start.4 = (bf16[256,256]{1,0:T(8,128)(2,1)S(1)}, bf16[256,256]{1,0:T(8,128)(2,1)}, u32[]{:S(2)}) copy-start(bf16[256,256]{1,0:T(8,128)(2,1)} %out_ref.1) | copy-start | bytes 393220
  17.4 2.3 %copy-start.8 = (f32[1024]{0:T(1024)S(1)}, f32[1024]{0:T(1024)}, u32[]{:S(2)}) copy-start(f32[1024]{0:T(1024)} %param.19) | copy-start | bytes 12292
  17.4 7.7 %collective-permute-start.8 = (bf16[4,16,2048]{2,1,0:T(8,128)(2,1)S(1)}, bf16[4,16,2048]{2,1,0:T(8,128)(2,1)S(1)}, u32[]{:S(2)}, u32[]{:S(2)}) collective-permute-start(bf16[4,16,2048]{2,1,0:T(8,128)(2,1)S(1)} %pad_maximum_fusion.1), channel_id=1, source_target_pairs={{0,2},{1,3},{2,0},{3,1},{4,6},{5,7},{6,4},{7,5},{8,10},{9,11},{10,... | collective-permute-start | bytes 786440 | tf_op jit(solution)/shard_map/ppermute | solution.py:593
  19.6 0.7 %copy-start.10 = (f32[256]{0:T(256)S(1)}, f32[256]{0:T(256)}, u32[]{:S(2)}) copy-start(f32[256]{0:T(256)} %param.18) | copy-start | bytes 3076
  24.7 1.5 %collective-permute-start.7 = (bf16[2,4,16,1024]{3,2,1,0:T(8,128)(2,1)S(1)}, bf16[2,4,16,1024]{3,2,1,0:T(8,128)(2,1)S(1)}, u32[]{:S(2)}, u32[]{:S(2)}) collective-permute-start(bf16[2,4,16,1024]{3,2,1,0:T(8,128)(2,1)S(1)} %get-tuple-element.68), channel_id=1, source_target_pairs={{0,1},{1,0},{2,3},{3,2},{4,5},{5,4},{6,7},{7,6},{8,9},{9,8},{10,11... | collective-permute-start | bytes 786440 | tf_op jit(solution)/shard_map/ppermute | solution.py:593
  25.1 1.5 %collective-permute-start.9 = (bf16[4,16,2048]{2,1,0:T(8,128)(2,1)S(1)}, bf16[4,16,2048]{2,1,0:T(8,128)(2,1)S(1)}, u32[]{:S(2)}, u32[]{:S(2)}) collective-permute-start(bf16[4,16,2048]{2,1,0:T(8,128)(2,1)S(1)} %collective-permute-done.8), channel_id=1, source_target_pairs={{0,1},{1,0},{2,3},{3,2},{4,5},{5,4},{6,7},{7,6},{8,9},{9,8},{10,11... | collective-permute-start | bytes 786440 | tf_op jit(solution)/shard_map/ppermute | solution.py:593
  25.2 2.9 %collective-permute-start.11 = (bf16[4,16,2048]{2,1,0:T(8,128)(2,1)S(1)}, bf16[4,16,2048]{2,1,0:T(8,128)(2,1)S(1)}, u32[]{:S(2)}, u32[]{:S(2)}) collective-permute-start(bf16[4,16,2048]{2,1,0:T(8,128)(2,1)S(1)} %pad_maximum_fusion.1), channel_id=1, source_target_pairs={{0,1},{1,0},{2,3},{3,2},{4,5},{5,4},{6,7},{7,6},{8,9},{9,8},{10,11... | collective-permute-start | bytes 786440 | tf_op jit(solution)/shard_map/ppermute | solution.py:593
  26.6 5.6 %collective-permute-start.10 = (bf16[4,16,1024]{2,1,0:T(8,128)(2,1)S(1)}, bf16[4,16,1024]{2,1,0:T(8,128)(2,1)S(1)}, u32[]{:S(2)}, u32[]{:S(2)}) collective-permute-start(bf16[4,16,1024]{2,1,0:T(8,128)(2,1)S(1)} %fusion.2), channel_id=1, source_target_pairs={{0,2},{1,3},{2,0},{3,1},{4,6},{5,7},{6,4},{7,5},{8,10},{9,11},{10,... | collective-permute-start | bytes 393224 | tf_op jit(solution)/shard_map/ppermute | solution.py:593
  28.3 1.0 %copy-start.3 = (bf16[3,64,1024]{2,1,0:T(8,128)(2,1)S(1)}, bf16[3,64,1024]{2,1,0:T(8,128)(2,1)}, u32[]{:S(2)}) copy-start(bf16[3,64,1024]{2,1,0:T(8,128)(2,1)} %qkv_hbm.1) | copy-start | bytes 1179652
  28.3 1.0 %copy-start.5 = (bf16[64,1024]{1,0:T(8,128)(2,1)S(1)}, bf16[64,1024]{1,0:T(8,128)(2,1)}, u32[]{:S(2)}) copy-start(bf16[64,1024]{1,0:T(8,128)(2,1)} %out_hbm.1) | copy-start | bytes 393220
  32.3 5.0 %collective-permute-start.12 = (bf16[4,16,1024]{2,1,0:T(8,128)(2,1)S(1)}, bf16[4,16,1024]{2,1,0:T(8,128)(2,1)S(1)}, u32[]{:S(2)}, u32[]{:S(2)}) collective-permute-start(bf16[4,16,1024]{2,1,0:T(8,128)(2,1)S(1)} %fusion.1), channel_id=1, source_target_pairs={{0,16},{16,0},{1,17},{17,1},{2,18},{18,2},{3,19},{19,3},{4,20},{20... | collective-permute-start | bytes 393224 | tf_op jit(solution)/shard_map/ppermute | solution.py:593
  33.9 3.5 %collective-permute-start.13 = (bf16[2,4,16,1024]{3,2,1,0:T(8,128)(2,1)S(1)}, bf16[2,4,16,1024]{3,2,1,0:T(8,128)(2,1)S(1)}, u32[]{:S(2)}, u32[]{:S(2)}) collective-permute-start(bf16[2,4,16,1024]{3,2,1,0:T(8,128)(2,1)S(1)} %bitcast.82), channel_id=1, source_target_pairs={{0,1},{1,0},{2,3},{3,2},{4,5},{5,4},{6,7},{7,6},{8,9},{9,8},{10,11... | collective-permute-start | bytes 786440 | tf_op jit(solution)/shard_map/ppermute | solution.py:593
  37.5 7.1 %collective-permute-start.14 = (bf16[128,1024]{1,0:T(8,128)(2,1)S(1)}, bf16[128,1024]{1,0:T(8,128)(2,1)S(1)}, u32[]{:S(2)}, u32[]{:S(2)}) collective-permute-start(bf16[128,1024]{1,0:T(8,128)(2,1)S(1)} %pad_maximum_fusion.2), channel_id=1, source_target_pairs={{0,4},{4,0},{8,12},{12,8},{1,5},{5,1},{9,13},{13,9},{2,6},{6,2},{1... | collective-permute-start | bytes 786440 | tf_op jit(solution)/shard_map/ppermute | solution.py:593
  39.8 6.1 %collective-permute-start.15 = (bf16[112,1024]{1,0:T(8,128)(2,1)S(1)}, bf16[112,1024]{1,0:T(8,128)(2,1)S(1)}, u32[]{:S(2)}, u32[]{:S(2)}) collective-permute-start(bf16[112,1024]{1,0:T(8,128)(2,1)S(1)} %slice.110), channel_id=1, source_target_pairs={{0,16},{16,0},{1,17},{17,1},{2,18},{18,2},{3,19},{19,3},{4,20},{20... | collective-permute-start | bytes 688136 | tf_op jit(solution)/shard_map/ppermute | solution.py:593
  46.0 9.1 %collective-permute-start.16 = (bf16[96,1024]{1,0:T(8,128)(2,1)S(1)}, bf16[96,1024]{1,0:T(8,128)(2,1)S(1)}, u32[]{:S(2)}, u32[]{:S(2)}) collective-permute-start(bf16[96,1024]{1,0:T(8,128)(2,1)S(1)} %pad_maximum_fusion.4), channel_id=1, source_target_pairs={{0,8},{4,12},{8,0},{12,4},{1,9},{5,13},{9,1},{13,5},{2,10},{6,14},... | collective-permute-start | bytes 589832 | tf_op jit(solution)/shard_map/ppermute | solution.py:593
  47.2 8.0 %collective-permute-start.17 = (bf16[144,1024]{1,0:T(8,128)(2,1)S(1)}, bf16[144,1024]{1,0:T(8,128)(2,1)S(1)}, u32[]{:S(2)}, u32[]{:S(2)}) collective-permute-start(bf16[144,1024]{1,0:T(8,128)(2,1)S(1)} %slice.115), channel_id=1, source_target_pairs={{0,16},{16,0},{1,17},{17,1},{2,18},{18,2},{3,19},{19,3},{4,20},{20... | collective-permute-start | bytes 884744 | tf_op jit(solution)/shard_map/ppermute | solution.py:593
  55.2 5.4 %collective-permute-start.18 = (bf16[80,1024]{1,0:T(8,128)(2,1)S(1)}, bf16[80,1024]{1,0:T(8,128)(2,1)S(1)}, u32[]{:S(2)}, u32[]{:S(2)}) collective-permute-start(bf16[80,1024]{1,0:T(8,128)(2,1)S(1)} %pad_maximum_fusion.5), channel_id=1, source_target_pairs={{0,2},{1,3},{2,0},{3,1},{4,6},{5,7},{6,4},{7,5},{8,10},{9,11},{10,... | collective-permute-start | bytes 491528 | tf_op jit(solution)/shard_map/ppermute | solution.py:593
  60.6 1.6 %collective-permute-start.19 = (bf16[2,64,1024]{2,1,0:T(8,128)(2,1)S(1)}, bf16[2,64,1024]{2,1,0:T(8,128)(2,1)S(1)}, u32[]{:S(2)}, u32[]{:S(2)}) collective-permute-start(bf16[2,64,1024]{2,1,0:T(8,128)(2,1)S(1)} %pad_maximum_fusion.3.near_ref), channel_id=1, source_target_pairs={{0,1},{1,0},{2,3},{3,2},{4,5},{5,4},{6,7},{7,6},{8,9},{9,8},{10,11... | collective-permute-start | bytes 786440 | tf_op jit(solution)/shard_map/ppermute | solution.py:593

commit v11 on v10

--- a/solution.py
+++ b/solution.py
@@ -21,7 +21,7 @@
 extent = side + 2 * RAD
 lanes_wide = 16
 thin = 4
-lag = 1
+lag = 2
 scale = 1.0 / math.sqrt(HD)
 vmem_bytes = 48 * 1024 * 1024
 
@@ -637,14 +637,16 @@
     row_near, row_far = neighbours(*payloads, "gy")
     own = packed(payloads, x_coarse[0], dy_coarse[0])
     count = own.shape[0]
-    row_group = all_rows(own)
+    pieces = [own] + [swapped(own, "gy", row) for row in range(1, downs)]
     edges = col_edges(picture, cotangent, row_far, row_near)
     *edges, step, gain_f, gain_c = tied(*edges, timestep, fine_gain, coarse_gain)
     col_near, col_far = neighbours(*edges, "gx")
     factor, coarse_factor = time_factors(step, gain_f, gain_c)
+    factor, *pieces = tied(factor, *pieces)
+    row_group = jnp.stack(pieces)
     cross = swapped(row_group, "gx", 2)
     beside = swapped(row_group, "gx", 1)
-    col_far, col_near, row_group, factor = tied(col_far, col_near, row_group, factor)
+    col_far, col_near, row_group = tied(col_far, col_near, row_group)
     dx_picture, fine_keep, fine_send = fine_block(
         (across, downs),
         picture,
@@ -659,7 +661,6 @@
     )
     fine_half = fine_keep + wide(swapped(fine_send, "gx", 1))
     opposite = swapped(cross, "gx", 1)
-    fine_half, opposite = tied(fine_half, opposite)
 
     fine_quarter = narrow(fine_half[0] + wide(swapped(narrow(fine_half[1]), "gx", 2)))
     everyone = jnp.stack([row_group, cross, beside, opposite]).reshape(-1, 2 * D_C)

time: 63.2 us -> 62.9 us (level)
  waiting for transfers between devices: 20.1 us -> 21.2 us
  starting transfers between devices: 28 us -> 27.3 us
    ppermute x16, waiting for transfers between devices: 20.1 us -> 21.2 us  [swapped(): lax.ppermute(value, axis, [(i, i ^ mask) for i in range(lax.axis_size(axi...]
    ppermute x16, starting transfers between devices: 17.7 us -> 17 us  [swapped(): lax.ppermute(value, axis, [(i, i ^ mask) for i in range(lax.axis_size(axi...]
  transfers between devices with their start and end apart: 20 -> 20, of which waited for: 11 -> 8; matrix products, arithmetic and copies ran while one was open for 1% -> 1% of each run, Pallas kernels for 14% -> 14%
where the time goes in v11:
time: 62.9 us; the launch traced here: 62.7 us
  starting transfers between devices  27.3 us (43%)
  waiting for transfers between devices  21.2 us (34%)
  Pallas kernels  9.73 us (15%)
  local copies, waits for them, and re-layouts  2.21 us (4%)
  between operations  1.72 us (3%)
    ppermute x16, waiting for transfers between devices, swapped(): lax.ppermute(value, axis, [(i, i ^ mask) for i in range(lax.axis_size(axi...  21.2 us
    ppermute x16, starting transfers between devices, swapped(): lax.ppermute(value, axis, [(i, i ^ mask) for i in range(lax.axis_size(axi...  17 us
    ppermute x2, starting transfers between devices, neighbours(): return (lax.ppermute(to_near, axis, near), from_far)  8.81 us
    pallas_call x1, Pallas kernels, fine_block(): pl.pallas_call(fine_body, out_shape=(jax.ShapeDtypeStruct((height, breadt...  4.33 us
    pallas_call x1, Pallas kernels, coarse_block(): pl.pallas_call(coarse_body, out_shape=(jax.ShapeDtypeStruct((count, D_C),...  2.23 us
    ppermute x2, starting transfers between devices, neighbours(): from_far = lax.ppermute(to_far, axis, far)  1.47 us
    pallas_call x1, Pallas kernels, near_step(): pl.pallas_call(near_body, out_shape=(jax.ShapeDtypeStruct((D_F, 3 * D_F),...  1.36 us
  transfers between devices with their start and end apart: 20, of which 8 were waited for; matrix products, arithmetic and copies ran while one was open for 1% of the time, Pallas kernels for 14%

profile of v11, /device:TPU:0, one launch (start us, length us, event | category | flops | bytes accessed | tf_op | source)
XLA Modules:
  0.0 62.7 jit_solution(12564875548335610026)
XLA Ops:
  0.6 1.0 %slice_bitcast_fusion.3 = (bf16[6,32,256]{2,1,0:T(8,128)(2,1)S(1)}, bf16[6,32,256]{2,1,0:T(8,128)(2,1)S(1)}) fusion(bf16[1,8,32,256]{3,2,1,0:T(8,128)(2,1)} %param.13), kind=kLoop, calls=%fused_computation.23 | loop fusion | bytes 393216 | tf_op jit(solution)/shard_map/slice | solution.py:419
  1.7 0.0 copy-start.6
  1.7 0.0 copy-start.7
  1.7 0.7 %collective-permute-start = (bf16[9,32,256]{2,1,0:T(8,128)(2,1)S(1)}, bf16[9,32,256]{2,1,0:T(8,128)(2,1)S(1)}, u32[]{:S(2)}, u32[]{:S(2)}) collective-permute-start(bf16[9,32,256]{2,1,0:T(8,128)(2,1)S(1)} %get-tuple-element.55.second), channel_id=1, source_target_pairs={{4,8},{8,4},{5,9},{9,5},{6,10},{10,6},{7,11},{11,7},{20,24},{24,20... | collective-permute-start | bytes 442376 | tf_op jit(solution)/shard_map/ppermute | solution.py:588
  2.4 5.9 %collective-permute-start.1 = (bf16[9,32,256]{2,1,0:T(8,128)(2,1)S(1)}, bf16[9,32,256]{2,1,0:T(8,128)(2,1)S(1)}, u32[]{:S(2)}, u32[]{:S(2)}) collective-permute-start(bf16[9,32,256]{2,1,0:T(8,128)(2,1)S(1)} %get-tuple-element.56.first), channel_id=1, source_target_pairs={{0,4},{4,0},{8,12},{12,8},{1,5},{5,1},{9,13},{13,9},{2,6},{6,2},{1... | collective-permute-start | bytes 442376 | tf_op jit(solution)/shard_map/ppermute | solution.py:589
  8.3 0.1 collective-permute-start.4
  8.4 1.9 %collective-permute-start.5 = (bf16[16,2048]{1,0:T(8,128)(2,1)S(1)}, bf16[16,2048]{1,0:T(8,128)(2,1)S(1)}, u32[]{:S(2)}, u32[]{:S(2)}) collective-permute-start(bf16[16,2048]{1,0:T(8,128)(2,1)S(1)} %pack_coarse.1), channel_id=1, source_target_pairs={{0,8},{4,12},{8,0},{12,4},{1,9},{5,13},{9,1},{13,5},{2,10},{6,14},... | collective-permute-start | bytes 196616 | tf_op jit(solution)/shard_map/ppermute | solution.py:593
  10.3 2.5 %collective-permute-start.6 = (bf16[16,2048]{1,0:T(8,128)(2,1)S(1)}, bf16[16,2048]{1,0:T(8,128)(2,1)S(1)}, u32[]{:S(2)}, u32[]{:S(2)}) collective-permute-start(bf16[16,2048]{1,0:T(8,128)(2,1)S(1)} %pack_coarse.1), channel_id=1, source_target_pairs={{0,12},{4,8},{8,4},{12,0},{1,13},{5,9},{9,5},{13,1},{2,14},{6,10},... | collective-permute-start | bytes 196616 | tf_op jit(solution)/shard_map/ppermute | solution.py:593
  13.4 0.0 collective-permute-done.row_far_ref
  13.5 0.0 collective-permute-done.1.row_near_ref
  13.5 0.0 copy-start.8
  13.5 0.0 copy-start.9
  13.5 0.0 copy-start.10
  13.5 0.0 copy-start.11
  13.5 0.1 col_edges.1
  13.6 0.0 copy-start.2
  13.6 0.8 %collective-permute-start.2 = (bf16[34,8,256]{2,1,0:T(8,128)(2,1)S(1)}, bf16[34,8,256]{2,1,0:T(8,128)(2,1)S(1)}, u32[]{:S(2)}, u32[]{:S(2)}) collective-permute-start(bf16[34,8,256]{2,1,0:T(8,128)(2,1)S(1)} %get-tuple-element.59), channel_id=1, source_target_pairs={{1,2},{2,1},{5,6},{6,5},{9,10},{10,9},{13,14},{14,13},{17,18},{18,... | collective-permute-start | bytes 417800 | tf_op jit(solution)/shard_map/ppermute | solution.py:588
  14.4 2.9 %collective-permute-start.3 = (bf16[34,8,256]{2,1,0:T(8,128)(2,1)S(1)}, bf16[34,8,256]{2,1,0:T(8,128)(2,1)S(1)}, u32[]{:S(2)}, u32[]{:S(2)}) collective-permute-start(bf16[34,8,256]{2,1,0:T(8,128)(2,1)S(1)} %get-tuple-element.60), channel_id=1, source_target_pairs={{0,1},{1,0},{2,3},{3,2},{4,5},{5,4},{6,7},{7,6},{8,9},{9,8},{10,11... | collective-permute-start | bytes 417800 | tf_op jit(solution)/shard_map/ppermute | solution.py:589
  17.4 0.1 time_factors.1
  17.4 0.0 collective-permute-done.4
  17.4 0.0 collective-permute-done.5
  17.4 0.0 collective-permute-done.6
  17.4 0.0 copy-start.4
  17.5 1.4 %collective-permute-start.9 = (bf16[4,16,2048]{2,1,0:T(8,128)(2,1)S(1)}, bf16[4,16,2048]{2,1,0:T(8,128)(2,1)S(1)}, u32[]{:S(2)}, u32[]{:S(2)}) collective-permute-start(bf16[4,16,2048]{2,1,0:T(8,128)(2,1)S(1)} %pad_maximum_fusion.1), channel_id=1, source_target_pairs={{0,2},{1,3},{2,0},{3,1},{4,6},{5,7},{6,4},{7,5},{8,10},{9,11},{10,... | collective-permute-start | bytes 786440 | tf_op jit(solution)/shard_map/ppermute | solution.py:593
  18.9 0.0 collective-permute-done.2.col_far_ref
  18.9 0.0 collective-permute-done.3.col_near_ref
  18.9 4.3 %fine_block.1 = (bf16[8,32,256]{2,1,0:T(8,128)(2,1)}, f32[2,4,16,1024]{3,2,1,0:T(8,128)S(1)}, bf16[2,4,16,1024]{3,2,1,0:T(8,128)(2,1)S(1)}) custom-call(bf16[8,32,256]{2,1,0:T(8,128)(2,1)S(1)} %bitcast.61, bf16[8,32,256]{2,1,0:T(8,128)(2,1)S(1)} %bitcast.63, bf16[9,32,256]{2,1,0:T(8,128)(2,1)S(1)} %collective-permute-done.row_far_ref, ...), custom_call_target="tpu_custom_call" | custom-call | tf_op jit(solution)/shard_map/fine_block/pallas_call | solution.py:297
  23.2 1.1 %collective-permute-start.7 = (bf16[2,4,16,1024]{3,2,1,0:T(8,128)(2,1)S(1)}, bf16[2,4,16,1024]{3,2,1,0:T(8,128)(2,1)S(1)}, u32[]{:S(2)}, u32[]{:S(2)}) collective-permute-start(bf16[2,4,16,1024]{3,2,1,0:T(8,128)(2,1)S(1)} %get-tuple-element.74), channel_id=1, source_target_pairs={{0,1},{1,0},{2,3},{3,2},{4,5},{5,4},{6,7},{7,6},{8,9},{9,8},{10,11... | collective-permute-start | bytes 786440 | tf_op jit(solution)/shard_map/ppermute | solution.py:593
  24.3 0.0 collective-permute-start.10
  24.3 1.5 %collective-permute-done.9 = bf16[4,16,2048]{2,1,0:T(8,128)(2,1)S(1)} collective-permute-done((bf16[4,16,2048]{2,1,0:T(8,128)(2,1)S(1)}, bf16[4,16,2048]{2,1,0:T(8,128)(2,1)S(1)}, u32[]{:S(2)}, u32[]{:S(2)}) %collective-permute-start.9) | collective-permute-done | bytes 262176 | tf_op jit(solution)/shard_map/ppermute | solution.py:593
  25.8 0.0 collective-permute-start.11
  25.8 0.0 collective-permute-done.7
  25.8 0.1 convert_add_fusion.1
  25.9 1.7 %collective-permute-start.8 = (bf16[4,16,1024]{2,1,0:T(8,128)(2,1)S(1)}, bf16[4,16,1024]{2,1,0:T(8,128)(2,1)S(1)}, u32[]{:S(2)}, u32[]{:S(2)}) collective-permute-start(bf16[4,16,1024]{2,1,0:T(8,128)(2,1)S(1)} %fusion.3), channel_id=1, source_target_pairs={{0,2},{1,3},{2,0},{3,1},{4,6},{5,7},{6,4},{7,5},{8,10},{9,11},{10,... | collective-permute-start | bytes 393224 | tf_op jit(solution)/shard_map/ppermute | solution.py:593
  27.7 0.0 collective-permute-done.10
  27.7 0.0 collective-permute-done.11
  27.7 0.1 pad_maximum_fusion
  27.8 0.0 copy-start.3
  27.8 0.0 copy-start.5
  27.8 0.1 fusion.6
  27.9 0.9 %copy-done.3 = bf16[3,64,1024]{2,1,0:T(8,128)(2,1)S(1)} copy-done((bf16[3,64,1024]{2,1,0:T(8,128)(2,1)S(1)}, bf16[3,64,1024]{2,1,0:T(8,128)(2,1)}, u32[]{:S(2)}) %copy-start.3) | copy-done | bytes 393240
  28.8 0.0 copy-done.5
  28.8 2.2 %coarse_block.1 = (bf16[256,1024]{1,0:T(8,128)(2,1)S(1)}, bf16[256,1024]{1,0:T(8,128)(2,1)S(1)}) custom-call(bf16[256,1024]{1,0:T(8,128)(2,1)S(1)} %get-tuple-element.105.x_ref, bf16[256,1024]{1,0:T(8,128)(2,1)S(1)} %get-tuple-element.104.dy_ref, f32[1,1024]{1,0:T(1,128)S(1)} %get-tuple-element.76.factor_ref, bf16[3,64,1024]{2,1,0:T(8,128)(2,1)S(1)} %copy-done.3, ...), custom_call_target="tpu_custom_call" | custom-call | tf_op jit(solution)/shard_map/coarse_block/pallas_call | solution.py:374
  31.1 0.8 %collective-permute-done.8 = bf16[4,16,1024]{2,1,0:T(8,128)(2,1)S(1)} collective-permute-done((bf16[4,16,1024]{2,1,0:T(8,128)(2,1)S(1)}, bf16[4,16,1024]{2,1,0:T(8,128)(2,1)S(1)}, u32[]{:S(2)}, u32[]{:S(2)}) %collective-permute-start.8) | collective-permute-done | bytes 131104 | tf_op jit(solution)/shard_map/ppermute | solution.py:593
  31.9 1.6 %collective-permute-start.12 = (bf16[4,16,1024]{2,1,0:T(8,128)(2,1)S(1)}, bf16[4,16,1024]{2,1,0:T(8,128)(2,1)S(1)}, u32[]{:S(2)}, u32[]{:S(2)}) collective-permute-start(bf16[4,16,1024]{2,1,0:T(8,128)(2,1)S(1)} %fusion.1), channel_id=1, source_target_pairs={{0,16},{16,0},{1,17},{17,1},{2,18},{18,2},{3,19},{19,3},{4,20},{20... | collective-permute-start | bytes 393224 | tf_op jit(solution)/shard_map/ppermute | solution.py:593
  33.6 0.1 collective-permute-start.13
  33.6 3.5 %collective-permute-done.12 = bf16[4,16,1024]{2,1,0:T(8,128)(2,1)S(1)} collective-permute-done((bf16[4,16,1024]{2,1,0:T(8,128)(2,1)S(1)}, bf16[4,16,1024]{2,1,0:T(8,128)(2,1)S(1)}, u32[]{:S(2)}, u32[]{:S(2)}) %collective-permute-start.12) | collective-permute-done | bytes 131104 | tf_op jit(solution)/shard_map/ppermute | solution.py:593
  37.2 0.0 collective-permute-done.13
  37.2 0.1 convert_add_fusion
  37.3 1.7 %collective-permute-start.14 = (bf16[128,1024]{1,0:T(8,128)(2,1)S(1)}, bf16[128,1024]{1,0:T(8,128)(2,1)S(1)}, u32[]{:S(2)}, u32[]{:S(2)}) collective-permute-start(bf16[128,1024]{1,0:T(8,128)(2,1)S(1)} %pad_maximum_fusion.2), channel_id=1, source_target_pairs={{0,4},{4,0},{8,12},{12,8},{1,5},{5,1},{9,13},{13,9},{2,6},{6,2},{1... | collective-permute-start | bytes 786440 | tf_op jit(solution)/shard_map/ppermute | solution.py:593
  39.0 1.6 %collective-permute-start.15 = (bf16[112,1024]{1,0:T(8,128)(2,1)S(1)}, bf16[112,1024]{1,0:T(8,128)(2,1)S(1)}, u32[]{:S(2)}, u32[]{:S(2)}) collective-permute-start(bf16[112,1024]{1,0:T(8,128)(2,1)S(1)} %slice.110), channel_id=1, source_target_pairs={{0,16},{16,0},{1,17},{17,1},{2,18},{18,2},{3,19},{19,3},{4,20},{20... | collective-permute-start | bytes 688136 | tf_op jit(solution)/shard_map/ppermute | solution.py:593
  40.6 3.9 %collective-permute-done.14 = bf16[128,1024]{1,0:T(8,128)(2,1)S(1)} collective-permute-done((bf16[128,1024]{1,0:T(8,128)(2,1)S(1)}, bf16[128,1024]{1,0:T(8,128)(2,1)S(1)}, u32[]{:S(2)}, u32[]{:S(2)}) %collective-permute-start.14) | collective-permute-done | bytes 262176 | tf_op jit(solution)/shard_map/ppermute | solution.py:593
  44.5 0.6 collective-permute-done.15.refs_0_
  45.1 1.0 %collective-permute-start.16 = (bf16[96,1024]{1,0:T(8,128)(2,1)S(1)}, bf16[96,1024]{1,0:T(8,128)(2,1)S(1)}, u32[]{:S(2)}, u32[]{:S(2)}) collective-permute-start(bf16[96,1024]{1,0:T(8,128)(2,1)S(1)} %pad_maximum_fusion.4), channel_id=1, source_target_pairs={{0,8},{4,12},{8,0},{12,4},{1,9},{5,13},{9,1},{13,5},{2,10},{6,14},... | collective-permute-start | bytes 589832 | tf_op jit(solution)/shard_map/ppermute | solution.py:593
  46.1 1.6 %collective-permute-start.17 = (bf16[144,1024]{1,0:T(8,128)(2,1)S(1)}, bf16[144,1024]{1,0:T(8,128)(2,1)S(1)}, u32[]{:S(2)}, u32[]{:S(2)}) collective-permute-start(bf16[144,1024]{1,0:T(8,128)(2,1)S(1)} %slice.115), channel_id=1, source_target_pairs={{0,16},{16,0},{1,17},{17,1},{2,18},{18,2},{3,19},{19,3},{4,20},{20... | collective-permute-start | bytes 884744 | tf_op jit(solution)/shard_map/ppermute | solution.py:593
  47.7 7.1 %collective-permute-done.16 = bf16[96,1024]{1,0:T(8,128)(2,1)S(1)} collective-permute-done((bf16[96,1024]{1,0:T(8,128)(2,1)S(1)}, bf16[96,1024]{1,0:T(8,128)(2,1)S(1)}, u32[]{:S(2)}, u32[]{:S(2)}) %collective-permute-start.16) | collective-permute-done | bytes 196640 | tf_op jit(solution)/shard_map/ppermute | solution.py:593
  54.8 0.0 collective-permute-done.17.refs_1_
  54.9 0.8 %collective-permute-start.18 = (bf16[80,1024]{1,0:T(8,128)(2,1)S(1)}, bf16[80,1024]{1,0:T(8,128)(2,1)S(1)}, u32[]{:S(2)}, u32[]{:S(2)}) collective-permute-start(bf16[80,1024]{1,0:T(8,128)(2,1)S(1)} %pad_maximum_fusion.5), channel_id=1, source_target_pairs={{0,2},{1,3},{2,0},{3,1},{4,6},{5,7},{6,4},{7,5},{8,10},{9,11},{10,... | collective-permute-start | bytes 491528 | tf_op jit(solution)/shard_map/ppermute | solution.py:593
  55.7 0.9 %pair_sum.1 = (bf16[3,64,1024]{2,1,0:T(8,128)(2,1)}, bf16[64,1024]{1,0:T(8,128)(2,1)}) custom-call(bf16[256,1024]{1,0:T(8,128)(2,1)S(1)} %get-tuple-element.84.own, bf16[112,1024]{1,0:T(8,128)(2,1)S(1)} %collective-permute-done.15.refs_0_, bf16[144,1024]{1,0:T(8,128)(2,1)S(1)} %collective-permute-done.17.refs_1_), custom_call_target="tpu_custom_call" | custom-call | tf_op jit(solution)/shard_map/pair_sum/pallas_call | solution.py:502
  56.6 3.7 %collective-permute-done.18 = bf16[80,1024]{1,0:T(8,128)(2,1)S(1)} collective-permute-done((bf16[80,1024]{1,0:T(8,128)(2,1)S(1)}, bf16[80,1024]{1,0:T(8,128)(2,1)S(1)}, u32[]{:S(2)}, u32[]{:S(2)}) %collective-permute-start.18) | collective-permute-done | bytes 163872 | tf_op jit(solution)/shard_map/ppermute | solution.py:593
  60.3 0.1 collective-permute-start.19
  60.4 1.4 %near_step.1 = (bf16[256,768]{1,0:T(8,128)(2,1)}, bf16[256,256]{1,0:T(8,128)(2,1)}, bf16[4,4,1024]{2,1,0:T(4,128)(2,1)}) custom-call(bf16[2,64,1024]{2,1,0:T(8,128)(2,1)S(1)} %pad_maximum_fusion.3.near_ref, bf16[4,4,1024]{2,1,0:T(4,128)(2,1)S(1)} %bitcast.66, f32[1,1024]{1,0:T(1,128)S(1)} %get-tuple-element.76.factor_ref, ...), custom_call_target="tpu_custom_call" | custom-call | tf_op jit(solution)/shard_map/near_step/pallas_call | solution.py:551
  61.8 0.1 collective-permute-done.19.far_ref
  61.9 0.7 %far_step.1 = (bf16[256,768]{1,0:T(8,128)(2,1)}, bf16[256,256]{1,0:T(8,128)(2,1)}) custom-call(bf16[2,64,1024]{2,1,0:T(8,128)(2,1)S(1)} %collective-permute-done.19.far_ref, bf16[256,768]{1,0:T(8,128)(2,1)} %get-tuple-element.98.qkv_in, bf16[256,256]{1,0:T(8,128)(2,1)} %get-tuple-element.99.out_in), custom_call_target="tpu_custom_call", output_to_operand_aliasing={{0}: (1, {}), {1}: (2, {})} | custom-call | tf_op jit(solution)/shard_map/far_step/pallas_call | solution.py:569
  (38 shorter events, 0.5 us)
Async XLA Ops:
  0.6 1.0 %copy-start.1 = (bf16[1,8,32,256]{3,2,1,0:T(8,128)(2,1)S(1)}, bf16[1,8,32,256]{3,2,1,0:T(8,128)(2,1)}, u32[]{:S(2)}) copy-start(bf16[1,8,32,256]{3,2,1,0:T(8,128)(2,1)} %param.14) | copy-start | bytes 393220
  1.7 6.7 %copy-start.6 = (bf16[1,4,4,1024]{3,2,1,0:T(4,128)(2,1)S(1)}, bf16[1,4,4,1024]{3,2,1,0:T(4,128)(2,1)}, u32[]{:S(2)}) copy-start(bf16[1,4,4,1024]{3,2,1,0:T(4,128)(2,1)} %param.15) | copy-start | bytes 98308
  1.7 6.6 %copy-start.7 = (bf16[1,4,4,1024]{3,2,1,0:T(4,128)(2,1)S(1)}, bf16[1,4,4,1024]{3,2,1,0:T(4,128)(2,1)}, u32[]{:S(2)}) copy-start(bf16[1,4,4,1024]{3,2,1,0:T(4,128)(2,1)} %param.16) | copy-start | bytes 98308
  1.7 11.7 %collective-permute-start = (bf16[9,32,256]{2,1,0:T(8,128)(2,1)S(1)}, bf16[9,32,256]{2,1,0:T(8,128)(2,1)S(1)}, u32[]{:S(2)}, u32[]{:S(2)}) collective-permute-start(bf16[9,32,256]{2,1,0:T(8,128)(2,1)S(1)} %get-tuple-element.55.second), channel_id=1, source_target_pairs={{4,8},{8,4},{5,9},{9,5},{6,10},{10,6},{7,11},{11,7},{20,24},{24,20... | collective-permute-start | bytes 442376 | tf_op jit(solution)/shard_map/ppermute | solution.py:588
  2.4 11.0 %collective-permute-start.1 = (bf16[9,32,256]{2,1,0:T(8,128)(2,1)S(1)}, bf16[9,32,256]{2,1,0:T(8,128)(2,1)S(1)}, u32[]{:S(2)}, u32[]{:S(2)}) collective-permute-start(bf16[9,32,256]{2,1,0:T(8,128)(2,1)S(1)} %get-tuple-element.56.first), channel_id=1, source_target_pairs={{0,4},{4,0},{8,12},{12,8},{1,5},{5,1},{9,13},{13,9},{2,6},{6,2},{1... | collective-permute-start | bytes 442376 | tf_op jit(solution)/shard_map/ppermute | solution.py:589
  8.3 5.1 %copy-start = (bf16[1,8,32,256]{3,2,1,0:T(8,128)(2,1)S(1)}, bf16[1,8,32,256]{3,2,1,0:T(8,128)(2,1)}, u32[]{:S(2)}) copy-start(bf16[1,8,32,256]{3,2,1,0:T(8,128)(2,1)} %param.13) | copy-start | bytes 393220
  8.3 9.1 %collective-permute-start.4 = (bf16[16,2048]{1,0:T(8,128)(2,1)S(1)}, bf16[16,2048]{1,0:T(8,128)(2,1)S(1)}, u32[]{:S(2)}, u32[]{:S(2)}) collective-permute-start(bf16[16,2048]{1,0:T(8,128)(2,1)S(1)} %pack_coarse.1), channel_id=1, source_target_pairs={{0,4},{4,0},{8,12},{12,8},{1,5},{5,1},{9,13},{13,9},{2,6},{6,2},{1... | collective-permute-start | bytes 196616 | tf_op jit(solution)/shard_map/ppermute | solution.py:593
  8.4 9.0 %collective-permute-start.5 = (bf16[16,2048]{1,0:T(8,128)(2,1)S(1)}, bf16[16,2048]{1,0:T(8,128)(2,1)S(1)}, u32[]{:S(2)}, u32[]{:S(2)}) collective-permute-start(bf16[16,2048]{1,0:T(8,128)(2,1)S(1)} %pack_coarse.1), channel_id=1, source_target_pairs={{0,8},{4,12},{8,0},{12,4},{1,9},{5,13},{9,1},{13,5},{2,10},{6,14},... | collective-permute-start | bytes 196616 | tf_op jit(solution)/shard_map/ppermute | solution.py:593
  10.3 7.1 %collective-permute-start.6 = (bf16[16,2048]{1,0:T(8,128)(2,1)S(1)}, bf16[16,2048]{1,0:T(8,128)(2,1)S(1)}, u32[]{:S(2)}, u32[]{:S(2)}) collective-permute-start(bf16[16,2048]{1,0:T(8,128)(2,1)S(1)} %pack_coarse.1), channel_id=1, source_target_pairs={{0,12},{4,8},{8,4},{12,0},{1,13},{5,9},{9,5},{13,1},{2,14},{6,10},... | collective-permute-start | bytes 196616 | tf_op jit(solution)/shard_map/ppermute | solution.py:593
  13.5 3.9 %copy-start.8 = (f32[1024]{0:T(1024)S(1)}, f32[1024]{0:T(1024)}, u32[]{:S(2)}) copy-start(f32[1024]{0:T(1024)} %param.19) | copy-start | bytes 12292
  13.5 3.9 %copy-start.9 = (f32[1,1024]{1,0:T(1,128)S(1)}, f32[1,1024]{1,0:T(1,128)}, u32[]{:S(2)}) copy-start(f32[1,1024]{1,0:T(1,128)} %constant.5.clone.coarse_freq) | copy-start | bytes 12292
  13.5 3.8 %copy-start.10 = (f32[256]{0:T(256)S(1)}, f32[256]{0:T(256)}, u32[]{:S(2)}) copy-start(f32[256]{0:T(256)} %param.18) | copy-start | bytes 3076
  13.5 3.8 %copy-start.11 = (f32[1,256]{1,0:T(1,128)S(1)}, f32[1,256]{1,0:T(1,128)}, u32[]{:S(2)}) copy-start(f32[1,256]{1,0:T(1,128)} %constant.4.clone.fine_freq) | copy-start | bytes 3076
  13.6 5.3 %copy-start.2 = (bf16[256,768]{1,0:T(8,128)(2,1)S(1)}, bf16[256,768]{1,0:T(8,128)(2,1)}, u32[]{:S(2)}) copy-start(bf16[256,768]{1,0:T(8,128)(2,1)} %qkv_ref.1) | copy-start | bytes 1179652
  13.6 5.2 %collective-permute-start.2 = (bf16[34,8,256]{2,1,0:T(8,128)(2,1)S(1)}, bf16[34,8,256]{2,1,0:T(8,128)(2,1)S(1)}, u32[]{:S(2)}, u32[]{:S(2)}) collective-permute-start(bf16[34,8,256]{2,1,0:T(8,128)(2,1)S(1)} %get-tuple-element.59), channel_id=1, source_target_pairs={{1,2},{2,1},{5,6},{6,5},{9,10},{10,9},{13,14},{14,13},{17,18},{18,... | collective-permute-start | bytes 417800 | tf_op jit(solution)/shard_map/ppermute | solution.py:588
  14.4 4.4 %collective-permute-start.3 = (bf16[34,8,256]{2,1,0:T(8,128)(2,1)S(1)}, bf16[34,8,256]{2,1,0:T(8,128)(2,1)S(1)}, u32[]{:S(2)}, u32[]{:S(2)}) collective-permute-start(bf16[34,8,256]{2,1,0:T(8,128)(2,1)S(1)} %get-tuple-element.60), channel_id=1, source_target_pairs={{0,1},{1,0},{2,3},{3,2},{4,5},{5,4},{6,7},{7,6},{8,9},{9,8},{10,11... | collective-permute-start | bytes 417800 | tf_op jit(solution)/shard_map/ppermute | solution.py:589
  17.4 1.4 %copy-start.4 = (bf16[256,256]{1,0:T(8,128)(2,1)S(1)}, bf16[256,256]{1,0:T(8,128)(2,1)}, u32[]{:S(2)}) copy-start(bf16[256,256]{1,0:T(8,128)(2,1)} %out_ref.1) | copy-start | bytes 393220
  17.5 8.3 %collective-permute-start.9 = (bf16[4,16,2048]{2,1,0:T(8,128)(2,1)S(1)}, bf16[4,16,2048]{2,1,0:T(8,128)(2,1)S(1)}, u32[]{:S(2)}, u32[]{:S(2)}) collective-permute-start(bf16[4,16,2048]{2,1,0:T(8,128)(2,1)S(1)} %pad_maximum_fusion.1), channel_id=1, source_target_pairs={{0,2},{1,3},{2,0},{3,1},{4,6},{5,7},{6,4},{7,5},{8,10},{9,11},{10,... | collective-permute-start | bytes 786440 | tf_op jit(solution)/shard_map/ppermute | solution.py:593
  23.2 2.6 %collective-permute-start.7 = (bf16[2,4,16,1024]{3,2,1,0:T(8,128)(2,1)S(1)}, bf16[2,4,16,1024]{3,2,1,0:T(8,128)(2,1)S(1)}, u32[]{:S(2)}, u32[]{:S(2)}) collective-permute-start(bf16[2,4,16,1024]{3,2,1,0:T(8,128)(2,1)S(1)} %get-tuple-element.74), channel_id=1, source_target_pairs={{0,1},{1,0},{2,3},{3,2},{4,5},{5,4},{6,7},{7,6},{8,9},{9,8},{10,11... | collective-permute-start | bytes 786440 | tf_op jit(solution)/shard_map/ppermute | solution.py:593
  24.3 3.3 %collective-permute-start.10 = (bf16[4,16,2048]{2,1,0:T(8,128)(2,1)S(1)}, bf16[4,16,2048]{2,1,0:T(8,128)(2,1)S(1)}, u32[]{:S(2)}, u32[]{:S(2)}) collective-permute-start(bf16[4,16,2048]{2,1,0:T(8,128)(2,1)S(1)} %pad_maximum_fusion.1), channel_id=1, source_target_pairs={{0,1},{1,0},{2,3},{3,2},{4,5},{5,4},{6,7},{7,6},{8,9},{9,8},{10,11... | collective-permute-start | bytes 786440 | tf_op jit(solution)/shard_map/ppermute | solution.py:593
  25.8 1.8 %collective-permute-start.11 = (bf16[4,16,2048]{2,1,0:T(8,128)(2,1)S(1)}, bf16[4,16,2048]{2,1,0:T(8,128)(2,1)S(1)}, u32[]{:S(2)}, u32[]{:S(2)}) collective-permute-start(bf16[4,16,2048]{2,1,0:T(8,128)(2,1)S(1)} %collective-permute-done.9), channel_id=1, source_target_pairs={{0,1},{1,0},{2,3},{3,2},{4,5},{5,4},{6,7},{7,6},{8,9},{9,8},{10,11... | collective-permute-start | bytes 786440 | tf_op jit(solution)/shard_map/ppermute | solution.py:593
  25.9 6.0 %collective-permute-start.8 = (bf16[4,16,1024]{2,1,0:T(8,128)(2,1)S(1)}, bf16[4,16,1024]{2,1,0:T(8,128)(2,1)S(1)}, u32[]{:S(2)}, u32[]{:S(2)}) collective-permute-start(bf16[4,16,1024]{2,1,0:T(8,128)(2,1)S(1)} %fusion.3), channel_id=1, source_target_pairs={{0,2},{1,3},{2,0},{3,1},{4,6},{5,7},{6,4},{7,5},{8,10},{9,11},{10,... | collective-permute-start | bytes 393224 | tf_op jit(solution)/shard_map/ppermute | solution.py:593
  27.8 1.0 %copy-start.3 = (bf16[3,64,1024]{2,1,0:T(8,128)(2,1)S(1)}, bf16[3,64,1024]{2,1,0:T(8,128)(2,1)}, u32[]{:S(2)}) copy-start(bf16[3,64,1024]{2,1,0:T(8,128)(2,1)} %qkv_hbm.1) | copy-start | bytes 1179652
  27.8 1.0 %copy-start.5 = (bf16[64,1024]{1,0:T(8,128)(2,1)S(1)}, bf16[64,1024]{1,0:T(8,128)(2,1)}, u32[]{:S(2)}) copy-start(bf16[64,1024]{1,0:T(8,128)(2,1)} %out_hbm.1) | copy-start | bytes 393220
  31.9 5.2 %collective-permute-start.12 = (bf16[4,16,1024]{2,1,0:T(8,128)(2,1)S(1)}, bf16[4,16,1024]{2,1,0:T(8,128)(2,1)S(1)}, u32[]{:S(2)}, u32[]{:S(2)}) collective-permute-start(bf16[4,16,1024]{2,1,0:T(8,128)(2,1)S(1)} %fusion.1), channel_id=1, source_target_pairs={{0,16},{16,0},{1,17},{17,1},{2,18},{18,2},{3,19},{19,3},{4,20},{20... | collective-permute-start | bytes 393224 | tf_op jit(solution)/shard_map/ppermute | solution.py:593
  33.6 3.6 %collective-permute-start.13 = (bf16[2,4,16,1024]{3,2,1,0:T(8,128)(2,1)S(1)}, bf16[2,4,16,1024]{3,2,1,0:T(8,128)(2,1)S(1)}, u32[]{:S(2)}, u32[]{:S(2)}) collective-permute-start(bf16[2,4,16,1024]{3,2,1,0:T(8,128)(2,1)S(1)} %bitcast.84), channel_id=1, source_target_pairs={{0,1},{1,0},{2,3},{3,2},{4,5},{5,4},{6,7},{7,6},{8,9},{9,8},{10,11... | collective-permute-start | bytes 786440 | tf_op jit(solution)/shard_map/ppermute | solution.py:593
  37.3 7.1 %collective-permute-start.14 = (bf16[128,1024]{1,0:T(8,128)(2,1)S(1)}, bf16[128,1024]{1,0:T(8,128)(2,1)S(1)}, u32[]{:S(2)}, u32[]{:S(2)}) collective-permute-start(bf16[128,1024]{1,0:T(8,128)(2,1)S(1)} %pad_maximum_fusion.2), channel_id=1, source_target_pairs={{0,4},{4,0},{8,12},{12,8},{1,5},{5,1},{9,13},{13,9},{2,6},{6,2},{1... | collective-permute-start | bytes 786440 | tf_op jit(solution)/shard_map/ppermute | solution.py:593
  39.0 6.1 %collective-permute-start.15 = (bf16[112,1024]{1,0:T(8,128)(2,1)S(1)}, bf16[112,1024]{1,0:T(8,128)(2,1)S(1)}, u32[]{:S(2)}, u32[]{:S(2)}) collective-permute-start(bf16[112,1024]{1,0:T(8,128)(2,1)S(1)} %slice.110), channel_id=1, source_target_pairs={{0,16},{16,0},{1,17},{17,1},{2,18},{18,2},{3,19},{19,3},{4,20},{20... | collective-permute-start | bytes 688136 | tf_op jit(solution)/shard_map/ppermute | solution.py:593
  45.1 9.6 %collective-permute-start.16 = (bf16[96,1024]{1,0:T(8,128)(2,1)S(1)}, bf16[96,1024]{1,0:T(8,128)(2,1)S(1)}, u32[]{:S(2)}, u32[]{:S(2)}) collective-permute-start(bf16[96,1024]{1,0:T(8,128)(2,1)S(1)} %pad_maximum_fusion.4), channel_id=1, source_target_pairs={{0,8},{4,12},{8,0},{12,4},{1,9},{5,13},{9,1},{13,5},{2,10},{6,14},... | collective-permute-start | bytes 589832 | tf_op jit(solution)/shard_map/ppermute | solution.py:593
  46.1 8.7 %collective-permute-start.17 = (bf16[144,1024]{1,0:T(8,128)(2,1)S(1)}, bf16[144,1024]{1,0:T(8,128)(2,1)S(1)}, u32[]{:S(2)}, u32[]{:S(2)}) collective-permute-start(bf16[144,1024]{1,0:T(8,128)(2,1)S(1)} %slice.115), channel_id=1, source_target_pairs={{0,16},{16,0},{1,17},{17,1},{2,18},{18,2},{3,19},{19,3},{4,20},{20... | collective-permute-start | bytes 884744 | tf_op jit(solution)/shard_map/ppermute | solution.py:593
  54.9 5.4 %collective-permute-start.18 = (bf16[80,1024]{1,0:T(8,128)(2,1)S(1)}, bf16[80,1024]{1,0:T(8,128)(2,1)S(1)}, u32[]{:S(2)}, u32[]{:S(2)}) collective-permute-start(bf16[80,1024]{1,0:T(8,128)(2,1)S(1)} %pad_maximum_fusion.5), channel_id=1, source_target_pairs={{0,2},{1,3},{2,0},{3,1},{4,6},{5,7},{6,4},{7,5},{8,10},{9,11},{10,... | collective-permute-start | bytes 491528 | tf_op jit(solution)/shard_map/ppermute | solution.py:593
  60.3 1.6 %collective-permute-start.19 = (bf16[2,64,1024]{2,1,0:T(8,128)(2,1)S(1)}, bf16[2,64,1024]{2,1,0:T(8,128)(2,1)S(1)}, u32[]{:S(2)}, u32[]{:S(2)}) collective-permute-start(bf16[2,64,1024]{2,1,0:T(8,128)(2,1)S(1)} %pad_maximum_fusion.3.near_ref), channel_id=1, source_target_pairs={{0,1},{1,0},{2,3},{3,2},{4,5},{5,4},{6,7},{7,6},{8,9},{9,8},{10,11... | collective-permute-start | bytes 786440 | tf_op jit(solution)/shard_map/ppermute | solution.py:593

commit v12 on v11

--- a/solution.py
+++ b/solution.py
@@ -93,7 +93,8 @@
 
     for grid, rows in ((x_grid, height + 2 * HALO), (dy_grid, height + 2 * RAD)):
         grid[rows:] = jnp.zeros((grid.shape[0] - rows,) + grid.shape[1:], floats)
-        cols = breadth + 2 * HALO
+        cols = HALO + breadth
+        grid[:rows, :HALO] = jnp.zeros((rows, HALO, D_F), floats)
         grid[:rows, cols:] = jnp.zeros((rows, grid_cols - cols, D_F), floats)
     dk_grid[...] = jnp.zeros_like(dk_grid)
     dv_grid[...] = jnp.zeros_like(dv_grid)
@@ -106,20 +107,18 @@
     dy_grid[0:RAD, inner] = above[HALO : HALO + RAD]
     dy_grid[RAD : RAD + height, inner] = dy_ref[...].astype(floats)
     dy_grid[RAD + height : RAD + height + RAD, inner] = below[HALO : HALO + RAD]
-    left, right = left[:, left.shape[1] - HALO :], right[:, :HALO]
-    for strip, first in ((left, 0), (right, HALO + breadth)):
-        span = slice(first, first + HALO)
+    for strip, x_first, dy_first in (
+        (left, 0, RAD),
+        (right, HALO + breadth, HALO + breadth),
+    ):
         at = 0
-        for grid, begin, count in (
-            (x_grid, 0, HALO),
-            (dy_grid, 0, RAD),
-            (x_grid, HALO, height),
-            (dy_grid, RAD, height),
-            (x_grid, HALO + height, HALO),
-            (dy_grid, RAD + height, RAD),
+        for grid, first, width, rows in (
+            (x_grid, x_first, HALO, height + 2 * HALO),
+            (dy_grid, dy_first, RAD, height + 2 * RAD),
         ):
-            grid[begin : begin + count, span] = strip[at : at + count]
-            at += count
+            for row in range(rows):
+                grid[row, first : first + width] = strip[at : at + width]
+                at += width
 
     tokens = x_grid[...].reshape(grid_rows * grid_cols, D_F)
     normed = (tokens * inverse_rms(tokens) * factor).astype(jnp.bfloat16)
@@ -419,28 +418,36 @@
     )(picture[:HALO], picture[height - HALO :], cotangent[:RAD], cotangent[height - RAD :])
 
 
-def col_edges_body(x_ref, dy_ref, row_far_ref, row_near_ref, near_ref, far_ref):
+def col_edges_body(x_ref, dy_ref, row_far_ref, row_near_ref, near_ref, far_ref, *scratch):
     above, below = in_order("gy", row_near_ref, row_far_ref)
     breadth = x_ref.shape[1]
     odd = odd_rank("gx")
+    x_rows = jnp.concatenate([above[:HALO], x_ref[...].astype(jnp.float32), below[:HALO]], axis=0)
+    dy_rows = jnp.concatenate([above[HALO:], dy_ref[...].astype(jnp.float32), below[HALO:]], axis=0)
     at = 0
-    for rows in (above, x_ref[...].astype(jnp.float32), dy_ref[...].astype(jnp.float32), below):
-        first, final = rows[:, :side], rows[:, breadth - side :]
-        span = slice(at, at + rows.shape[0])
-        near_ref[span] = jnp.where(odd, first, final).astype(jnp.bfloat16)
-        far_ref[span] = jnp.where(odd, final, first).astype(jnp.bfloat16)
-        at += rows.shape[0]
+    for rows, width in ((x_rows, HALO), (dy_rows, RAD)):
+        for row in range(rows.shape[0]):
+            first, final = rows[row, :width], rows[row, breadth - width :]
+            scratch[0][at : at + width] = jnp.where(odd, first, final)
+            scratch[1][at : at + width] = jnp.where(odd, final, first)
+            at += width
+    pad = jnp.zeros((scratch[0].shape[0] - at, D_F), jnp.float32)
+    for held, target in zip(scratch, (near_ref, far_ref)):
+        held[at:] = pad
+        target[...] = held[...].astype(jnp.bfloat16)
 
 
 def col_edges(picture, cotangent, row_far, row_near):
     vmem = pl.BlockSpec(memory_space=pltpu.VMEM)
-    rows = 2 * (picture.shape[0] + row_near.shape[0])
-    shape = jax.ShapeDtypeStruct((rows, side, D_F), jnp.bfloat16)
+    height = picture.shape[0]
+    rows = round_up((height + 2 * HALO) * HALO + (height + 2 * RAD) * RAD, 16)
+    shape = jax.ShapeDtypeStruct((rows, D_F), jnp.bfloat16)
     return pl.pallas_call(
         col_edges_body,
         out_shape=(shape, shape),
         in_specs=[vmem] * 4,
         out_specs=(vmem, vmem),
+        scratch_shapes=[pltpu.VMEM((rows, D_F), jnp.float32)] * 2,
         compiler_params=pltpu.CompilerParams(vmem_limit_bytes=vmem_bytes),
         name="col_edges",
     )(picture, cotangent, row_far, row_near)
@@ -661,6 +668,7 @@
     )
     fine_half = fine_keep + wide(swapped(fine_send, "gx", 1))
     opposite = swapped(cross, "gx", 1)
+    fine_half, opposite = tied(fine_half, opposite)
 
     fine_quarter = narrow(fine_half[0] + wide(swapped(narrow(fine_half[1]), "gx", 2)))
     everyone = jnp.stack([row_group, cross, beside, opposite]).reshape(-1, 2 * D_C)

time: 62.9 us -> 63.3 us (level)
  waiting for transfers between devices: 21.2 us -> 22.7 us
  starting transfers between devices: 27.3 us -> 26.1 us
    ppermute x16, waiting for transfers between devices: 21.2 us -> 22.7 us  [swapped(): lax.ppermute(value, axis, [(i, i ^ mask) for i in range(lax.axis_size(axi...]
    ppermute x16, starting transfers between devices: 17 us -> 15.8 us  [swapped(): lax.ppermute(value, axis, [(i, i ^ mask) for i in range(lax.axis_size(axi...]
  transfers between devices with their start and end apart: 20 -> 20, of which waited for: 8 -> 9; matrix products, arithmetic and copies ran while one was open for 1% -> 1% of each run, Pallas kernels for 14% -> 14%
where the time goes in v12:
time: 63.3 us; the launch traced here: 63.1 us
  starting transfers between devices  26.1 us (41%)
  waiting for transfers between devices  22.7 us (36%)
  Pallas kernels  9.83 us (16%)
  local copies, waits for them, and re-layouts  2.21 us (3%)
  between operations  1.72 us (3%)
    ppermute x16, waiting for transfers between devices, swapped(): lax.ppermute(value, axis, [(i, i ^ mask) for i in range(lax.axis_size(axi...  22.7 us
    ppermute x16, starting transfers between devices, swapped(): lax.ppermute(value, axis, [(i, i ^ mask) for i in range(lax.axis_size(axi...  15.8 us
    ppermute x2, starting transfers between devices, neighbours(): return (lax.ppermute(to_near, axis, near), from_far)  8.82 us
    pallas_call x1, Pallas kernels, fine_block(): pl.pallas_call(fine_body, out_shape=(jax.ShapeDtypeStruct((height, breadt...  4.37 us
    pallas_call x1, Pallas kernels, coarse_block(): pl.pallas_call(coarse_body, out_shape=(jax.ShapeDtypeStruct((count, D_C),...  2.23 us
    ppermute x2, starting transfers between devices, neighbours(): from_far = lax.ppermute(to_far, axis, far)  1.47 us
    pallas_call x1, Pallas kernels, near_step(): pl.pallas_call(near_body, out_shape=(jax.ShapeDtypeStruct((D_F, 3 * D_F),...  1.36 us
  transfers between devices with their start and end apart: 20, of which 9 were waited for; matrix products, arithmetic and copies ran while one was open for 1% of the time, Pallas kernels for 14%

profile of v12, /device:TPU:0, one launch (start us, length us, event | category | flops | bytes accessed | tf_op | source)
XLA Modules:
  0.0 63.1 jit_solution(4007074716211910529)
XLA Ops:
  0.6 1.0 %slice_bitcast_fusion.2 = (bf16[6,32,256]{2,1,0:T(8,128)(2,1)S(1)}, bf16[6,32,256]{2,1,0:T(8,128)(2,1)S(1)}) fusion(bf16[1,8,32,256]{3,2,1,0:T(8,128)(2,1)} %param.13), kind=kLoop, calls=%fused_computation.22 | loop fusion | bytes 393216 | tf_op jit(solution)/shard_map/slice | solution.py:418
  1.7 0.0 copy-start.5
  1.7 0.0 copy-start.7
  1.7 0.7 %collective-permute-start = (bf16[9,32,256]{2,1,0:T(8,128)(2,1)S(1)}, bf16[9,32,256]{2,1,0:T(8,128)(2,1)S(1)}, u32[]{:S(2)}, u32[]{:S(2)}) collective-permute-start(bf16[9,32,256]{2,1,0:T(8,128)(2,1)S(1)} %get-tuple-element.57.second), channel_id=1, source_target_pairs={{4,8},{8,4},{5,9},{9,5},{6,10},{10,6},{7,11},{11,7},{20,24},{24,20... | collective-permute-start | bytes 442376 | tf_op jit(solution)/shard_map/ppermute | solution.py:595
  2.4 5.9 %collective-permute-start.1 = (bf16[9,32,256]{2,1,0:T(8,128)(2,1)S(1)}, bf16[9,32,256]{2,1,0:T(8,128)(2,1)S(1)}, u32[]{:S(2)}, u32[]{:S(2)}) collective-permute-start(bf16[9,32,256]{2,1,0:T(8,128)(2,1)S(1)} %get-tuple-element.58.first), channel_id=1, source_target_pairs={{0,4},{4,0},{8,12},{12,8},{1,5},{5,1},{9,13},{13,9},{2,6},{6,2},{1... | collective-permute-start | bytes 442376 | tf_op jit(solution)/shard_map/ppermute | solution.py:596
  8.3 0.1 collective-permute-start.4
  8.4 1.9 %collective-permute-start.5 = (bf16[16,2048]{1,0:T(8,128)(2,1)S(1)}, bf16[16,2048]{1,0:T(8,128)(2,1)S(1)}, u32[]{:S(2)}, u32[]{:S(2)}) collective-permute-start(bf16[16,2048]{1,0:T(8,128)(2,1)S(1)} %pack_coarse.1), channel_id=1, source_target_pairs={{0,8},{4,12},{8,0},{12,4},{1,9},{5,13},{9,1},{13,5},{2,10},{6,14},... | collective-permute-start | bytes 196616 | tf_op jit(solution)/shard_map/ppermute | solution.py:600
  10.3 2.5 %collective-permute-start.6 = (bf16[16,2048]{1,0:T(8,128)(2,1)S(1)}, bf16[16,2048]{1,0:T(8,128)(2,1)S(1)}, u32[]{:S(2)}, u32[]{:S(2)}) collective-permute-start(bf16[16,2048]{1,0:T(8,128)(2,1)S(1)} %pack_coarse.1), channel_id=1, source_target_pairs={{0,12},{4,8},{8,4},{12,0},{1,13},{5,9},{9,5},{13,1},{2,14},{6,10},... | collective-permute-start | bytes 196616 | tf_op jit(solution)/shard_map/ppermute | solution.py:600
  13.4 0.0 collective-permute-done.row_far_ref
  13.5 0.0 collective-permute-done.1.row_near_ref
  13.5 0.0 copy-start.8
  13.5 0.0 copy-start.9
  13.5 0.0 copy-start.10
  13.5 0.0 copy-start.11
  13.5 0.1 col_edges.1
  13.7 0.0 copy-start.2
  13.7 0.8 %collective-permute-start.2 = (bf16[176,256]{1,0:T(8,128)(2,1)S(1)}, bf16[176,256]{1,0:T(8,128)(2,1)S(1)}, u32[]{:S(2)}, u32[]{:S(2)}) collective-permute-start(bf16[176,256]{1,0:T(8,128)(2,1)S(1)} %get-tuple-element.61), channel_id=1, source_target_pairs={{1,2},{2,1},{5,6},{6,5},{9,10},{10,9},{13,14},{14,13},{17,18},{18,... | collective-permute-start | bytes 270344 | tf_op jit(solution)/shard_map/ppermute | solution.py:595
  14.5 2.9 %collective-permute-start.3 = (bf16[176,256]{1,0:T(8,128)(2,1)S(1)}, bf16[176,256]{1,0:T(8,128)(2,1)S(1)}, u32[]{:S(2)}, u32[]{:S(2)}) collective-permute-start(bf16[176,256]{1,0:T(8,128)(2,1)S(1)} %get-tuple-element.62), channel_id=1, source_target_pairs={{0,1},{1,0},{2,3},{3,2},{4,5},{5,4},{6,7},{7,6},{8,9},{9,8},{10,11... | collective-permute-start | bytes 270344 | tf_op jit(solution)/shard_map/ppermute | solution.py:596
  17.4 0.1 time_factors.1
  17.5 0.0 collective-permute-done.4
  17.5 0.0 collective-permute-done.5
  17.5 0.0 collective-permute-done.6
  17.5 0.0 copy-start.6
  17.6 1.3 %collective-permute-start.8 = (bf16[4,16,2048]{2,1,0:T(8,128)(2,1)S(1)}, bf16[4,16,2048]{2,1,0:T(8,128)(2,1)S(1)}, u32[]{:S(2)}, u32[]{:S(2)}) collective-permute-start(bf16[4,16,2048]{2,1,0:T(8,128)(2,1)S(1)} %pad_maximum_fusion.1), channel_id=1, source_target_pairs={{0,2},{1,3},{2,0},{3,1},{4,6},{5,7},{6,4},{7,5},{8,10},{9,11},{10,... | collective-permute-start | bytes 786440 | tf_op jit(solution)/shard_map/ppermute | solution.py:600
  18.9 0.0 collective-permute-done.2.col_far_ref
  18.9 0.0 collective-permute-done.3.col_near_ref
  18.9 4.4 %fine_block.1 = (bf16[8,32,256]{2,1,0:T(8,128)(2,1)}, f32[2,4,16,1024]{3,2,1,0:T(8,128)S(1)}, bf16[2,4,16,1024]{3,2,1,0:T(8,128)(2,1)S(1)}) custom-call(bf16[8,32,256]{2,1,0:T(8,128)(2,1)S(1)} %bitcast.59, bf16[8,32,256]{2,1,0:T(8,128)(2,1)S(1)} %bitcast.61, bf16[9,32,256]{2,1,0:T(8,128)(2,1)S(1)} %collective-permute-done.row_far_ref, ...), custom_call_target="tpu_custom_call" | custom-call | tf_op jit(solution)/shard_map/fine_block/pallas_call | solution.py:296
  23.3 0.7 %collective-permute-start.7 = (bf16[2,4,16,1024]{3,2,1,0:T(8,128)(2,1)S(1)}, bf16[2,4,16,1024]{3,2,1,0:T(8,128)(2,1)S(1)}, u32[]{:S(2)}, u32[]{:S(2)}) collective-permute-start(bf16[2,4,16,1024]{3,2,1,0:T(8,128)(2,1)S(1)} %get-tuple-element.76), channel_id=1, source_target_pairs={{0,1},{1,0},{2,3},{3,2},{4,5},{5,4},{6,7},{7,6},{8,9},{9,8},{10,11... | collective-permute-start | bytes 786440 | tf_op jit(solution)/shard_map/ppermute | solution.py:600
  23.9 2.0 %collective-permute-done.8 = bf16[4,16,2048]{2,1,0:T(8,128)(2,1)S(1)} collective-permute-done((bf16[4,16,2048]{2,1,0:T(8,128)(2,1)S(1)}, bf16[4,16,2048]{2,1,0:T(8,128)(2,1)S(1)}, u32[]{:S(2)}, u32[]{:S(2)}) %collective-permute-start.8) | collective-permute-done | bytes 262176 | tf_op jit(solution)/shard_map/ppermute | solution.py:600
  25.9 0.0 collective-permute-start.9
  25.9 0.5 collective-permute-start.11
  26.4 0.0 collective-permute-done.7
  26.4 0.1 convert_add_fusion.1
  26.5 1.0 %collective-permute-done.9 = bf16[4,16,2048]{2,1,0:T(8,128)(2,1)S(1)} collective-permute-done((bf16[4,16,2048]{2,1,0:T(8,128)(2,1)S(1)}, bf16[4,16,2048]{2,1,0:T(8,128)(2,1)S(1)}, u32[]{:S(2)}, u32[]{:S(2)}) %collective-permute-start.9) | collective-permute-done | bytes 262176 | tf_op jit(solution)/shard_map/ppermute | solution.py:600
  27.4 1.0 %collective-permute-start.10 = (bf16[4,16,1024]{2,1,0:T(8,128)(2,1)S(1)}, bf16[4,16,1024]{2,1,0:T(8,128)(2,1)S(1)}, u32[]{:S(2)}, u32[]{:S(2)}) collective-permute-start(bf16[4,16,1024]{2,1,0:T(8,128)(2,1)S(1)} %fusion.2), channel_id=1, source_target_pairs={{0,2},{1,3},{2,0},{3,1},{4,6},{5,7},{6,4},{7,5},{8,10},{9,11},{10,... | collective-permute-start | bytes 393224 | tf_op jit(solution)/shard_map/ppermute | solution.py:600
  28.4 0.0 collective-permute-done.11
  28.4 0.1 pad_maximum_fusion
  28.5 0.0 copy-start.3
  28.5 0.0 copy-start.4
  28.6 0.1 fusion.5
  28.6 0.9 %copy-done.3 = bf16[3,64,1024]{2,1,0:T(8,128)(2,1)S(1)} copy-done((bf16[3,64,1024]{2,1,0:T(8,128)(2,1)S(1)}, bf16[3,64,1024]{2,1,0:T(8,128)(2,1)}, u32[]{:S(2)}) %copy-start.3) | copy-done | bytes 393240
  29.5 0.0 copy-done.4
  29.6 2.2 %coarse_block.1 = (bf16[256,1024]{1,0:T(8,128)(2,1)S(1)}, bf16[256,1024]{1,0:T(8,128)(2,1)S(1)}) custom-call(bf16[256,1024]{1,0:T(8,128)(2,1)S(1)} %get-tuple-element.109.x_ref, bf16[256,1024]{1,0:T(8,128)(2,1)S(1)} %get-tuple-element.108.dy_ref, f32[1,1024]{1,0:T(1,128)S(1)} %get-tuple-element.80.factor_ref, bf16[3,64,1024]{2,1,0:T(8,128)(2,1)S(1)} %copy-done.3, ...), custom_call_target="tpu_custom_call" | custom-call | tf_op jit(solution)/shard_map/coarse_block/pallas_call | solution.py:373
  31.8 1.2 %collective-permute-done.10 = bf16[4,16,1024]{2,1,0:T(8,128)(2,1)S(1)} collective-permute-done((bf16[4,16,1024]{2,1,0:T(8,128)(2,1)S(1)}, bf16[4,16,1024]{2,1,0:T(8,128)(2,1)S(1)}, u32[]{:S(2)}, u32[]{:S(2)}) %collective-permute-start.10) | collective-permute-done | bytes 131104 | tf_op jit(solution)/shard_map/ppermute | solution.py:600
  33.1 1.6 %collective-permute-start.12 = (bf16[4,16,1024]{2,1,0:T(8,128)(2,1)S(1)}, bf16[4,16,1024]{2,1,0:T(8,128)(2,1)S(1)}, u32[]{:S(2)}, u32[]{:S(2)}) collective-permute-start(bf16[4,16,1024]{2,1,0:T(8,128)(2,1)S(1)} %fusion.1), channel_id=1, source_target_pairs={{0,16},{16,0},{1,17},{17,1},{2,18},{18,2},{3,19},{19,3},{4,20},{20... | collective-permute-start | bytes 393224 | tf_op jit(solution)/shard_map/ppermute | solution.py:600
  34.7 0.1 collective-permute-start.13
  34.8 3.3 %collective-permute-done.12 = bf16[4,16,1024]{2,1,0:T(8,128)(2,1)S(1)} collective-permute-done((bf16[4,16,1024]{2,1,0:T(8,128)(2,1)S(1)}, bf16[4,16,1024]{2,1,0:T(8,128)(2,1)S(1)}, u32[]{:S(2)}, u32[]{:S(2)}) %collective-permute-start.12) | collective-permute-done | bytes 131104 | tf_op jit(solution)/shard_map/ppermute | solution.py:600
  38.1 0.0 collective-permute-done.13
  38.2 0.1 convert_add_fusion
  38.3 1.7 %collective-permute-start.14 = (bf16[128,1024]{1,0:T(8,128)(2,1)S(1)}, bf16[128,1024]{1,0:T(8,128)(2,1)S(1)}, u32[]{:S(2)}, u32[]{:S(2)}) collective-permute-start(bf16[128,1024]{1,0:T(8,128)(2,1)S(1)} %pad_maximum_fusion.2), channel_id=1, source_target_pairs={{0,4},{4,0},{8,12},{12,8},{1,5},{5,1},{9,13},{13,9},{2,6},{6,2},{1... | collective-permute-start | bytes 786440 | tf_op jit(solution)/shard_map/ppermute | solution.py:600
  39.9 1.6 %collective-permute-start.15 = (bf16[112,1024]{1,0:T(8,128)(2,1)S(1)}, bf16[112,1024]{1,0:T(8,128)(2,1)S(1)}, u32[]{:S(2)}, u32[]{:S(2)}) collective-permute-start(bf16[112,1024]{1,0:T(8,128)(2,1)S(1)} %slice.110), channel_id=1, source_target_pairs={{0,16},{16,0},{1,17},{17,1},{2,18},{18,2},{3,19},{19,3},{4,20},{20... | collective-permute-start | bytes 688136 | tf_op jit(solution)/shard_map/ppermute | solution.py:600
  41.5 3.3 %collective-permute-done.14 = bf16[128,1024]{1,0:T(8,128)(2,1)S(1)} collective-permute-done((bf16[128,1024]{1,0:T(8,128)(2,1)S(1)}, bf16[128,1024]{1,0:T(8,128)(2,1)S(1)}, u32[]{:S(2)}, u32[]{:S(2)}) %collective-permute-start.14) | collective-permute-done | bytes 262176 | tf_op jit(solution)/shard_map/ppermute | solution.py:600
  44.9 1.1 %collective-permute-done.15.refs_0_ = bf16[112,1024]{1,0:T(8,128)(2,1)S(1)} collective-permute-done((bf16[112,1024]{1,0:T(8,128)(2,1)S(1)}, bf16[112,1024]{1,0:T(8,128)(2,1)S(1)}, u32[]{:S(2)}, u32[]{:S(2)}) %collective-permute-start.15) | collective-permute-done | bytes 229408 | tf_op jit(solution)/shard_map/ppermute | solution.py:600
  46.1 0.4 collective-permute-start.16
  46.5 1.5 %collective-permute-start.17 = (bf16[144,1024]{1,0:T(8,128)(2,1)S(1)}, bf16[144,1024]{1,0:T(8,128)(2,1)S(1)}, u32[]{:S(2)}, u32[]{:S(2)}) collective-permute-start(bf16[144,1024]{1,0:T(8,128)(2,1)S(1)} %slice.115), channel_id=1, source_target_pairs={{0,16},{16,0},{1,17},{17,1},{2,18},{18,2},{3,19},{19,3},{4,20},{20... | collective-permute-start | bytes 884744 | tf_op jit(solution)/shard_map/ppermute | solution.py:600
  48.1 7.1 %collective-permute-done.16 = bf16[96,1024]{1,0:T(8,128)(2,1)S(1)} collective-permute-done((bf16[96,1024]{1,0:T(8,128)(2,1)S(1)}, bf16[96,1024]{1,0:T(8,128)(2,1)S(1)}, u32[]{:S(2)}, u32[]{:S(2)}) %collective-permute-start.16) | collective-permute-done | bytes 196640 | tf_op jit(solution)/shard_map/ppermute | solution.py:600
  55.3 0.0 collective-permute-done.17.refs_1_
  55.3 1.0 %collective-permute-start.18 = (bf16[80,1024]{1,0:T(8,128)(2,1)S(1)}, bf16[80,1024]{1,0:T(8,128)(2,1)S(1)}, u32[]{:S(2)}, u32[]{:S(2)}) collective-permute-start(bf16[80,1024]{1,0:T(8,128)(2,1)S(1)} %pad_maximum_fusion.5), channel_id=1, source_target_pairs={{0,2},{1,3},{2,0},{3,1},{4,6},{5,7},{6,4},{7,5},{8,10},{9,11},{10,... | collective-permute-start | bytes 491528 | tf_op jit(solution)/shard_map/ppermute | solution.py:600
  56.3 0.9 %pair_sum.1 = (bf16[3,64,1024]{2,1,0:T(8,128)(2,1)}, bf16[64,1024]{1,0:T(8,128)(2,1)}) custom-call(bf16[256,1024]{1,0:T(8,128)(2,1)S(1)} %get-tuple-element.88.own, bf16[112,1024]{1,0:T(8,128)(2,1)S(1)} %collective-permute-done.15.refs_0_, bf16[144,1024]{1,0:T(8,128)(2,1)S(1)} %collective-permute-done.17.refs_1_), custom_call_target="tpu_custom_call" | custom-call | tf_op jit(solution)/shard_map/pair_sum/pallas_call | solution.py:509
  57.2 3.5 %collective-permute-done.18 = bf16[80,1024]{1,0:T(8,128)(2,1)S(1)} collective-permute-done((bf16[80,1024]{1,0:T(8,128)(2,1)S(1)}, bf16[80,1024]{1,0:T(8,128)(2,1)S(1)}, u32[]{:S(2)}, u32[]{:S(2)}) %collective-permute-start.18) | collective-permute-done | bytes 163872 | tf_op jit(solution)/shard_map/ppermute | solution.py:600
  60.7 0.1 collective-permute-start.19
  60.8 1.4 %near_step.1 = (bf16[256,768]{1,0:T(8,128)(2,1)}, bf16[256,256]{1,0:T(8,128)(2,1)}, bf16[4,4,1024]{2,1,0:T(4,128)(2,1)}) custom-call(bf16[2,64,1024]{2,1,0:T(8,128)(2,1)S(1)} %pad_maximum_fusion.3.near_ref, bf16[4,4,1024]{2,1,0:T(4,128)(2,1)S(1)} %bitcast.64, f32[1,1024]{1,0:T(1,128)S(1)} %get-tuple-element.80.factor_ref, ...), custom_call_target="tpu_custom_call" | custom-call | tf_op jit(solution)/shard_map/near_step/pallas_call | solution.py:558
  62.2 0.1 collective-permute-done.19.far_ref
  62.3 0.7 %far_step.1 = (bf16[256,768]{1,0:T(8,128)(2,1)}, bf16[256,256]{1,0:T(8,128)(2,1)}) custom-call(bf16[2,64,1024]{2,1,0:T(8,128)(2,1)S(1)} %collective-permute-done.19.far_ref, bf16[256,768]{1,0:T(8,128)(2,1)} %get-tuple-element.102.qkv_in, bf16[256,256]{1,0:T(8,128)(2,1)} %get-tuple-element.103.out_in), custom_call_target="tpu_custom_call", output_to_operand_aliasing={{0}: (1, {}), {1}: (2, {})} | custom-call | tf_op jit(solution)/shard_map/far_step/pallas_call | solution.py:576
  (38 shorter events, 0.5 us)
Async XLA Ops:
  0.6 1.0 %copy-start.1 = (bf16[1,8,32,256]{3,2,1,0:T(8,128)(2,1)S(1)}, bf16[1,8,32,256]{3,2,1,0:T(8,128)(2,1)}, u32[]{:S(2)}) copy-start(bf16[1,8,32,256]{3,2,1,0:T(8,128)(2,1)} %param.14) | copy-start | bytes 393220
  1.7 6.7 %copy-start.5 = (bf16[1,4,4,1024]{3,2,1,0:T(4,128)(2,1)S(1)}, bf16[1,4,4,1024]{3,2,1,0:T(4,128)(2,1)}, u32[]{:S(2)}) copy-start(bf16[1,4,4,1024]{3,2,1,0:T(4,128)(2,1)} %param.15) | copy-start | bytes 98308
  1.7 6.6 %copy-start.7 = (bf16[1,4,4,1024]{3,2,1,0:T(4,128)(2,1)S(1)}, bf16[1,4,4,1024]{3,2,1,0:T(4,128)(2,1)}, u32[]{:S(2)}) copy-start(bf16[1,4,4,1024]{3,2,1,0:T(4,128)(2,1)} %param.16) | copy-start | bytes 98308
  1.7 11.7 %collective-permute-start = (bf16[9,32,256]{2,1,0:T(8,128)(2,1)S(1)}, bf16[9,32,256]{2,1,0:T(8,128)(2,1)S(1)}, u32[]{:S(2)}, u32[]{:S(2)}) collective-permute-start(bf16[9,32,256]{2,1,0:T(8,128)(2,1)S(1)} %get-tuple-element.57.second), channel_id=1, source_target_pairs={{4,8},{8,4},{5,9},{9,5},{6,10},{10,6},{7,11},{11,7},{20,24},{24,20... | collective-permute-start | bytes 442376 | tf_op jit(solution)/shard_map/ppermute | solution.py:595
  2.4 11.0 %collective-permute-start.1 = (bf16[9,32,256]{2,1,0:T(8,128)(2,1)S(1)}, bf16[9,32,256]{2,1,0:T(8,128)(2,1)S(1)}, u32[]{:S(2)}, u32[]{:S(2)}) collective-permute-start(bf16[9,32,256]{2,1,0:T(8,128)(2,1)S(1)} %get-tuple-element.58.first), channel_id=1, source_target_pairs={{0,4},{4,0},{8,12},{12,8},{1,5},{5,1},{9,13},{13,9},{2,6},{6,2},{1... | collective-permute-start | bytes 442376 | tf_op jit(solution)/shard_map/ppermute | solution.py:596
  8.3 5.1 %copy-start = (bf16[1,8,32,256]{3,2,1,0:T(8,128)(2,1)S(1)}, bf16[1,8,32,256]{3,2,1,0:T(8,128)(2,1)}, u32[]{:S(2)}) copy-start(bf16[1,8,32,256]{3,2,1,0:T(8,128)(2,1)} %param.13) | copy-start | bytes 393220
  8.3 9.1 %collective-permute-start.4 = (bf16[16,2048]{1,0:T(8,128)(2,1)S(1)}, bf16[16,2048]{1,0:T(8,128)(2,1)S(1)}, u32[]{:S(2)}, u32[]{:S(2)}) collective-permute-start(bf16[16,2048]{1,0:T(8,128)(2,1)S(1)} %pack_coarse.1), channel_id=1, source_target_pairs={{0,4},{4,0},{8,12},{12,8},{1,5},{5,1},{9,13},{13,9},{2,6},{6,2},{1... | collective-permute-start | bytes 196616 | tf_op jit(solution)/shard_map/ppermute | solution.py:600
  8.4 9.0 %collective-permute-start.5 = (bf16[16,2048]{1,0:T(8,128)(2,1)S(1)}, bf16[16,2048]{1,0:T(8,128)(2,1)S(1)}, u32[]{:S(2)}, u32[]{:S(2)}) collective-permute-start(bf16[16,2048]{1,0:T(8,128)(2,1)S(1)} %pack_coarse.1), channel_id=1, source_target_pairs={{0,8},{4,12},{8,0},{12,4},{1,9},{5,13},{9,1},{13,5},{2,10},{6,14},... | collective-permute-start | bytes 196616 | tf_op jit(solution)/shard_map/ppermute | solution.py:600
  10.3 7.2 %collective-permute-start.6 = (bf16[16,2048]{1,0:T(8,128)(2,1)S(1)}, bf16[16,2048]{1,0:T(8,128)(2,1)S(1)}, u32[]{:S(2)}, u32[]{:S(2)}) collective-permute-start(bf16[16,2048]{1,0:T(8,128)(2,1)S(1)} %pack_coarse.1), channel_id=1, source_target_pairs={{0,12},{4,8},{8,4},{12,0},{1,13},{5,9},{9,5},{13,1},{2,14},{6,10},... | collective-permute-start | bytes 196616 | tf_op jit(solution)/shard_map/ppermute | solution.py:600
  13.5 3.9 %copy-start.8 = (f32[1024]{0:T(1024)S(1)}, f32[1024]{0:T(1024)}, u32[]{:S(2)}) copy-start(f32[1024]{0:T(1024)} %param.19) | copy-start | bytes 12292
  13.5 3.9 %copy-start.9 = (f32[1,1024]{1,0:T(1,128)S(1)}, f32[1,1024]{1,0:T(1,128)}, u32[]{:S(2)}) copy-start(f32[1,1024]{1,0:T(1,128)} %constant.5.clone.coarse_freq) | copy-start | bytes 12292
  13.5 3.9 %copy-start.10 = (f32[256]{0:T(256)S(1)}, f32[256]{0:T(256)}, u32[]{:S(2)}) copy-start(f32[256]{0:T(256)} %param.18) | copy-start | bytes 3076
  13.5 3.9 %copy-start.11 = (f32[1,256]{1,0:T(1,128)S(1)}, f32[1,256]{1,0:T(1,128)}, u32[]{:S(2)}) copy-start(f32[1,256]{1,0:T(1,128)} %constant.4.clone.fine_freq) | copy-start | bytes 3076
  13.7 5.2 %copy-start.2 = (bf16[256,768]{1,0:T(8,128)(2,1)S(1)}, bf16[256,768]{1,0:T(8,128)(2,1)}, u32[]{:S(2)}) copy-start(bf16[256,768]{1,0:T(8,128)(2,1)} %qkv_ref.1) | copy-start | bytes 1179652
  13.7 5.2 %collective-permute-start.2 = (bf16[176,256]{1,0:T(8,128)(2,1)S(1)}, bf16[176,256]{1,0:T(8,128)(2,1)S(1)}, u32[]{:S(2)}, u32[]{:S(2)}) collective-permute-start(bf16[176,256]{1,0:T(8,128)(2,1)S(1)} %get-tuple-element.61), channel_id=1, source_target_pairs={{1,2},{2,1},{5,6},{6,5},{9,10},{10,9},{13,14},{14,13},{17,18},{18,... | collective-permute-start | bytes 270344 | tf_op jit(solution)/shard_map/ppermute | solution.py:595
  14.5 4.4 %collective-permute-start.3 = (bf16[176,256]{1,0:T(8,128)(2,1)S(1)}, bf16[176,256]{1,0:T(8,128)(2,1)S(1)}, u32[]{:S(2)}, u32[]{:S(2)}) collective-permute-start(bf16[176,256]{1,0:T(8,128)(2,1)S(1)} %get-tuple-element.62), channel_id=1, source_target_pairs={{0,1},{1,0},{2,3},{3,2},{4,5},{5,4},{6,7},{7,6},{8,9},{9,8},{10,11... | collective-permute-start | bytes 270344 | tf_op jit(solution)/shard_map/ppermute | solution.py:596
  17.5 1.4 %copy-start.6 = (bf16[256,256]{1,0:T(8,128)(2,1)S(1)}, bf16[256,256]{1,0:T(8,128)(2,1)}, u32[]{:S(2)}) copy-start(bf16[256,256]{1,0:T(8,128)(2,1)} %out_ref.1) | copy-start | bytes 393220
  17.6 8.3 %collective-permute-start.8 = (bf16[4,16,2048]{2,1,0:T(8,128)(2,1)S(1)}, bf16[4,16,2048]{2,1,0:T(8,128)(2,1)S(1)}, u32[]{:S(2)}, u32[]{:S(2)}) collective-permute-start(bf16[4,16,2048]{2,1,0:T(8,128)(2,1)S(1)} %pad_maximum_fusion.1), channel_id=1, source_target_pairs={{0,2},{1,3},{2,0},{3,1},{4,6},{5,7},{6,4},{7,5},{8,10},{9,11},{10,... | collective-permute-start | bytes 786440 | tf_op jit(solution)/shard_map/ppermute | solution.py:600
  23.3 3.1 %collective-permute-start.7 = (bf16[2,4,16,1024]{3,2,1,0:T(8,128)(2,1)S(1)}, bf16[2,4,16,1024]{3,2,1,0:T(8,128)(2,1)S(1)}, u32[]{:S(2)}, u32[]{:S(2)}) collective-permute-start(bf16[2,4,16,1024]{3,2,1,0:T(8,128)(2,1)S(1)} %get-tuple-element.76), channel_id=1, source_target_pairs={{0,1},{1,0},{2,3},{3,2},{4,5},{5,4},{6,7},{7,6},{8,9},{9,8},{10,11... | collective-permute-start | bytes 786440 | tf_op jit(solution)/shard_map/ppermute | solution.py:600
  25.9 1.5 %collective-permute-start.9 = (bf16[4,16,2048]{2,1,0:T(8,128)(2,1)S(1)}, bf16[4,16,2048]{2,1,0:T(8,128)(2,1)S(1)}, u32[]{:S(2)}, u32[]{:S(2)}) collective-permute-start(bf16[4,16,2048]{2,1,0:T(8,128)(2,1)S(1)} %collective-permute-done.8), channel_id=1, source_target_pairs={{0,1},{1,0},{2,3},{3,2},{4,5},{5,4},{6,7},{7,6},{8,9},{9,8},{10,11... | collective-permute-start | bytes 786440 | tf_op jit(solution)/shard_map/ppermute | solution.py:600
  25.9 2.5 %collective-permute-start.11 = (bf16[4,16,2048]{2,1,0:T(8,128)(2,1)S(1)}, bf16[4,16,2048]{2,1,0:T(8,128)(2,1)S(1)}, u32[]{:S(2)}, u32[]{:S(2)}) collective-permute-start(bf16[4,16,2048]{2,1,0:T(8,128)(2,1)S(1)} %pad_maximum_fusion.1), channel_id=1, source_target_pairs={{0,1},{1,0},{2,3},{3,2},{4,5},{5,4},{6,7},{7,6},{8,9},{9,8},{10,11... | collective-permute-start | bytes 786440 | tf_op jit(solution)/shard_map/ppermute | solution.py:600
  27.4 5.6 %collective-permute-start.10 = (bf16[4,16,1024]{2,1,0:T(8,128)(2,1)S(1)}, bf16[4,16,1024]{2,1,0:T(8,128)(2,1)S(1)}, u32[]{:S(2)}, u32[]{:S(2)}) collective-permute-start(bf16[4,16,1024]{2,1,0:T(8,128)(2,1)S(1)} %fusion.2), channel_id=1, source_target_pairs={{0,2},{1,3},{2,0},{3,1},{4,6},{5,7},{6,4},{7,5},{8,10},{9,11},{10,... | collective-permute-start | bytes 393224 | tf_op jit(solution)/shard_map/ppermute | solution.py:600
  28.5 1.0 %copy-start.3 = (bf16[3,64,1024]{2,1,0:T(8,128)(2,1)S(1)}, bf16[3,64,1024]{2,1,0:T(8,128)(2,1)}, u32[]{:S(2)}) copy-start(bf16[3,64,1024]{2,1,0:T(8,128)(2,1)} %qkv_hbm.1) | copy-start | bytes 1179652
  28.5 1.0 %copy-start.4 = (bf16[64,1024]{1,0:T(8,128)(2,1)S(1)}, bf16[64,1024]{1,0:T(8,128)(2,1)}, u32[]{:S(2)}) copy-start(bf16[64,1024]{1,0:T(8,128)(2,1)} %out_hbm.1) | copy-start | bytes 393220
  33.1 5.0 %collective-permute-start.12 = (bf16[4,16,1024]{2,1,0:T(8,128)(2,1)S(1)}, bf16[4,16,1024]{2,1,0:T(8,128)(2,1)S(1)}, u32[]{:S(2)}, u32[]{:S(2)}) collective-permute-start(bf16[4,16,1024]{2,1,0:T(8,128)(2,1)S(1)} %fusion.1), channel_id=1, source_target_pairs={{0,16},{16,0},{1,17},{17,1},{2,18},{18,2},{3,19},{19,3},{4,20},{20... | collective-permute-start | bytes 393224 | tf_op jit(solution)/shard_map/ppermute | solution.py:600
  34.7 3.5 %collective-permute-start.13 = (bf16[2,4,16,1024]{3,2,1,0:T(8,128)(2,1)S(1)}, bf16[2,4,16,1024]{3,2,1,0:T(8,128)(2,1)S(1)}, u32[]{:S(2)}, u32[]{:S(2)}) collective-permute-start(bf16[2,4,16,1024]{3,2,1,0:T(8,128)(2,1)S(1)} %bitcast.82), channel_id=1, source_target_pairs={{0,1},{1,0},{2,3},{3,2},{4,5},{5,4},{6,7},{7,6},{8,9},{9,8},{10,11... | collective-permute-start | bytes 786440 | tf_op jit(solution)/shard_map/ppermute | solution.py:600
  38.3 6.5 %collective-permute-start.14 = (bf16[128,1024]{1,0:T(8,128)(2,1)S(1)}, bf16[128,1024]{1,0:T(8,128)(2,1)S(1)}, u32[]{:S(2)}, u32[]{:S(2)}) collective-permute-start(bf16[128,1024]{1,0:T(8,128)(2,1)S(1)} %pad_maximum_fusion.2), channel_id=1, source_target_pairs={{0,4},{4,0},{8,12},{12,8},{1,5},{5,1},{9,13},{13,9},{2,6},{6,2},{1... | collective-permute-start | bytes 786440 | tf_op jit(solution)/shard_map/ppermute | solution.py:600
  39.9 6.1 %collective-permute-start.15 = (bf16[112,1024]{1,0:T(8,128)(2,1)S(1)}, bf16[112,1024]{1,0:T(8,128)(2,1)S(1)}, u32[]{:S(2)}, u32[]{:S(2)}) collective-permute-start(bf16[112,1024]{1,0:T(8,128)(2,1)S(1)} %slice.110), channel_id=1, source_target_pairs={{0,16},{16,0},{1,17},{17,1},{2,18},{18,2},{3,19},{19,3},{4,20},{20... | collective-permute-start | bytes 688136 | tf_op jit(solution)/shard_map/ppermute | solution.py:600
  46.1 9.1 %collective-permute-start.16 = (bf16[96,1024]{1,0:T(8,128)(2,1)S(1)}, bf16[96,1024]{1,0:T(8,128)(2,1)S(1)}, u32[]{:S(2)}, u32[]{:S(2)}) collective-permute-start(bf16[96,1024]{1,0:T(8,128)(2,1)S(1)} %pad_maximum_fusion.4), channel_id=1, source_target_pairs={{0,8},{4,12},{8,0},{12,4},{1,9},{5,13},{9,1},{13,5},{2,10},{6,14},... | collective-permute-start | bytes 589832 | tf_op jit(solution)/shard_map/ppermute | solution.py:600
  46.5 8.7 %collective-permute-start.17 = (bf16[144,1024]{1,0:T(8,128)(2,1)S(1)}, bf16[144,1024]{1,0:T(8,128)(2,1)S(1)}, u32[]{:S(2)}, u32[]{:S(2)}) collective-permute-start(bf16[144,1024]{1,0:T(8,128)(2,1)S(1)} %slice.115), channel_id=1, source_target_pairs={{0,16},{16,0},{1,17},{17,1},{2,18},{18,2},{3,19},{19,3},{4,20},{20... | collective-permute-start | bytes 884744 | tf_op jit(solution)/shard_map/ppermute | solution.py:600
  55.3 5.4 %collective-permute-start.18 = (bf16[80,1024]{1,0:T(8,128)(2,1)S(1)}, bf16[80,1024]{1,0:T(8,128)(2,1)S(1)}, u32[]{:S(2)}, u32[]{:S(2)}) collective-permute-start(bf16[80,1024]{1,0:T(8,128)(2,1)S(1)} %pad_maximum_fusion.5), channel_id=1, source_target_pairs={{0,2},{1,3},{2,0},{3,1},{4,6},{5,7},{6,4},{7,5},{8,10},{9,11},{10,... | collective-permute-start | bytes 491528 | tf_op jit(solution)/shard_map/ppermute | solution.py:600
  60.7 1.6 %collective-permute-start.19 = (bf16[2,64,1024]{2,1,0:T(8,128)(2,1)S(1)}, bf16[2,64,1024]{2,1,0:T(8,128)(2,1)S(1)}, u32[]{:S(2)}, u32[]{:S(2)}) collective-permute-start(bf16[2,64,1024]{2,1,0:T(8,128)(2,1)S(1)} %pad_maximum_fusion.3.near_ref), channel_id=1, source_target_pairs={{0,1},{1,0},{2,3},{3,2},{4,5},{5,4},{6,7},{7,6},{8,9},{9,8},{10,11... | collective-permute-start | bytes 786440 | tf_op jit(solution)/shard_map/ppermute | solution.py:600

commit v13 on v11

--- a/solution.py
+++ b/solution.py
@@ -679,31 +679,30 @@
     cut = 7 * HD // 4
     halves = (coarse_partial[:cut], coarse_partial[cut:])
     others = [swapped(half, "batch", 1) if pair_batch else half for half in halves]
-    mask = 1
-    while mask < downs:
-        last = 2 * mask == downs
+    masks = [1 << bit for bit in range(downs.bit_length() - 1)]
+    for mask in masks:
+        fine_quarter = narrow(wide(fine_quarter) + wide(swapped(fine_quarter, "gy", mask)))
+    for turn, mask in enumerate(masks):
         coarse_kept = coarse_kept.reshape(2, -1, 2, count, D_C)
-        sent = narrow(coarse_kept[:, :, 1]).reshape(-1, D_C)
-        come = swapped(jnp.concatenate([fine_quarter, sent], axis=0), "gy", mask)
-        coarse_kept = coarse_kept[:, :, 0]
-        coarse_kept = coarse_kept + wide(come[rows:]).reshape(coarse_kept.shape)
-        fine_quarter = narrow(wide(fine_quarter) + wide(come[:rows]))
-        at = int(last)
-        fine_quarter, coarse_kept, others[at] = tied(fine_quarter, coarse_kept, others[at])
-        mask *= 2
-
+        come = swapped(narrow(coarse_kept[:, :, 1]), "gy", mask)
+        coarse_kept = coarse_kept[:, :, 0] + wide(come)
+        at = min(turn, 1)
+        coarse_kept, others[at] = tied(coarse_kept, others[at])
     coarse_kept = coarse_kept.reshape(2, count, D_C)
-    come = swapped(jnp.concatenate([fine_quarter, narrow(coarse_kept[1])], axis=0), "gx", 2)
+    come = swapped(narrow(coarse_kept[1]), "gx", 2)
     if pair_batch:
         grad_coarse_qkv, grad_coarse_out = pair_sum(coarse_partial, *others)
     else:
-        coarse_sum = narrow(batch_sum(wide(coarse_partial)))
+        coarse_sum = narrow(lax.psum(wide(coarse_partial), "batch"))
         grad_coarse_qkv = coarse_sum[: 3 * HD].reshape(coarse_qkv.shape)
         grad_coarse_out = coarse_sum[3 * HD :]
-    come, grad_coarse_qkv, grad_coarse_out = tied(come, grad_coarse_qkv, grad_coarse_out)
-    fine_pair = jnp.stack([fine_quarter, come[:rows]])
+    fine_other = swapped(fine_quarter, "gx", 2)
+    fine_other, come, grad_coarse_qkv, grad_coarse_out = tied(
+        fine_other, come, grad_coarse_qkv, grad_coarse_out
+    )
+    fine_pair = jnp.stack([fine_quarter, fine_other])
     near_qkv, near_out, dx_coarse = near_step(
-        fine_pair, x_coarse[0], coarse_factor, coarse_kept[0], come[rows:]
+        fine_pair, x_coarse[0], coarse_factor, coarse_kept[0], come
     )
     far_pair = swapped(fine_pair, "gx", 1)
     far_pair, near_qkv, near_out = tied(far_pair, near_qkv, near_out)

time: 62.9 us -> 59.9 us (0.952)
  waiting for transfers between devices: 21.2 us -> 15.6 us
  starting transfers between devices: 27.3 us -> 29.9 us
    ppermute x16 -> x19, waiting for transfers between devices: 21.2 us -> 15.6 us  [swapped(): lax.ppermute(value, axis, [(i, i ^ mask) for i in range(lax.axis_size(axi...]
    ppermute x16 -> x19, starting transfers between devices: 17 us -> 19.6 us  [swapped(): lax.ppermute(value, axis, [(i, i ^ mask) for i in range(lax.axis_size(axi...]
  transfers between devices with their start and end apart: 20 -> 23, of which waited for: 8 -> 10; matrix products, arithmetic and copies ran while one was open for 1% -> 1% of each run, Pallas kernels for 14% -> 15%
where the time goes in v13:
time: 59.9 us; the launch traced here: 59.6 us
  starting transfers between devices  29.9 us (50%)
  waiting for transfers between devices  15.6 us (26%)
  Pallas kernels  9.73 us (16%)
  local copies, waits for them, and re-layouts  2.19 us (4%)
  between operations  1.67 us (3%)
    ppermute x19, starting transfers between devices, swapped(): lax.ppermute(value, axis, [(i, i ^ mask) for i in range(lax.axis_size(axi...  19.6 us
    ppermute x19, waiting for transfers between devices, swapped(): lax.ppermute(value, axis, [(i, i ^ mask) for i in range(lax.axis_size(axi...  15.6 us
    ppermute x2, starting transfers between devices, neighbours(): return (lax.ppermute(to_near, axis, near), from_far)  8.81 us
    pallas_call x1, Pallas kernels, fine_block(): pl.pallas_call(fine_body, out_shape=(jax.ShapeDtypeStruct((height, breadt...  4.33 us
    pallas_call x1, Pallas kernels, coarse_block(): pl.pallas_call(coarse_body, out_shape=(jax.ShapeDtypeStruct((count, D_C),...  2.23 us
    ppermute x2, starting transfers between devices, neighbours(): from_far = lax.ppermute(to_far, axis, far)  1.47 us
    pallas_call x1, Pallas kernels, near_step(): pl.pallas_call(near_body, out_shape=(jax.ShapeDtypeStruct((D_F, 3 * D_F),...  1.36 us
  transfers between devices with their start and end apart: 23, of which 10 were waited for; matrix products, arithmetic and copies ran while one was open for 1% of the time, Pallas kernels for 15%

profile of v13, /device:TPU:0, one launch (start us, length us, event | category | flops | bytes accessed | tf_op | source)
XLA Modules:
  0.0 59.6 jit_solution(439269086160617725)
XLA Ops:
  0.6 1.0 %slice_bitcast_fusion.2 = (bf16[6,32,256]{2,1,0:T(8,128)(2,1)S(1)}, bf16[6,32,256]{2,1,0:T(8,128)(2,1)S(1)}) fusion(bf16[1,8,32,256]{3,2,1,0:T(8,128)(2,1)} %param.13), kind=kLoop, calls=%fused_computation.20 | loop fusion | bytes 393216 | tf_op jit(solution)/shard_map/slice | solution.py:419
  1.7 0.0 copy-start.6
  1.7 0.0 copy-start.7
  1.7 0.7 %collective-permute-start = (bf16[9,32,256]{2,1,0:T(8,128)(2,1)S(1)}, bf16[9,32,256]{2,1,0:T(8,128)(2,1)S(1)}, u32[]{:S(2)}, u32[]{:S(2)}) collective-permute-start(bf16[9,32,256]{2,1,0:T(8,128)(2,1)S(1)} %get-tuple-element.54.second), channel_id=1, source_target_pairs={{4,8},{8,4},{5,9},{9,5},{6,10},{10,6},{7,11},{11,7},{20,24},{24,20... | collective-permute-start | bytes 442376 | tf_op jit(solution)/shard_map/ppermute | solution.py:588
  2.4 5.9 %collective-permute-start.1 = (bf16[9,32,256]{2,1,0:T(8,128)(2,1)S(1)}, bf16[9,32,256]{2,1,0:T(8,128)(2,1)S(1)}, u32[]{:S(2)}, u32[]{:S(2)}) collective-permute-start(bf16[9,32,256]{2,1,0:T(8,128)(2,1)S(1)} %get-tuple-element.55.first), channel_id=1, source_target_pairs={{0,4},{4,0},{8,12},{12,8},{1,5},{5,1},{9,13},{13,9},{2,6},{6,2},{1... | collective-permute-start | bytes 442376 | tf_op jit(solution)/shard_map/ppermute | solution.py:589
  8.3 0.1 collective-permute-start.4
  8.4 1.9 %collective-permute-start.5 = (bf16[16,2048]{1,0:T(8,128)(2,1)S(1)}, bf16[16,2048]{1,0:T(8,128)(2,1)S(1)}, u32[]{:S(2)}, u32[]{:S(2)}) collective-permute-start(bf16[16,2048]{1,0:T(8,128)(2,1)S(1)} %pack_coarse.1), channel_id=1, source_target_pairs={{0,8},{4,12},{8,0},{12,4},{1,9},{5,13},{9,1},{13,5},{2,10},{6,14},... | collective-permute-start | bytes 196616 | tf_op jit(solution)/shard_map/ppermute | solution.py:593
  10.3 2.5 %collective-permute-start.6 = (bf16[16,2048]{1,0:T(8,128)(2,1)S(1)}, bf16[16,2048]{1,0:T(8,128)(2,1)S(1)}, u32[]{:S(2)}, u32[]{:S(2)}) collective-permute-start(bf16[16,2048]{1,0:T(8,128)(2,1)S(1)} %pack_coarse.1), channel_id=1, source_target_pairs={{0,12},{4,8},{8,4},{12,0},{1,13},{5,9},{9,5},{13,1},{2,14},{6,10},... | collective-permute-start | bytes 196616 | tf_op jit(solution)/shard_map/ppermute | solution.py:593
  13.4 0.0 collective-permute-done.row_far_ref
  13.5 0.0 collective-permute-done.1.row_near_ref
  13.5 0.0 copy-start.8
  13.5 0.0 copy-start.9
  13.5 0.0 copy-start.10
  13.5 0.0 copy-start.11
  13.5 0.1 col_edges.1
  13.6 0.0 copy-start.2
  13.6 0.8 %collective-permute-start.2 = (bf16[34,8,256]{2,1,0:T(8,128)(2,1)S(1)}, bf16[34,8,256]{2,1,0:T(8,128)(2,1)S(1)}, u32[]{:S(2)}, u32[]{:S(2)}) collective-permute-start(bf16[34,8,256]{2,1,0:T(8,128)(2,1)S(1)} %get-tuple-element.58), channel_id=1, source_target_pairs={{1,2},{2,1},{5,6},{6,5},{9,10},{10,9},{13,14},{14,13},{17,18},{18,... | collective-permute-start | bytes 417800 | tf_op jit(solution)/shard_map/ppermute | solution.py:588
  14.4 2.9 %collective-permute-start.3 = (bf16[34,8,256]{2,1,0:T(8,128)(2,1)S(1)}, bf16[34,8,256]{2,1,0:T(8,128)(2,1)S(1)}, u32[]{:S(2)}, u32[]{:S(2)}) collective-permute-start(bf16[34,8,256]{2,1,0:T(8,128)(2,1)S(1)} %get-tuple-element.59), channel_id=1, source_target_pairs={{0,1},{1,0},{2,3},{3,2},{4,5},{5,4},{6,7},{7,6},{8,9},{9,8},{10,11... | collective-permute-start | bytes 417800 | tf_op jit(solution)/shard_map/ppermute | solution.py:589
  17.4 0.1 time_factors.1
  17.4 0.0 collective-permute-done.6
  17.4 0.0 copy-start.4
  17.5 1.4 %collective-permute-start.9 = (bf16[4,16,2048]{2,1,0:T(8,128)(2,1)S(1)}, bf16[4,16,2048]{2,1,0:T(8,128)(2,1)S(1)}, u32[]{:S(2)}, u32[]{:S(2)}) collective-permute-start(bf16[4,16,2048]{2,1,0:T(8,128)(2,1)S(1)} %pad_maximum_fusion.1), channel_id=1, source_target_pairs={{0,2},{1,3},{2,0},{3,1},{4,6},{5,7},{6,4},{7,5},{8,10},{9,11},{10,... | collective-permute-start | bytes 786440 | tf_op jit(solution)/shard_map/ppermute | solution.py:593
  18.9 0.0 collective-permute-done.2.col_far_ref
  18.9 0.0 collective-permute-done.3.col_near_ref
  18.9 4.3 %fine_block.1 = (bf16[8,32,256]{2,1,0:T(8,128)(2,1)}, f32[2,4,16,1024]{3,2,1,0:T(8,128)S(1)}, bf16[2,4,16,1024]{3,2,1,0:T(8,128)(2,1)S(1)}) custom-call(bf16[8,32,256]{2,1,0:T(8,128)(2,1)S(1)} %bitcast.60, bf16[8,32,256]{2,1,0:T(8,128)(2,1)S(1)} %bitcast.62, bf16[9,32,256]{2,1,0:T(8,128)(2,1)S(1)} %collective-permute-done.row_far_ref, ...), custom_call_target="tpu_custom_call" | custom-call | tf_op jit(solution)/shard_map/fine_block/pallas_call | solution.py:297
  23.2 1.1 %collective-permute-start.7 = (bf16[2,4,16,1024]{3,2,1,0:T(8,128)(2,1)S(1)}, bf16[2,4,16,1024]{3,2,1,0:T(8,128)(2,1)S(1)}, u32[]{:S(2)}, u32[]{:S(2)}) collective-permute-start(bf16[2,4,16,1024]{3,2,1,0:T(8,128)(2,1)S(1)} %get-tuple-element.73), channel_id=1, source_target_pairs={{0,1},{1,0},{2,3},{3,2},{4,5},{5,4},{6,7},{7,6},{8,9},{9,8},{10,11... | collective-permute-start | bytes 786440 | tf_op jit(solution)/shard_map/ppermute | solution.py:593
  24.3 0.0 collective-permute-start.10
  24.3 1.5 %collective-permute-done.9 = bf16[4,16,2048]{2,1,0:T(8,128)(2,1)S(1)} collective-permute-done((bf16[4,16,2048]{2,1,0:T(8,128)(2,1)S(1)}, bf16[4,16,2048]{2,1,0:T(8,128)(2,1)S(1)}, u32[]{:S(2)}, u32[]{:S(2)}) %collective-permute-start.9) | collective-permute-done | bytes 262176 | tf_op jit(solution)/shard_map/ppermute | solution.py:593
  25.8 0.1 convert_add_fusion.1
  25.9 1.7 %collective-permute-start.8 = (bf16[4,16,1024]{2,1,0:T(8,128)(2,1)S(1)}, bf16[4,16,1024]{2,1,0:T(8,128)(2,1)S(1)}, u32[]{:S(2)}, u32[]{:S(2)}) collective-permute-start(bf16[4,16,1024]{2,1,0:T(8,128)(2,1)S(1)} %fusion.3), channel_id=1, source_target_pairs={{0,2},{1,3},{2,0},{3,1},{4,6},{5,7},{6,4},{7,5},{8,10},{9,11},{10,... | collective-permute-start | bytes 393224 | tf_op jit(solution)/shard_map/ppermute | solution.py:593
  27.7 0.0 collective-permute-done.11
  27.7 0.1 pad_maximum_fusion
  27.8 0.0 copy-start.3
  27.8 0.0 copy-start.5
  27.8 0.1 fusion.8
  27.9 0.9 %copy-done.3 = bf16[3,64,1024]{2,1,0:T(8,128)(2,1)S(1)} copy-done((bf16[3,64,1024]{2,1,0:T(8,128)(2,1)S(1)}, bf16[3,64,1024]{2,1,0:T(8,128)(2,1)}, u32[]{:S(2)}) %copy-start.3) | copy-done | bytes 393240
  28.8 0.0 copy-done.5
  28.8 2.2 %coarse_block.1 = (bf16[256,1024]{1,0:T(8,128)(2,1)S(1)}, bf16[256,1024]{1,0:T(8,128)(2,1)S(1)}) custom-call(bf16[256,1024]{1,0:T(8,128)(2,1)S(1)} %get-tuple-element.103.x_ref, bf16[256,1024]{1,0:T(8,128)(2,1)S(1)} %get-tuple-element.102.dy_ref, f32[1,1024]{1,0:T(1,128)S(1)} %get-tuple-element.75.factor_ref, bf16[3,64,1024]{2,1,0:T(8,128)(2,1)S(1)} %copy-done.3, ...), custom_call_target="tpu_custom_call" | custom-call | tf_op jit(solution)/shard_map/coarse_block/pallas_call | solution.py:374
  31.1 0.8 %collective-permute-done.8 = bf16[4,16,1024]{2,1,0:T(8,128)(2,1)S(1)} collective-permute-done((bf16[4,16,1024]{2,1,0:T(8,128)(2,1)S(1)}, bf16[4,16,1024]{2,1,0:T(8,128)(2,1)S(1)}, u32[]{:S(2)}, u32[]{:S(2)}) %collective-permute-start.8) | collective-permute-done | bytes 131104 | tf_op jit(solution)/shard_map/ppermute | solution.py:593
  31.9 1.6 %collective-permute-start.12 = (bf16[4,16,1024]{2,1,0:T(8,128)(2,1)S(1)}, bf16[4,16,1024]{2,1,0:T(8,128)(2,1)S(1)}, u32[]{:S(2)}, u32[]{:S(2)}) collective-permute-start(bf16[4,16,1024]{2,1,0:T(8,128)(2,1)S(1)} %fusion.2), channel_id=1, source_target_pairs={{0,16},{16,0},{1,17},{17,1},{2,18},{18,2},{3,19},{19,3},{4,20},{20... | collective-permute-start | bytes 393224 | tf_op jit(solution)/shard_map/ppermute | solution.py:593
  33.6 0.1 collective-permute-start.13
  33.6 3.5 %collective-permute-done.12 = bf16[4,16,1024]{2,1,0:T(8,128)(2,1)S(1)} collective-permute-done((bf16[4,16,1024]{2,1,0:T(8,128)(2,1)S(1)}, bf16[4,16,1024]{2,1,0:T(8,128)(2,1)S(1)}, u32[]{:S(2)}, u32[]{:S(2)}) %collective-permute-start.12) | collective-permute-done | bytes 131104 | tf_op jit(solution)/shard_map/ppermute | solution.py:593
  37.2 0.1 convert_add_fusion
  37.3 1.7 %collective-permute-start.14 = (bf16[64,1024]{1,0:T(8,128)(2,1)S(1)}, bf16[64,1024]{1,0:T(8,128)(2,1)S(1)}, u32[]{:S(2)}, u32[]{:S(2)}) collective-permute-start(bf16[64,1024]{1,0:T(8,128)(2,1)S(1)} %bitcast.76), channel_id=1, source_target_pairs={{0,4},{4,0},{8,12},{12,8},{1,5},{5,1},{9,13},{13,9},{2,6},{6,2},{1... | collective-permute-start | bytes 393224 | tf_op jit(solution)/shard_map/ppermute | solution.py:593
  39.0 0.5 collective-permute-start.17
  39.5 1.5 %collective-permute-start.18 = (bf16[112,1024]{1,0:T(8,128)(2,1)S(1)}, bf16[112,1024]{1,0:T(8,128)(2,1)S(1)}, u32[]{:S(2)}, u32[]{:S(2)}) collective-permute-start(bf16[112,1024]{1,0:T(8,128)(2,1)S(1)} %slice.90), channel_id=1, source_target_pairs={{0,16},{16,0},{1,17},{17,1},{2,18},{18,2},{3,19},{19,3},{4,20},{20... | collective-permute-start | bytes 688136 | tf_op jit(solution)/shard_map/ppermute | solution.py:593
  41.0 0.5 collective-permute-start.20
  41.5 1.5 %collective-permute-done.14 = bf16[64,1024]{1,0:T(8,128)(2,1)S(1)} collective-permute-done((bf16[64,1024]{1,0:T(8,128)(2,1)S(1)}, bf16[64,1024]{1,0:T(8,128)(2,1)S(1)}, u32[]{:S(2)}, u32[]{:S(2)}) %collective-permute-start.14) | collective-permute-done | bytes 131104 | tf_op jit(solution)/shard_map/ppermute | solution.py:593
  43.0 1.5 %collective-permute-start.15 = (bf16[64,1024]{1,0:T(8,128)(2,1)S(1)}, bf16[64,1024]{1,0:T(8,128)(2,1)S(1)}, u32[]{:S(2)}, u32[]{:S(2)}) collective-permute-start(bf16[64,1024]{1,0:T(8,128)(2,1)S(1)} %add_convert_fusion.1), channel_id=1, source_target_pairs={{0,8},{4,12},{8,0},{12,4},{1,9},{5,13},{9,1},{13,5},{2,10},{6,14},... | collective-permute-start | bytes 393224 | tf_op jit(solution)/shard_map/ppermute | solution.py:593
  44.6 1.2 %collective-permute-done.17 = bf16[2,2,16,1024]{3,2,0,1:T(8,128)(2,1)S(1)} collective-permute-done((bf16[2,2,16,1024]{3,2,0,1:T(8,128)(2,1)S(1)}, bf16[2,2,16,1024]{3,2,0,1:T(8,128)(2,1)S(1)}, u32[]{:S(2)}, u32[]{:S(2)}) %collective-permute-start.17) | collective-permute-done | bytes 131104 | tf_op jit(solution)/shard_map/ppermute | solution.py:593
  45.9 2.2 %collective-permute-done.18.refs_0_ = bf16[112,1024]{1,0:T(8,128)(2,1)S(1)} collective-permute-done((bf16[112,1024]{1,0:T(8,128)(2,1)S(1)}, bf16[112,1024]{1,0:T(8,128)(2,1)S(1)}, u32[]{:S(2)}, u32[]{:S(2)}) %collective-permute-start.18) | collective-permute-done | bytes 229408 | tf_op jit(solution)/shard_map/ppermute | solution.py:593
  48.0 1.5 %collective-permute-start.19 = (bf16[2,1,16,1024]{3,2,1,0:T(8,128)(2,1)S(1)}, bf16[2,1,16,1024]{3,2,1,0:T(8,128)(2,1)S(1)}, u32[]{:S(2)}, u32[]{:S(2)}) collective-permute-start(bf16[2,1,16,1024]{3,2,1,0:T(8,128)(2,1)S(1)} %fusion.6), channel_id=1, source_target_pairs={{0,8},{4,12},{8,0},{12,4},{1,9},{5,13},{9,1},{13,5},{2,10},{6,14},... | collective-permute-start | bytes 196616 | tf_op jit(solution)/shard_map/ppermute | solution.py:593
  49.6 1.5 %collective-permute-done.15 = bf16[64,1024]{1,0:T(8,128)(2,1)S(1)} collective-permute-done((bf16[64,1024]{1,0:T(8,128)(2,1)S(1)}, bf16[64,1024]{1,0:T(8,128)(2,1)S(1)}, u32[]{:S(2)}, u32[]{:S(2)}) %collective-permute-start.15) | collective-permute-done | bytes 131104 | tf_op jit(solution)/shard_map/ppermute | solution.py:593
  51.1 0.8 %collective-permute-start.16 = (bf16[64,1024]{1,0:T(8,128)(2,1)S(1)}, bf16[64,1024]{1,0:T(8,128)(2,1)S(1)}, u32[]{:S(2)}, u32[]{:S(2)}) collective-permute-start(bf16[64,1024]{1,0:T(8,128)(2,1)S(1)} %add_convert_fusion), channel_id=1, source_target_pairs={{0,2},{1,3},{2,0},{3,1},{4,6},{5,7},{6,4},{7,5},{8,10},{9,11},{10,... | collective-permute-start | bytes 393224 | tf_op jit(solution)/shard_map/ppermute | solution.py:593
  51.9 1.4 %collective-permute-done.19 = bf16[2,1,16,1024]{3,2,1,0:T(8,128)(2,1)S(1)} collective-permute-done((bf16[2,1,16,1024]{3,2,1,0:T(8,128)(2,1)S(1)}, bf16[2,1,16,1024]{3,2,1,0:T(8,128)(2,1)S(1)}, u32[]{:S(2)}, u32[]{:S(2)}) %collective-permute-start.19) | collective-permute-done | bytes 65568 | tf_op jit(solution)/shard_map/ppermute | solution.py:593
  53.3 0.0 collective-permute-done.20.refs_1_
  53.3 1.2 %collective-permute-start.21 = (bf16[16,1024]{1,0:T(8,128)(2,1)S(1)}, bf16[16,1024]{1,0:T(8,128)(2,1)S(1)}, u32[]{:S(2)}, u32[]{:S(2)}) collective-permute-start(bf16[16,1024]{1,0:T(8,128)(2,1)S(1)} %fusion.7), channel_id=1, source_target_pairs={{0,2},{1,3},{2,0},{3,1},{4,6},{5,7},{6,4},{7,5},{8,10},{9,11},{10,... | collective-permute-start | bytes 98312 | tf_op jit(solution)/shard_map/ppermute | solution.py:593
  54.5 0.9 %pair_sum.1 = (bf16[3,64,1024]{2,1,0:T(8,128)(2,1)}, bf16[64,1024]{1,0:T(8,128)(2,1)}) custom-call(bf16[256,1024]{1,0:T(8,128)(2,1)S(1)} %get-tuple-element.83.own, bf16[112,1024]{1,0:T(8,128)(2,1)S(1)} %collective-permute-done.18.refs_0_, bf16[144,1024]{1,0:T(8,128)(2,1)S(1)} %collective-permute-done.20.refs_1_), custom_call_target="tpu_custom_call" | custom-call | tf_op jit(solution)/shard_map/pair_sum/pallas_call | solution.py:502
  55.4 1.9 %collective-permute-done.21.come_ref = bf16[16,1024]{1,0:T(8,128)(2,1)S(1)} collective-permute-done((bf16[16,1024]{1,0:T(8,128)(2,1)S(1)}, bf16[16,1024]{1,0:T(8,128)(2,1)S(1)}, u32[]{:S(2)}, u32[]{:S(2)}) %collective-permute-start.21) | collective-permute-done | bytes 32800 | tf_op jit(solution)/shard_map/ppermute | solution.py:593
  57.3 0.0 collective-permute-done.16
  57.3 0.1 collective-permute-start.22
  57.4 1.4 %near_step.1 = (bf16[256,768]{1,0:T(8,128)(2,1)}, bf16[256,256]{1,0:T(8,128)(2,1)}, bf16[4,4,1024]{2,1,0:T(4,128)(2,1)}) custom-call(bf16[2,64,1024]{2,1,0:T(8,128)(2,1)S(1)} %pad_maximum_fusion.2.near_ref, bf16[4,4,1024]{2,1,0:T(4,128)(2,1)S(1)} %bitcast.65, f32[1,1024]{1,0:T(1,128)S(1)} %get-tuple-element.75.factor_ref, ...), custom_call_target="tpu_custom_call" | custom-call | tf_op jit(solution)/shard_map/near_step/pallas_call | solution.py:551
  58.8 0.1 collective-permute-done.22.far_ref
  58.9 0.7 %far_step.1 = (bf16[256,768]{1,0:T(8,128)(2,1)}, bf16[256,256]{1,0:T(8,128)(2,1)}) custom-call(bf16[2,64,1024]{2,1,0:T(8,128)(2,1)S(1)} %collective-permute-done.22.far_ref, bf16[256,768]{1,0:T(8,128)(2,1)} %get-tuple-element.96.qkv_in, bf16[256,256]{1,0:T(8,128)(2,1)} %get-tuple-element.97.out_in), custom_call_target="tpu_custom_call", output_to_operand_aliasing={{0}: (1, {}), {1}: (2, {})} | custom-call | tf_op jit(solution)/shard_map/far_step/pallas_call | solution.py:569
  (37 shorter events, 0.5 us)
Async XLA Ops:
  0.6 1.0 %copy-start.1 = (bf16[1,8,32,256]{3,2,1,0:T(8,128)(2,1)S(1)}, bf16[1,8,32,256]{3,2,1,0:T(8,128)(2,1)}, u32[]{:S(2)}) copy-start(bf16[1,8,32,256]{3,2,1,0:T(8,128)(2,1)} %param.14) | copy-start | bytes 393220
  1.7 6.7 %copy-start.6 = (bf16[1,4,4,1024]{3,2,1,0:T(4,128)(2,1)S(1)}, bf16[1,4,4,1024]{3,2,1,0:T(4,128)(2,1)}, u32[]{:S(2)}) copy-start(bf16[1,4,4,1024]{3,2,1,0:T(4,128)(2,1)} %param.15) | copy-start | bytes 98308
  1.7 6.6 %copy-start.7 = (bf16[1,4,4,1024]{3,2,1,0:T(4,128)(2,1)S(1)}, bf16[1,4,4,1024]{3,2,1,0:T(4,128)(2,1)}, u32[]{:S(2)}) copy-start(bf16[1,4,4,1024]{3,2,1,0:T(4,128)(2,1)} %param.16) | copy-start | bytes 98308
  1.7 11.7 %collective-permute-start = (bf16[9,32,256]{2,1,0:T(8,128)(2,1)S(1)}, bf16[9,32,256]{2,1,0:T(8,128)(2,1)S(1)}, u32[]{:S(2)}, u32[]{:S(2)}) collective-permute-start(bf16[9,32,256]{2,1,0:T(8,128)(2,1)S(1)} %get-tuple-element.54.second), channel_id=1, source_target_pairs={{4,8},{8,4},{5,9},{9,5},{6,10},{10,6},{7,11},{11,7},{20,24},{24,20... | collective-permute-start | bytes 442376 | tf_op jit(solution)/shard_map/ppermute | solution.py:588
  2.4 11.0 %collective-permute-start.1 = (bf16[9,32,256]{2,1,0:T(8,128)(2,1)S(1)}, bf16[9,32,256]{2,1,0:T(8,128)(2,1)S(1)}, u32[]{:S(2)}, u32[]{:S(2)}) collective-permute-start(bf16[9,32,256]{2,1,0:T(8,128)(2,1)S(1)} %get-tuple-element.55.first), channel_id=1, source_target_pairs={{0,4},{4,0},{8,12},{12,8},{1,5},{5,1},{9,13},{13,9},{2,6},{6,2},{1... | collective-permute-start | bytes 442376 | tf_op jit(solution)/shard_map/ppermute | solution.py:589
  8.3 5.1 %copy-start = (bf16[1,8,32,256]{3,2,1,0:T(8,128)(2,1)S(1)}, bf16[1,8,32,256]{3,2,1,0:T(8,128)(2,1)}, u32[]{:S(2)}) copy-start(bf16[1,8,32,256]{3,2,1,0:T(8,128)(2,1)} %param.13) | copy-start | bytes 393220
  8.3 9.1 %collective-permute-start.4 = (bf16[16,2048]{1,0:T(8,128)(2,1)S(1)}, bf16[16,2048]{1,0:T(8,128)(2,1)S(1)}, u32[]{:S(2)}, u32[]{:S(2)}) collective-permute-start(bf16[16,2048]{1,0:T(8,128)(2,1)S(1)} %pack_coarse.1), channel_id=1, source_target_pairs={{0,4},{4,0},{8,12},{12,8},{1,5},{5,1},{9,13},{13,9},{2,6},{6,2},{1... | collective-permute-start | bytes 196616 | tf_op jit(solution)/shard_map/ppermute | solution.py:593
  8.4 9.0 %collective-permute-start.5 = (bf16[16,2048]{1,0:T(8,128)(2,1)S(1)}, bf16[16,2048]{1,0:T(8,128)(2,1)S(1)}, u32[]{:S(2)}, u32[]{:S(2)}) collective-permute-start(bf16[16,2048]{1,0:T(8,128)(2,1)S(1)} %pack_coarse.1), channel_id=1, source_target_pairs={{0,8},{4,12},{8,0},{12,4},{1,9},{5,13},{9,1},{13,5},{2,10},{6,14},... | collective-permute-start | bytes 196616 | tf_op jit(solution)/shard_map/ppermute | solution.py:593
  10.3 7.1 %collective-permute-start.6 = (bf16[16,2048]{1,0:T(8,128)(2,1)S(1)}, bf16[16,2048]{1,0:T(8,128)(2,1)S(1)}, u32[]{:S(2)}, u32[]{:S(2)}) collective-permute-start(bf16[16,2048]{1,0:T(8,128)(2,1)S(1)} %pack_coarse.1), channel_id=1, source_target_pairs={{0,12},{4,8},{8,4},{12,0},{1,13},{5,9},{9,5},{13,1},{2,14},{6,10},... | collective-permute-start | bytes 196616 | tf_op jit(solution)/shard_map/ppermute | solution.py:593
  13.5 3.9 %copy-start.8 = (f32[1024]{0:T(1024)S(1)}, f32[1024]{0:T(1024)}, u32[]{:S(2)}) copy-start(f32[1024]{0:T(1024)} %param.19) | copy-start | bytes 12292
  13.5 3.9 %copy-start.9 = (f32[1,1024]{1,0:T(1,128)S(1)}, f32[1,1024]{1,0:T(1,128)}, u32[]{:S(2)}) copy-start(f32[1,1024]{1,0:T(1,128)} %constant.5.clone.coarse_freq) | copy-start | bytes 12292
  13.5 3.8 %copy-start.10 = (f32[256]{0:T(256)S(1)}, f32[256]{0:T(256)}, u32[]{:S(2)}) copy-start(f32[256]{0:T(256)} %param.18) | copy-start | bytes 3076
  13.5 3.8 %copy-start.11 = (f32[1,256]{1,0:T(1,128)S(1)}, f32[1,256]{1,0:T(1,128)}, u32[]{:S(2)}) copy-start(f32[1,256]{1,0:T(1,128)} %constant.4.clone.fine_freq) | copy-start | bytes 3076
  13.6 5.3 %copy-start.2 = (bf16[256,768]{1,0:T(8,128)(2,1)S(1)}, bf16[256,768]{1,0:T(8,128)(2,1)}, u32[]{:S(2)}) copy-start(bf16[256,768]{1,0:T(8,128)(2,1)} %qkv_ref.1) | copy-start | bytes 1179652
  13.6 5.2 %collective-permute-start.2 = (bf16[34,8,256]{2,1,0:T(8,128)(2,1)S(1)}, bf16[34,8,256]{2,1,0:T(8,128)(2,1)S(1)}, u32[]{:S(2)}, u32[]{:S(2)}) collective-permute-start(bf16[34,8,256]{2,1,0:T(8,128)(2,1)S(1)} %get-tuple-element.58), channel_id=1, source_target_pairs={{1,2},{2,1},{5,6},{6,5},{9,10},{10,9},{13,14},{14,13},{17,18},{18,... | collective-permute-start | bytes 417800 | tf_op jit(solution)/shard_map/ppermute | solution.py:588
  14.4 4.4 %collective-permute-start.3 = (bf16[34,8,256]{2,1,0:T(8,128)(2,1)S(1)}, bf16[34,8,256]{2,1,0:T(8,128)(2,1)S(1)}, u32[]{:S(2)}, u32[]{:S(2)}) collective-permute-start(bf16[34,8,256]{2,1,0:T(8,128)(2,1)S(1)} %get-tuple-element.59), channel_id=1, source_target_pairs={{0,1},{1,0},{2,3},{3,2},{4,5},{5,4},{6,7},{7,6},{8,9},{9,8},{10,11... | collective-permute-start | bytes 417800 | tf_op jit(solution)/shard_map/ppermute | solution.py:589
  17.4 1.4 %copy-start.4 = (bf16[256,256]{1,0:T(8,128)(2,1)S(1)}, bf16[256,256]{1,0:T(8,128)(2,1)}, u32[]{:S(2)}) copy-start(bf16[256,256]{1,0:T(8,128)(2,1)} %out_ref.1) | copy-start | bytes 393220
  17.5 8.3 %collective-permute-start.9 = (bf16[4,16,2048]{2,1,0:T(8,128)(2,1)S(1)}, bf16[4,16,2048]{2,1,0:T(8,128)(2,1)S(1)}, u32[]{:S(2)}, u32[]{:S(2)}) collective-permute-start(bf16[4,16,2048]{2,1,0:T(8,128)(2,1)S(1)} %pad_maximum_fusion.1), channel_id=1, source_target_pairs={{0,2},{1,3},{2,0},{3,1},{4,6},{5,7},{6,4},{7,5},{8,10},{9,11},{10,... | collective-permute-start | bytes 786440 | tf_op jit(solution)/shard_map/ppermute | solution.py:593
  23.2 2.6 %collective-permute-start.7 = (bf16[2,4,16,1024]{3,2,1,0:T(8,128)(2,1)S(1)}, bf16[2,4,16,1024]{3,2,1,0:T(8,128)(2,1)S(1)}, u32[]{:S(2)}, u32[]{:S(2)}) collective-permute-start(bf16[2,4,16,1024]{3,2,1,0:T(8,128)(2,1)S(1)} %get-tuple-element.73), channel_id=1, source_target_pairs={{0,1},{1,0},{2,3},{3,2},{4,5},{5,4},{6,7},{7,6},{8,9},{9,8},{10,11... | collective-permute-start | bytes 786440 | tf_op jit(solution)/shard_map/ppermute | solution.py:593
  24.3 3.3 %collective-permute-start.10 = (bf16[4,16,2048]{2,1,0:T(8,128)(2,1)S(1)}, bf16[4,16,2048]{2,1,0:T(8,128)(2,1)S(1)}, u32[]{:S(2)}, u32[]{:S(2)}) collective-permute-start(bf16[4,16,2048]{2,1,0:T(8,128)(2,1)S(1)} %pad_maximum_fusion.1), channel_id=1, source_target_pairs={{0,1},{1,0},{2,3},{3,2},{4,5},{5,4},{6,7},{7,6},{8,9},{9,8},{10,11... | collective-permute-start | bytes 786440 | tf_op jit(solution)/shard_map/ppermute | solution.py:593
  25.8 1.8 %collective-permute-start.11 = (bf16[4,16,2048]{2,1,0:T(8,128)(2,1)S(1)}, bf16[4,16,2048]{2,1,0:T(8,128)(2,1)S(1)}, u32[]{:S(2)}, u32[]{:S(2)}) collective-permute-start(bf16[4,16,2048]{2,1,0:T(8,128)(2,1)S(1)} %collective-permute-done.9), channel_id=1, source_target_pairs={{0,1},{1,0},{2,3},{3,2},{4,5},{5,4},{6,7},{7,6},{8,9},{9,8},{10,11... | collective-permute-start | bytes 786440 | tf_op jit(solution)/shard_map/ppermute | solution.py:593
  25.9 6.0 %collective-permute-start.8 = (bf16[4,16,1024]{2,1,0:T(8,128)(2,1)S(1)}, bf16[4,16,1024]{2,1,0:T(8,128)(2,1)S(1)}, u32[]{:S(2)}, u32[]{:S(2)}) collective-permute-start(bf16[4,16,1024]{2,1,0:T(8,128)(2,1)S(1)} %fusion.3), channel_id=1, source_target_pairs={{0,2},{1,3},{2,0},{3,1},{4,6},{5,7},{6,4},{7,5},{8,10},{9,11},{10,... | collective-permute-start | bytes 393224 | tf_op jit(solution)/shard_map/ppermute | solution.py:593
  27.8 1.0 %copy-start.3 = (bf16[3,64,1024]{2,1,0:T(8,128)(2,1)S(1)}, bf16[3,64,1024]{2,1,0:T(8,128)(2,1)}, u32[]{:S(2)}) copy-start(bf16[3,64,1024]{2,1,0:T(8,128)(2,1)} %qkv_hbm.1) | copy-start | bytes 1179652
  27.8 1.0 %copy-start.5 = (bf16[64,1024]{1,0:T(8,128)(2,1)S(1)}, bf16[64,1024]{1,0:T(8,128)(2,1)}, u32[]{:S(2)}) copy-start(bf16[64,1024]{1,0:T(8,128)(2,1)} %out_hbm.1) | copy-start | bytes 393220
  31.9 5.2 %collective-permute-start.12 = (bf16[4,16,1024]{2,1,0:T(8,128)(2,1)S(1)}, bf16[4,16,1024]{2,1,0:T(8,128)(2,1)S(1)}, u32[]{:S(2)}, u32[]{:S(2)}) collective-permute-start(bf16[4,16,1024]{2,1,0:T(8,128)(2,1)S(1)} %fusion.2), channel_id=1, source_target_pairs={{0,16},{16,0},{1,17},{17,1},{2,18},{18,2},{3,19},{19,3},{4,20},{20... | collective-permute-start | bytes 393224 | tf_op jit(solution)/shard_map/ppermute | solution.py:593
  33.6 3.6 %collective-permute-start.13 = (bf16[2,4,16,1024]{3,2,1,0:T(8,128)(2,1)S(1)}, bf16[2,4,16,1024]{3,2,1,0:T(8,128)(2,1)S(1)}, u32[]{:S(2)}, u32[]{:S(2)}) collective-permute-start(bf16[2,4,16,1024]{3,2,1,0:T(8,128)(2,1)S(1)} %bitcast.79), channel_id=1, source_target_pairs={{0,1},{1,0},{2,3},{3,2},{4,5},{5,4},{6,7},{7,6},{8,9},{9,8},{10,11... | collective-permute-start | bytes 786440 | tf_op jit(solution)/shard_map/ppermute | solution.py:593
  37.3 5.7 %collective-permute-start.14 = (bf16[64,1024]{1,0:T(8,128)(2,1)S(1)}, bf16[64,1024]{1,0:T(8,128)(2,1)S(1)}, u32[]{:S(2)}, u32[]{:S(2)}) collective-permute-start(bf16[64,1024]{1,0:T(8,128)(2,1)S(1)} %bitcast.76), channel_id=1, source_target_pairs={{0,4},{4,0},{8,12},{12,8},{1,5},{5,1},{9,13},{13,9},{2,6},{6,2},{1... | collective-permute-start | bytes 393224 | tf_op jit(solution)/shard_map/ppermute | solution.py:593
  39.0 6.8 %collective-permute-start.17 = (bf16[2,2,16,1024]{3,2,0,1:T(8,128)(2,1)S(1)}, bf16[2,2,16,1024]{3,2,0,1:T(8,128)(2,1)S(1)}, u32[]{:S(2)}, u32[]{:S(2)}) collective-permute-start(bf16[2,2,16,1024]{3,2,0,1:T(8,128)(2,1)S(1)} %fusion.4), channel_id=1, source_target_pairs={{0,4},{4,0},{8,12},{12,8},{1,5},{5,1},{9,13},{13,9},{2,6},{6,2},{1... | collective-permute-start | bytes 393224 | tf_op jit(solution)/shard_map/ppermute | solution.py:593
  39.5 8.5 %collective-permute-start.18 = (bf16[112,1024]{1,0:T(8,128)(2,1)S(1)}, bf16[112,1024]{1,0:T(8,128)(2,1)S(1)}, u32[]{:S(2)}, u32[]{:S(2)}) collective-permute-start(bf16[112,1024]{1,0:T(8,128)(2,1)S(1)} %slice.90), channel_id=1, source_target_pairs={{0,16},{16,0},{1,17},{17,1},{2,18},{18,2},{3,19},{19,3},{4,20},{20... | collective-permute-start | bytes 688136 | tf_op jit(solution)/shard_map/ppermute | solution.py:593
  41.0 12.3 %collective-permute-start.20 = (bf16[144,1024]{1,0:T(8,128)(2,1)S(1)}, bf16[144,1024]{1,0:T(8,128)(2,1)S(1)}, u32[]{:S(2)}, u32[]{:S(2)}) collective-permute-start(bf16[144,1024]{1,0:T(8,128)(2,1)S(1)} %slice.93), channel_id=1, source_target_pairs={{0,16},{16,0},{1,17},{17,1},{2,18},{18,2},{3,19},{19,3},{4,20},{20... | collective-permute-start | bytes 884744 | tf_op jit(solution)/shard_map/ppermute | solution.py:593
  43.0 8.0 %collective-permute-start.15 = (bf16[64,1024]{1,0:T(8,128)(2,1)S(1)}, bf16[64,1024]{1,0:T(8,128)(2,1)S(1)}, u32[]{:S(2)}, u32[]{:S(2)}) collective-permute-start(bf16[64,1024]{1,0:T(8,128)(2,1)S(1)} %add_convert_fusion.1), channel_id=1, source_target_pairs={{0,8},{4,12},{8,0},{12,4},{1,9},{5,13},{9,1},{13,5},{2,10},{6,14},... | collective-permute-start | bytes 393224 | tf_op jit(solution)/shard_map/ppermute | solution.py:593
  48.0 5.2 %collective-permute-start.19 = (bf16[2,1,16,1024]{3,2,1,0:T(8,128)(2,1)S(1)}, bf16[2,1,16,1024]{3,2,1,0:T(8,128)(2,1)S(1)}, u32[]{:S(2)}, u32[]{:S(2)}) collective-permute-start(bf16[2,1,16,1024]{3,2,1,0:T(8,128)(2,1)S(1)} %fusion.6), channel_id=1, source_target_pairs={{0,8},{4,12},{8,0},{12,4},{1,9},{5,13},{9,1},{13,5},{2,10},{6,14},... | collective-permute-start | bytes 196616 | tf_op jit(solution)/shard_map/ppermute | solution.py:593
  51.1 6.2 %collective-permute-start.16 = (bf16[64,1024]{1,0:T(8,128)(2,1)S(1)}, bf16[64,1024]{1,0:T(8,128)(2,1)S(1)}, u32[]{:S(2)}, u32[]{:S(2)}) collective-permute-start(bf16[64,1024]{1,0:T(8,128)(2,1)S(1)} %add_convert_fusion), channel_id=1, source_target_pairs={{0,2},{1,3},{2,0},{3,1},{4,6},{5,7},{6,4},{7,5},{8,10},{9,11},{10,... | collective-permute-start | bytes 393224 | tf_op jit(solution)/shard_map/ppermute | solution.py:593
  53.3 4.0 %collective-permute-start.21 = (bf16[16,1024]{1,0:T(8,128)(2,1)S(1)}, bf16[16,1024]{1,0:T(8,128)(2,1)S(1)}, u32[]{:S(2)}, u32[]{:S(2)}) collective-permute-start(bf16[16,1024]{1,0:T(8,128)(2,1)S(1)} %fusion.7), channel_id=1, source_target_pairs={{0,2},{1,3},{2,0},{3,1},{4,6},{5,7},{6,4},{7,5},{8,10},{9,11},{10,... | collective-permute-start | bytes 98312 | tf_op jit(solution)/shard_map/ppermute | solution.py:593
  57.3 1.6 %collective-permute-start.22 = (bf16[2,64,1024]{2,1,0:T(8,128)(2,1)S(1)}, bf16[2,64,1024]{2,1,0:T(8,128)(2,1)S(1)}, u32[]{:S(2)}, u32[]{:S(2)}) collective-permute-start(bf16[2,64,1024]{2,1,0:T(8,128)(2,1)S(1)} %pad_maximum_fusion.2.near_ref), channel_id=1, source_target_pairs={{0,1},{1,0},{2,3},{3,2},{4,5},{5,4},{6,7},{7,6},{8,9},{9,8},{10,11... | collective-permute-start | bytes 786440 | tf_op jit(solution)/shard_map/ppermute | solution.py:593

commit v14 on v13

--- a/solution.py
+++ b/solution.py
@@ -676,7 +676,7 @@
     fine_quarter, coarse_kept, coarse_partial = tied(fine_quarter, coarse_kept, coarse_partial)
 
     pair_batch = lax.axis_size("batch") == 2
-    cut = 7 * HD // 4
+    cut = 6 * HD // 4
     halves = (coarse_partial[:cut], coarse_partial[cut:])
     others = [swapped(half, "batch", 1) if pair_batch else half for half in halves]
     masks = [1 << bit for bit in range(downs.bit_length() - 1)]
@@ -686,8 +686,8 @@
         coarse_kept = coarse_kept.reshape(2, -1, 2, count, D_C)
         come = swapped(narrow(coarse_kept[:, :, 1]), "gy", mask)
         coarse_kept = coarse_kept[:, :, 0] + wide(come)
-        at = min(turn, 1)
-        coarse_kept, others[at] = tied(coarse_kept, others[at])
+        if turn == 0:
+            coarse_kept, others[0] = tied(coarse_kept, others[0])
     coarse_kept = coarse_kept.reshape(2, count, D_C)
     come = swapped(narrow(coarse_kept[1]), "gx", 2)
     if pair_batch:

time: 59.9 us -> 59.2 us (0.988)
  waiting for transfers between devices: 15.6 us -> 14.8 us
    ppermute x19, waiting for transfers between devices: 15.6 us -> 14.8 us  [swapped(): lax.ppermute(value, axis, [(i, i ^ mask) for i in range(lax.axis_size(axi...]
where the time goes in v14:
time: 59.2 us; the launch traced here: 58.9 us
  starting transfers between devices  30 us (51%)
  waiting for transfers between devices  14.8 us (25%)
  Pallas kernels  9.73 us (16%)
  local copies, waits for them, and re-layouts  2.19 us (4%)
  between operations  1.67 us (3%)
    ppermute x19, starting transfers between devices, swapped(): lax.ppermute(value, axis, [(i, i ^ mask) for i in range(lax.axis_size(axi...  19.8 us
    ppermute x19, waiting for transfers between devices, swapped(): lax.ppermute(value, axis, [(i, i ^ mask) for i in range(lax.axis_size(axi...  14.8 us
    ppermute x2, starting transfers between devices, neighbours(): return (lax.ppermute(to_near, axis, near), from_far)  8.81 us
    pallas_call x1, Pallas kernels, fine_block(): pl.pallas_call(fine_body, out_shape=(jax.ShapeDtypeStruct((height, breadt...  4.33 us
    pallas_call x1, Pallas kernels, coarse_block(): pl.pallas_call(coarse_body, out_shape=(jax.ShapeDtypeStruct((count, D_C),...  2.23 us
    ppermute x2, starting transfers between devices, neighbours(): from_far = lax.ppermute(to_far, axis, far)  1.47 us
    pallas_call x1, Pallas kernels, near_step(): pl.pallas_call(near_body, out_shape=(jax.ShapeDtypeStruct((D_F, 3 * D_F),...  1.36 us
  transfers between devices with their start and end apart: 23, of which 10 were waited for; matrix products, arithmetic and copies ran while one was open for 1% of the time, Pallas kernels for 15%

profile of v14, /device:TPU:0, one launch (start us, length us, event | category | flops | bytes accessed | tf_op | source)
XLA Modules:
  0.0 58.9 jit_solution(10509489819899917060)
XLA Ops:
  0.6 1.0 %slice_bitcast_fusion.2 = (bf16[6,32,256]{2,1,0:T(8,128)(2,1)S(1)}, bf16[6,32,256]{2,1,0:T(8,128)(2,1)S(1)}) fusion(bf16[1,8,32,256]{3,2,1,0:T(8,128)(2,1)} %param.13), kind=kLoop, calls=%fused_computation.20 | loop fusion | bytes 393216 | tf_op jit(solution)/shard_map/slice | solution.py:419
  1.7 0.0 copy-start.6
  1.7 0.0 copy-start.7
  1.7 0.7 %collective-permute-start = (bf16[9,32,256]{2,1,0:T(8,128)(2,1)S(1)}, bf16[9,32,256]{2,1,0:T(8,128)(2,1)S(1)}, u32[]{:S(2)}, u32[]{:S(2)}) collective-permute-start(bf16[9,32,256]{2,1,0:T(8,128)(2,1)S(1)} %get-tuple-element.52.second), channel_id=1, source_target_pairs={{4,8},{8,4},{5,9},{9,5},{6,10},{10,6},{7,11},{11,7},{20,24},{24,20... | collective-permute-start | bytes 442376 | tf_op jit(solution)/shard_map/ppermute | solution.py:588
  2.4 5.9 %collective-permute-start.1 = (bf16[9,32,256]{2,1,0:T(8,128)(2,1)S(1)}, bf16[9,32,256]{2,1,0:T(8,128)(2,1)S(1)}, u32[]{:S(2)}, u32[]{:S(2)}) collective-permute-start(bf16[9,32,256]{2,1,0:T(8,128)(2,1)S(1)} %get-tuple-element.53.first), channel_id=1, source_target_pairs={{0,4},{4,0},{8,12},{12,8},{1,5},{5,1},{9,13},{13,9},{2,6},{6,2},{1... | collective-permute-start | bytes 442376 | tf_op jit(solution)/shard_map/ppermute | solution.py:589
  8.3 0.1 collective-permute-start.4
  8.4 1.9 %collective-permute-start.5 = (bf16[16,2048]{1,0:T(8,128)(2,1)S(1)}, bf16[16,2048]{1,0:T(8,128)(2,1)S(1)}, u32[]{:S(2)}, u32[]{:S(2)}) collective-permute-start(bf16[16,2048]{1,0:T(8,128)(2,1)S(1)} %pack_coarse.1), channel_id=1, source_target_pairs={{0,8},{4,12},{8,0},{12,4},{1,9},{5,13},{9,1},{13,5},{2,10},{6,14},... | collective-permute-start | bytes 196616 | tf_op jit(solution)/shard_map/ppermute | solution.py:593
  10.3 2.5 %collective-permute-start.6 = (bf16[16,2048]{1,0:T(8,128)(2,1)S(1)}, bf16[16,2048]{1,0:T(8,128)(2,1)S(1)}, u32[]{:S(2)}, u32[]{:S(2)}) collective-permute-start(bf16[16,2048]{1,0:T(8,128)(2,1)S(1)} %pack_coarse.1), channel_id=1, source_target_pairs={{0,12},{4,8},{8,4},{12,0},{1,13},{5,9},{9,5},{13,1},{2,14},{6,10},... | collective-permute-start | bytes 196616 | tf_op jit(solution)/shard_map/ppermute | solution.py:593
  13.4 0.0 collective-permute-done.row_far_ref
  13.5 0.0 collective-permute-done.1.row_near_ref
  13.5 0.0 copy-start.8
  13.5 0.0 copy-start.9
  13.5 0.0 copy-start.10
  13.5 0.0 copy-start.11
  13.5 0.1 col_edges.1
  13.6 0.0 copy-start.2
  13.6 0.8 %collective-permute-start.2 = (bf16[34,8,256]{2,1,0:T(8,128)(2,1)S(1)}, bf16[34,8,256]{2,1,0:T(8,128)(2,1)S(1)}, u32[]{:S(2)}, u32[]{:S(2)}) collective-permute-start(bf16[34,8,256]{2,1,0:T(8,128)(2,1)S(1)} %get-tuple-element.56), channel_id=1, source_target_pairs={{1,2},{2,1},{5,6},{6,5},{9,10},{10,9},{13,14},{14,13},{17,18},{18,... | collective-permute-start | bytes 417800 | tf_op jit(solution)/shard_map/ppermute | solution.py:588
  14.4 2.9 %collective-permute-start.3 = (bf16[34,8,256]{2,1,0:T(8,128)(2,1)S(1)}, bf16[34,8,256]{2,1,0:T(8,128)(2,1)S(1)}, u32[]{:S(2)}, u32[]{:S(2)}) collective-permute-start(bf16[34,8,256]{2,1,0:T(8,128)(2,1)S(1)} %get-tuple-element.57), channel_id=1, source_target_pairs={{0,1},{1,0},{2,3},{3,2},{4,5},{5,4},{6,7},{7,6},{8,9},{9,8},{10,11... | collective-permute-start | bytes 417800 | tf_op jit(solution)/shard_map/ppermute | solution.py:589
  17.4 0.1 time_factors.1
  17.4 0.0 collective-permute-done.4
  17.4 0.0 collective-permute-done.5
  17.4 0.0 copy-start.4
  17.5 1.4 %collective-permute-start.9 = (bf16[4,16,2048]{2,1,0:T(8,128)(2,1)S(1)}, bf16[4,16,2048]{2,1,0:T(8,128)(2,1)S(1)}, u32[]{:S(2)}, u32[]{:S(2)}) collective-permute-start(bf16[4,16,2048]{2,1,0:T(8,128)(2,1)S(1)} %pad_maximum_fusion.1), channel_id=1, source_target_pairs={{0,2},{1,3},{2,0},{3,1},{4,6},{5,7},{6,4},{7,5},{8,10},{9,11},{10,... | collective-permute-start | bytes 786440 | tf_op jit(solution)/shard_map/ppermute | solution.py:593
  18.9 0.0 collective-permute-done.3.col_near_ref
  18.9 4.3 %fine_block.1 = (bf16[8,32,256]{2,1,0:T(8,128)(2,1)}, f32[2,4,16,1024]{3,2,1,0:T(8,128)S(1)}, bf16[2,4,16,1024]{3,2,1,0:T(8,128)(2,1)S(1)}) custom-call(bf16[8,32,256]{2,1,0:T(8,128)(2,1)S(1)} %bitcast.60, bf16[8,32,256]{2,1,0:T(8,128)(2,1)S(1)} %bitcast.62, bf16[9,32,256]{2,1,0:T(8,128)(2,1)S(1)} %collective-permute-done.row_far_ref, ...), custom_call_target="tpu_custom_call" | custom-call | tf_op jit(solution)/shard_map/fine_block/pallas_call | solution.py:297
  23.2 1.1 %collective-permute-start.7 = (bf16[2,4,16,1024]{3,2,1,0:T(8,128)(2,1)S(1)}, bf16[2,4,16,1024]{3,2,1,0:T(8,128)(2,1)S(1)}, u32[]{:S(2)}, u32[]{:S(2)}) collective-permute-start(bf16[2,4,16,1024]{3,2,1,0:T(8,128)(2,1)S(1)} %get-tuple-element.71), channel_id=1, source_target_pairs={{0,1},{1,0},{2,3},{3,2},{4,5},{5,4},{6,7},{7,6},{8,9},{9,8},{10,11... | collective-permute-start | bytes 786440 | tf_op jit(solution)/shard_map/ppermute | solution.py:593
  24.3 1.5 %collective-permute-done.9 = bf16[4,16,2048]{2,1,0:T(8,128)(2,1)S(1)} collective-permute-done((bf16[4,16,2048]{2,1,0:T(8,128)(2,1)S(1)}, bf16[4,16,2048]{2,1,0:T(8,128)(2,1)S(1)}, u32[]{:S(2)}, u32[]{:S(2)}) %collective-permute-start.9) | collective-permute-done | bytes 262176 | tf_op jit(solution)/shard_map/ppermute | solution.py:593
  25.8 0.0 collective-permute-start.11
  25.8 0.0 collective-permute-done.7
  25.8 0.1 convert_add_fusion.1
  25.9 1.7 %collective-permute-start.8 = (bf16[4,16,1024]{2,1,0:T(8,128)(2,1)S(1)}, bf16[4,16,1024]{2,1,0:T(8,128)(2,1)S(1)}, u32[]{:S(2)}, u32[]{:S(2)}) collective-permute-start(bf16[4,16,1024]{2,1,0:T(8,128)(2,1)S(1)} %fusion.3), channel_id=1, source_target_pairs={{0,2},{1,3},{2,0},{3,1},{4,6},{5,7},{6,4},{7,5},{8,10},{9,11},{10,... | collective-permute-start | bytes 393224 | tf_op jit(solution)/shard_map/ppermute | solution.py:593
  27.7 0.0 collective-permute-done.10
  27.7 0.0 collective-permute-done.11
  27.7 0.1 pad_maximum_fusion
  27.8 0.0 copy-start.3
  27.8 0.0 copy-start.5
  27.8 0.1 fusion.8
  27.9 0.9 %copy-done.3 = bf16[3,64,1024]{2,1,0:T(8,128)(2,1)S(1)} copy-done((bf16[3,64,1024]{2,1,0:T(8,128)(2,1)S(1)}, bf16[3,64,1024]{2,1,0:T(8,128)(2,1)}, u32[]{:S(2)}) %copy-start.3) | copy-done | bytes 393240
  28.8 0.0 copy-done.5
  28.8 2.2 %coarse_block.1 = (bf16[256,1024]{1,0:T(8,128)(2,1)S(1)}, bf16[256,1024]{1,0:T(8,128)(2,1)S(1)}) custom-call(bf16[256,1024]{1,0:T(8,128)(2,1)S(1)} %get-tuple-element.99.x_ref, bf16[256,1024]{1,0:T(8,128)(2,1)S(1)} %get-tuple-element.98.dy_ref, f32[1,1024]{1,0:T(1,128)S(1)} %get-tuple-element.73.factor_ref, bf16[3,64,1024]{2,1,0:T(8,128)(2,1)S(1)} %copy-done.3, ...), custom_call_target="tpu_custom_call" | custom-call | tf_op jit(solution)/shard_map/coarse_block/pallas_call | solution.py:374
  31.1 0.8 %collective-permute-done.8 = bf16[4,16,1024]{2,1,0:T(8,128)(2,1)S(1)} collective-permute-done((bf16[4,16,1024]{2,1,0:T(8,128)(2,1)S(1)}, bf16[4,16,1024]{2,1,0:T(8,128)(2,1)S(1)}, u32[]{:S(2)}, u32[]{:S(2)}) %collective-permute-start.8) | collective-permute-done | bytes 131104 | tf_op jit(solution)/shard_map/ppermute | solution.py:593
  31.9 1.6 %collective-permute-start.12 = (bf16[4,16,1024]{2,1,0:T(8,128)(2,1)S(1)}, bf16[4,16,1024]{2,1,0:T(8,128)(2,1)S(1)}, u32[]{:S(2)}, u32[]{:S(2)}) collective-permute-start(bf16[4,16,1024]{2,1,0:T(8,128)(2,1)S(1)} %fusion.2), channel_id=1, source_target_pairs={{0,16},{16,0},{1,17},{17,1},{2,18},{18,2},{3,19},{19,3},{4,20},{20... | collective-permute-start | bytes 393224 | tf_op jit(solution)/shard_map/ppermute | solution.py:593
  33.6 0.1 collective-permute-start.13
  33.6 3.5 %collective-permute-done.12 = bf16[4,16,1024]{2,1,0:T(8,128)(2,1)S(1)} collective-permute-done((bf16[4,16,1024]{2,1,0:T(8,128)(2,1)S(1)}, bf16[4,16,1024]{2,1,0:T(8,128)(2,1)S(1)}, u32[]{:S(2)}, u32[]{:S(2)}) %collective-permute-start.12) | collective-permute-done | bytes 131104 | tf_op jit(solution)/shard_map/ppermute | solution.py:593
  37.2 0.1 convert_add_fusion
  37.3 1.7 %collective-permute-start.14 = (bf16[64,1024]{1,0:T(8,128)(2,1)S(1)}, bf16[64,1024]{1,0:T(8,128)(2,1)S(1)}, u32[]{:S(2)}, u32[]{:S(2)}) collective-permute-start(bf16[64,1024]{1,0:T(8,128)(2,1)S(1)} %bitcast.76), channel_id=1, source_target_pairs={{0,4},{4,0},{8,12},{12,8},{1,5},{5,1},{9,13},{13,9},{2,6},{6,2},{1... | collective-permute-start | bytes 393224 | tf_op jit(solution)/shard_map/ppermute | solution.py:593
  39.0 0.5 collective-permute-start.17
  39.5 1.5 %collective-permute-start.18 = (bf16[96,1024]{1,0:T(8,128)(2,1)S(1)}, bf16[96,1024]{1,0:T(8,128)(2,1)S(1)}, u32[]{:S(2)}, u32[]{:S(2)}) collective-permute-start(bf16[96,1024]{1,0:T(8,128)(2,1)S(1)} %slice.90), channel_id=1, source_target_pairs={{0,16},{16,0},{1,17},{17,1},{2,18},{18,2},{3,19},{19,3},{4,20},{20... | collective-permute-start | bytes 589832 | tf_op jit(solution)/shard_map/ppermute | solution.py:593
  41.0 0.5 collective-permute-start.21
  41.5 1.5 %collective-permute-done.14 = bf16[64,1024]{1,0:T(8,128)(2,1)S(1)} collective-permute-done((bf16[64,1024]{1,0:T(8,128)(2,1)S(1)}, bf16[64,1024]{1,0:T(8,128)(2,1)S(1)}, u32[]{:S(2)}, u32[]{:S(2)}) %collective-permute-start.14) | collective-permute-done | bytes 131104 | tf_op jit(solution)/shard_map/ppermute | solution.py:593
  43.0 1.5 %collective-permute-start.15 = (bf16[64,1024]{1,0:T(8,128)(2,1)S(1)}, bf16[64,1024]{1,0:T(8,128)(2,1)S(1)}, u32[]{:S(2)}, u32[]{:S(2)}) collective-permute-start(bf16[64,1024]{1,0:T(8,128)(2,1)S(1)} %add_convert_fusion.1), channel_id=1, source_target_pairs={{0,8},{4,12},{8,0},{12,4},{1,9},{5,13},{9,1},{13,5},{2,10},{6,14},... | collective-permute-start | bytes 393224 | tf_op jit(solution)/shard_map/ppermute | solution.py:593
  44.6 1.2 %collective-permute-done.17 = bf16[2,2,16,1024]{3,2,0,1:T(8,128)(2,1)S(1)} collective-permute-done((bf16[2,2,16,1024]{3,2,0,1:T(8,128)(2,1)S(1)}, bf16[2,2,16,1024]{3,2,0,1:T(8,128)(2,1)S(1)}, u32[]{:S(2)}, u32[]{:S(2)}) %collective-permute-start.17) | collective-permute-done | bytes 131104 | tf_op jit(solution)/shard_map/ppermute | solution.py:593
  45.9 1.5 %collective-permute-done.18.refs_0_ = bf16[96,1024]{1,0:T(8,128)(2,1)S(1)} collective-permute-done((bf16[96,1024]{1,0:T(8,128)(2,1)S(1)}, bf16[96,1024]{1,0:T(8,128)(2,1)S(1)}, u32[]{:S(2)}, u32[]{:S(2)}) %collective-permute-start.18) | collective-permute-done | bytes 196640 | tf_op jit(solution)/shard_map/ppermute | solution.py:593
  47.3 1.5 %collective-permute-start.19 = (bf16[2,1,16,1024]{3,2,1,0:T(8,128)(2,1)S(1)}, bf16[2,1,16,1024]{3,2,1,0:T(8,128)(2,1)S(1)}, u32[]{:S(2)}, u32[]{:S(2)}) collective-permute-start(bf16[2,1,16,1024]{3,2,1,0:T(8,128)(2,1)S(1)} %fusion.6), channel_id=1, source_target_pairs={{0,8},{4,12},{8,0},{12,4},{1,9},{5,13},{9,1},{13,5},{2,10},{6,14},... | collective-permute-start | bytes 196616 | tf_op jit(solution)/shard_map/ppermute | solution.py:593
  48.9 2.1 %collective-permute-done.15 = bf16[64,1024]{1,0:T(8,128)(2,1)S(1)} collective-permute-done((bf16[64,1024]{1,0:T(8,128)(2,1)S(1)}, bf16[64,1024]{1,0:T(8,128)(2,1)S(1)}, u32[]{:S(2)}, u32[]{:S(2)}) %collective-permute-start.15) | collective-permute-done | bytes 131104 | tf_op jit(solution)/shard_map/ppermute | solution.py:593
  51.0 0.8 %collective-permute-start.16 = (bf16[64,1024]{1,0:T(8,128)(2,1)S(1)}, bf16[64,1024]{1,0:T(8,128)(2,1)S(1)}, u32[]{:S(2)}, u32[]{:S(2)}) collective-permute-start(bf16[64,1024]{1,0:T(8,128)(2,1)S(1)} %add_convert_fusion), channel_id=1, source_target_pairs={{0,2},{1,3},{2,0},{3,1},{4,6},{5,7},{6,4},{7,5},{8,10},{9,11},{10,... | collective-permute-start | bytes 393224 | tf_op jit(solution)/shard_map/ppermute | solution.py:593
  51.8 0.8 %collective-permute-done.19 = bf16[2,1,16,1024]{3,2,1,0:T(8,128)(2,1)S(1)} collective-permute-done((bf16[2,1,16,1024]{3,2,1,0:T(8,128)(2,1)S(1)}, bf16[2,1,16,1024]{3,2,1,0:T(8,128)(2,1)S(1)}, u32[]{:S(2)}, u32[]{:S(2)}) %collective-permute-start.19) | collective-permute-done | bytes 65568 | tf_op jit(solution)/shard_map/ppermute | solution.py:593
  52.6 1.3 %collective-permute-start.20 = (bf16[16,1024]{1,0:T(8,128)(2,1)S(1)}, bf16[16,1024]{1,0:T(8,128)(2,1)S(1)}, u32[]{:S(2)}, u32[]{:S(2)}) collective-permute-start(bf16[16,1024]{1,0:T(8,128)(2,1)S(1)} %fusion.7), channel_id=1, source_target_pairs={{0,2},{1,3},{2,0},{3,1},{4,6},{5,7},{6,4},{7,5},{8,10},{9,11},{10,... | collective-permute-start | bytes 98312 | tf_op jit(solution)/shard_map/ppermute | solution.py:593
  53.9 0.9 %pair_sum.1 = (bf16[3,64,1024]{2,1,0:T(8,128)(2,1)}, bf16[64,1024]{1,0:T(8,128)(2,1)}) custom-call(bf16[256,1024]{1,0:T(8,128)(2,1)S(1)} %get-tuple-element.81.own, bf16[96,1024]{1,0:T(8,128)(2,1)S(1)} %collective-permute-done.18.refs_0_, bf16[160,1024]{1,0:T(8,128)(2,1)S(1)} %collective-permute-done.21.refs_1_), custom_call_target="tpu_custom_call" | custom-call | tf_op jit(solution)/shard_map/pair_sum/pallas_call | solution.py:502
  54.8 1.8 %collective-permute-done.20.come_ref = bf16[16,1024]{1,0:T(8,128)(2,1)S(1)} collective-permute-done((bf16[16,1024]{1,0:T(8,128)(2,1)S(1)}, bf16[16,1024]{1,0:T(8,128)(2,1)S(1)}, u32[]{:S(2)}, u32[]{:S(2)}) %collective-permute-start.20) | collective-permute-done | bytes 32800 | tf_op jit(solution)/shard_map/ppermute | solution.py:593
  56.6 0.1 collective-permute-start.22
  56.7 1.4 %near_step.1 = (bf16[256,768]{1,0:T(8,128)(2,1)}, bf16[256,256]{1,0:T(8,128)(2,1)}, bf16[4,4,1024]{2,1,0:T(4,128)(2,1)}) custom-call(bf16[2,64,1024]{2,1,0:T(8,128)(2,1)S(1)} %pad_maximum_fusion.2.near_ref, bf16[4,4,1024]{2,1,0:T(4,128)(2,1)S(1)} %bitcast.65, f32[1,1024]{1,0:T(1,128)S(1)} %get-tuple-element.73.factor_ref, ...), custom_call_target="tpu_custom_call" | custom-call | tf_op jit(solution)/shard_map/near_step/pallas_call | solution.py:551
  58.1 0.1 collective-permute-done.22.far_ref
  58.2 0.7 %far_step.1 = (bf16[256,768]{1,0:T(8,128)(2,1)}, bf16[256,256]{1,0:T(8,128)(2,1)}) custom-call(bf16[2,64,1024]{2,1,0:T(8,128)(2,1)S(1)} %collective-permute-done.22.far_ref, bf16[256,768]{1,0:T(8,128)(2,1)} %get-tuple-element.92.qkv_in, bf16[256,256]{1,0:T(8,128)(2,1)} %get-tuple-element.93.out_in), custom_call_target="tpu_custom_call", output_to_operand_aliasing={{0}: (1, {}), {1}: (2, {})} | custom-call | tf_op jit(solution)/shard_map/far_step/pallas_call | solution.py:569
  (37 shorter events, 0.5 us)
Async XLA Ops:
  0.6 1.0 %copy-start.1 = (bf16[1,8,32,256]{3,2,1,0:T(8,128)(2,1)S(1)}, bf16[1,8,32,256]{3,2,1,0:T(8,128)(2,1)}, u32[]{:S(2)}) copy-start(bf16[1,8,32,256]{3,2,1,0:T(8,128)(2,1)} %param.14) | copy-start | bytes 393220
  1.7 6.7 %copy-start.6 = (bf16[1,4,4,1024]{3,2,1,0:T(4,128)(2,1)S(1)}, bf16[1,4,4,1024]{3,2,1,0:T(4,128)(2,1)}, u32[]{:S(2)}) copy-start(bf16[1,4,4,1024]{3,2,1,0:T(4,128)(2,1)} %param.15) | copy-start | bytes 98308
  1.7 6.6 %copy-start.7 = (bf16[1,4,4,1024]{3,2,1,0:T(4,128)(2,1)S(1)}, bf16[1,4,4,1024]{3,2,1,0:T(4,128)(2,1)}, u32[]{:S(2)}) copy-start(bf16[1,4,4,1024]{3,2,1,0:T(4,128)(2,1)} %param.16) | copy-start | bytes 98308
  1.7 11.7 %collective-permute-start = (bf16[9,32,256]{2,1,0:T(8,128)(2,1)S(1)}, bf16[9,32,256]{2,1,0:T(8,128)(2,1)S(1)}, u32[]{:S(2)}, u32[]{:S(2)}) collective-permute-start(bf16[9,32,256]{2,1,0:T(8,128)(2,1)S(1)} %get-tuple-element.52.second), channel_id=1, source_target_pairs={{4,8},{8,4},{5,9},{9,5},{6,10},{10,6},{7,11},{11,7},{20,24},{24,20... | collective-permute-start | bytes 442376 | tf_op jit(solution)/shard_map/ppermute | solution.py:588
  2.4 11.0 %collective-permute-start.1 = (bf16[9,32,256]{2,1,0:T(8,128)(2,1)S(1)}, bf16[9,32,256]{2,1,0:T(8,128)(2,1)S(1)}, u32[]{:S(2)}, u32[]{:S(2)}) collective-permute-start(bf16[9,32,256]{2,1,0:T(8,128)(2,1)S(1)} %get-tuple-element.53.first), channel_id=1, source_target_pairs={{0,4},{4,0},{8,12},{12,8},{1,5},{5,1},{9,13},{13,9},{2,6},{6,2},{1... | collective-permute-start | bytes 442376 | tf_op jit(solution)/shard_map/ppermute | solution.py:589
  8.3 5.1 %copy-start = (bf16[1,8,32,256]{3,2,1,0:T(8,128)(2,1)S(1)}, bf16[1,8,32,256]{3,2,1,0:T(8,128)(2,1)}, u32[]{:S(2)}) copy-start(bf16[1,8,32,256]{3,2,1,0:T(8,128)(2,1)} %param.13) | copy-start | bytes 393220
  8.3 9.1 %collective-permute-start.4 = (bf16[16,2048]{1,0:T(8,128)(2,1)S(1)}, bf16[16,2048]{1,0:T(8,128)(2,1)S(1)}, u32[]{:S(2)}, u32[]{:S(2)}) collective-permute-start(bf16[16,2048]{1,0:T(8,128)(2,1)S(1)} %pack_coarse.1), channel_id=1, source_target_pairs={{0,4},{4,0},{8,12},{12,8},{1,5},{5,1},{9,13},{13,9},{2,6},{6,2},{1... | collective-permute-start | bytes 196616 | tf_op jit(solution)/shard_map/ppermute | solution.py:593
  8.4 9.0 %collective-permute-start.5 = (bf16[16,2048]{1,0:T(8,128)(2,1)S(1)}, bf16[16,2048]{1,0:T(8,128)(2,1)S(1)}, u32[]{:S(2)}, u32[]{:S(2)}) collective-permute-start(bf16[16,2048]{1,0:T(8,128)(2,1)S(1)} %pack_coarse.1), channel_id=1, source_target_pairs={{0,8},{4,12},{8,0},{12,4},{1,9},{5,13},{9,1},{13,5},{2,10},{6,14},... | collective-permute-start | bytes 196616 | tf_op jit(solution)/shard_map/ppermute | solution.py:593
  10.3 7.1 %collective-permute-start.6 = (bf16[16,2048]{1,0:T(8,128)(2,1)S(1)}, bf16[16,2048]{1,0:T(8,128)(2,1)S(1)}, u32[]{:S(2)}, u32[]{:S(2)}) collective-permute-start(bf16[16,2048]{1,0:T(8,128)(2,1)S(1)} %pack_coarse.1), channel_id=1, source_target_pairs={{0,12},{4,8},{8,4},{12,0},{1,13},{5,9},{9,5},{13,1},{2,14},{6,10},... | collective-permute-start | bytes 196616 | tf_op jit(solution)/shard_map/ppermute | solution.py:593
  13.5 3.9 %copy-start.8 = (f32[1024]{0:T(1024)S(1)}, f32[1024]{0:T(1024)}, u32[]{:S(2)}) copy-start(f32[1024]{0:T(1024)} %param.19) | copy-start | bytes 12292
  13.5 3.9 %copy-start.9 = (f32[1,1024]{1,0:T(1,128)S(1)}, f32[1,1024]{1,0:T(1,128)}, u32[]{:S(2)}) copy-start(f32[1,1024]{1,0:T(1,128)} %constant.5.clone.coarse_freq) | copy-start | bytes 12292
  13.5 3.8 %copy-start.10 = (f32[256]{0:T(256)S(1)}, f32[256]{0:T(256)}, u32[]{:S(2)}) copy-start(f32[256]{0:T(256)} %param.18) | copy-start | bytes 3076
  13.5 3.8 %copy-start.11 = (f32[1,256]{1,0:T(1,128)S(1)}, f32[1,256]{1,0:T(1,128)}, u32[]{:S(2)}) copy-start(f32[1,256]{1,0:T(1,128)} %constant.4.clone.fine_freq) | copy-start | bytes 3076
  13.6 5.3 %copy-start.2 = (bf16[256,768]{1,0:T(8,128)(2,1)S(1)}, bf16[256,768]{1,0:T(8,128)(2,1)}, u32[]{:S(2)}) copy-start(bf16[256,768]{1,0:T(8,128)(2,1)} %qkv_ref.1) | copy-start | bytes 1179652
  13.6 5.2 %collective-permute-start.2 = (bf16[34,8,256]{2,1,0:T(8,128)(2,1)S(1)}, bf16[34,8,256]{2,1,0:T(8,128)(2,1)S(1)}, u32[]{:S(2)}, u32[]{:S(2)}) collective-permute-start(bf16[34,8,256]{2,1,0:T(8,128)(2,1)S(1)} %get-tuple-element.56), channel_id=1, source_target_pairs={{1,2},{2,1},{5,6},{6,5},{9,10},{10,9},{13,14},{14,13},{17,18},{18,... | collective-permute-start | bytes 417800 | tf_op jit(solution)/shard_map/ppermute | solution.py:588
  14.4 4.4 %collective-permute-start.3 = (bf16[34,8,256]{2,1,0:T(8,128)(2,1)S(1)}, bf16[34,8,256]{2,1,0:T(8,128)(2,1)S(1)}, u32[]{:S(2)}, u32[]{:S(2)}) collective-permute-start(bf16[34,8,256]{2,1,0:T(8,128)(2,1)S(1)} %get-tuple-element.57), channel_id=1, source_target_pairs={{0,1},{1,0},{2,3},{3,2},{4,5},{5,4},{6,7},{7,6},{8,9},{9,8},{10,11... | collective-permute-start | bytes 417800 | tf_op jit(solution)/shard_map/ppermute | solution.py:589
  17.4 1.4 %copy-start.4 = (bf16[256,256]{1,0:T(8,128)(2,1)S(1)}, bf16[256,256]{1,0:T(8,128)(2,1)}, u32[]{:S(2)}) copy-start(bf16[256,256]{1,0:T(8,128)(2,1)} %out_ref.1) | copy-start | bytes 393220
  17.5 8.3 %collective-permute-start.9 = (bf16[4,16,2048]{2,1,0:T(8,128)(2,1)S(1)}, bf16[4,16,2048]{2,1,0:T(8,128)(2,1)S(1)}, u32[]{:S(2)}, u32[]{:S(2)}) collective-permute-start(bf16[4,16,2048]{2,1,0:T(8,128)(2,1)S(1)} %pad_maximum_fusion.1), channel_id=1, source_target_pairs={{0,2},{1,3},{2,0},{3,1},{4,6},{5,7},{6,4},{7,5},{8,10},{9,11},{10,... | collective-permute-start | bytes 786440 | tf_op jit(solution)/shard_map/ppermute | solution.py:593
  23.2 2.6 %collective-permute-start.7 = (bf16[2,4,16,1024]{3,2,1,0:T(8,128)(2,1)S(1)}, bf16[2,4,16,1024]{3,2,1,0:T(8,128)(2,1)S(1)}, u32[]{:S(2)}, u32[]{:S(2)}) collective-permute-start(bf16[2,4,16,1024]{3,2,1,0:T(8,128)(2,1)S(1)} %get-tuple-element.71), channel_id=1, source_target_pairs={{0,1},{1,0},{2,3},{3,2},{4,5},{5,4},{6,7},{7,6},{8,9},{9,8},{10,11... | collective-permute-start | bytes 786440 | tf_op jit(solution)/shard_map/ppermute | solution.py:593
  24.3 3.3 %collective-permute-start.10 = (bf16[4,16,2048]{2,1,0:T(8,128)(2,1)S(1)}, bf16[4,16,2048]{2,1,0:T(8,128)(2,1)S(1)}, u32[]{:S(2)}, u32[]{:S(2)}) collective-permute-start(bf16[4,16,2048]{2,1,0:T(8,128)(2,1)S(1)} %pad_maximum_fusion.1), channel_id=1, source_target_pairs={{0,1},{1,0},{2,3},{3,2},{4,5},{5,4},{6,7},{7,6},{8,9},{9,8},{10,11... | collective-permute-start | bytes 786440 | tf_op jit(solution)/shard_map/ppermute | solution.py:593
  25.8 1.8 %collective-permute-start.11 = (bf16[4,16,2048]{2,1,0:T(8,128)(2,1)S(1)}, bf16[4,16,2048]{2,1,0:T(8,128)(2,1)S(1)}, u32[]{:S(2)}, u32[]{:S(2)}) collective-permute-start(bf16[4,16,2048]{2,1,0:T(8,128)(2,1)S(1)} %collective-permute-done.9), channel_id=1, source_target_pairs={{0,1},{1,0},{2,3},{3,2},{4,5},{5,4},{6,7},{7,6},{8,9},{9,8},{10,11... | collective-permute-start | bytes 786440 | tf_op jit(solution)/shard_map/ppermute | solution.py:593
  25.9 6.0 %collective-permute-start.8 = (bf16[4,16,1024]{2,1,0:T(8,128)(2,1)S(1)}, bf16[4,16,1024]{2,1,0:T(8,128)(2,1)S(1)}, u32[]{:S(2)}, u32[]{:S(2)}) collective-permute-start(bf16[4,16,1024]{2,1,0:T(8,128)(2,1)S(1)} %fusion.3), channel_id=1, source_target_pairs={{0,2},{1,3},{2,0},{3,1},{4,6},{5,7},{6,4},{7,5},{8,10},{9,11},{10,... | collective-permute-start | bytes 393224 | tf_op jit(solution)/shard_map/ppermute | solution.py:593
  27.8 1.0 %copy-start.3 = (bf16[3,64,1024]{2,1,0:T(8,128)(2,1)S(1)}, bf16[3,64,1024]{2,1,0:T(8,128)(2,1)}, u32[]{:S(2)}) copy-start(bf16[3,64,1024]{2,1,0:T(8,128)(2,1)} %qkv_hbm.1) | copy-start | bytes 1179652
  27.8 1.0 %copy-start.5 = (bf16[64,1024]{1,0:T(8,128)(2,1)S(1)}, bf16[64,1024]{1,0:T(8,128)(2,1)}, u32[]{:S(2)}) copy-start(bf16[64,1024]{1,0:T(8,128)(2,1)} %out_hbm.1) | copy-start | bytes 393220
  31.9 5.2 %collective-permute-start.12 = (bf16[4,16,1024]{2,1,0:T(8,128)(2,1)S(1)}, bf16[4,16,1024]{2,1,0:T(8,128)(2,1)S(1)}, u32[]{:S(2)}, u32[]{:S(2)}) collective-permute-start(bf16[4,16,1024]{2,1,0:T(8,128)(2,1)S(1)} %fusion.2), channel_id=1, source_target_pairs={{0,16},{16,0},{1,17},{17,1},{2,18},{18,2},{3,19},{19,3},{4,20},{20... | collective-permute-start | bytes 393224 | tf_op jit(solution)/shard_map/ppermute | solution.py:593
  33.6 3.6 %collective-permute-start.13 = (bf16[2,4,16,1024]{3,2,1,0:T(8,128)(2,1)S(1)}, bf16[2,4,16,1024]{3,2,1,0:T(8,128)(2,1)S(1)}, u32[]{:S(2)}, u32[]{:S(2)}) collective-permute-start(bf16[2,4,16,1024]{3,2,1,0:T(8,128)(2,1)S(1)} %bitcast.79), channel_id=1, source_target_pairs={{0,1},{1,0},{2,3},{3,2},{4,5},{5,4},{6,7},{7,6},{8,9},{9,8},{10,11... | collective-permute-start | bytes 786440 | tf_op jit(solution)/shard_map/ppermute | solution.py:593
  37.3 5.7 %collective-permute-start.14 = (bf16[64,1024]{1,0:T(8,128)(2,1)S(1)}, bf16[64,1024]{1,0:T(8,128)(2,1)S(1)}, u32[]{:S(2)}, u32[]{:S(2)}) collective-permute-start(bf16[64,1024]{1,0:T(8,128)(2,1)S(1)} %bitcast.76), channel_id=1, source_target_pairs={{0,4},{4,0},{8,12},{12,8},{1,5},{5,1},{9,13},{13,9},{2,6},{6,2},{1... | collective-permute-start | bytes 393224 | tf_op jit(solution)/shard_map/ppermute | solution.py:593
  39.0 6.8 %collective-permute-start.17 = (bf16[2,2,16,1024]{3,2,0,1:T(8,128)(2,1)S(1)}, bf16[2,2,16,1024]{3,2,0,1:T(8,128)(2,1)S(1)}, u32[]{:S(2)}, u32[]{:S(2)}) collective-permute-start(bf16[2,2,16,1024]{3,2,0,1:T(8,128)(2,1)S(1)} %fusion.4), channel_id=1, source_target_pairs={{0,4},{4,0},{8,12},{12,8},{1,5},{5,1},{9,13},{13,9},{2,6},{6,2},{1... | collective-permute-start | bytes 393224 | tf_op jit(solution)/shard_map/ppermute | solution.py:593
  39.5 7.8 %collective-permute-start.18 = (bf16[96,1024]{1,0:T(8,128)(2,1)S(1)}, bf16[96,1024]{1,0:T(8,128)(2,1)S(1)}, u32[]{:S(2)}, u32[]{:S(2)}) collective-permute-start(bf16[96,1024]{1,0:T(8,128)(2,1)S(1)} %slice.90), channel_id=1, source_target_pairs={{0,16},{16,0},{1,17},{17,1},{2,18},{18,2},{3,19},{19,3},{4,20},{20... | collective-permute-start | bytes 589832 | tf_op jit(solution)/shard_map/ppermute | solution.py:593
  41.0 12.9 %collective-permute-start.21 = (bf16[160,1024]{1,0:T(8,128)(2,1)S(1)}, bf16[160,1024]{1,0:T(8,128)(2,1)S(1)}, u32[]{:S(2)}, u32[]{:S(2)}) collective-permute-start(bf16[160,1024]{1,0:T(8,128)(2,1)S(1)} %slice.94), channel_id=1, source_target_pairs={{0,16},{16,0},{1,17},{17,1},{2,18},{18,2},{3,19},{19,3},{4,20},{20... | collective-permute-start | bytes 983048 | tf_op jit(solution)/shard_map/ppermute | solution.py:593
  43.0 7.9 %collective-permute-start.15 = (bf16[64,1024]{1,0:T(8,128)(2,1)S(1)}, bf16[64,1024]{1,0:T(8,128)(2,1)S(1)}, u32[]{:S(2)}, u32[]{:S(2)}) collective-permute-start(bf16[64,1024]{1,0:T(8,128)(2,1)S(1)} %add_convert_fusion.1), channel_id=1, source_target_pairs={{0,8},{4,12},{8,0},{12,4},{1,9},{5,13},{9,1},{13,5},{2,10},{6,14},... | collective-permute-start | bytes 393224 | tf_op jit(solution)/shard_map/ppermute | solution.py:593
  47.3 5.2 %collective-permute-start.19 = (bf16[2,1,16,1024]{3,2,1,0:T(8,128)(2,1)S(1)}, bf16[2,1,16,1024]{3,2,1,0:T(8,128)(2,1)S(1)}, u32[]{:S(2)}, u32[]{:S(2)}) collective-permute-start(bf16[2,1,16,1024]{3,2,1,0:T(8,128)(2,1)S(1)} %fusion.6), channel_id=1, source_target_pairs={{0,8},{4,12},{8,0},{12,4},{1,9},{5,13},{9,1},{13,5},{2,10},{6,14},... | collective-permute-start | bytes 196616 | tf_op jit(solution)/shard_map/ppermute | solution.py:593
  51.0 5.6 %collective-permute-start.16 = (bf16[64,1024]{1,0:T(8,128)(2,1)S(1)}, bf16[64,1024]{1,0:T(8,128)(2,1)S(1)}, u32[]{:S(2)}, u32[]{:S(2)}) collective-permute-start(bf16[64,1024]{1,0:T(8,128)(2,1)S(1)} %add_convert_fusion), channel_id=1, source_target_pairs={{0,2},{1,3},{2,0},{3,1},{4,6},{5,7},{6,4},{7,5},{8,10},{9,11},{10,... | collective-permute-start | bytes 393224 | tf_op jit(solution)/shard_map/ppermute | solution.py:593
  52.6 4.0 %collective-permute-start.20 = (bf16[16,1024]{1,0:T(8,128)(2,1)S(1)}, bf16[16,1024]{1,0:T(8,128)(2,1)S(1)}, u32[]{:S(2)}, u32[]{:S(2)}) collective-permute-start(bf16[16,1024]{1,0:T(8,128)(2,1)S(1)} %fusion.7), channel_id=1, source_target_pairs={{0,2},{1,3},{2,0},{3,1},{4,6},{5,7},{6,4},{7,5},{8,10},{9,11},{10,... | collective-permute-start | bytes 98312 | tf_op jit(solution)/shard_map/ppermute | solution.py:593
  56.6 1.6 %collective-permute-start.22 = (bf16[2,64,1024]{2,1,0:T(8,128)(2,1)S(1)}, bf16[2,64,1024]{2,1,0:T(8,128)(2,1)S(1)}, u32[]{:S(2)}, u32[]{:S(2)}) collective-permute-start(bf16[2,64,1024]{2,1,0:T(8,128)(2,1)S(1)} %pad_maximum_fusion.2.near_ref), channel_id=1, source_target_pairs={{0,1},{1,0},{2,3},{3,2},{4,5},{5,4},{6,7},{7,6},{8,9},{9,8},{10,11... | collective-permute-start | bytes 786440 | tf_op jit(solution)/shard_map/ppermute | solution.py:593

commit v15 on v14

--- a/solution.py
+++ b/solution.py
@@ -686,8 +686,6 @@
         coarse_kept = coarse_kept.reshape(2, -1, 2, count, D_C)
         come = swapped(narrow(coarse_kept[:, :, 1]), "gy", mask)
         coarse_kept = coarse_kept[:, :, 0] + wide(come)
-        if turn == 0:
-            coarse_kept, others[0] = tied(coarse_kept, others[0])
     coarse_kept = coarse_kept.reshape(2, count, D_C)
     come = swapped(narrow(coarse_kept[1]), "gx", 2)
     if pair_batch:

time: 59.2 us -> 61.1 us (1.032)
  waiting for transfers between devices: 14.8 us -> 16.9 us
    ppermute x19, waiting for transfers between devices: 14.8 us -> 16.9 us  [swapped(): lax.ppermute(value, axis, [(i, i ^ mask) for i in range(lax.axis_size(axi...]
  transfers between devices with their start and end apart: 23 -> 23, of which waited for: 10 -> 9; matrix products, arithmetic and copies ran while one was open for 1% -> 1% of each run, Pallas kernels for 15% -> 15%
where the time goes in v15:
time: 61.1 us; the launch traced here: 60.8 us
  starting transfers between devices  29.9 us (49%)
  waiting for transfers between devices  16.9 us (28%)
  Pallas kernels  9.73 us (16%)
  local copies, waits for them, and re-layouts  2.19 us (4%)
  between operations  1.68 us (3%)
    ppermute x19, starting transfers between devices, swapped(): lax.ppermute(value, axis, [(i, i ^ mask) for i in range(lax.axis_size(axi...  19.6 us
    ppermute x19, waiting for transfers between devices, swapped(): lax.ppermute(value, axis, [(i, i ^ mask) for i in range(lax.axis_size(axi...  16.9 us
    ppermute x2, starting transfers between devices, neighbours(): return (lax.ppermute(to_near, axis, near), from_far)  8.81 us
    pallas_call x1, Pallas kernels, fine_block(): pl.pallas_call(fine_body, out_shape=(jax.ShapeDtypeStruct((height, breadt...  4.33 us
    pallas_call x1, Pallas kernels, coarse_block(): pl.pallas_call(coarse_body, out_shape=(jax.ShapeDtypeStruct((count, D_C),...  2.23 us
    ppermute x2, starting transfers between devices, neighbours(): from_far = lax.ppermute(to_far, axis, far)  1.47 us
    pallas_call x1, Pallas kernels, near_step(): pl.pallas_call(near_body, out_shape=(jax.ShapeDtypeStruct((D_F, 3 * D_F),...  1.36 us
  transfers between devices with their start and end apart: 23, of which 9 were waited for; matrix products, arithmetic and copies ran while one was open for 1% of the time, Pallas kernels for 15%

profile of v15, /device:TPU:0, one launch (start us, length us, event | category | flops | bytes accessed | tf_op | source)
XLA Modules:
  0.0 60.8 jit_solution(5789731505170019195)
XLA Ops:
  0.6 1.0 %slice_bitcast_fusion.2 = (bf16[6,32,256]{2,1,0:T(8,128)(2,1)S(1)}, bf16[6,32,256]{2,1,0:T(8,128)(2,1)S(1)}) fusion(bf16[1,8,32,256]{3,2,1,0:T(8,128)(2,1)} %param.13), kind=kLoop, calls=%fused_computation.21 | loop fusion | bytes 393216 | tf_op jit(solution)/shard_map/slice | solution.py:419
  1.7 0.0 copy-start.6
  1.7 0.0 copy-start.7
  1.7 0.7 %collective-permute-start = (bf16[9,32,256]{2,1,0:T(8,128)(2,1)S(1)}, bf16[9,32,256]{2,1,0:T(8,128)(2,1)S(1)}, u32[]{:S(2)}, u32[]{:S(2)}) collective-permute-start(bf16[9,32,256]{2,1,0:T(8,128)(2,1)S(1)} %get-tuple-element.50.second), channel_id=1, source_target_pairs={{4,8},{8,4},{5,9},{9,5},{6,10},{10,6},{7,11},{11,7},{20,24},{24,20... | collective-permute-start | bytes 442376 | tf_op jit(solution)/shard_map/ppermute | solution.py:588
  2.4 5.9 %collective-permute-start.1 = (bf16[9,32,256]{2,1,0:T(8,128)(2,1)S(1)}, bf16[9,32,256]{2,1,0:T(8,128)(2,1)S(1)}, u32[]{:S(2)}, u32[]{:S(2)}) collective-permute-start(bf16[9,32,256]{2,1,0:T(8,128)(2,1)S(1)} %get-tuple-element.51.first), channel_id=1, source_target_pairs={{0,4},{4,0},{8,12},{12,8},{1,5},{5,1},{9,13},{13,9},{2,6},{6,2},{1... | collective-permute-start | bytes 442376 | tf_op jit(solution)/shard_map/ppermute | solution.py:589
  8.3 0.1 collective-permute-start.4
  8.4 1.9 %collective-permute-start.5 = (bf16[16,2048]{1,0:T(8,128)(2,1)S(1)}, bf16[16,2048]{1,0:T(8,128)(2,1)S(1)}, u32[]{:S(2)}, u32[]{:S(2)}) collective-permute-start(bf16[16,2048]{1,0:T(8,128)(2,1)S(1)} %pack_coarse.1), channel_id=1, source_target_pairs={{0,8},{4,12},{8,0},{12,4},{1,9},{5,13},{9,1},{13,5},{2,10},{6,14},... | collective-permute-start | bytes 196616 | tf_op jit(solution)/shard_map/ppermute | solution.py:593
  10.3 2.5 %collective-permute-start.6 = (bf16[16,2048]{1,0:T(8,128)(2,1)S(1)}, bf16[16,2048]{1,0:T(8,128)(2,1)S(1)}, u32[]{:S(2)}, u32[]{:S(2)}) collective-permute-start(bf16[16,2048]{1,0:T(8,128)(2,1)S(1)} %pack_coarse.1), channel_id=1, source_target_pairs={{0,12},{4,8},{8,4},{12,0},{1,13},{5,9},{9,5},{13,1},{2,14},{6,10},... | collective-permute-start | bytes 196616 | tf_op jit(solution)/shard_map/ppermute | solution.py:593
  13.4 0.0 collective-permute-done.row_far_ref
  13.5 0.0 collective-permute-done.1.row_near_ref
  13.5 0.0 copy-start.8
  13.5 0.0 copy-start.9
  13.5 0.0 copy-start.10
  13.5 0.0 copy-start.11
  13.5 0.1 col_edges.1
  13.6 0.0 copy-start.2
  13.6 0.8 %collective-permute-start.2 = (bf16[34,8,256]{2,1,0:T(8,128)(2,1)S(1)}, bf16[34,8,256]{2,1,0:T(8,128)(2,1)S(1)}, u32[]{:S(2)}, u32[]{:S(2)}) collective-permute-start(bf16[34,8,256]{2,1,0:T(8,128)(2,1)S(1)} %get-tuple-element.54), channel_id=1, source_target_pairs={{1,2},{2,1},{5,6},{6,5},{9,10},{10,9},{13,14},{14,13},{17,18},{18,... | collective-permute-start | bytes 417800 | tf_op jit(solution)/shard_map/ppermute | solution.py:588
  14.4 2.9 %collective-permute-start.3 = (bf16[34,8,256]{2,1,0:T(8,128)(2,1)S(1)}, bf16[34,8,256]{2,1,0:T(8,128)(2,1)S(1)}, u32[]{:S(2)}, u32[]{:S(2)}) collective-permute-start(bf16[34,8,256]{2,1,0:T(8,128)(2,1)S(1)} %get-tuple-element.55), channel_id=1, source_target_pairs={{0,1},{1,0},{2,3},{3,2},{4,5},{5,4},{6,7},{7,6},{8,9},{9,8},{10,11... | collective-permute-start | bytes 417800 | tf_op jit(solution)/shard_map/ppermute | solution.py:589
  17.4 0.1 time_factors.1
  17.4 0.0 collective-permute-done.4
  17.4 0.0 collective-permute-done.5
  17.4 0.0 copy-start.4
  17.5 1.4 %collective-permute-start.9 = (bf16[4,16,2048]{2,1,0:T(8,128)(2,1)S(1)}, bf16[4,16,2048]{2,1,0:T(8,128)(2,1)S(1)}, u32[]{:S(2)}, u32[]{:S(2)}) collective-permute-start(bf16[4,16,2048]{2,1,0:T(8,128)(2,1)S(1)} %pad_maximum_fusion.1), channel_id=1, source_target_pairs={{0,2},{1,3},{2,0},{3,1},{4,6},{5,7},{6,4},{7,5},{8,10},{9,11},{10,... | collective-permute-start | bytes 786440 | tf_op jit(solution)/shard_map/ppermute | solution.py:593
  18.9 0.0 collective-permute-done.3.col_near_ref
  18.9 4.3 %fine_block.1 = (bf16[8,32,256]{2,1,0:T(8,128)(2,1)}, f32[2,4,16,1024]{3,2,1,0:T(8,128)S(1)}, bf16[2,4,16,1024]{3,2,1,0:T(8,128)(2,1)S(1)}) custom-call(bf16[8,32,256]{2,1,0:T(8,128)(2,1)S(1)} %bitcast.63, bf16[8,32,256]{2,1,0:T(8,128)(2,1)S(1)} %bitcast.65, bf16[9,32,256]{2,1,0:T(8,128)(2,1)S(1)} %collective-permute-done.row_far_ref, ...), custom_call_target="tpu_custom_call" | custom-call | tf_op jit(solution)/shard_map/fine_block/pallas_call | solution.py:297
  23.2 1.1 %collective-permute-start.7 = (bf16[2,4,16,1024]{3,2,1,0:T(8,128)(2,1)S(1)}, bf16[2,4,16,1024]{3,2,1,0:T(8,128)(2,1)S(1)}, u32[]{:S(2)}, u32[]{:S(2)}) collective-permute-start(bf16[2,4,16,1024]{3,2,1,0:T(8,128)(2,1)S(1)} %get-tuple-element.69), channel_id=1, source_target_pairs={{0,1},{1,0},{2,3},{3,2},{4,5},{5,4},{6,7},{7,6},{8,9},{9,8},{10,11... | collective-permute-start | bytes 786440 | tf_op jit(solution)/shard_map/ppermute | solution.py:593
  24.3 1.5 %collective-permute-done.9 = bf16[4,16,2048]{2,1,0:T(8,128)(2,1)S(1)} collective-permute-done((bf16[4,16,2048]{2,1,0:T(8,128)(2,1)S(1)}, bf16[4,16,2048]{2,1,0:T(8,128)(2,1)S(1)}, u32[]{:S(2)}, u32[]{:S(2)}) %collective-permute-start.9) | collective-permute-done | bytes 262176 | tf_op jit(solution)/shard_map/ppermute | solution.py:593
  25.8 0.0 collective-permute-start.11
  25.8 0.0 collective-permute-done.7
  25.8 0.1 convert_add_fusion.1
  25.9 1.7 %collective-permute-start.8 = (bf16[4,16,1024]{2,1,0:T(8,128)(2,1)S(1)}, bf16[4,16,1024]{2,1,0:T(8,128)(2,1)S(1)}, u32[]{:S(2)}, u32[]{:S(2)}) collective-permute-start(bf16[4,16,1024]{2,1,0:T(8,128)(2,1)S(1)} %fusion.4), channel_id=1, source_target_pairs={{0,2},{1,3},{2,0},{3,1},{4,6},{5,7},{6,4},{7,5},{8,10},{9,11},{10,... | collective-permute-start | bytes 393224 | tf_op jit(solution)/shard_map/ppermute | solution.py:593
  27.7 0.0 collective-permute-done.10
  27.7 0.0 collective-permute-done.11
  27.7 0.1 pad_maximum_fusion
  27.8 0.0 copy-start.3
  27.8 0.0 copy-start.5
  27.8 0.1 fusion.9
  27.9 0.9 %copy-done.3 = bf16[3,64,1024]{2,1,0:T(8,128)(2,1)S(1)} copy-done((bf16[3,64,1024]{2,1,0:T(8,128)(2,1)S(1)}, bf16[3,64,1024]{2,1,0:T(8,128)(2,1)}, u32[]{:S(2)}) %copy-start.3) | copy-done | bytes 393240
  28.8 0.0 copy-done.5
  28.8 2.2 %coarse_block.1 = (bf16[256,1024]{1,0:T(8,128)(2,1)S(1)}, bf16[256,1024]{1,0:T(8,128)(2,1)S(1)}) custom-call(bf16[256,1024]{1,0:T(8,128)(2,1)S(1)} %get-tuple-element.95.x_ref, bf16[256,1024]{1,0:T(8,128)(2,1)S(1)} %get-tuple-element.94.dy_ref, f32[1,1024]{1,0:T(1,128)S(1)} %get-tuple-element.71.factor_ref, bf16[3,64,1024]{2,1,0:T(8,128)(2,1)S(1)} %copy-done.3, ...), custom_call_target="tpu_custom_call" | custom-call | tf_op jit(solution)/shard_map/coarse_block/pallas_call | solution.py:374
  31.1 0.8 %collective-permute-done.8 = bf16[4,16,1024]{2,1,0:T(8,128)(2,1)S(1)} collective-permute-done((bf16[4,16,1024]{2,1,0:T(8,128)(2,1)S(1)}, bf16[4,16,1024]{2,1,0:T(8,128)(2,1)S(1)}, u32[]{:S(2)}, u32[]{:S(2)}) %collective-permute-start.8) | collective-permute-done | bytes 131104 | tf_op jit(solution)/shard_map/ppermute | solution.py:593
  31.9 1.6 %collective-permute-start.12 = (bf16[4,16,1024]{2,1,0:T(8,128)(2,1)S(1)}, bf16[4,16,1024]{2,1,0:T(8,128)(2,1)S(1)}, u32[]{:S(2)}, u32[]{:S(2)}) collective-permute-start(bf16[4,16,1024]{2,1,0:T(8,128)(2,1)S(1)} %fusion.3), channel_id=1, source_target_pairs={{0,16},{16,0},{1,17},{17,1},{2,18},{18,2},{3,19},{19,3},{4,20},{20... | collective-permute-start | bytes 393224 | tf_op jit(solution)/shard_map/ppermute | solution.py:593
  33.6 0.1 collective-permute-start.13
  33.6 3.5 %collective-permute-done.12 = bf16[4,16,1024]{2,1,0:T(8,128)(2,1)S(1)} collective-permute-done((bf16[4,16,1024]{2,1,0:T(8,128)(2,1)S(1)}, bf16[4,16,1024]{2,1,0:T(8,128)(2,1)S(1)}, u32[]{:S(2)}, u32[]{:S(2)}) %collective-permute-start.12) | collective-permute-done | bytes 131104 | tf_op jit(solution)/shard_map/ppermute | solution.py:593
  37.2 0.0 collective-permute-done.13
  37.2 0.1 convert_add_fusion
  37.3 1.7 %collective-permute-start.17 = (bf16[2,2,16,1024]{3,2,0,1:T(8,128)(2,1)S(1)}, bf16[2,2,16,1024]{3,2,0,1:T(8,128)(2,1)S(1)}, u32[]{:S(2)}, u32[]{:S(2)}) collective-permute-start(bf16[2,2,16,1024]{3,2,0,1:T(8,128)(2,1)S(1)} %fusion.5), channel_id=1, source_target_pairs={{0,4},{4,0},{8,12},{12,8},{1,5},{5,1},{9,13},{13,9},{2,6},{6,2},{1... | collective-permute-start | bytes 393224 | tf_op jit(solution)/shard_map/ppermute | solution.py:593
  39.0 0.5 collective-permute-start.14
  39.5 1.5 %collective-permute-start.20 = (bf16[96,1024]{1,0:T(8,128)(2,1)S(1)}, bf16[96,1024]{1,0:T(8,128)(2,1)S(1)}, u32[]{:S(2)}, u32[]{:S(2)}) collective-permute-start(bf16[96,1024]{1,0:T(8,128)(2,1)S(1)} %slice.93), channel_id=1, source_target_pairs={{0,16},{16,0},{1,17},{17,1},{2,18},{18,2},{3,19},{19,3},{4,20},{20... | collective-permute-start | bytes 589832 | tf_op jit(solution)/shard_map/ppermute | solution.py:593
  41.0 0.5 collective-permute-start.21
  41.5 1.5 %collective-permute-done.17 = bf16[2,2,16,1024]{3,2,0,1:T(8,128)(2,1)S(1)} collective-permute-done((bf16[2,2,16,1024]{3,2,0,1:T(8,128)(2,1)S(1)}, bf16[2,2,16,1024]{3,2,0,1:T(8,128)(2,1)S(1)}, u32[]{:S(2)}, u32[]{:S(2)}) %collective-permute-start.17) | collective-permute-done | bytes 131104 | tf_op jit(solution)/shard_map/ppermute | solution.py:593
  43.0 1.5 %collective-permute-start.18 = (bf16[2,1,16,1024]{3,2,1,0:T(8,128)(2,1)S(1)}, bf16[2,1,16,1024]{3,2,1,0:T(8,128)(2,1)S(1)}, u32[]{:S(2)}, u32[]{:S(2)}) collective-permute-start(bf16[2,1,16,1024]{3,2,1,0:T(8,128)(2,1)S(1)} %fusion.7), channel_id=1, source_target_pairs={{0,8},{4,12},{8,0},{12,4},{1,9},{5,13},{9,1},{13,5},{2,10},{6,14},... | collective-permute-start | bytes 196616 | tf_op jit(solution)/shard_map/ppermute | solution.py:593
  44.6 0.5 collective-permute-done.14
  45.1 1.4 %collective-permute-start.15 = (bf16[64,1024]{1,0:T(8,128)(2,1)S(1)}, bf16[64,1024]{1,0:T(8,128)(2,1)S(1)}, u32[]{:S(2)}, u32[]{:S(2)}) collective-permute-start(bf16[64,1024]{1,0:T(8,128)(2,1)S(1)} %add_convert_fusion.1), channel_id=1, source_target_pairs={{0,8},{4,12},{8,0},{12,4},{1,9},{5,13},{9,1},{13,5},{2,10},{6,14},... | collective-permute-start | bytes 393224 | tf_op jit(solution)/shard_map/ppermute | solution.py:593
  46.6 3.7 %collective-permute-done.18 = bf16[2,1,16,1024]{3,2,1,0:T(8,128)(2,1)S(1)} collective-permute-done((bf16[2,1,16,1024]{3,2,1,0:T(8,128)(2,1)S(1)}, bf16[2,1,16,1024]{3,2,1,0:T(8,128)(2,1)S(1)}, u32[]{:S(2)}, u32[]{:S(2)}) %collective-permute-start.18) | collective-permute-done | bytes 65568 | tf_op jit(solution)/shard_map/ppermute | solution.py:593
  50.3 2.8 %collective-permute-done.15 = bf16[64,1024]{1,0:T(8,128)(2,1)S(1)} collective-permute-done((bf16[64,1024]{1,0:T(8,128)(2,1)S(1)}, bf16[64,1024]{1,0:T(8,128)(2,1)S(1)}, u32[]{:S(2)}, u32[]{:S(2)}) %collective-permute-start.15) | collective-permute-done | bytes 131104 | tf_op jit(solution)/shard_map/ppermute | solution.py:593
  53.1 0.1 collective-permute-start.16
  53.2 2.0 %collective-permute-start.19 = (bf16[16,1024]{1,0:T(8,128)(2,1)S(1)}, bf16[16,1024]{1,0:T(8,128)(2,1)S(1)}, u32[]{:S(2)}, u32[]{:S(2)}) collective-permute-start(bf16[16,1024]{1,0:T(8,128)(2,1)S(1)} %fusion.8), channel_id=1, source_target_pairs={{0,2},{1,3},{2,0},{3,1},{4,6},{5,7},{6,4},{7,5},{8,10},{9,11},{10,... | collective-permute-start | bytes 98312 | tf_op jit(solution)/shard_map/ppermute | solution.py:593
  55.2 0.9 %pair_sum.1 = (bf16[3,64,1024]{2,1,0:T(8,128)(2,1)}, bf16[64,1024]{1,0:T(8,128)(2,1)}) custom-call(bf16[256,1024]{1,0:T(8,128)(2,1)S(1)} %get-tuple-element.79.own, bf16[96,1024]{1,0:T(8,128)(2,1)S(1)} %collective-permute-done.20.refs_0_, bf16[160,1024]{1,0:T(8,128)(2,1)S(1)} %collective-permute-done.21.refs_1_), custom_call_target="tpu_custom_call" | custom-call | tf_op jit(solution)/shard_map/pair_sum/pallas_call | solution.py:502
  56.1 2.4 %collective-permute-done.19.come_ref = bf16[16,1024]{1,0:T(8,128)(2,1)S(1)} collective-permute-done((bf16[16,1024]{1,0:T(8,128)(2,1)S(1)}, bf16[16,1024]{1,0:T(8,128)(2,1)S(1)}, u32[]{:S(2)}, u32[]{:S(2)}) %collective-permute-start.19) | collective-permute-done | bytes 32800 | tf_op jit(solution)/shard_map/ppermute | solution.py:593
  58.5 0.1 collective-permute-start.22
  58.6 1.4 %near_step.1 = (bf16[256,768]{1,0:T(8,128)(2,1)}, bf16[256,256]{1,0:T(8,128)(2,1)}, bf16[4,4,1024]{2,1,0:T(4,128)(2,1)}) custom-call(bf16[2,64,1024]{2,1,0:T(8,128)(2,1)S(1)} %pad_maximum_fusion.2.near_ref, bf16[4,4,1024]{2,1,0:T(4,128)(2,1)S(1)} %bitcast.68, f32[1,1024]{1,0:T(1,128)S(1)} %get-tuple-element.71.factor_ref, ...), custom_call_target="tpu_custom_call" | custom-call | tf_op jit(solution)/shard_map/near_step/pallas_call | solution.py:551
  60.0 0.1 collective-permute-done.22.far_ref
  60.1 0.7 %far_step.1 = (bf16[256,768]{1,0:T(8,128)(2,1)}, bf16[256,256]{1,0:T(8,128)(2,1)}) custom-call(bf16[2,64,1024]{2,1,0:T(8,128)(2,1)S(1)} %collective-permute-done.22.far_ref, bf16[256,768]{1,0:T(8,128)(2,1)} %get-tuple-element.88.qkv_in, bf16[256,256]{1,0:T(8,128)(2,1)} %get-tuple-element.89.out_in), custom_call_target="tpu_custom_call", output_to_operand_aliasing={{0}: (1, {}), {1}: (2, {})} | custom-call | tf_op jit(solution)/shard_map/far_step/pallas_call | solution.py:569
  (37 shorter events, 0.5 us)
Async XLA Ops:
  0.6 1.0 %copy-start.1 = (bf16[1,8,32,256]{3,2,1,0:T(8,128)(2,1)S(1)}, bf16[1,8,32,256]{3,2,1,0:T(8,128)(2,1)}, u32[]{:S(2)}) copy-start(bf16[1,8,32,256]{3,2,1,0:T(8,128)(2,1)} %param.14) | copy-start | bytes 393220
  1.7 6.7 %copy-start.6 = (bf16[1,4,4,1024]{3,2,1,0:T(4,128)(2,1)S(1)}, bf16[1,4,4,1024]{3,2,1,0:T(4,128)(2,1)}, u32[]{:S(2)}) copy-start(bf16[1,4,4,1024]{3,2,1,0:T(4,128)(2,1)} %param.15) | copy-start | bytes 98308
  1.7 6.6 %copy-start.7 = (bf16[1,4,4,1024]{3,2,1,0:T(4,128)(2,1)S(1)}, bf16[1,4,4,1024]{3,2,1,0:T(4,128)(2,1)}, u32[]{:S(2)}) copy-start(bf16[1,4,4,1024]{3,2,1,0:T(4,128)(2,1)} %param.16) | copy-start | bytes 98308
  1.7 11.7 %collective-permute-start = (bf16[9,32,256]{2,1,0:T(8,128)(2,1)S(1)}, bf16[9,32,256]{2,1,0:T(8,128)(2,1)S(1)}, u32[]{:S(2)}, u32[]{:S(2)}) collective-permute-start(bf16[9,32,256]{2,1,0:T(8,128)(2,1)S(1)} %get-tuple-element.50.second), channel_id=1, source_target_pairs={{4,8},{8,4},{5,9},{9,5},{6,10},{10,6},{7,11},{11,7},{20,24},{24,20... | collective-permute-start | bytes 442376 | tf_op jit(solution)/shard_map/ppermute | solution.py:588
  2.4 11.0 %collective-permute-start.1 = (bf16[9,32,256]{2,1,0:T(8,128)(2,1)S(1)}, bf16[9,32,256]{2,1,0:T(8,128)(2,1)S(1)}, u32[]{:S(2)}, u32[]{:S(2)}) collective-permute-start(bf16[9,32,256]{2,1,0:T(8,128)(2,1)S(1)} %get-tuple-element.51.first), channel_id=1, source_target_pairs={{0,4},{4,0},{8,12},{12,8},{1,5},{5,1},{9,13},{13,9},{2,6},{6,2},{1... | collective-permute-start | bytes 442376 | tf_op jit(solution)/shard_map/ppermute | solution.py:589
  8.3 5.1 %copy-start = (bf16[1,8,32,256]{3,2,1,0:T(8,128)(2,1)S(1)}, bf16[1,8,32,256]{3,2,1,0:T(8,128)(2,1)}, u32[]{:S(2)}) copy-start(bf16[1,8,32,256]{3,2,1,0:T(8,128)(2,1)} %param.13) | copy-start | bytes 393220
  8.3 9.1 %collective-permute-start.4 = (bf16[16,2048]{1,0:T(8,128)(2,1)S(1)}, bf16[16,2048]{1,0:T(8,128)(2,1)S(1)}, u32[]{:S(2)}, u32[]{:S(2)}) collective-permute-start(bf16[16,2048]{1,0:T(8,128)(2,1)S(1)} %pack_coarse.1), channel_id=1, source_target_pairs={{0,4},{4,0},{8,12},{12,8},{1,5},{5,1},{9,13},{13,9},{2,6},{6,2},{1... | collective-permute-start | bytes 196616 | tf_op jit(solution)/shard_map/ppermute | solution.py:593
  8.4 9.0 %collective-permute-start.5 = (bf16[16,2048]{1,0:T(8,128)(2,1)S(1)}, bf16[16,2048]{1,0:T(8,128)(2,1)S(1)}, u32[]{:S(2)}, u32[]{:S(2)}) collective-permute-start(bf16[16,2048]{1,0:T(8,128)(2,1)S(1)} %pack_coarse.1), channel_id=1, source_target_pairs={{0,8},{4,12},{8,0},{12,4},{1,9},{5,13},{9,1},{13,5},{2,10},{6,14},... | collective-permute-start | bytes 196616 | tf_op jit(solution)/shard_map/ppermute | solution.py:593
  10.3 7.1 %collective-permute-start.6 = (bf16[16,2048]{1,0:T(8,128)(2,1)S(1)}, bf16[16,2048]{1,0:T(8,128)(2,1)S(1)}, u32[]{:S(2)}, u32[]{:S(2)}) collective-permute-start(bf16[16,2048]{1,0:T(8,128)(2,1)S(1)} %pack_coarse.1), channel_id=1, source_target_pairs={{0,12},{4,8},{8,4},{12,0},{1,13},{5,9},{9,5},{13,1},{2,14},{6,10},... | collective-permute-start | bytes 196616 | tf_op jit(solution)/shard_map/ppermute | solution.py:593
  13.5 3.9 %copy-start.8 = (f32[1024]{0:T(1024)S(1)}, f32[1024]{0:T(1024)}, u32[]{:S(2)}) copy-start(f32[1024]{0:T(1024)} %param.19) | copy-start | bytes 12292
  13.5 3.9 %copy-start.9 = (f32[1,1024]{1,0:T(1,128)S(1)}, f32[1,1024]{1,0:T(1,128)}, u32[]{:S(2)}) copy-start(f32[1,1024]{1,0:T(1,128)} %constant.5.clone.coarse_freq) | copy-start | bytes 12292
  13.5 3.8 %copy-start.10 = (f32[256]{0:T(256)S(1)}, f32[256]{0:T(256)}, u32[]{:S(2)}) copy-start(f32[256]{0:T(256)} %param.18) | copy-start | bytes 3076
  13.5 3.8 %copy-start.11 = (f32[1,256]{1,0:T(1,128)S(1)}, f32[1,256]{1,0:T(1,128)}, u32[]{:S(2)}) copy-start(f32[1,256]{1,0:T(1,128)} %constant.4.clone.fine_freq) | copy-start | bytes 3076
  13.6 5.3 %copy-start.2 = (bf16[256,768]{1,0:T(8,128)(2,1)S(1)}, bf16[256,768]{1,0:T(8,128)(2,1)}, u32[]{:S(2)}) copy-start(bf16[256,768]{1,0:T(8,128)(2,1)} %qkv_ref.1) | copy-start | bytes 1179652
  13.6 5.2 %collective-permute-start.2 = (bf16[34,8,256]{2,1,0:T(8,128)(2,1)S(1)}, bf16[34,8,256]{2,1,0:T(8,128)(2,1)S(1)}, u32[]{:S(2)}, u32[]{:S(2)}) collective-permute-start(bf16[34,8,256]{2,1,0:T(8,128)(2,1)S(1)} %get-tuple-element.54), channel_id=1, source_target_pairs={{1,2},{2,1},{5,6},{6,5},{9,10},{10,9},{13,14},{14,13},{17,18},{18,... | collective-permute-start | bytes 417800 | tf_op jit(solution)/shard_map/ppermute | solution.py:588
  14.4 4.4 %collective-permute-start.3 = (bf16[34,8,256]{2,1,0:T(8,128)(2,1)S(1)}, bf16[34,8,256]{2,1,0:T(8,128)(2,1)S(1)}, u32[]{:S(2)}, u32[]{:S(2)}) collective-permute-start(bf16[34,8,256]{2,1,0:T(8,128)(2,1)S(1)} %get-tuple-element.55), channel_id=1, source_target_pairs={{0,1},{1,0},{2,3},{3,2},{4,5},{5,4},{6,7},{7,6},{8,9},{9,8},{10,11... | collective-permute-start | bytes 417800 | tf_op jit(solution)/shard_map/ppermute | solution.py:589
  17.4 1.4 %copy-start.4 = (bf16[256,256]{1,0:T(8,128)(2,1)S(1)}, bf16[256,256]{1,0:T(8,128)(2,1)}, u32[]{:S(2)}) copy-start(bf16[256,256]{1,0:T(8,128)(2,1)} %out_ref.1) | copy-start | bytes 393220
  17.5 8.3 %collective-permute-start.9 = (bf16[4,16,2048]{2,1,0:T(8,128)(2,1)S(1)}, bf16[4,16,2048]{2,1,0:T(8,128)(2,1)S(1)}, u32[]{:S(2)}, u32[]{:S(2)}) collective-permute-start(bf16[4,16,2048]{2,1,0:T(8,128)(2,1)S(1)} %pad_maximum_fusion.1), channel_id=1, source_target_pairs={{0,2},{1,3},{2,0},{3,1},{4,6},{5,7},{6,4},{7,5},{8,10},{9,11},{10,... | collective-permute-start | bytes 786440 | tf_op jit(solution)/shard_map/ppermute | solution.py:593
  23.2 2.6 %collective-permute-start.7 = (bf16[2,4,16,1024]{3,2,1,0:T(8,128)(2,1)S(1)}, bf16[2,4,16,1024]{3,2,1,0:T(8,128)(2,1)S(1)}, u32[]{:S(2)}, u32[]{:S(2)}) collective-permute-start(bf16[2,4,16,1024]{3,2,1,0:T(8,128)(2,1)S(1)} %get-tuple-element.69), channel_id=1, source_target_pairs={{0,1},{1,0},{2,3},{3,2},{4,5},{5,4},{6,7},{7,6},{8,9},{9,8},{10,11... | collective-permute-start | bytes 786440 | tf_op jit(solution)/shard_map/ppermute | solution.py:593
  24.3 3.3 %collective-permute-start.10 = (bf16[4,16,2048]{2,1,0:T(8,128)(2,1)S(1)}, bf16[4,16,2048]{2,1,0:T(8,128)(2,1)S(1)}, u32[]{:S(2)}, u32[]{:S(2)}) collective-permute-start(bf16[4,16,2048]{2,1,0:T(8,128)(2,1)S(1)} %pad_maximum_fusion.1), channel_id=1, source_target_pairs={{0,1},{1,0},{2,3},{3,2},{4,5},{5,4},{6,7},{7,6},{8,9},{9,8},{10,11... | collective-permute-start | bytes 786440 | tf_op jit(solution)/shard_map/ppermute | solution.py:593
  25.8 1.8 %collective-permute-start.11 = (bf16[4,16,2048]{2,1,0:T(8,128)(2,1)S(1)}, bf16[4,16,2048]{2,1,0:T(8,128)(2,1)S(1)}, u32[]{:S(2)}, u32[]{:S(2)}) collective-permute-start(bf16[4,16,2048]{2,1,0:T(8,128)(2,1)S(1)} %collective-permute-done.9), channel_id=1, source_target_pairs={{0,1},{1,0},{2,3},{3,2},{4,5},{5,4},{6,7},{7,6},{8,9},{9,8},{10,11... | collective-permute-start | bytes 786440 | tf_op jit(solution)/shard_map/ppermute | solution.py:593
  25.9 6.0 %collective-permute-start.8 = (bf16[4,16,1024]{2,1,0:T(8,128)(2,1)S(1)}, bf16[4,16,1024]{2,1,0:T(8,128)(2,1)S(1)}, u32[]{:S(2)}, u32[]{:S(2)}) collective-permute-start(bf16[4,16,1024]{2,1,0:T(8,128)(2,1)S(1)} %fusion.4), channel_id=1, source_target_pairs={{0,2},{1,3},{2,0},{3,1},{4,6},{5,7},{6,4},{7,5},{8,10},{9,11},{10,... | collective-permute-start | bytes 393224 | tf_op jit(solution)/shard_map/ppermute | solution.py:593
  27.8 1.0 %copy-start.3 = (bf16[3,64,1024]{2,1,0:T(8,128)(2,1)S(1)}, bf16[3,64,1024]{2,1,0:T(8,128)(2,1)}, u32[]{:S(2)}) copy-start(bf16[3,64,1024]{2,1,0:T(8,128)(2,1)} %qkv_hbm.1) | copy-start | bytes 1179652
  27.8 1.0 %copy-start.5 = (bf16[64,1024]{1,0:T(8,128)(2,1)S(1)}, bf16[64,1024]{1,0:T(8,128)(2,1)}, u32[]{:S(2)}) copy-start(bf16[64,1024]{1,0:T(8,128)(2,1)} %out_hbm.1) | copy-start | bytes 393220
  31.9 5.2 %collective-permute-start.12 = (bf16[4,16,1024]{2,1,0:T(8,128)(2,1)S(1)}, bf16[4,16,1024]{2,1,0:T(8,128)(2,1)S(1)}, u32[]{:S(2)}, u32[]{:S(2)}) collective-permute-start(bf16[4,16,1024]{2,1,0:T(8,128)(2,1)S(1)} %fusion.3), channel_id=1, source_target_pairs={{0,16},{16,0},{1,17},{17,1},{2,18},{18,2},{3,19},{19,3},{4,20},{20... | collective-permute-start | bytes 393224 | tf_op jit(solution)/shard_map/ppermute | solution.py:593
  33.6 3.6 %collective-permute-start.13 = (bf16[2,4,16,1024]{3,2,1,0:T(8,128)(2,1)S(1)}, bf16[2,4,16,1024]{3,2,1,0:T(8,128)(2,1)S(1)}, u32[]{:S(2)}, u32[]{:S(2)}) collective-permute-start(bf16[2,4,16,1024]{3,2,1,0:T(8,128)(2,1)S(1)} %bitcast.80), channel_id=1, source_target_pairs={{0,1},{1,0},{2,3},{3,2},{4,5},{5,4},{6,7},{7,6},{8,9},{9,8},{10,11... | collective-permute-start | bytes 786440 | tf_op jit(solution)/shard_map/ppermute | solution.py:593
  37.3 5.7 %collective-permute-start.17 = (bf16[2,2,16,1024]{3,2,0,1:T(8,128)(2,1)S(1)}, bf16[2,2,16,1024]{3,2,0,1:T(8,128)(2,1)S(1)}, u32[]{:S(2)}, u32[]{:S(2)}) collective-permute-start(bf16[2,2,16,1024]{3,2,0,1:T(8,128)(2,1)S(1)} %fusion.5), channel_id=1, source_target_pairs={{0,4},{4,0},{8,12},{12,8},{1,5},{5,1},{9,13},{13,9},{2,6},{6,2},{1... | collective-permute-start | bytes 393224 | tf_op jit(solution)/shard_map/ppermute | solution.py:593
  39.0 6.1 %collective-permute-start.14 = (bf16[64,1024]{1,0:T(8,128)(2,1)S(1)}, bf16[64,1024]{1,0:T(8,128)(2,1)S(1)}, u32[]{:S(2)}, u32[]{:S(2)}) collective-permute-start(bf16[64,1024]{1,0:T(8,128)(2,1)S(1)} %bitcast.77), channel_id=1, source_target_pairs={{0,4},{4,0},{8,12},{12,8},{1,5},{5,1},{9,13},{13,9},{2,6},{6,2},{1... | collective-permute-start | bytes 393224 | tf_op jit(solution)/shard_map/ppermute | solution.py:593
  39.5 15.7 %collective-permute-start.20 = (bf16[96,1024]{1,0:T(8,128)(2,1)S(1)}, bf16[96,1024]{1,0:T(8,128)(2,1)S(1)}, u32[]{:S(2)}, u32[]{:S(2)}) collective-permute-start(bf16[96,1024]{1,0:T(8,128)(2,1)S(1)} %slice.93), channel_id=1, source_target_pairs={{0,16},{16,0},{1,17},{17,1},{2,18},{18,2},{3,19},{19,3},{4,20},{20... | collective-permute-start | bytes 589832 | tf_op jit(solution)/shard_map/ppermute | solution.py:593
  41.0 14.2 %collective-permute-start.21 = (bf16[160,1024]{1,0:T(8,128)(2,1)S(1)}, bf16[160,1024]{1,0:T(8,128)(2,1)S(1)}, u32[]{:S(2)}, u32[]{:S(2)}) collective-permute-start(bf16[160,1024]{1,0:T(8,128)(2,1)S(1)} %slice.94), channel_id=1, source_target_pairs={{0,16},{16,0},{1,17},{17,1},{2,18},{18,2},{3,19},{19,3},{4,20},{20... | collective-permute-start | bytes 983048 | tf_op jit(solution)/shard_map/ppermute | solution.py:593
  43.0 7.2 %collective-permute-start.18 = (bf16[2,1,16,1024]{3,2,1,0:T(8,128)(2,1)S(1)}, bf16[2,1,16,1024]{3,2,1,0:T(8,128)(2,1)S(1)}, u32[]{:S(2)}, u32[]{:S(2)}) collective-permute-start(bf16[2,1,16,1024]{3,2,1,0:T(8,128)(2,1)S(1)} %fusion.7), channel_id=1, source_target_pairs={{0,8},{4,12},{8,0},{12,4},{1,9},{5,13},{9,1},{13,5},{2,10},{6,14},... | collective-permute-start | bytes 196616 | tf_op jit(solution)/shard_map/ppermute | solution.py:593
  45.1 7.9 %collective-permute-start.15 = (bf16[64,1024]{1,0:T(8,128)(2,1)S(1)}, bf16[64,1024]{1,0:T(8,128)(2,1)S(1)}, u32[]{:S(2)}, u32[]{:S(2)}) collective-permute-start(bf16[64,1024]{1,0:T(8,128)(2,1)S(1)} %add_convert_fusion.1), channel_id=1, source_target_pairs={{0,8},{4,12},{8,0},{12,4},{1,9},{5,13},{9,1},{13,5},{2,10},{6,14},... | collective-permute-start | bytes 393224 | tf_op jit(solution)/shard_map/ppermute | solution.py:593
  53.1 5.4 %collective-permute-start.16 = (bf16[64,1024]{1,0:T(8,128)(2,1)S(1)}, bf16[64,1024]{1,0:T(8,128)(2,1)S(1)}, u32[]{:S(2)}, u32[]{:S(2)}) collective-permute-start(bf16[64,1024]{1,0:T(8,128)(2,1)S(1)} %add_convert_fusion), channel_id=1, source_target_pairs={{0,2},{1,3},{2,0},{3,1},{4,6},{5,7},{6,4},{7,5},{8,10},{9,11},{10,... | collective-permute-start | bytes 393224 | tf_op jit(solution)/shard_map/ppermute | solution.py:593
  53.2 5.3 %collective-permute-start.19 = (bf16[16,1024]{1,0:T(8,128)(2,1)S(1)}, bf16[16,1024]{1,0:T(8,128)(2,1)S(1)}, u32[]{:S(2)}, u32[]{:S(2)}) collective-permute-start(bf16[16,1024]{1,0:T(8,128)(2,1)S(1)} %fusion.8), channel_id=1, source_target_pairs={{0,2},{1,3},{2,0},{3,1},{4,6},{5,7},{6,4},{7,5},{8,10},{9,11},{10,... | collective-permute-start | bytes 98312 | tf_op jit(solution)/shard_map/ppermute | solution.py:593
  58.5 1.6 %collective-permute-start.22 = (bf16[2,64,1024]{2,1,0:T(8,128)(2,1)S(1)}, bf16[2,64,1024]{2,1,0:T(8,128)(2,1)S(1)}, u32[]{:S(2)}, u32[]{:S(2)}) collective-permute-start(bf16[2,64,1024]{2,1,0:T(8,128)(2,1)S(1)} %pad_maximum_fusion.2.near_ref), channel_id=1, source_target_pairs={{0,1},{1,0},{2,3},{3,2},{4,5},{5,4},{6,7},{7,6},{8,9},{9,8},{10,11... | collective-permute-start | bytes 786440 | tf_op jit(solution)/shard_map/ppermute | solution.py:593
